TPU v7x, 128 devices: a whole 4x4x4 slice. The times are simulated.
128 devices in a mesh: seq: 64 (over x, y, z_hi, core), head: 2 (over z_lo).
Axes of the slice: x: 4, y: 4, z: 4 (z_hi: 2, z_lo: 2; z = z_hi * 2 + z_lo), core: 2. Of those that a mesh axis runs over, the one named last changes fastest.
Arguments:
- queries: bfloat16 [8, 32768, 128], P('head', 'seq'), may hold values from -6 to 6
- key_rows: bfloat16 [32768, 128], P('seq'), may hold values from -6 to 6
- value_rows: bfloat16 [32768, 128], P('seq'), may hold values from -6 to 6
- d_out: bfloat16 [8, 32768, 128], P('head', 'seq'), may hold values from -6 to 6
- seq_lengths: int32 [16], replicated, may hold values from 1 to 4096, 32768 in all
Outputs:
- attended: bfloat16 [8, 32768, 128], P('head', 'seq')
- grad_queries: bfloat16 [8, 32768, 128], P('head', 'seq')
- grad_keys: bfloat16 [32768, 128], P('seq')
- grad_values: bfloat16 [32768, 128], P('seq')
All inputs are finite; a program needn't handle non-finite values.
Results may differ from a plain program's by a relative error of at most 0.034.
Values may be sent and summed in bfloat16 or wider, within the bound.
No kernel may reach another device: no remote copies, remote signals or barrier semaphores. Data moves between devices by JAX's collectives and lax.ppermute only.
A program may use at most 128 MiB of HBM per device.

v0:
```python
from functools import partial
import math

import jax
import jax.numpy as jnp
from jax import lax
from jax.experimental import pallas as pl
from jax.experimental.pallas import tpu as pltpu
from jax.sharding import Mesh, PartitionSpec as P

NEGATIVE = -1e30
BLK = 512
HEADS = 4
HD = 128
NQ = HEADS * BLK
ROWS = 3
SLOTS = 4 * ROWS
SPAN = 9
SCALE = HD ** -0.5
LOG2 = SCALE * math.log2(math.e)
F32 = jnp.float32
BF16 = jnp.bfloat16
SEQ = ("x", "y", "zh", "core")


def dot(a, b):
    return lax.dot_general(a, b, (((1,), (0,)), ((), ())), preferred_element_type=F32)


def attention_kernel(*refs):
    len_ref, q_ref, do_ref = refs[:3]
    kv_refs = refs[3:15]
    o_ref, dq_ref = refs[15:17]
    out_refs = refs[17:23]
    (kvs, dkvs, qt, dot_t, probs, tile_max, run_max, total, acc, dq_acc, stage_p, stage_s, delta, in_sem, out_sem) = refs[23:]
    row = lax.axis_index("x") * 4 + lax.axis_index("y")
    zh = lax.axis_index("zh")
    core = lax.axis_index("core")
    place = zh * 2 + core

    def slot_of(j, dz, dc):
        return (2 - j) * 4 + (1 - zh if dz else zh) * 2 + (1 - core if dc else core)

    order = [(j, dz, dc) for j in range(ROWS) for dz in range(2) for dc in range(2)]
    copies = []
    for n, (j, dz, dc) in enumerate(order):
        copies.append(pltpu.make_async_copy(kv_refs[n], kvs.at[slot_of(j, dz, dc)], in_sem.at[n]))
        copies[-1].start()

    base = (row - 2) * (4 * BLK)
    first = base + (8 + place) * BLK
    q_pos = lax.broadcasted_iota(jnp.int32, (1, BLK), 1) + (8 + place) * BLK
    starts = jnp.zeros((1, BLK), jnp.int32) - base
    first_start = -base
    last_start = -base
    end = jnp.int32(0)
    for c in range(16):
        end = end + len_ref[c]
        rel = end - base
        starts = jnp.where(q_pos >= rel, rel, starts)
        first_start = jnp.where(end <= first, rel, first_start)
        last_start = jnp.where(end <= first + BLK - 1, rel, last_start)
    lo = first_start // BLK
    hi = 8 + place

    for h in range(HEADS):
        cols = slice(h * BLK, (h + 1) * BLK)
        qt[:, cols] = q_ref[h].T
        dot_t[:, cols] = do_ref[h].T
    run_max[...] = jnp.full((1, NQ), NEGATIVE, F32)
    total[...] = jnp.zeros((1, NQ), F32)
    acc[...] = jnp.zeros((HD, NQ), F32)
    dq_acc[...] = jnp.zeros((HD, NQ), F32)
    for copy in copies:
        copy.wait()

    def forward(t, masked):
        k = kvs[t, 0]
        v_t = kvs[t, 1].T
        if masked:
            k_pos = lax.broadcasted_iota(jnp.int32, (BLK, BLK), 0) + t * BLK
            allowed = (k_pos >= starts) & (k_pos <= q_pos)
        for h in range(HEADS):
            cols = slice(h * BLK, (h + 1) * BLK)
            s = dot(k, qt[:, cols])
            if masked:
                s = jnp.where(allowed, s, NEGATIVE)
            old = run_max[:, cols]
            new = jnp.maximum(old, jnp.max(s, axis=0, keepdims=True))
            p = jnp.exp2((s - new) * LOG2)
            factor = jnp.exp2((old - new) * LOG2)
            total[:, cols] = total[:, cols] * factor + jnp.sum(p, axis=0, keepdims=True)
            run_max[:, cols] = new
            tile_max[t - lo, :, cols] = new
            p = p.astype(BF16)
            probs[t - lo, :, cols] = p
            acc[:, cols] = acc[:, cols] * factor + dot(v_t, p)

    def forward_step(t, carry):
        masked = (t * BLK < last_start) | (t == hi)

        @pl.when(masked)
        def _():
            forward(t, True)

        @pl.when(jnp.logical_not(masked))
        def _():
            forward(t, False)

        return carry

    lax.fori_loop(lo, hi + 1, forward_step, 0)

    total[...] = 1.0 / total[...]
    for h in range(HEADS):
        cols = slice(h * BLK, (h + 1) * BLK)
        o = (acc[:, cols] * total[:, cols]).astype(BF16)
        o_ref[h] = o.T
        delta[:, cols] = jnp.sum(o.astype(F32) * dot_t[:, cols].astype(F32), axis=0, keepdims=True)

    def backward_step(t, carry):
        k_t = kvs[t, 0].T
        v = kvs[t, 1]
        for h in range(HEADS):
            cols = slice(h * BLK, (h + 1) * BLK)
            factor = jnp.exp2((tile_max[t - lo, :, cols] - run_max[:, cols]) * LOG2) * total[:, cols]
            p = probs[t - lo, :, cols].astype(F32) * factor
            stage_p[:, cols] = p.astype(BF16)
            dp = dot(v, dot_t[:, cols])
            ds = (p * (dp - delta[:, cols])).astype(BF16)
            stage_s[:, cols] = ds
            dq_acc[:, cols] += dot(k_t, ds)
        dkvs[t, 1] = dot(stage_p[...], do_ref[...].reshape(NQ, HD)).astype(BF16)
        dkvs[t, 0] = (dot(stage_s[...], q_ref[...].reshape(NQ, HD)) * SCALE).astype(BF16)
        return carry

    lax.fori_loop(lo, hi + 1, backward_step, 0)

    def clear(t, carry):
        dkvs[t] = jnp.zeros((2, BLK, HD), BF16)
        return carry

    lax.fori_loop(0, lo, clear, 0)
    lax.fori_loop(hi + 1, SLOTS, clear, 0)
    copies = []
    for n, (j, dz, dc) in enumerate(order):
        copies.append(pltpu.make_async_copy(dkvs.at[slot_of(j, dz, dc)], out_refs[j * 2 + dc].at[dz], out_sem.at[n]))
        copies[-1].start()
    for h in range(HEADS):
        cols = slice(h * BLK, (h + 1) * BLK)
        dq_ref[h] = (dq_acc[:, cols] * SCALE).astype(BF16).T
    for copy in copies:
        copy.wait()


def attention(seq_lengths, queries, d_out, blocks):
    vmem = pl.BlockSpec(memory_space=pltpu.VMEM)
    anywhere = pl.BlockSpec(memory_space=pl.ANY)
    pair = jax.ShapeDtypeStruct((2, 2, BLK, HD), BF16)
    rows = jax.ShapeDtypeStruct((HEADS, BLK, HD), BF16)
    return pl.pallas_call(
        attention_kernel,
        out_shape=(rows, rows) + (pair,) * 6,
        in_specs=[pl.BlockSpec(memory_space=pltpu.SMEM), vmem, vmem] + [anywhere] * 12,
        out_specs=[vmem, vmem] + [anywhere] * 6,
        scratch_shapes=[
            pltpu.VMEM((SLOTS, 2, BLK, HD), BF16),
            pltpu.VMEM((SLOTS, 2, BLK, HD), BF16),
            pltpu.VMEM((HD, NQ), BF16),
            pltpu.VMEM((HD, NQ), BF16),
            pltpu.VMEM((SPAN, BLK, NQ), BF16),
            pltpu.VMEM((SPAN, 1, NQ), F32),
            pltpu.VMEM((1, NQ), F32),
            pltpu.VMEM((1, NQ), F32),
            pltpu.VMEM((HD, NQ), F32),
            pltpu.VMEM((HD, NQ), F32),
            pltpu.VMEM((BLK, NQ), BF16),
            pltpu.VMEM((BLK, NQ), BF16),
            pltpu.VMEM((1, NQ), F32),
            pltpu.SemaphoreType.DMA((SLOTS,)),
            pltpu.SemaphoreType.DMA((SLOTS,)),
        ],
        compiler_params=pltpu.CompilerParams(vmem_limit_bytes=56 << 20),
        cost_estimate=pl.CostEstimate(flops=8 << 30, bytes_accessed=16 << 20, transcendentals=9 << 20),
        name="attention",
    )(seq_lengths, queries, d_out, *blocks)


def swap_core(value):
    return lax.ppermute(value, "core", [(0, 1), (1, 0)])


def swap_z(value):
    return lax.ppermute(value, ("zh", "zl"), [(0, 3), (3, 0), (1, 2), (2, 1)])


def swap_head(value):
    return lax.ppermute(value, "zl", [(0, 1), (1, 0)])


def shift_row(value, by):
    return lax.ppermute(value, ("x", "y"), [(r, (r + by) % 16) for r in range(16)])


def added(a, b):
    return (a.astype(F32) + b.astype(F32)).astype(BF16)


def on_device(queries, key_rows, value_rows, d_out, seq_lengths):
    own = jnp.stack([key_rows, value_rows])
    row1 = shift_row(own, 1)
    side0 = swap_z(own)
    row2 = shift_row(row1, 1)
    side1 = swap_z(row1)
    side2 = swap_z(row2)
    mine = [own, side0, row1, side1, row2, side2]
    blocks = []
    for block in mine:
        blocks += [block, swap_core(block)]
    attended, grad_queries, *parts = attention(seq_lengths, queries, d_out, blocks)

    def column(j):
        keep, send = parts[2 * j], parts[2 * j + 1]
        both = added(keep, swap_core(send))
        return added(both[0], swap_z(both[1]))

    back = shift_row(column(2), -1)
    back = shift_row(added(column(1), back), -1)
    half = added(column(0), back)
    other = swap_head(half)
    grads = half.astype(F32) + other.astype(F32)
    grads = grads.astype(BF16)
    return attended, grad_queries, grads[0], grads[1]


def solution(mesh):
    fine = Mesh(mesh.devices.reshape(4, 4, 2, 2, 2), ("x", "y", "zh", "core", "zl"))
    tokens = P("zl", SEQ, None)
    rows = P(SEQ, None)
    return jax.shard_map(
        on_device,
        mesh=fine,
        in_specs=(tokens, rows, rows, tokens, P()),
        out_specs=(tokens, tokens, rows, rows),
        check_vma=False,
    )
```

profile of v0, /device:TPU:30, one launch (start us, length us, event | category | flops | bytes accessed | tf_op | source)
XLA Modules:
  0.0 133.1 jit_solution(7501632363312153741)
XLA Ops:
  0.6 1.0 pad_maximum_fusion.refs_3_
  1.6 0.1 collective-permute-start.3
  1.8 8.0 %collective-permute-done.3.refs_7_ = bf16[2,512,128]{2,1,0:T(8,128)(2,1)S(1)} collective-permute-done((bf16[2,512,128]{2,1,0:T(8,128)(2,1)S(1)}, bf16[2,512,128]{2,1,0:T(8,128)(2,1)S(1)}, u32[]{:S(2)}, u32[]{:S(2)}) %collective-permute-start.3) | collective-permute-done | bytes 262176 | tf_op jit(solution)/shard_map/ppermute | solution.py:202
  9.8 3.6 %collective-permute-start.7 = (bf16[2,512,128]{2,1,0:T(8,128)(2,1)S(1)}, bf16[2,512,128]{2,1,0:T(8,128)(2,1)S(1)}, u32[]{:S(2)}, u32[]{:S(2)}) collective-permute-start(bf16[2,512,128]{2,1,0:T(8,128)(2,1)S(1)} %collective-permute-done.3.refs_7_), channel_id=1, source_target_pairs={{0,8},{8,16},{16,24},{24,32},{32,40},{40,48},{48,56},{56,64},{64,7... | collective-permute-start | bytes 786440 | tf_op jit(solution)/shard_map/ppermute | solution.py:202
  13.4 4.0 %collective-permute-start.1 = (bf16[2,512,128]{2,1,0:T(8,128)(2,1)S(1)}, bf16[2,512,128]{2,1,0:T(8,128)(2,1)S(1)}, u32[]{:S(2)}, u32[]{:S(2)}) collective-permute-start(bf16[2,512,128]{2,1,0:T(8,128)(2,1)S(1)} %pad_maximum_fusion.refs_3_), channel_id=1, source_target_pairs={{0,5},{5,0},{1,4},{4,1},{2,7},{7,2},{3,6},{6,3},{8,13},{13,8},{9,1... | collective-permute-start | bytes 786440 | tf_op jit(solution)/shard_map/ppermute | solution.py:194
  17.4 0.0 collective-permute-start
  17.4 0.0 collective-permute-start.5
  17.4 0.9 collective-permute-done.7.refs_11_
  18.3 3.9 %collective-permute-start.9 = (bf16[2,512,128]{2,1,0:T(8,128)(2,1)S(1)}, bf16[2,512,128]{2,1,0:T(8,128)(2,1)S(1)}, u32[]{:S(2)}, u32[]{:S(2)}) collective-permute-start(bf16[2,512,128]{2,1,0:T(8,128)(2,1)S(1)} %collective-permute-done.7.refs_11_), channel_id=1, source_target_pairs={{0,5},{5,0},{1,4},{4,1},{2,7},{7,2},{3,6},{6,3},{8,13},{13,8},{9,1... | collective-permute-start | bytes 786440 | tf_op jit(solution)/shard_map/ppermute | solution.py:194
  22.3 0.0 collective-permute-start.4
  22.3 1.9 %collective-permute-done.1.refs_5_ = bf16[2,512,128]{2,1,0:T(8,128)(2,1)S(1)} collective-permute-done((bf16[2,512,128]{2,1,0:T(8,128)(2,1)S(1)}, bf16[2,512,128]{2,1,0:T(8,128)(2,1)S(1)}, u32[]{:S(2)}, u32[]{:S(2)}) %collective-permute-start.1) | collective-permute-done | bytes 262176 | tf_op jit(solution)/shard_map/ppermute | solution.py:194
  24.2 0.0 collective-permute-start.2
  24.2 0.0 collective-permute-done.refs_4_
  24.2 0.5 collective-permute-start.8
  24.7 5.1 %collective-permute-done.5.refs_9_ = bf16[2,512,128]{2,1,0:T(8,128)(2,1)S(1)} collective-permute-done((bf16[2,512,128]{2,1,0:T(8,128)(2,1)S(1)}, bf16[2,512,128]{2,1,0:T(8,128)(2,1)S(1)}, u32[]{:S(2)}, u32[]{:S(2)}) %collective-permute-start.5) | collective-permute-done | bytes 262176 | tf_op jit(solution)/shard_map/ppermute | solution.py:194
  29.8 0.0 collective-permute-start.6
  29.8 4.2 %collective-permute-done.9.refs_13_ = bf16[2,512,128]{2,1,0:T(8,128)(2,1)S(1)} collective-permute-done((bf16[2,512,128]{2,1,0:T(8,128)(2,1)S(1)}, bf16[2,512,128]{2,1,0:T(8,128)(2,1)S(1)}, u32[]{:S(2)}, u32[]{:S(2)}) %collective-permute-start.9) | collective-permute-done | bytes 262176 | tf_op jit(solution)/shard_map/ppermute | solution.py:194
  34.0 0.0 collective-permute-start.10
  34.0 0.0 collective-permute-done.4.refs_8_
  34.0 0.0 collective-permute-done.8.refs_12_
  34.0 0.0 collective-permute-done.6.refs_10_
  34.0 1.5 %collective-permute-done.10.refs_14_ = bf16[2,512,128]{2,1,0:T(8,128)(2,1)S(1)} collective-permute-done((bf16[2,512,128]{2,1,0:T(8,128)(2,1)S(1)}, bf16[2,512,128]{2,1,0:T(8,128)(2,1)S(1)}, u32[]{:S(2)}, u32[]{:S(2)}) %collective-permute-start.10) | collective-permute-done | bytes 262176 | tf_op jit(solution)/shard_map/ppermute | solution.py:190
  35.6 0.7 copy-done.13
  36.3 37.7 %attention.1 = (bf16[4,512,128]{2,1,0:T(8,128)(2,1)}, bf16[4,512,128]{2,1,0:T(8,128)(2,1)}, bf16[2,2,512,128]{3,2,1,0:T(8,128)(2,1)}, bf16[2,2,512,128]{3,2,1,0:...) custom-call(s32[16]{0:T(128)} %refs_0_.1, ...), custom_call_target="tpu_custom_call" | custom-call | flops 8589934592 | bytes 16777216 | tf_op jit(solution)/shard_map/attention/pallas_call | solution.py:161
  74.0 5.2 %collective-permute-start.15 = (bf16[2,2,512,128]{3,2,1,0:T(8,128)(2,1)}, bf16[2,2,512,128]{3,2,1,0:T(8,128)(2,1)S(1)}, u32[]{:S(2)}, u32[]{:S(2)}) collective-permute-start(bf16[2,2,512,128]{3,2,1,0:T(8,128)(2,1)} %get-tuple-element.19), channel_id=1, source_target_pairs={{0,2},{2,0},{1,3},{3,1},{4,6},{6,4},{5,7},{7,5},{8,10},{10,8},{9,1... | collective-permute-start | bytes 1572872 | tf_op jit(solution)/shard_map/ppermute | solution.py:190
  79.2 0.1 collective-permute-start.13
  79.3 0.4 collective-permute-start.11
  79.7 1.2 collective-permute-done.15
  81.0 1.2 add_convert_fusion
  82.2 15.0 %collective-permute-start.16 = (bf16[2,512,128]{2,1,0:T(8,128)(2,1)S(1)}, bf16[2,512,128]{2,1,0:T(8,128)(2,1)S(1)}, u32[]{:S(2)}, u32[]{:S(2)}) collective-permute-start(bf16[2,512,128]{2,1,0:T(8,128)(2,1)S(1)} %slice_bitcast_fusion), channel_id=1, source_target_pairs={{0,5},{5,0},{1,4},{4,1},{2,7},{7,2},{3,6},{6,3},{8,13},{13,8},{9,1... | collective-permute-start | bytes 786440 | tf_op jit(solution)/shard_map/ppermute | solution.py:194
  97.2 0.1 add_convert_fusion.1
  97.4 1.0 collective-permute-start.14
  98.4 6.0 %collective-permute-done.16 = bf16[2,512,128]{2,1,0:T(8,128)(2,1)S(1)} collective-permute-done((bf16[2,512,128]{2,1,0:T(8,128)(2,1)S(1)}, bf16[2,512,128]{2,1,0:T(8,128)(2,1)S(1)}, u32[]{:S(2)}, u32[]{:S(2)}) %collective-permute-start.16) | collective-permute-done | bytes 262176 | tf_op jit(solution)/shard_map/ppermute | solution.py:194
  104.3 0.1 fusion
  104.4 0.1 collective-permute-start.17
  104.5 0.0 collective-permute-done.11
  104.5 0.1 add_convert_fusion.2
  104.7 3.3 %collective-permute-start.12 = (bf16[2,512,128]{2,1,0:T(8,128)(2,1)S(1)}, bf16[2,512,128]{2,1,0:T(8,128)(2,1)S(1)}, u32[]{:S(2)}, u32[]{:S(2)}) collective-permute-start(bf16[2,512,128]{2,1,0:T(8,128)(2,1)S(1)} %slice_bitcast_fusion.4), channel_id=1, source_target_pairs={{0,5},{5,0},{1,4},{4,1},{2,7},{7,2},{3,6},{6,3},{8,13},{13,8},{9,1... | collective-permute-start | bytes 786440 | tf_op jit(solution)/shard_map/ppermute | solution.py:194
  108.0 2.0 %collective-permute-done.14 = bf16[2,512,128]{2,1,0:T(8,128)(2,1)S(1)} collective-permute-done((bf16[2,512,128]{2,1,0:T(8,128)(2,1)S(1)}, bf16[2,512,128]{2,1,0:T(8,128)(2,1)S(1)}, u32[]{:S(2)}, u32[]{:S(2)}) %collective-permute-start.14) | collective-permute-done | bytes 262176 | tf_op jit(solution)/shard_map/ppermute | solution.py:194
  109.9 5.5 %collective-permute-done.17 = bf16[2,512,128]{2,1,0:T(8,128)(2,1)S(1)} collective-permute-done((bf16[2,512,128]{2,1,0:T(8,128)(2,1)S(1)}, bf16[2,512,128]{2,1,0:T(8,128)(2,1)S(1)}, u32[]{:S(2)}, u32[]{:S(2)}) %collective-permute-start.17) | collective-permute-done | bytes 262176 | tf_op jit(solution)/shard_map/ppermute | solution.py:202
  115.5 0.1 add_convert_fusion.5
  115.6 0.1 collective-permute-start.18
  115.7 10.1 %collective-permute-done.18 = bf16[2,512,128]{2,1,0:T(8,128)(2,1)S(1)} collective-permute-done((bf16[2,512,128]{2,1,0:T(8,128)(2,1)S(1)}, bf16[2,512,128]{2,1,0:T(8,128)(2,1)S(1)}, u32[]{:S(2)}, u32[]{:S(2)}) %collective-permute-start.18) | collective-permute-done | bytes 262176 | tf_op jit(solution)/shard_map/ppermute | solution.py:202
  125.8 0.1 add_convert_fusion.4
  125.9 0.1 collective-permute-start.19
  126.0 6.4 %collective-permute-done.19 = bf16[2,512,128]{2,1,0:T(8,128)(2,1)S(1)} collective-permute-done((bf16[2,512,128]{2,1,0:T(8,128)(2,1)S(1)}, bf16[2,512,128]{2,1,0:T(8,128)(2,1)S(1)}, u32[]{:S(2)}, u32[]{:S(2)}) %collective-permute-start.19) | collective-permute-done | bytes 262176 | tf_op jit(solution)/shard_map/ppermute | solution.py:198
  132.3 0.1 add_convert_fusion.3
  132.4 0.7 slice_bitcast_fusion.6
  (33 shorter events, 0.1 us)
Async XLA Ops:
  1.6 33.9 %copy-start.2 = (bf16[2,512,128]{2,1,0:T(8,128)(2,1)}, bf16[2,512,128]{2,1,0:T(8,128)(2,1)S(1)}, u32[]{:S(2)}) copy-start(bf16[2,512,128]{2,1,0:T(8,128)(2,1)S(1)} %pad_maximum_fusion.refs_3_) | copy-start | bytes 786436
  1.6 8.1 %collective-permute-start.3 = (bf16[2,512,128]{2,1,0:T(8,128)(2,1)S(1)}, bf16[2,512,128]{2,1,0:T(8,128)(2,1)S(1)}, u32[]{:S(2)}, u32[]{:S(2)}) collective-permute-start(bf16[2,512,128]{2,1,0:T(8,128)(2,1)S(1)} %pad_maximum_fusion.refs_3_), channel_id=1, source_target_pairs={{0,8},{8,16},{16,24},{24,32},{32,40},{40,48},{48,56},{56,64},{64,7... | collective-permute-start | bytes 786440 | tf_op jit(solution)/shard_map/ppermute | solution.py:202
  9.8 25.7 %copy-start.3 = (bf16[2,512,128]{2,1,0:T(8,128)(2,1)}, bf16[2,512,128]{2,1,0:T(8,128)(2,1)S(1)}, u32[]{:S(2)}) copy-start(bf16[2,512,128]{2,1,0:T(8,128)(2,1)S(1)} %collective-permute-done.3.refs_7_) | copy-start | bytes 786436
  9.8 8.6 %collective-permute-start.7 = (bf16[2,512,128]{2,1,0:T(8,128)(2,1)S(1)}, bf16[2,512,128]{2,1,0:T(8,128)(2,1)S(1)}, u32[]{:S(2)}, u32[]{:S(2)}) collective-permute-start(bf16[2,512,128]{2,1,0:T(8,128)(2,1)S(1)} %collective-permute-done.3.refs_7_), channel_id=1, source_target_pairs={{0,8},{8,16},{16,24},{24,32},{32,40},{40,48},{48,56},{56,64},{64,7... | collective-permute-start | bytes 786440 | tf_op jit(solution)/shard_map/ppermute | solution.py:202
  13.4 10.8 %collective-permute-start.1 = (bf16[2,512,128]{2,1,0:T(8,128)(2,1)S(1)}, bf16[2,512,128]{2,1,0:T(8,128)(2,1)S(1)}, u32[]{:S(2)}, u32[]{:S(2)}) collective-permute-start(bf16[2,512,128]{2,1,0:T(8,128)(2,1)S(1)} %pad_maximum_fusion.refs_3_), channel_id=1, source_target_pairs={{0,5},{5,0},{1,4},{4,1},{2,7},{7,2},{3,6},{6,3},{8,13},{13,8},{9,1... | collective-permute-start | bytes 786440 | tf_op jit(solution)/shard_map/ppermute | solution.py:194
  17.4 6.8 %collective-permute-start = (bf16[2,512,128]{2,1,0:T(8,128)(2,1)S(1)}, bf16[2,512,128]{2,1,0:T(8,128)(2,1)S(1)}, u32[]{:S(2)}, u32[]{:S(2)}) collective-permute-start(bf16[2,512,128]{2,1,0:T(8,128)(2,1)S(1)} %pad_maximum_fusion.refs_3_), channel_id=1, source_target_pairs={{0,2},{2,0},{1,3},{3,1},{4,6},{6,4},{5,7},{7,5},{8,10},{10,8},{9,1... | collective-permute-start | bytes 786440 | tf_op jit(solution)/shard_map/ppermute | solution.py:190
  17.4 12.4 %collective-permute-start.5 = (bf16[2,512,128]{2,1,0:T(8,128)(2,1)S(1)}, bf16[2,512,128]{2,1,0:T(8,128)(2,1)S(1)}, u32[]{:S(2)}, u32[]{:S(2)}) collective-permute-start(bf16[2,512,128]{2,1,0:T(8,128)(2,1)S(1)} %collective-permute-done.3.refs_7_), channel_id=1, source_target_pairs={{0,5},{5,0},{1,4},{4,1},{2,7},{7,2},{3,6},{6,3},{8,13},{13,8},{9,1... | collective-permute-start | bytes 786440 | tf_op jit(solution)/shard_map/ppermute | solution.py:194
  18.3 17.2 %copy-start.4 = (bf16[2,512,128]{2,1,0:T(8,128)(2,1)}, bf16[2,512,128]{2,1,0:T(8,128)(2,1)S(1)}, u32[]{:S(2)}) copy-start(bf16[2,512,128]{2,1,0:T(8,128)(2,1)S(1)} %collective-permute-done.7.refs_11_) | copy-start | bytes 786436
  18.3 15.6 %collective-permute-start.9 = (bf16[2,512,128]{2,1,0:T(8,128)(2,1)S(1)}, bf16[2,512,128]{2,1,0:T(8,128)(2,1)S(1)}, u32[]{:S(2)}, u32[]{:S(2)}) collective-permute-start(bf16[2,512,128]{2,1,0:T(8,128)(2,1)S(1)} %collective-permute-done.7.refs_11_), channel_id=1, source_target_pairs={{0,5},{5,0},{1,4},{4,1},{2,7},{7,2},{3,6},{6,3},{8,13},{13,8},{9,1... | collective-permute-start | bytes 786440 | tf_op jit(solution)/shard_map/ppermute | solution.py:194
  22.3 11.7 %collective-permute-start.4 = (bf16[2,512,128]{2,1,0:T(8,128)(2,1)S(1)}, bf16[2,512,128]{2,1,0:T(8,128)(2,1)S(1)}, u32[]{:S(2)}, u32[]{:S(2)}) collective-permute-start(bf16[2,512,128]{2,1,0:T(8,128)(2,1)S(1)} %collective-permute-done.3.refs_7_), channel_id=1, source_target_pairs={{0,2},{2,0},{1,3},{3,1},{4,6},{6,4},{5,7},{7,5},{8,10},{10,8},{9,1... | collective-permute-start | bytes 786440 | tf_op jit(solution)/shard_map/ppermute | solution.py:190
  24.2 11.3 %copy-start.5 = (bf16[2,512,128]{2,1,0:T(8,128)(2,1)}, bf16[2,512,128]{2,1,0:T(8,128)(2,1)S(1)}, u32[]{:S(2)}) copy-start(bf16[2,512,128]{2,1,0:T(8,128)(2,1)S(1)} %collective-permute-done.1.refs_5_) | copy-start | bytes 786436
  24.2 9.8 %collective-permute-start.2 = (bf16[2,512,128]{2,1,0:T(8,128)(2,1)S(1)}, bf16[2,512,128]{2,1,0:T(8,128)(2,1)S(1)}, u32[]{:S(2)}, u32[]{:S(2)}) collective-permute-start(bf16[2,512,128]{2,1,0:T(8,128)(2,1)S(1)} %collective-permute-done.1.refs_5_), channel_id=1, source_target_pairs={{0,2},{2,0},{1,3},{3,1},{4,6},{6,4},{5,7},{7,5},{8,10},{10,8},{9,1... | collective-permute-start | bytes 786440 | tf_op jit(solution)/shard_map/ppermute | solution.py:190
  24.2 11.3 %copy-start.6 = (bf16[2,512,128]{2,1,0:T(8,128)(2,1)}, bf16[2,512,128]{2,1,0:T(8,128)(2,1)S(1)}, u32[]{:S(2)}) copy-start(bf16[2,512,128]{2,1,0:T(8,128)(2,1)S(1)} %collective-permute-done.refs_4_) | copy-start | bytes 786436
  24.2 9.8 %collective-permute-start.8 = (bf16[2,512,128]{2,1,0:T(8,128)(2,1)S(1)}, bf16[2,512,128]{2,1,0:T(8,128)(2,1)S(1)}, u32[]{:S(2)}, u32[]{:S(2)}) collective-permute-start(bf16[2,512,128]{2,1,0:T(8,128)(2,1)S(1)} %collective-permute-done.7.refs_11_), channel_id=1, source_target_pairs={{0,2},{2,0},{1,3},{3,1},{4,6},{6,4},{5,7},{7,5},{8,10},{10,8},{9,1... | collective-permute-start | bytes 786440 | tf_op jit(solution)/shard_map/ppermute | solution.py:190
  29.8 5.7 %copy-start.7 = (bf16[2,512,128]{2,1,0:T(8,128)(2,1)}, bf16[2,512,128]{2,1,0:T(8,128)(2,1)S(1)}, u32[]{:S(2)}) copy-start(bf16[2,512,128]{2,1,0:T(8,128)(2,1)S(1)} %collective-permute-done.5.refs_9_) | copy-start | bytes 786436
  29.8 4.2 %collective-permute-start.6 = (bf16[2,512,128]{2,1,0:T(8,128)(2,1)S(1)}, bf16[2,512,128]{2,1,0:T(8,128)(2,1)S(1)}, u32[]{:S(2)}, u32[]{:S(2)}) collective-permute-start(bf16[2,512,128]{2,1,0:T(8,128)(2,1)S(1)} %collective-permute-done.5.refs_9_), channel_id=1, source_target_pairs={{0,2},{2,0},{1,3},{3,1},{4,6},{6,4},{5,7},{7,5},{8,10},{10,8},{9,1... | collective-permute-start | bytes 786440 | tf_op jit(solution)/shard_map/ppermute | solution.py:190
  34.0 1.6 %copy-start.8 = (bf16[2,512,128]{2,1,0:T(8,128)(2,1)}, bf16[2,512,128]{2,1,0:T(8,128)(2,1)S(1)}, u32[]{:S(2)}) copy-start(bf16[2,512,128]{2,1,0:T(8,128)(2,1)S(1)} %collective-permute-done.9.refs_13_) | copy-start | bytes 786436
  34.0 1.5 %collective-permute-start.10 = (bf16[2,512,128]{2,1,0:T(8,128)(2,1)S(1)}, bf16[2,512,128]{2,1,0:T(8,128)(2,1)S(1)}, u32[]{:S(2)}, u32[]{:S(2)}) collective-permute-start(bf16[2,512,128]{2,1,0:T(8,128)(2,1)S(1)} %collective-permute-done.9.refs_13_), channel_id=1, source_target_pairs={{0,2},{2,0},{1,3},{3,1},{4,6},{6,4},{5,7},{7,5},{8,10},{10,8},{9,1... | collective-permute-start | bytes 786440 | tf_op jit(solution)/shard_map/ppermute | solution.py:190
  34.0 1.6 %copy-start.9 = (bf16[2,512,128]{2,1,0:T(8,128)(2,1)}, bf16[2,512,128]{2,1,0:T(8,128)(2,1)S(1)}, u32[]{:S(2)}) copy-start(bf16[2,512,128]{2,1,0:T(8,128)(2,1)S(1)} %collective-permute-done.4.refs_8_) | copy-start | bytes 786436
  34.0 1.6 %copy-start.10 = (bf16[2,512,128]{2,1,0:T(8,128)(2,1)}, bf16[2,512,128]{2,1,0:T(8,128)(2,1)S(1)}, u32[]{:S(2)}) copy-start(bf16[2,512,128]{2,1,0:T(8,128)(2,1)S(1)} %collective-permute-done.2.refs_6_) | copy-start | bytes 786436
  34.0 1.6 %copy-start.11 = (bf16[2,512,128]{2,1,0:T(8,128)(2,1)}, bf16[2,512,128]{2,1,0:T(8,128)(2,1)S(1)}, u32[]{:S(2)}) copy-start(bf16[2,512,128]{2,1,0:T(8,128)(2,1)S(1)} %collective-permute-done.8.refs_12_) | copy-start | bytes 786436
  34.0 1.5 %copy-start.12 = (bf16[2,512,128]{2,1,0:T(8,128)(2,1)}, bf16[2,512,128]{2,1,0:T(8,128)(2,1)S(1)}, u32[]{:S(2)}) copy-start(bf16[2,512,128]{2,1,0:T(8,128)(2,1)S(1)} %collective-permute-done.6.refs_10_) | copy-start | bytes 786436
  35.6 0.7 copy-start.13
  74.0 7.0 %collective-permute-start.15 = (bf16[2,2,512,128]{3,2,1,0:T(8,128)(2,1)}, bf16[2,2,512,128]{3,2,1,0:T(8,128)(2,1)S(1)}, u32[]{:S(2)}, u32[]{:S(2)}) collective-permute-start(bf16[2,2,512,128]{3,2,1,0:T(8,128)(2,1)} %get-tuple-element.19), channel_id=1, source_target_pairs={{0,2},{2,0},{1,3},{3,1},{4,6},{6,4},{5,7},{7,5},{8,10},{10,8},{9,1... | collective-permute-start | bytes 1572872 | tf_op jit(solution)/shard_map/ppermute | solution.py:190
  79.2 18.0 %collective-permute-start.13 = (bf16[2,2,512,128]{3,2,1,0:T(8,128)(2,1)}, bf16[2,2,512,128]{3,2,1,0:T(8,128)(2,1)S(1)}, u32[]{:S(2)}, u32[]{:S(2)}) collective-permute-start(bf16[2,2,512,128]{3,2,1,0:T(8,128)(2,1)} %get-tuple-element.17), channel_id=1, source_target_pairs={{0,2},{2,0},{1,3},{3,1},{4,6},{6,4},{5,7},{7,5},{8,10},{10,8},{9,1... | collective-permute-start | bytes 1572872 | tf_op jit(solution)/shard_map/ppermute | solution.py:190
  79.3 25.2 %collective-permute-start.11 = (bf16[2,2,512,128]{3,2,1,0:T(8,128)(2,1)}, bf16[2,2,512,128]{3,2,1,0:T(8,128)(2,1)S(1)}, u32[]{:S(2)}, u32[]{:S(2)}) collective-permute-start(bf16[2,2,512,128]{3,2,1,0:T(8,128)(2,1)} %get-tuple-element.15), channel_id=1, source_target_pairs={{0,2},{2,0},{1,3},{3,1},{4,6},{6,4},{5,7},{7,5},{8,10},{10,8},{9,1... | collective-permute-start | bytes 1572872 | tf_op jit(solution)/shard_map/ppermute | solution.py:190
  82.1 15.1 %copy-start.1 = (bf16[2,2,512,128]{3,2,1,0:T(8,128)(2,1)S(1)}, bf16[2,2,512,128]{3,2,1,0:T(8,128)(2,1)}, u32[]{:S(2)}) copy-start(bf16[2,2,512,128]{3,2,1,0:T(8,128)(2,1)} %get-tuple-element.16) | copy-start | bytes 1572868
  82.2 22.2 %collective-permute-start.16 = (bf16[2,512,128]{2,1,0:T(8,128)(2,1)S(1)}, bf16[2,512,128]{2,1,0:T(8,128)(2,1)S(1)}, u32[]{:S(2)}, u32[]{:S(2)}) collective-permute-start(bf16[2,512,128]{2,1,0:T(8,128)(2,1)S(1)} %slice_bitcast_fusion), channel_id=1, source_target_pairs={{0,5},{5,0},{1,4},{4,1},{2,7},{7,2},{3,6},{6,3},{8,13},{13,8},{9,1... | collective-permute-start | bytes 786440 | tf_op jit(solution)/shard_map/ppermute | solution.py:194
  97.4 7.1 %copy-start = (bf16[2,2,512,128]{3,2,1,0:T(8,128)(2,1)S(1)}, bf16[2,2,512,128]{3,2,1,0:T(8,128)(2,1)}, u32[]{:S(2)}) copy-start(bf16[2,2,512,128]{3,2,1,0:T(8,128)(2,1)} %get-tuple-element.14) | copy-start | bytes 1572868
  97.4 12.6 %collective-permute-start.14 = (bf16[2,512,128]{2,1,0:T(8,128)(2,1)S(1)}, bf16[2,512,128]{2,1,0:T(8,128)(2,1)S(1)}, u32[]{:S(2)}, u32[]{:S(2)}) collective-permute-start(bf16[2,512,128]{2,1,0:T(8,128)(2,1)S(1)} %slice_bitcast_fusion.2), channel_id=1, source_target_pairs={{0,5},{5,0},{1,4},{4,1},{2,7},{7,2},{3,6},{6,3},{8,13},{13,8},{9,1... | collective-permute-start | bytes 786440 | tf_op jit(solution)/shard_map/ppermute | solution.py:194
  104.4 11.1 %collective-permute-start.17 = (bf16[2,512,128]{2,1,0:T(8,128)(2,1)S(1)}, bf16[2,512,128]{2,1,0:T(8,128)(2,1)S(1)}, u32[]{:S(2)}, u32[]{:S(2)}) collective-permute-start(bf16[2,512,128]{2,1,0:T(8,128)(2,1)S(1)} %fusion), channel_id=1, source_target_pairs={{0,120},{8,0},{16,8},{24,16},{32,24},{40,32},{48,40},{56,48},{64,5... | collective-permute-start | bytes 786440 | tf_op jit(solution)/shard_map/ppermute | solution.py:202
  104.7 11.0 %collective-permute-start.12 = (bf16[2,512,128]{2,1,0:T(8,128)(2,1)S(1)}, bf16[2,512,128]{2,1,0:T(8,128)(2,1)S(1)}, u32[]{:S(2)}, u32[]{:S(2)}) collective-permute-start(bf16[2,512,128]{2,1,0:T(8,128)(2,1)S(1)} %slice_bitcast_fusion.4), channel_id=1, source_target_pairs={{0,5},{5,0},{1,4},{4,1},{2,7},{7,2},{3,6},{6,3},{8,13},{13,8},{9,1... | collective-permute-start | bytes 786440 | tf_op jit(solution)/shard_map/ppermute | solution.py:194
  115.6 10.2 %collective-permute-start.18 = (bf16[2,512,128]{2,1,0:T(8,128)(2,1)S(1)}, bf16[2,512,128]{2,1,0:T(8,128)(2,1)S(1)}, u32[]{:S(2)}, u32[]{:S(2)}) collective-permute-start(bf16[2,512,128]{2,1,0:T(8,128)(2,1)S(1)} %add_convert_fusion.5), channel_id=1, source_target_pairs={{0,120},{8,0},{16,8},{24,16},{32,24},{40,32},{48,40},{56,48},{64,5... | collective-permute-start | bytes 786440 | tf_op jit(solution)/shard_map/ppermute | solution.py:202
  125.9 6.5 %collective-permute-start.19 = (bf16[2,512,128]{2,1,0:T(8,128)(2,1)S(1)}, bf16[2,512,128]{2,1,0:T(8,128)(2,1)S(1)}, u32[]{:S(2)}, u32[]{:S(2)}) collective-permute-start(bf16[2,512,128]{2,1,0:T(8,128)(2,1)S(1)} %add_convert_fusion.4), channel_id=1, source_target_pairs={{0,1},{1,0},{2,3},{3,2},{4,5},{5,4},{6,7},{7,6},{8,9},{9,8},{10,11... | collective-permute-start | bytes 786440 | tf_op jit(solution)/shard_map/ppermute | solution.py:198
where the time goes:
time: 131 us; the launch traced here: 133 us
  waiting for transfers between devices  52.7 us (40%)
  Pallas kernels  37.7 us (29%)
  starting transfers between devices  37.5 us (29%)
  other arithmetic  2.81 us (2%)
  local copies, waits for them, and re-layouts  1.52 us (1%)
    pallas_call x1, Pallas kernels, attention(): pl.pallas_call(attention_kernel, out_shape=(rows, rows) + (pair,) * 6, in...  37.7 us
    ppermute x6, starting transfers between devices, swap_z(): return lax.ppermute(value, ('zh', 'zl'), [(0, 3), (3, 0), (1, 2), (2, 1)])  27.3 us
    ppermute x4, waiting for transfers between devices, shift_row(): lax.ppermute(value, ('x', 'y'), [(r, (r + by) % 16) for r in range(16)])  24.5 us
    ppermute x6, waiting for transfers between devices, swap_z(): return lax.ppermute(value, ('zh', 'zl'), [(0, 3), (3, 0), (1, 2), (2, 1)])  19.1 us
    ppermute x1, waiting for transfers between devices, swap_head(): return lax.ppermute(value, 'zl', [(0, 1), (1, 0)])  6.36 us
    ppermute x9, starting transfers between devices, swap_core(): return lax.ppermute(value, 'core', [(0, 1), (1, 0)])  6.27 us
    ppermute x4, starting transfers between devices, shift_row(): lax.ppermute(value, ('x', 'y'), [(r, (r + by) % 16) for r in range(16)])  3.88 us
    ppermute x9, waiting for transfers between devices, swap_core(): return lax.ppermute(value, 'core', [(0, 1), (1, 0)])  2.71 us
  transfers between devices with their start and end apart: 20, of which 12 were waited for; matrix products, arithmetic and copies ran while one was open for 1% of the time, Pallas kernels for 0%

commit v1 on v0

v1 whole, which is shorter than its diff:
```python
from functools import partial
import math

import jax
import jax.numpy as jnp
from jax import lax
from jax.experimental import pallas as pl
from jax.experimental.pallas import tpu as pltpu
from jax.sharding import Mesh, PartitionSpec as P

NEGATIVE = -1e30
BLK = 512
HEADS = 4
HD = 128
NQ = HEADS * BLK
HALF = BLK // 2
ROWS = 3
SLOTS = 4 * ROWS
SPAN = 9
SCALE = HD ** -0.5
LOG2 = SCALE * math.log2(math.e)
BOUND = 64.0
F32 = jnp.float32
BF16 = jnp.bfloat16
SEQ = ("x", "y", "zh", "core")


def dot(a, b):
    return lax.dot_general(a, b, (((1,), (0,)), ((), ())), preferred_element_type=F32)


def attention_kernel(*refs):
    len_ref, q_ref, do_ref = refs[:3]
    kv_refs = refs[3:27]
    o_ref, dq_ref = refs[27:29]
    out_refs = refs[29:35]
    (kvs, dkvs, qt, dot_t, do_s, probs, row_max, total, acc, dq_acc, stage_s, delta, in_sem, out_sem) = refs[35:]
    row = lax.axis_index("x") * 4 + lax.axis_index("y")
    zh = lax.axis_index("zh")
    core = lax.axis_index("core")
    zl = lax.axis_index("zl")
    place = zh * 2 + core

    def slot_of(j, dz, dc):
        return (2 - j) * 4 + (1 - zh if dz else zh) * 2 + (1 - core if dc else core)

    def part_of(dp):
        return 1 - zl if dp else zl

    order = [(j, dz, dp, dc) for j in range(ROWS) for dz in range(2) for dp in range(2) for dc in range(2)]

    def in_copy(n):
        j, dz, dp, dc = order[n]
        slot = slot_of(j, dz, dc)
        return pltpu.make_async_copy(kv_refs[n], kvs.at[slot, part_of(dp)], in_sem.at[n])

    for n in range(len(order)):
        in_copy(n).start()

    base = (row - 2) * (4 * BLK)
    first = base + (8 + place) * BLK
    q_pos = lax.broadcasted_iota(jnp.int32, (1, BLK), 1) + (8 + place) * BLK
    starts = jnp.zeros((1, BLK), jnp.int32) - base
    first_start = -base
    last_start = -base
    end = jnp.int32(0)
    for c in range(16):
        end = end + len_ref[c]
        rel = end - base
        starts = jnp.where(q_pos >= rel, rel, starts)
        first_start = jnp.where(end <= first, rel, first_start)
        last_start = jnp.where(end <= first + BLK - 1, rel, last_start)
    lo = first_start // BLK
    hi = 8 + place

    for h in range(HEADS):
        cols = slice(h * BLK, (h + 1) * BLK)
        qt[:, cols] = q_ref[h].T
        dot_t[:, cols] = do_ref[h].T
    row_max[...] = jnp.zeros((1, NQ), F32)
    total[...] = jnp.zeros((1, NQ), F32)
    acc[...] = jnp.zeros((HD, NQ), F32)
    dq_acc[...] = jnp.zeros((HD, NQ), F32)
    q_norm = jnp.max(dot(jnp.ones((8, HD), BF16), jnp.square(qt[...].astype(F32)).astype(BF16)))
    for n in range(len(order)):
        in_copy(n).wait()

    def norm_step(t, k_norm):
        norms = dot(jnp.square(kvs[t, 0].astype(F32)).astype(BF16), jnp.ones((HD, HD), BF16))
        return jnp.maximum(k_norm, jnp.max(norms.reshape(BLK // 8, 8, HD), axis=0))

    k_norm = jnp.max(lax.fori_loop(lo, hi + 1, norm_step, jnp.zeros((8, HD), F32)))
    safe = q_norm * k_norm <= 0.98 * (BOUND / LOG2) ** 2

    def tile_mask(t):
        k_pos = lax.broadcasted_iota(jnp.int32, (BLK, BLK), 0) + t * BLK
        return (k_pos >= starts) & (k_pos <= q_pos)

    def max_step(t, carry):
        allowed = tile_mask(t)
        for h in range(HEADS):
            cols = slice(h * BLK, (h + 1) * BLK)
            s = jnp.where(allowed, dot(kvs[t, 0], qt[:, cols]), NEGATIVE)
            row_max[:, cols] = jnp.maximum(row_max[:, cols], jnp.max(s, axis=0, keepdims=True))
        return carry

    @pl.when(jnp.logical_not(safe))
    def _():
        row_max[...] = jnp.full((1, NQ), NEGATIVE, F32)
        lax.fori_loop(lo, hi + 1, max_step, 0)
        row_max[...] = row_max[...] * LOG2

    def forward(t, masked):
        k = kvs[t, 0]
        v_t = kvs[t, 1].T
        if masked:
            allowed = tile_mask(t)
        def score(h):
            s = dot(k, qt[:, h * HALF:(h + 1) * HALF])
            return jnp.where(allowed[:, (h % 2) * HALF:(h % 2 + 1) * HALF], s, NEGATIVE) if masked else s

        def soft(h, s):
            cols = slice(h * HALF, (h + 1) * HALF)
            p = jnp.exp2(s * LOG2 - row_max[:, cols])
            total[:, cols] += jnp.sum(p, axis=0, keepdims=True)
            p = p.astype(BF16)
            probs[t - lo, :, cols] = p
            return p

        def pv(h, p):
            cols = slice(h * HALF, (h + 1) * HALF)
            acc[:, cols] += dot(v_t, p)

        weights = soft(0, score(0))
        s = score(1)
        for h in range(1, 2 * HEADS):
            held, weights = weights, soft(h, s)
            if h + 1 < 2 * HEADS:
                s = score(h + 1)
            pv(h - 1, held)
        pv(2 * HEADS - 1, weights)

    def forward_step(t, carry):
        masked = (t * BLK < last_start) | (t == hi)

        @pl.when(masked)
        def _():
            forward(t, True)

        @pl.when(jnp.logical_not(masked))
        def _():
            forward(t, False)

        return carry

    lax.fori_loop(lo, hi + 1, forward_step, 0)

    for h in range(HEADS):
        cols = slice(h * BLK, (h + 1) * BLK)
        inverse = 1.0 / total[:, cols]
        o = (acc[:, cols] * inverse).astype(BF16)
        o_ref[h] = o.T
        scaled = (dot_t[:, cols].astype(F32) * inverse).astype(BF16)
        dot_t[:, cols] = scaled
        do_s[h * BLK:(h + 1) * BLK] = scaled.T
        delta[:, cols] = jnp.sum(o.astype(F32) * scaled.astype(F32), axis=0, keepdims=True)

    def out_copy(n, t):
        j, dz, dp, dc = order[n]
        return pltpu.make_async_copy(dkvs.at[t, part_of(dp)], out_refs[j * 2 + dc].at[dz, dp], out_sem.at[n])

    def send_out(t):
        for n, (j, dz, dp, dc) in enumerate(order):
            if dp == 0:
                @pl.when(slot_of(j, dz, dc) == t)
                def _():
                    out_copy(n, t).start()
                    out_copy(n + 2, t).start()

    dkvs[SLOTS] = jnp.zeros((2, BLK, HD), BF16)
    for n, (j, dz, dp, dc) in enumerate(order):
        slot = slot_of(j, dz, dc)

        @pl.when((slot < lo) | (slot > hi))
        def _():
            out_copy(n, SLOTS).start()

    def backward_step(t, carry):
        k_t = kvs[t, 0].T
        v = kvs[t, 1]
        def dp_of(h):
            return dot(v, dot_t[:, h * BLK:(h + 1) * BLK])

        def ds_of(h, dp):
            cols = slice(h * BLK, (h + 1) * BLK)
            ds = (probs[t - lo, :, cols].astype(F32) * (dp - delta[:, cols])).astype(BF16)
            stage_s[:, cols] = ds
            return ds

        def dq_of(h, ds):
            dq_acc[:, h * BLK:(h + 1) * BLK] += dot(k_t, ds)

        d0 = dp_of(0)
        d1 = dp_of(1)
        s0 = ds_of(0, d0)
        dkvs[t, 1] = dot(probs[t - lo], do_s[...]).astype(BF16)
        d2 = dp_of(2)
        dq_of(0, s0)
        s1 = ds_of(1, d1)
        d3 = dp_of(3)
        dq_of(1, s1)
        s2 = ds_of(2, d2)
        dq_of(2, s2)
        s3 = ds_of(3, d3)
        dq_of(3, s3)
        dkvs[t, 0] = (dot(stage_s[...], q_ref[...].reshape(NQ, HD)) * SCALE).astype(BF16)
        send_out(t)
        return carry

    lax.fori_loop(lo, hi + 1, backward_step, 0)

    copies = [out_copy(n, 0) for n in range(len(order))]
    for h in range(HEADS):
        cols = slice(h * BLK, (h + 1) * BLK)
        dq_ref[h] = (dq_acc[:, cols] * SCALE).astype(BF16).T
    for copy in copies:
        copy.wait()


def attention(seq_lengths, queries, d_out, blocks):
    vmem = pl.BlockSpec(memory_space=pltpu.VMEM)
    anywhere = pl.BlockSpec(memory_space=pl.ANY)
    pair = jax.ShapeDtypeStruct((2, 2, BLK, HD), BF16)
    rows = jax.ShapeDtypeStruct((HEADS, BLK, HD), BF16)
    return pl.pallas_call(
        attention_kernel,
        out_shape=(rows, rows) + (pair,) * 6,
        in_specs=[pl.BlockSpec(memory_space=pltpu.SMEM), vmem, vmem] + [anywhere] * 24,
        out_specs=[vmem, vmem] + [anywhere] * 6,
        scratch_shapes=[
            pltpu.VMEM((SLOTS, 2, BLK, HD), BF16),
            pltpu.VMEM((SLOTS + 1, 2, BLK, HD), BF16),
            pltpu.VMEM((HD, NQ), BF16),
            pltpu.VMEM((HD, NQ), BF16),
            pltpu.VMEM((NQ, HD), BF16),
            pltpu.VMEM((SPAN, BLK, NQ), BF16),
            pltpu.VMEM((1, NQ), F32),
            pltpu.VMEM((1, NQ), F32),
            pltpu.VMEM((HD, NQ), F32),
            pltpu.VMEM((HD, NQ), F32),
            pltpu.VMEM((BLK, NQ), BF16),
            pltpu.VMEM((1, NQ), F32),
            pltpu.SemaphoreType.DMA((2 * SLOTS,)),
            pltpu.SemaphoreType.DMA((2 * SLOTS,)),
        ],
        compiler_params=pltpu.CompilerParams(vmem_limit_bytes=56 << 20),
        cost_estimate=pl.CostEstimate(flops=8 << 30, bytes_accessed=16 << 20, transcendentals=9 << 20),
        name="attention",
    )(seq_lengths, queries, d_out, *blocks)


def swap_core(value):
    return lax.ppermute(value, "core", [(0, 1), (1, 0)])


def to_column(value, dz, dp, sources=(0, 1)):
    pairs = [(2 * zh + zl, 2 * (zh ^ dz) + (zl ^ dp)) for zh in sources for zl in range(2)]
    return lax.ppermute(value, ("zh", "zl"), pairs)


def shift_row(value, by):
    return lax.ppermute(value, ("x", "y"), [(r, (r + by) % 16) for r in range(16)])


def added(*values):
    total = values[0].astype(F32)
    for value in values[1:]:
        total = total + value.astype(F32)
    return total.astype(BF16)


def on_device(queries, key_rows, value_rows, d_out, seq_lengths):
    zl = lax.axis_index("zl")
    mine = jnp.where(zl == 0, key_rows, value_rows)
    other = jnp.where(zl == 0, value_rows, key_rows)
    row1 = shift_row(mine, 1)
    row2 = shift_row(row1, 1)
    pieces = [
        mine, other, to_column(other, 1, 1, (0,)), to_column(mine, 1, 1, (0,)),
        row1, to_column(row1, 0, 1), to_column(row1, 1, 0), to_column(row1, 1, 1),
        row2, to_column(row2, 0, 1), to_column(row2, 1, 0, (1,)), to_column(row2, 1, 1, (1,)),
    ]
    blocks = []
    for piece in pieces:
        blocks += [piece, swap_core(piece)]
    attended, grad_queries, *parts = attention(seq_lengths, queries, d_out, blocks)

    def column(j, sources):
        both = added(parts[2 * j], swap_core(parts[2 * j + 1]))
        return added(
            both[0, 0],
            to_column(both[0, 1], 0, 1),
            to_column(both[1, 0], 1, 0, sources),
            to_column(both[1, 1], 1, 1, sources),
        )

    back = shift_row(column(2, (0,)), -1)
    back = shift_row(added(column(1, (0, 1)), back), -1)
    done = added(column(0, (1,)), back)
    given = to_column(done, 0, 1)
    grad_keys = jnp.where(zl == 0, done, given)
    grad_values = jnp.where(zl == 0, given, done)
    return attended, grad_queries, grad_keys, grad_values


def solution(mesh):
    fine = Mesh(mesh.devices.reshape(4, 4, 2, 2, 2), ("x", "y", "zh", "core", "zl"))
    tokens = P("zl", SEQ, None)
    rows = P(SEQ, None)
    return jax.shard_map(
        on_device,
        mesh=fine,
        in_specs=(tokens, rows, rows, tokens, P()),
        out_specs=(tokens, tokens, rows, rows),
        check_vma=False,
    )
```

time: 131 us -> 123 us (0.939)
  the two profiles are of different devices: /device:TPU:30 before, /device:TPU:26 now
where the time goes in v1:
time: 123 us; the launch traced here: 122 us
  starting transfers between devices  50.1 us (41%)
  waiting for transfers between devices  33.8 us (27%)
  Pallas kernels  32.9 us (27%)
  other arithmetic  3.42 us (3%)
    ppermute x18, starting transfers between devices, to_column(): return lax.ppermute(value, ('zh', 'zl'), pairs)  37.6 us
    pallas_call x1, Pallas kernels, attention(): pl.pallas_call(attention_kernel, out_shape=(rows, rows) + (pair,) * 6, in...  32.9 us
    ppermute x18, waiting for transfers between devices, to_column(): return lax.ppermute(value, ('zh', 'zl'), pairs)  20.9 us
    ppermute x4, waiting for transfers between devices, shift_row(): lax.ppermute(value, ('x', 'y'), [(r, (r + by) % 16) for r in range(16)])  10.6 us
    ppermute x15, starting transfers between devices, swap_core(): return lax.ppermute(value, 'core', [(0, 1), (1, 0)])  7.86 us
    ppermute x4, starting transfers between devices, shift_row(): lax.ppermute(value, ('x', 'y'), [(r, (r + by) % 16) for r in range(16)])  4.63 us
  transfers between devices with their start and end apart: 37, of which 16 were waited for; matrix products, arithmetic and copies ran while one was open for 1% of the time, Pallas kernels for 0%

profile of v1, /device:TPU:26, one launch (start us, length us, event | category | flops | bytes accessed | tf_op | source)
XLA Modules:
  0.0 122.4 jit_solution(17548266821548739909)
XLA Ops:
  0.6 1.0 broadcast_select_fusion.2
  1.7 5.9 %collective-permute-start.2 = (bf16[512,128]{1,0:T(8,128)(2,1)S(1)}, bf16[512,128]{1,0:T(8,128)(2,1)S(1)}, u32[]{:S(2)}, u32[]{:S(2)}) collective-permute-start(bf16[512,128]{1,0:T(8,128)(2,1)S(1)} %get-tuple-element.31.refs_5_), channel_id=1, source_target_pairs={{0,5},{1,4},{2,7},{3,6},{8,13},{9,12},{10,15},{11,14},{16,21},{17,... | collective-permute-start | bytes 393224 | tf_op jit(solution)/shard_map/ppermute | solution.py:268
  7.6 1.2 collective-permute-start.6
  8.8 1.3 %collective-permute-start.4 = (bf16[512,128]{1,0:T(8,128)(2,1)S(1)}, bf16[512,128]{1,0:T(8,128)(2,1)S(1)}, u32[]{:S(2)}, u32[]{:S(2)}) collective-permute-start(bf16[512,128]{1,0:T(8,128)(2,1)S(1)} %get-tuple-element.32.refs_3_), channel_id=1, source_target_pairs={{0,5},{1,4},{2,7},{3,6},{8,13},{9,12},{10,15},{11,14},{16,21},{17,... | collective-permute-start | bytes 393224 | tf_op jit(solution)/shard_map/ppermute | solution.py:268
  10.1 0.6 collective-permute-start
  10.7 0.1 collective-permute-start.3
  10.8 1.8 %collective-permute-done.6.refs_11_ = bf16[512,128]{1,0:T(8,128)(2,1)S(1)} collective-permute-done((bf16[512,128]{1,0:T(8,128)(2,1)S(1)}, bf16[512,128]{1,0:T(8,128)(2,1)S(1)}, u32[]{:S(2)}, u32[]{:S(2)}) %collective-permute-start.6) | collective-permute-done | bytes 131104 | tf_op jit(solution)/shard_map/ppermute | solution.py:272
  12.6 3.3 %collective-permute-start.14 = (bf16[512,128]{1,0:T(8,128)(2,1)S(1)}, bf16[512,128]{1,0:T(8,128)(2,1)S(1)}, u32[]{:S(2)}, u32[]{:S(2)}) collective-permute-start(bf16[512,128]{1,0:T(8,128)(2,1)S(1)} %collective-permute-done.6.refs_11_), channel_id=1, source_target_pairs={{0,8},{8,16},{16,24},{24,32},{32,40},{40,48},{48,56},{56,64},{64,7... | collective-permute-start | bytes 393224 | tf_op jit(solution)/shard_map/ppermute | solution.py:272
  15.9 1.8 %collective-permute-start.10 = (bf16[512,128]{1,0:T(8,128)(2,1)S(1)}, bf16[512,128]{1,0:T(8,128)(2,1)S(1)}, u32[]{:S(2)}, u32[]{:S(2)}) collective-permute-start(bf16[512,128]{1,0:T(8,128)(2,1)S(1)} %collective-permute-done.6.refs_11_), channel_id=1, source_target_pairs={{0,4},{1,5},{4,0},{5,1},{2,6},{3,7},{6,2},{7,3},{8,12},{9,13},{12,... | collective-permute-start | bytes 393224 | tf_op jit(solution)/shard_map/ppermute | solution.py:268
  17.8 2.2 %collective-permute-start.8 = (bf16[512,128]{1,0:T(8,128)(2,1)S(1)}, bf16[512,128]{1,0:T(8,128)(2,1)S(1)}, u32[]{:S(2)}, u32[]{:S(2)}) collective-permute-start(bf16[512,128]{1,0:T(8,128)(2,1)S(1)} %collective-permute-done.6.refs_11_), channel_id=1, source_target_pairs={{0,1},{1,0},{4,5},{5,4},{2,3},{3,2},{6,7},{7,6},{8,9},{9,8},{12,13... | collective-permute-start | bytes 393224 | tf_op jit(solution)/shard_map/ppermute | solution.py:268
  20.1 0.5 collective-permute-start.5
  20.5 2.5 %collective-permute-done.12.refs_17_ = bf16[512,128]{1,0:T(8,128)(2,1)S(1)} collective-permute-done((bf16[512,128]{1,0:T(8,128)(2,1)S(1)}, bf16[512,128]{1,0:T(8,128)(2,1)S(1)}, u32[]{:S(2)}, u32[]{:S(2)}) %collective-permute-start.12) | collective-permute-done | bytes 131104 | tf_op jit(solution)/shard_map/ppermute | solution.py:268
  23.0 1.3 %collective-permute-start.20 = (bf16[512,128]{1,0:T(8,128)(2,1)S(1)}, bf16[512,128]{1,0:T(8,128)(2,1)S(1)}, u32[]{:S(2)}, u32[]{:S(2)}) collective-permute-start(bf16[512,128]{1,0:T(8,128)(2,1)S(1)} %collective-permute-done.14.refs_19_), channel_id=1, source_target_pairs={{4,1},{5,0},{6,3},{7,2},{12,9},{13,8},{14,11},{15,10},{20,17},{21,... | collective-permute-start | bytes 393224 | tf_op jit(solution)/shard_map/ppermute | solution.py:268
  24.3 1.3 %collective-permute-start.18 = (bf16[512,128]{1,0:T(8,128)(2,1)S(1)}, bf16[512,128]{1,0:T(8,128)(2,1)S(1)}, u32[]{:S(2)}, u32[]{:S(2)}) collective-permute-start(bf16[512,128]{1,0:T(8,128)(2,1)S(1)} %collective-permute-done.14.refs_19_), channel_id=1, source_target_pairs={{4,0},{5,1},{6,2},{7,3},{12,8},{13,9},{14,10},{15,11},{20,16},{21,... | collective-permute-start | bytes 393224 | tf_op jit(solution)/shard_map/ppermute | solution.py:268
  25.9 0.5 collective-permute-start.13
  26.3 4.7 %collective-permute-done.20.refs_25_ = bf16[512,128]{1,0:T(8,128)(2,1)S(1)} collective-permute-done((bf16[512,128]{1,0:T(8,128)(2,1)S(1)}, bf16[512,128]{1,0:T(8,128)(2,1)S(1)}, u32[]{:S(2)}, u32[]{:S(2)}) %collective-permute-start.20) | collective-permute-done | bytes 131104 | tf_op jit(solution)/shard_map/ppermute | solution.py:268
  31.1 1.6 %collective-permute-done.18.refs_23_ = bf16[512,128]{1,0:T(8,128)(2,1)S(1)} collective-permute-done((bf16[512,128]{1,0:T(8,128)(2,1)S(1)}, bf16[512,128]{1,0:T(8,128)(2,1)S(1)}, u32[]{:S(2)}, u32[]{:S(2)}) %collective-permute-start.18) | collective-permute-done | bytes 131104 | tf_op jit(solution)/shard_map/ppermute | solution.py:268
  32.7 0.5 collective-permute-start.21
  33.3 0.4 collective-permute-start.17
  33.7 0.3 collective-permute-done.9.refs_14_
  34.0 0.2 collective-permute-done.21.refs_26_
  34.2 0.3 collective-permute-done.19.refs_24_
  34.6 0.2 collective-permute-done.17.refs_22_
  34.9 0.3 copy-done.24
  35.2 0.6 copy-done.25
  35.9 32.9 %attention.1 = (bf16[4,512,128]{2,1,0:T(8,128)(2,1)}, bf16[4,512,128]{2,1,0:T(8,128)(2,1)}, bf16[2,2,512,128]{3,2,1,0:T(8,128)(2,1)}, bf16[2,2,512,128]{3,2,1,0:...) custom-call(s32[16]{0:T(128)} %refs_0_.1, ...), custom_call_target="tpu_custom_call" | custom-call | flops 8589934592 | bytes 16777216 | tf_op jit(solution)/shard_map/attention/pallas_call | solution.py:235
  68.7 4.6 %collective-permute-start.26 = (bf16[2,2,512,128]{3,2,1,0:T(8,128)(2,1)}, bf16[2,2,512,128]{3,2,1,0:T(8,128)(2,1)S(1)}, u32[]{:S(2)}, u32[]{:S(2)}) collective-permute-start(bf16[2,2,512,128]{3,2,1,0:T(8,128)(2,1)} %get-tuple-element.17), channel_id=1, source_target_pairs={{0,2},{2,0},{1,3},{3,1},{4,6},{6,4},{5,7},{7,5},{8,10},{10,8},{9,1... | collective-permute-start | bytes 1572872 | tf_op jit(solution)/shard_map/ppermute | solution.py:263
  73.4 0.4 collective-permute-start.22
  73.8 1.2 %collective-permute-done.26 = bf16[2,2,512,128]{3,2,1,0:T(8,128)(2,1)S(1)} collective-permute-done((bf16[2,2,512,128]{3,2,1,0:T(8,128)(2,1)}, bf16[2,2,512,128]{3,2,1,0:T(8,128)(2,1)S(1)}, u32[]{:S(2)}, u32[]{:S(2)}) %collective-permute-start.26) | collective-permute-done | bytes 524320 | tf_op jit(solution)/shard_map/ppermute | solution.py:263
  75.0 1.2 add_convert_fusion.1
  76.3 0.7 collective-permute-start.27
  76.9 13.0 %collective-permute-start.29 = (bf16[512,128]{1,0:T(8,128)(2,1)S(1)}, bf16[512,128]{1,0:T(8,128)(2,1)S(1)}, u32[]{:S(2)}, u32[]{:S(2)}) collective-permute-start(bf16[512,128]{1,0:T(8,128)(2,1)S(1)} %get-tuple-element.24), channel_id=1, source_target_pairs={{0,5},{1,4},{4,1},{5,0},{2,7},{3,6},{6,3},{7,2},{8,13},{9,12},{12,... | collective-permute-start | bytes 393224 | tf_op jit(solution)/shard_map/ppermute | solution.py:268
  89.9 0.1 add_convert_fusion
  90.1 0.3 collective-permute-start.31
  90.4 2.6 %collective-permute-start.33 = (bf16[512,128]{1,0:T(8,128)(2,1)S(1)}, bf16[512,128]{1,0:T(8,128)(2,1)S(1)}, u32[]{:S(2)}, u32[]{:S(2)}) collective-permute-start(bf16[512,128]{1,0:T(8,128)(2,1)S(1)} %get-tuple-element.27), channel_id=1, source_target_pairs={{0,5},{1,4},{2,7},{3,6},{8,13},{9,12},{10,15},{11,14},{16,21},{17,... | collective-permute-start | bytes 393224 | tf_op jit(solution)/shard_map/ppermute | solution.py:268
  93.0 1.9 %collective-permute-start.32 = (bf16[512,128]{1,0:T(8,128)(2,1)S(1)}, bf16[512,128]{1,0:T(8,128)(2,1)S(1)}, u32[]{:S(2)}, u32[]{:S(2)}) collective-permute-start(bf16[512,128]{1,0:T(8,128)(2,1)S(1)} %get-tuple-element.28), channel_id=1, source_target_pairs={{0,4},{1,5},{2,6},{3,7},{8,12},{9,13},{10,14},{11,15},{16,20},{17,... | collective-permute-start | bytes 393224 | tf_op jit(solution)/shard_map/ppermute | solution.py:268
  94.9 0.1 add_convert_fusion.2
  95.0 0.4 collective-permute-done.31
  95.4 2.5 %collective-permute-start.28 = (bf16[512,128]{1,0:T(8,128)(2,1)S(1)}, bf16[512,128]{1,0:T(8,128)(2,1)S(1)}, u32[]{:S(2)}, u32[]{:S(2)}) collective-permute-start(bf16[512,128]{1,0:T(8,128)(2,1)S(1)} %get-tuple-element.25), channel_id=1, source_target_pairs={{0,4},{1,5},{4,0},{5,1},{2,6},{3,7},{6,2},{7,3},{8,12},{9,13},{12,... | collective-permute-start | bytes 393224 | tf_op jit(solution)/shard_map/ppermute | solution.py:268
  97.9 3.6 %collective-permute-done.33 = bf16[512,128]{1,0:T(8,128)(2,1)S(1)} collective-permute-done((bf16[512,128]{1,0:T(8,128)(2,1)S(1)}, bf16[512,128]{1,0:T(8,128)(2,1)S(1)}, u32[]{:S(2)}, u32[]{:S(2)}) %collective-permute-start.33) | collective-permute-done | bytes 131104 | tf_op jit(solution)/shard_map/ppermute | solution.py:268
  101.8 1.3 %collective-permute-start.25 = (bf16[512,128]{1,0:T(8,128)(2,1)S(1)}, bf16[512,128]{1,0:T(8,128)(2,1)S(1)}, u32[]{:S(2)}, u32[]{:S(2)}) collective-permute-start(bf16[512,128]{1,0:T(8,128)(2,1)S(1)} %get-tuple-element.21), channel_id=1, source_target_pairs={{4,1},{5,0},{6,3},{7,2},{12,9},{13,8},{14,11},{15,10},{20,17},{21,... | collective-permute-start | bytes 393224 | tf_op jit(solution)/shard_map/ppermute | solution.py:268
  103.1 1.3 %collective-permute-start.24 = (bf16[512,128]{1,0:T(8,128)(2,1)S(1)}, bf16[512,128]{1,0:T(8,128)(2,1)S(1)}, u32[]{:S(2)}, u32[]{:S(2)}) collective-permute-start(bf16[512,128]{1,0:T(8,128)(2,1)S(1)} %get-tuple-element.22), channel_id=1, source_target_pairs={{4,0},{5,1},{6,2},{7,3},{12,8},{13,9},{14,10},{15,11},{20,16},{21,... | collective-permute-start | bytes 393224 | tf_op jit(solution)/shard_map/ppermute | solution.py:268
  104.4 4.9 %collective-permute-done.34 = bf16[512,128]{1,0:T(8,128)(2,1)S(1)} collective-permute-done((bf16[512,128]{1,0:T(8,128)(2,1)S(1)}, bf16[512,128]{1,0:T(8,128)(2,1)S(1)}, u32[]{:S(2)}, u32[]{:S(2)}) %collective-permute-start.34) | collective-permute-done | bytes 131104 | tf_op jit(solution)/shard_map/ppermute | solution.py:272
  109.5 1.6 %collective-permute-done.25 = bf16[512,128]{1,0:T(8,128)(2,1)S(1)} collective-permute-done((bf16[512,128]{1,0:T(8,128)(2,1)S(1)}, bf16[512,128]{1,0:T(8,128)(2,1)S(1)}, u32[]{:S(2)}, u32[]{:S(2)}) %collective-permute-start.25) | collective-permute-done | bytes 131104 | tf_op jit(solution)/shard_map/ppermute | solution.py:268
  111.2 1.6 %collective-permute-done.24 = bf16[512,128]{1,0:T(8,128)(2,1)S(1)} collective-permute-done((bf16[512,128]{1,0:T(8,128)(2,1)S(1)}, bf16[512,128]{1,0:T(8,128)(2,1)S(1)}, u32[]{:S(2)}, u32[]{:S(2)}) %collective-permute-start.24) | collective-permute-done | bytes 131104 | tf_op jit(solution)/shard_map/ppermute | solution.py:268
  112.8 3.8 %collective-permute-done.35 = bf16[512,128]{1,0:T(8,128)(2,1)S(1)} collective-permute-done((bf16[512,128]{1,0:T(8,128)(2,1)S(1)}, bf16[512,128]{1,0:T(8,128)(2,1)S(1)}, u32[]{:S(2)}, u32[]{:S(2)}) %collective-permute-start.35) | collective-permute-done | bytes 131104 | tf_op jit(solution)/shard_map/ppermute | solution.py:272
  116.8 5.0 %collective-permute-done.36 = bf16[512,128]{1,0:T(8,128)(2,1)S(1)} collective-permute-done((bf16[512,128]{1,0:T(8,128)(2,1)S(1)}, bf16[512,128]{1,0:T(8,128)(2,1)S(1)}, u32[]{:S(2)}, u32[]{:S(2)}) %collective-permute-start.36) | collective-permute-done | bytes 131104 | tf_op jit(solution)/shard_map/ppermute | solution.py:268
  121.7 0.7 broadcast_select_fusion
  (90 shorter events, 1.2 us)
Async XLA Ops:
  1.6 33.1 %copy-start.2 = (bf16[512,128]{1,0:T(8,128)(2,1)}, bf16[512,128]{1,0:T(8,128)(2,1)S(1)}, u32[]{:S(2)}) copy-start(bf16[512,128]{1,0:T(8,128)(2,1)S(1)} %get-tuple-element.31.refs_5_) | copy-start | bytes 393220
  1.6 33.1 %copy-start.3 = (bf16[512,128]{1,0:T(8,128)(2,1)}, bf16[512,128]{1,0:T(8,128)(2,1)S(1)}, u32[]{:S(2)}) copy-start(bf16[512,128]{1,0:T(8,128)(2,1)S(1)} %get-tuple-element.32.refs_3_) | copy-start | bytes 393220
  1.7 9.1 %collective-permute-start.2 = (bf16[512,128]{1,0:T(8,128)(2,1)S(1)}, bf16[512,128]{1,0:T(8,128)(2,1)S(1)}, u32[]{:S(2)}, u32[]{:S(2)}) collective-permute-start(bf16[512,128]{1,0:T(8,128)(2,1)S(1)} %get-tuple-element.31.refs_5_), channel_id=1, source_target_pairs={{0,5},{1,4},{2,7},{3,6},{8,13},{9,12},{10,15},{11,14},{16,21},{17,... | collective-permute-start | bytes 393224 | tf_op jit(solution)/shard_map/ppermute | solution.py:268
  7.6 5.0 %collective-permute-start.6 = (bf16[512,128]{1,0:T(8,128)(2,1)S(1)}, bf16[512,128]{1,0:T(8,128)(2,1)S(1)}, u32[]{:S(2)}, u32[]{:S(2)}) collective-permute-start(bf16[512,128]{1,0:T(8,128)(2,1)S(1)} %get-tuple-element.32.refs_3_), channel_id=1, source_target_pairs={{0,8},{8,16},{16,24},{24,32},{32,40},{40,48},{48,56},{56,64},{64,7... | collective-permute-start | bytes 393224 | tf_op jit(solution)/shard_map/ppermute | solution.py:272
  8.8 7.1 %collective-permute-start.1 = (bf16[512,128]{1,0:T(8,128)(2,1)S(1)}, bf16[512,128]{1,0:T(8,128)(2,1)S(1)}, u32[]{:S(2)}, u32[]{:S(2)}) collective-permute-start(bf16[512,128]{1,0:T(8,128)(2,1)S(1)} %get-tuple-element.31.refs_5_), channel_id=1, source_target_pairs={{0,2},{2,0},{1,3},{3,1},{4,6},{6,4},{5,7},{7,5},{8,10},{10,8},{9,1... | collective-permute-start | bytes 393224 | tf_op jit(solution)/shard_map/ppermute | solution.py:263
  8.8 7.1 %collective-permute-start.4 = (bf16[512,128]{1,0:T(8,128)(2,1)S(1)}, bf16[512,128]{1,0:T(8,128)(2,1)S(1)}, u32[]{:S(2)}, u32[]{:S(2)}) collective-permute-start(bf16[512,128]{1,0:T(8,128)(2,1)S(1)} %get-tuple-element.32.refs_3_), channel_id=1, source_target_pairs={{0,5},{1,4},{2,7},{3,6},{8,13},{9,12},{10,15},{11,14},{16,21},{17,... | collective-permute-start | bytes 393224 | tf_op jit(solution)/shard_map/ppermute | solution.py:268
  10.1 7.7 %collective-permute-start = (bf16[512,128]{1,0:T(8,128)(2,1)S(1)}, bf16[512,128]{1,0:T(8,128)(2,1)S(1)}, u32[]{:S(2)}, u32[]{:S(2)}) collective-permute-start(bf16[512,128]{1,0:T(8,128)(2,1)S(1)} %get-tuple-element.32.refs_3_), channel_id=1, source_target_pairs={{0,2},{2,0},{1,3},{3,1},{4,6},{6,4},{5,7},{7,5},{8,10},{10,8},{9,1... | collective-permute-start | bytes 393224 | tf_op jit(solution)/shard_map/ppermute | solution.py:263
  10.7 24.0 %copy-start.4 = (bf16[512,128]{1,0:T(8,128)(2,1)}, bf16[512,128]{1,0:T(8,128)(2,1)S(1)}, u32[]{:S(2)}) copy-start(bf16[512,128]{1,0:T(8,128)(2,1)S(1)} %collective-permute-done.2.refs_7_) | copy-start | bytes 393220
  10.7 9.3 %collective-permute-start.3 = (bf16[512,128]{1,0:T(8,128)(2,1)S(1)}, bf16[512,128]{1,0:T(8,128)(2,1)S(1)}, u32[]{:S(2)}, u32[]{:S(2)}) collective-permute-start(bf16[512,128]{1,0:T(8,128)(2,1)S(1)} %collective-permute-done.2.refs_7_), channel_id=1, source_target_pairs={{0,2},{2,0},{1,3},{3,1},{4,6},{6,4},{5,7},{7,5},{8,10},{10,8},{9,1... | collective-permute-start | bytes 393224 | tf_op jit(solution)/shard_map/ppermute | solution.py:263
  12.6 22.1 %copy-start.5 = (bf16[512,128]{1,0:T(8,128)(2,1)}, bf16[512,128]{1,0:T(8,128)(2,1)S(1)}, u32[]{:S(2)}) copy-start(bf16[512,128]{1,0:T(8,128)(2,1)S(1)} %collective-permute-done.6.refs_11_) | copy-start | bytes 393220
  12.6 7.4 %collective-permute-start.14 = (bf16[512,128]{1,0:T(8,128)(2,1)S(1)}, bf16[512,128]{1,0:T(8,128)(2,1)S(1)}, u32[]{:S(2)}, u32[]{:S(2)}) collective-permute-start(bf16[512,128]{1,0:T(8,128)(2,1)S(1)} %collective-permute-done.6.refs_11_), channel_id=1, source_target_pairs={{0,8},{8,16},{16,24},{24,32},{32,40},{40,48},{48,56},{56,64},{64,7... | collective-permute-start | bytes 393224 | tf_op jit(solution)/shard_map/ppermute | solution.py:272
  15.9 18.9 %copy-start.6 = (bf16[512,128]{1,0:T(8,128)(2,1)}, bf16[512,128]{1,0:T(8,128)(2,1)S(1)}, u32[]{:S(2)}) copy-start(bf16[512,128]{1,0:T(8,128)(2,1)S(1)} %collective-permute-done.1.refs_6_) | copy-start | bytes 393220
  15.9 7.1 %collective-permute-start.12 = (bf16[512,128]{1,0:T(8,128)(2,1)S(1)}, bf16[512,128]{1,0:T(8,128)(2,1)S(1)}, u32[]{:S(2)}, u32[]{:S(2)}) collective-permute-start(bf16[512,128]{1,0:T(8,128)(2,1)S(1)} %collective-permute-done.6.refs_11_), channel_id=1, source_target_pairs={{0,5},{1,4},{4,1},{5,0},{2,7},{3,6},{6,3},{7,2},{8,13},{9,12},{12,... | collective-permute-start | bytes 393224 | tf_op jit(solution)/shard_map/ppermute | solution.py:268
  15.9 18.8 %copy-start.7 = (bf16[512,128]{1,0:T(8,128)(2,1)}, bf16[512,128]{1,0:T(8,128)(2,1)S(1)}, u32[]{:S(2)}) copy-start(bf16[512,128]{1,0:T(8,128)(2,1)S(1)} %collective-permute-done.4.refs_9_) | copy-start | bytes 393220
  15.9 8.4 %collective-permute-start.10 = (bf16[512,128]{1,0:T(8,128)(2,1)S(1)}, bf16[512,128]{1,0:T(8,128)(2,1)S(1)}, u32[]{:S(2)}, u32[]{:S(2)}) collective-permute-start(bf16[512,128]{1,0:T(8,128)(2,1)S(1)} %collective-permute-done.6.refs_11_), channel_id=1, source_target_pairs={{0,4},{1,5},{4,0},{5,1},{2,6},{3,7},{6,2},{7,3},{8,12},{9,13},{12,... | collective-permute-start | bytes 393224 | tf_op jit(solution)/shard_map/ppermute | solution.py:268
  17.8 17.0 %copy-start.8 = (bf16[512,128]{1,0:T(8,128)(2,1)}, bf16[512,128]{1,0:T(8,128)(2,1)S(1)}, u32[]{:S(2)}) copy-start(bf16[512,128]{1,0:T(8,128)(2,1)S(1)} %collective-permute-done.refs_4_) | copy-start | bytes 393220
  17.8 7.8 %collective-permute-start.8 = (bf16[512,128]{1,0:T(8,128)(2,1)S(1)}, bf16[512,128]{1,0:T(8,128)(2,1)S(1)}, u32[]{:S(2)}, u32[]{:S(2)}) collective-permute-start(bf16[512,128]{1,0:T(8,128)(2,1)S(1)} %collective-permute-done.6.refs_11_), channel_id=1, source_target_pairs={{0,1},{1,0},{4,5},{5,4},{2,3},{3,2},{6,7},{7,6},{8,9},{9,8},{12,13... | collective-permute-start | bytes 393224 | tf_op jit(solution)/shard_map/ppermute | solution.py:268
  20.0 14.8 %copy-start.9 = (bf16[512,128]{1,0:T(8,128)(2,1)}, bf16[512,128]{1,0:T(8,128)(2,1)S(1)}, u32[]{:S(2)}) copy-start(bf16[512,128]{1,0:T(8,128)(2,1)S(1)} %collective-permute-done.3.refs_8_) | copy-start | bytes 393220
  20.0 5.7 %collective-permute-start.7 = (bf16[512,128]{1,0:T(8,128)(2,1)S(1)}, bf16[512,128]{1,0:T(8,128)(2,1)S(1)}, u32[]{:S(2)}, u32[]{:S(2)}) collective-permute-start(bf16[512,128]{1,0:T(8,128)(2,1)S(1)} %collective-permute-done.6.refs_11_), channel_id=1, source_target_pairs={{0,2},{2,0},{1,3},{3,1},{4,6},{6,4},{5,7},{7,5},{8,10},{10,8},{9,1... | collective-permute-start | bytes 393224 | tf_op jit(solution)/shard_map/ppermute | solution.py:263
  20.0 14.8 %copy-start.10 = (bf16[512,128]{1,0:T(8,128)(2,1)}, bf16[512,128]{1,0:T(8,128)(2,1)S(1)}, u32[]{:S(2)}) copy-start(bf16[512,128]{1,0:T(8,128)(2,1)S(1)} %collective-permute-done.14.refs_19_) | copy-start | bytes 393220
  20.1 5.8 %collective-permute-start.5 = (bf16[512,128]{1,0:T(8,128)(2,1)S(1)}, bf16[512,128]{1,0:T(8,128)(2,1)S(1)}, u32[]{:S(2)}, u32[]{:S(2)}) collective-permute-start(bf16[512,128]{1,0:T(8,128)(2,1)S(1)} %collective-permute-done.4.refs_9_), channel_id=1, source_target_pairs={{0,2},{2,0},{1,3},{3,1},{4,6},{6,4},{5,7},{7,5},{8,10},{10,8},{9,1... | collective-permute-start | bytes 393224 | tf_op jit(solution)/shard_map/ppermute | solution.py:263
  23.0 11.8 %copy-start.11 = (bf16[512,128]{1,0:T(8,128)(2,1)}, bf16[512,128]{1,0:T(8,128)(2,1)S(1)}, u32[]{:S(2)}) copy-start(bf16[512,128]{1,0:T(8,128)(2,1)S(1)} %collective-permute-done.12.refs_17_) | copy-start | bytes 393220
  23.0 8.1 %collective-permute-start.20 = (bf16[512,128]{1,0:T(8,128)(2,1)S(1)}, bf16[512,128]{1,0:T(8,128)(2,1)S(1)}, u32[]{:S(2)}, u32[]{:S(2)}) collective-permute-start(bf16[512,128]{1,0:T(8,128)(2,1)S(1)} %collective-permute-done.14.refs_19_), channel_id=1, source_target_pairs={{4,1},{5,0},{6,3},{7,2},{12,9},{13,8},{14,11},{15,10},{20,17},{21,... | collective-permute-start | bytes 393224 | tf_op jit(solution)/shard_map/ppermute | solution.py:268
  24.3 8.4 %collective-permute-start.18 = (bf16[512,128]{1,0:T(8,128)(2,1)S(1)}, bf16[512,128]{1,0:T(8,128)(2,1)S(1)}, u32[]{:S(2)}, u32[]{:S(2)}) collective-permute-start(bf16[512,128]{1,0:T(8,128)(2,1)S(1)} %collective-permute-done.14.refs_19_), channel_id=1, source_target_pairs={{4,0},{5,1},{6,2},{7,3},{12,8},{13,9},{14,10},{15,11},{20,16},{21,... | collective-permute-start | bytes 393224 | tf_op jit(solution)/shard_map/ppermute | solution.py:268
  25.6 7.1 %collective-permute-start.16 = (bf16[512,128]{1,0:T(8,128)(2,1)S(1)}, bf16[512,128]{1,0:T(8,128)(2,1)S(1)}, u32[]{:S(2)}, u32[]{:S(2)}) collective-permute-start(bf16[512,128]{1,0:T(8,128)(2,1)S(1)} %collective-permute-done.14.refs_19_), channel_id=1, source_target_pairs={{0,1},{1,0},{4,5},{5,4},{2,3},{3,2},{6,7},{7,6},{8,9},{9,8},{12,13... | collective-permute-start | bytes 393224 | tf_op jit(solution)/shard_map/ppermute | solution.py:268
  25.7 7.5 %collective-permute-start.15 = (bf16[512,128]{1,0:T(8,128)(2,1)S(1)}, bf16[512,128]{1,0:T(8,128)(2,1)S(1)}, u32[]{:S(2)}, u32[]{:S(2)}) collective-permute-start(bf16[512,128]{1,0:T(8,128)(2,1)S(1)} %collective-permute-done.14.refs_19_), channel_id=1, source_target_pairs={{0,2},{2,0},{1,3},{3,1},{4,6},{6,4},{5,7},{7,5},{8,10},{10,8},{9,1... | collective-permute-start | bytes 393224 | tf_op jit(solution)/shard_map/ppermute | solution.py:263
  25.9 7.4 %collective-permute-start.13 = (bf16[512,128]{1,0:T(8,128)(2,1)S(1)}, bf16[512,128]{1,0:T(8,128)(2,1)S(1)}, u32[]{:S(2)}, u32[]{:S(2)}) collective-permute-start(bf16[512,128]{1,0:T(8,128)(2,1)S(1)} %collective-permute-done.12.refs_17_), channel_id=1, source_target_pairs={{0,2},{2,0},{1,3},{3,1},{4,6},{6,4},{5,7},{7,5},{8,10},{10,8},{9,1... | collective-permute-start | bytes 393224 | tf_op jit(solution)/shard_map/ppermute | solution.py:263
  31.1 2.7 %collective-permute-start.11 = (bf16[512,128]{1,0:T(8,128)(2,1)S(1)}, bf16[512,128]{1,0:T(8,128)(2,1)S(1)}, u32[]{:S(2)}, u32[]{:S(2)}) collective-permute-start(bf16[512,128]{1,0:T(8,128)(2,1)S(1)} %collective-permute-done.10.refs_15_), channel_id=1, source_target_pairs={{0,2},{2,0},{1,3},{3,1},{4,6},{6,4},{5,7},{7,5},{8,10},{10,8},{9,1... | collective-permute-start | bytes 393224 | tf_op jit(solution)/shard_map/ppermute | solution.py:263
  32.7 1.3 %collective-permute-start.9 = (bf16[512,128]{1,0:T(8,128)(2,1)S(1)}, bf16[512,128]{1,0:T(8,128)(2,1)S(1)}, u32[]{:S(2)}, u32[]{:S(2)}) collective-permute-start(bf16[512,128]{1,0:T(8,128)(2,1)S(1)} %collective-permute-done.8.refs_13_), channel_id=1, source_target_pairs={{0,2},{2,0},{1,3},{3,1},{4,6},{6,4},{5,7},{7,5},{8,10},{10,8},{9,1... | collective-permute-start | bytes 393224 | tf_op jit(solution)/shard_map/ppermute | solution.py:263
  32.7 1.5 %collective-permute-start.21 = (bf16[512,128]{1,0:T(8,128)(2,1)S(1)}, bf16[512,128]{1,0:T(8,128)(2,1)S(1)}, u32[]{:S(2)}, u32[]{:S(2)}) collective-permute-start(bf16[512,128]{1,0:T(8,128)(2,1)S(1)} %collective-permute-done.20.refs_25_), channel_id=1, source_target_pairs={{0,2},{2,0},{1,3},{3,1},{4,6},{6,4},{5,7},{7,5},{8,10},{10,8},{9,1... | collective-permute-start | bytes 393224 | tf_op jit(solution)/shard_map/ppermute | solution.py:263
  33.2 1.3 %collective-permute-start.19 = (bf16[512,128]{1,0:T(8,128)(2,1)S(1)}, bf16[512,128]{1,0:T(8,128)(2,1)S(1)}, u32[]{:S(2)}, u32[]{:S(2)}) collective-permute-start(bf16[512,128]{1,0:T(8,128)(2,1)S(1)} %collective-permute-done.18.refs_23_), channel_id=1, source_target_pairs={{0,2},{2,0},{1,3},{3,1},{4,6},{6,4},{5,7},{7,5},{8,10},{10,8},{9,1... | collective-permute-start | bytes 393224 | tf_op jit(solution)/shard_map/ppermute | solution.py:263
  33.3 1.4 %collective-permute-start.17 = (bf16[512,128]{1,0:T(8,128)(2,1)S(1)}, bf16[512,128]{1,0:T(8,128)(2,1)S(1)}, u32[]{:S(2)}, u32[]{:S(2)}) collective-permute-start(bf16[512,128]{1,0:T(8,128)(2,1)S(1)} %collective-permute-done.16.refs_21_), channel_id=1, source_target_pairs={{0,2},{2,0},{1,3},{3,1},{4,6},{6,4},{5,7},{7,5},{8,10},{10,8},{9,1... | collective-permute-start | bytes 393224 | tf_op jit(solution)/shard_map/ppermute | solution.py:263
  68.7 6.3 %collective-permute-start.26 = (bf16[2,2,512,128]{3,2,1,0:T(8,128)(2,1)}, bf16[2,2,512,128]{3,2,1,0:T(8,128)(2,1)S(1)}, u32[]{:S(2)}, u32[]{:S(2)}) collective-permute-start(bf16[2,2,512,128]{3,2,1,0:T(8,128)(2,1)} %get-tuple-element.17), channel_id=1, source_target_pairs={{0,2},{2,0},{1,3},{3,1},{4,6},{6,4},{5,7},{7,5},{8,10},{10,8},{9,1... | collective-permute-start | bytes 1572872 | tf_op jit(solution)/shard_map/ppermute | solution.py:263
  73.3 16.6 %collective-permute-start.30 = (bf16[2,2,512,128]{3,2,1,0:T(8,128)(2,1)}, bf16[2,2,512,128]{3,2,1,0:T(8,128)(2,1)S(1)}, u32[]{:S(2)}, u32[]{:S(2)}) collective-permute-start(bf16[2,2,512,128]{3,2,1,0:T(8,128)(2,1)} %get-tuple-element.19), channel_id=1, source_target_pairs={{0,2},{2,0},{1,3},{3,1},{4,6},{6,4},{5,7},{7,5},{8,10},{10,8},{9,1... | collective-permute-start | bytes 1572872 | tf_op jit(solution)/shard_map/ppermute | solution.py:263
  73.4 19.6 %collective-permute-start.22 = (bf16[2,2,512,128]{3,2,1,0:T(8,128)(2,1)}, bf16[2,2,512,128]{3,2,1,0:T(8,128)(2,1)S(1)}, u32[]{:S(2)}, u32[]{:S(2)}) collective-permute-start(bf16[2,2,512,128]{3,2,1,0:T(8,128)(2,1)} %get-tuple-element.15), channel_id=1, source_target_pairs={{0,2},{2,0},{1,3},{3,1},{4,6},{6,4},{5,7},{7,5},{8,10},{10,8},{9,1... | collective-permute-start | bytes 1572872 | tf_op jit(solution)/shard_map/ppermute | solution.py:263
  76.2 13.7 %copy-start.1 = (bf16[2,2,512,128]{3,2,1,0:T(8,128)(2,1)S(1)}, bf16[2,2,512,128]{3,2,1,0:T(8,128)(2,1)}, u32[]{:S(2)}) copy-start(bf16[2,2,512,128]{3,2,1,0:T(8,128)(2,1)} %get-tuple-element.18) | copy-start | bytes 1572868
  76.3 25.5 %collective-permute-start.27 = (bf16[512,128]{1,0:T(8,128)(2,1)S(1)}, bf16[512,128]{1,0:T(8,128)(2,1)S(1)}, u32[]{:S(2)}, u32[]{:S(2)}) collective-permute-start(bf16[512,128]{1,0:T(8,128)(2,1)S(1)} %get-tuple-element.23), channel_id=1, source_target_pairs={{0,1},{1,0},{4,5},{5,4},{2,3},{3,2},{6,7},{7,6},{8,9},{9,8},{12,13... | collective-permute-start | bytes 393224 | tf_op jit(solution)/shard_map/ppermute | solution.py:268
  76.9 26.2 %collective-permute-start.29 = (bf16[512,128]{1,0:T(8,128)(2,1)S(1)}, bf16[512,128]{1,0:T(8,128)(2,1)S(1)}, u32[]{:S(2)}, u32[]{:S(2)}) collective-permute-start(bf16[512,128]{1,0:T(8,128)(2,1)S(1)} %get-tuple-element.24), channel_id=1, source_target_pairs={{0,5},{1,4},{4,1},{5,0},{2,7},{3,6},{6,3},{7,2},{8,13},{9,12},{12,... | collective-permute-start | bytes 393224 | tf_op jit(solution)/shard_map/ppermute | solution.py:268
  90.1 5.3 %collective-permute-start.31 = (bf16[512,128]{1,0:T(8,128)(2,1)S(1)}, bf16[512,128]{1,0:T(8,128)(2,1)S(1)}, u32[]{:S(2)}, u32[]{:S(2)}) collective-permute-start(bf16[512,128]{1,0:T(8,128)(2,1)S(1)} %get-tuple-element.26), channel_id=1, source_target_pairs={{0,1},{1,0},{4,5},{5,4},{2,3},{3,2},{6,7},{7,6},{8,9},{9,8},{12,13... | collective-permute-start | bytes 393224 | tf_op jit(solution)/shard_map/ppermute | solution.py:268
  90.4 11.1 %collective-permute-start.33 = (bf16[512,128]{1,0:T(8,128)(2,1)S(1)}, bf16[512,128]{1,0:T(8,128)(2,1)S(1)}, u32[]{:S(2)}, u32[]{:S(2)}) collective-permute-start(bf16[512,128]{1,0:T(8,128)(2,1)S(1)} %get-tuple-element.27), channel_id=1, source_target_pairs={{0,5},{1,4},{2,7},{3,6},{8,13},{9,12},{10,15},{11,14},{16,21},{17,... | collective-permute-start | bytes 393224 | tf_op jit(solution)/shard_map/ppermute | solution.py:268
  93.0 8.5 %collective-permute-start.32 = (bf16[512,128]{1,0:T(8,128)(2,1)S(1)}, bf16[512,128]{1,0:T(8,128)(2,1)S(1)}, u32[]{:S(2)}, u32[]{:S(2)}) collective-permute-start(bf16[512,128]{1,0:T(8,128)(2,1)S(1)} %get-tuple-element.28), channel_id=1, source_target_pairs={{0,4},{1,5},{2,6},{3,7},{8,12},{9,13},{10,14},{11,15},{16,20},{17,... | collective-permute-start | bytes 393224 | tf_op jit(solution)/shard_map/ppermute | solution.py:268
  95.4 9.0 %collective-permute-start.28 = (bf16[512,128]{1,0:T(8,128)(2,1)S(1)}, bf16[512,128]{1,0:T(8,128)(2,1)S(1)}, u32[]{:S(2)}, u32[]{:S(2)}) collective-permute-start(bf16[512,128]{1,0:T(8,128)(2,1)S(1)} %get-tuple-element.25), channel_id=1, source_target_pairs={{0,4},{1,5},{4,0},{5,1},{2,6},{3,7},{6,2},{7,3},{8,12},{9,13},{12,... | collective-permute-start | bytes 393224 | tf_op jit(solution)/shard_map/ppermute | solution.py:268
  101.6 7.8 %collective-permute-start.34 = (bf16[512,128]{1,0:T(8,128)(2,1)S(1)}, bf16[512,128]{1,0:T(8,128)(2,1)S(1)}, u32[]{:S(2)}, u32[]{:S(2)}) collective-permute-start(bf16[512,128]{1,0:T(8,128)(2,1)S(1)} %fusion.2), channel_id=1, source_target_pairs={{0,120},{8,0},{16,8},{24,16},{32,24},{40,32},{48,40},{56,48},{64,5... | collective-permute-start | bytes 393224 | tf_op jit(solution)/shard_map/ppermute | solution.py:272
  101.7 7.8 %collective-permute-start.23 = (bf16[512,128]{1,0:T(8,128)(2,1)S(1)}, bf16[512,128]{1,0:T(8,128)(2,1)S(1)}, u32[]{:S(2)}, u32[]{:S(2)}) collective-permute-start(bf16[512,128]{1,0:T(8,128)(2,1)S(1)} %get-tuple-element.20), channel_id=1, source_target_pairs={{0,1},{1,0},{4,5},{5,4},{2,3},{3,2},{6,7},{7,6},{8,9},{9,8},{12,13... | collective-permute-start | bytes 393224 | tf_op jit(solution)/shard_map/ppermute | solution.py:268
  101.8 9.4 %collective-permute-start.25 = (bf16[512,128]{1,0:T(8,128)(2,1)S(1)}, bf16[512,128]{1,0:T(8,128)(2,1)S(1)}, u32[]{:S(2)}, u32[]{:S(2)}) collective-permute-start(bf16[512,128]{1,0:T(8,128)(2,1)S(1)} %get-tuple-element.21), channel_id=1, source_target_pairs={{4,1},{5,0},{6,3},{7,2},{12,9},{13,8},{14,11},{15,10},{20,17},{21,... | collective-permute-start | bytes 393224 | tf_op jit(solution)/shard_map/ppermute | solution.py:268
  103.1 9.7 %collective-permute-start.24 = (bf16[512,128]{1,0:T(8,128)(2,1)S(1)}, bf16[512,128]{1,0:T(8,128)(2,1)S(1)}, u32[]{:S(2)}, u32[]{:S(2)}) collective-permute-start(bf16[512,128]{1,0:T(8,128)(2,1)S(1)} %get-tuple-element.22), channel_id=1, source_target_pairs={{4,0},{5,1},{6,2},{7,3},{12,8},{13,9},{14,10},{15,11},{20,16},{21,... | collective-permute-start | bytes 393224 | tf_op jit(solution)/shard_map/ppermute | solution.py:268
  109.4 7.1 %collective-permute-start.35 = (bf16[512,128]{1,0:T(8,128)(2,1)S(1)}, bf16[512,128]{1,0:T(8,128)(2,1)S(1)}, u32[]{:S(2)}, u32[]{:S(2)}) collective-permute-start(bf16[512,128]{1,0:T(8,128)(2,1)S(1)} %add_convert_fusion.4), channel_id=1, source_target_pairs={{0,120},{8,0},{16,8},{24,16},{32,24},{40,32},{48,40},{56,48},{64,5... | collective-permute-start | bytes 393224 | tf_op jit(solution)/shard_map/ppermute | solution.py:272
  116.7 5.0 %collective-permute-start.36 = (bf16[512,128]{1,0:T(8,128)(2,1)S(1)}, bf16[512,128]{1,0:T(8,128)(2,1)S(1)}, u32[]{:S(2)}, u32[]{:S(2)}) collective-permute-start(bf16[512,128]{1,0:T(8,128)(2,1)S(1)} %add_convert_fusion.3), channel_id=1, source_target_pairs={{0,1},{1,0},{4,5},{5,4},{2,3},{3,2},{6,7},{7,6},{8,9},{9,8},{12,13... | collective-permute-start | bytes 393224 | tf_op jit(solution)/shard_map/ppermute | solution.py:268
  (15 other events, 58.2 us)

commit v2 on v1

--- a/solution.py
+++ b/solution.py
@@ -33,26 +33,21 @@
     len_ref, q_ref, do_ref = refs[:3]
     kv_refs = refs[3:27]
     o_ref, dq_ref = refs[27:29]
-    out_refs = refs[29:35]
-    (kvs, dkvs, qt, dot_t, do_s, probs, row_max, total, acc, dq_acc, stage_s, delta, in_sem, out_sem) = refs[35:]
+    out_refs = refs[29:33]
+    (kvs, dkvs, qt, dot_t, do_s, probs, row_max, total, acc, dq_acc, stage_s, delta, in_sem, out_sem) = refs[33:]
     row = lax.axis_index("x") * 4 + lax.axis_index("y")
     zh = lax.axis_index("zh")
     core = lax.axis_index("core")
-    zl = lax.axis_index("zl")
     place = zh * 2 + core
 
     def slot_of(j, dz, dc):
         return (2 - j) * 4 + (1 - zh if dz else zh) * 2 + (1 - core if dc else core)
 
-    def part_of(dp):
-        return 1 - zl if dp else zl
-
-    order = [(j, dz, dp, dc) for j in range(ROWS) for dz in range(2) for dp in range(2) for dc in range(2)]
+    order = [(j, dz, part, dc) for j in range(ROWS) for dz in range(2) for part in range(2) for dc in range(2)]
 
     def in_copy(n):
-        j, dz, dp, dc = order[n]
-        slot = slot_of(j, dz, dc)
-        return pltpu.make_async_copy(kv_refs[n], kvs.at[slot, part_of(dp)], in_sem.at[n])
+        j, dz, part, dc = order[n]
+        return pltpu.make_async_copy(kv_refs[n], kvs.at[slot_of(j, dz, dc), part], in_sem.at[n])
 
     for n in range(len(order)):
         in_copy(n).start()
@@ -166,19 +161,19 @@
         delta[:, cols] = jnp.sum(o.astype(F32) * scaled.astype(F32), axis=0, keepdims=True)
 
     def out_copy(n, t):
-        j, dz, dp, dc = order[n]
-        return pltpu.make_async_copy(dkvs.at[t, part_of(dp)], out_refs[j * 2 + dc].at[dz, dp], out_sem.at[n])
+        j, dz, part, dc = order[n]
+        return pltpu.make_async_copy(dkvs.at[t, part], out_refs[part * 2 + dc].at[j, dz], out_sem.at[n])
 
     def send_out(t):
-        for n, (j, dz, dp, dc) in enumerate(order):
-            if dp == 0:
+        for n, (j, dz, part, dc) in enumerate(order):
+            if part == 0:
                 @pl.when(slot_of(j, dz, dc) == t)
                 def _():
                     out_copy(n, t).start()
                     out_copy(n + 2, t).start()
 
     dkvs[SLOTS] = jnp.zeros((2, BLK, HD), BF16)
-    for n, (j, dz, dp, dc) in enumerate(order):
+    for n, (j, dz, part, dc) in enumerate(order):
         slot = slot_of(j, dz, dc)
 
         @pl.when((slot < lo) | (slot > hi))
@@ -230,13 +225,13 @@
 def attention(seq_lengths, queries, d_out, blocks):
     vmem = pl.BlockSpec(memory_space=pltpu.VMEM)
     anywhere = pl.BlockSpec(memory_space=pl.ANY)
-    pair = jax.ShapeDtypeStruct((2, 2, BLK, HD), BF16)
+    grads = jax.ShapeDtypeStruct((ROWS, 2, BLK, HD), BF16)
     rows = jax.ShapeDtypeStruct((HEADS, BLK, HD), BF16)
     return pl.pallas_call(
         attention_kernel,
-        out_shape=(rows, rows) + (pair,) * 6,
+        out_shape=(rows, rows) + (grads,) * 4,
         in_specs=[pl.BlockSpec(memory_space=pltpu.SMEM), vmem, vmem] + [anywhere] * 24,
-        out_specs=[vmem, vmem] + [anywhere] * 6,
+        out_specs=[vmem, vmem] + [anywhere] * 4,
         scratch_shapes=[
             pltpu.VMEM((SLOTS, 2, BLK, HD), BF16),
             pltpu.VMEM((SLOTS + 1, 2, BLK, HD), BF16),
@@ -263,9 +258,13 @@
     return lax.ppermute(value, "core", [(0, 1), (1, 0)])
 
 
-def to_column(value, dz, dp, sources=(0, 1)):
-    pairs = [(2 * zh + zl, 2 * (zh ^ dz) + (zl ^ dp)) for zh in sources for zl in range(2)]
+def swap_z(value, sources=(0, 1)):
+    pairs = [(2 * zh + zl, 2 * (1 - zh) + (1 - zl)) for zh in sources for zl in range(2)]
     return lax.ppermute(value, ("zh", "zl"), pairs)
+
+
+def swap_head(value):
+    return lax.ppermute(value, "zl", [(0, 1), (1, 0)])
 
 
 def shift_row(value, by):
@@ -279,38 +278,35 @@
     return total.astype(BF16)
 
 
+def gathered(own):
+    row1 = shift_row(own, 1)
+    side0 = swap_z(own, (0,))
+    row1, side0 = lax.optimization_barrier((row1, side0))
+    row2 = shift_row(row1, 1)
+    side1 = swap_z(row1)
+    row2, side1 = lax.optimization_barrier((row2, side1))
+    side2 = swap_z(row2, (1,))
+    return [(block, swap_core(block)) for block in (own, side0, row1, side1, row2, side2)]
+
+
+def returned(keep, send):
+    first = lax.axis_index("zh") == 0
+    given = swap_core(send)
+    outer = swap_z(added(jnp.where(first, keep[2, 1], keep[0, 1]), jnp.where(first, given[2, 1], given[0, 1])))
+    middle = swap_z(added(keep[1, 1], given[1, 1]))
+    zero = jnp.zeros((), BF16)
+    back = shift_row(added(keep[2, 0], given[2, 0], jnp.where(first, zero, outer)), -1)
+    back = shift_row(added(keep[1, 0], given[1, 0], middle, back), -1)
+    half = added(keep[0, 0], given[0, 0], jnp.where(first, outer, zero), back)
+    return added(half, swap_head(half))
+
+
 def on_device(queries, key_rows, value_rows, d_out, seq_lengths):
-    zl = lax.axis_index("zl")
-    mine = jnp.where(zl == 0, key_rows, value_rows)
-    other = jnp.where(zl == 0, value_rows, key_rows)
-    row1 = shift_row(mine, 1)
-    row2 = shift_row(row1, 1)
-    pieces = [
-        mine, other, to_column(other, 1, 1, (0,)), to_column(mine, 1, 1, (0,)),
-        row1, to_column(row1, 0, 1), to_column(row1, 1, 0), to_column(row1, 1, 1),
-        row2, to_column(row2, 0, 1), to_column(row2, 1, 0, (1,)), to_column(row2, 1, 1, (1,)),
-    ]
     blocks = []
-    for piece in pieces:
-        blocks += [piece, swap_core(piece)]
+    for keys, values in zip(gathered(key_rows), gathered(value_rows)):
+        blocks += [*keys, *values]
     attended, grad_queries, *parts = attention(seq_lengths, queries, d_out, blocks)
-
-    def column(j, sources):
-        both = added(parts[2 * j], swap_core(parts[2 * j + 1]))
-        return added(
-            both[0, 0],
-            to_column(both[0, 1], 0, 1),
-            to_column(both[1, 0], 1, 0, sources),
-            to_column(both[1, 1], 1, 1, sources),
-        )
-
-    back = shift_row(column(2, (0,)), -1)
-    back = shift_row(added(column(1, (0, 1)), back), -1)
-    done = added(column(0, (1,)), back)
-    given = to_column(done, 0, 1)
-    grad_keys = jnp.where(zl == 0, done, given)
-    grad_values = jnp.where(zl == 0, given, done)
-    return attended, grad_queries, grad_keys, grad_values
+    return attended, grad_queries, returned(*parts[:2]), returned(*parts[2:])
 
 
 def solution(mesh):

time: 123 us -> 124 us (level)
  starting transfers between devices: 50.1 us -> 30.4 us
  Pallas kernels: 32.9 us -> 47.7 us
  waiting for transfers between devices: 33.8 us -> 40.6 us
    ppermute x18 -> x12, starting transfers between devices: 37.6 us -> 20.8 us  [the longest x10 20.7 us: swap_z(): return lax.ppermute(value, ('zh', 'zl'), pairs)]
    pallas_call x1, Pallas kernels: 32.9 us -> 47.7 us  [attention(): pl.pallas_call(attention_kernel, out_shape=(rows, rows) + (grads,) * 4, i...]
    ppermute x15 -> x14, starting transfers between devices: 7.86 us -> 2.79 us  [swap_core(): return lax.ppermute(value, 'core', [(0, 1), (1, 0)])]
    ppermute x4 -> x8, waiting for transfers between devices: 10.6 us -> 15.2 us  [shift_row(): lax.ppermute(value, ('x', 'y'), [(r, (r + by) % 16) for r in range(16)])]
    ppermute x4 -> x8, starting transfers between devices: 4.63 us -> 6.79 us  [shift_row(): lax.ppermute(value, ('x', 'y'), [(r, (r + by) % 16) for r in range(16)])]
    select_n x2 -> x0, other arithmetic: 1.71 us -> none  [the longest x1 0.99 us: on_device(): other = jnp.where(zl == 0, value_rows, key_rows)]
    ppermute x18 -> x12, waiting for transfers between devices: 20.9 us -> 22.4 us  [the longest x10 18.2 us: swap_z(): return lax.ppermute(value, ('zh', 'zl'), pairs)]
    convert_element_type x6 -> x10, other arithmetic: 1.71 us -> 3.07 us  [added(): return total.astype(BF16)]
  transfers between devices with their start and end apart: 37 -> 34, of which waited for: 16 -> 16; matrix products, arithmetic and copies ran while one was open for 1% -> 2% of each run, Pallas kernels for 0% -> 0%
where the time goes in v2:
time: 124 us
  Pallas kernels  47.7 us (38%)
  waiting for transfers between devices  40.6 us (33%)
  starting transfers between devices  30.4 us (25%)
  other arithmetic  3.07 us (2%)
    pallas_call x1, Pallas kernels, attention(): pl.pallas_call(attention_kernel, out_shape=(rows, rows) + (grads,) * 4, i...  47.7 us
    ppermute x10, starting transfers between devices, swap_z(): return lax.ppermute(value, ('zh', 'zl'), pairs)  20.7 us
    ppermute x10, waiting for transfers between devices, swap_z(): return lax.ppermute(value, ('zh', 'zl'), pairs)  18.2 us
    ppermute x8, waiting for transfers between devices, shift_row(): lax.ppermute(value, ('x', 'y'), [(r, (r + by) % 16) for r in range(16)])  15.2 us
    ppermute x8, starting transfers between devices, shift_row(): lax.ppermute(value, ('x', 'y'), [(r, (r + by) % 16) for r in range(16)])  6.79 us
    ppermute x2, waiting for transfers between devices, swap_head(): return lax.ppermute(value, 'zl', [(0, 1), (1, 0)])  4.25 us
    convert_element_type x10, other arithmetic, added(): return total.astype(BF16)  3.07 us
    ppermute x14, waiting for transfers between devices, swap_core(): return lax.ppermute(value, 'core', [(0, 1), (1, 0)])  2.99 us
  transfers between devices with their start and end apart: 34, of which 16 were waited for; matrix products, arithmetic and copies ran while one was open for 2% of the time, Pallas kernels for 0%

profile of v2, /device:TPU:26, one launch (start us, length us, event | category | flops | bytes accessed | tf_op | source)
XLA Modules:
  0.0 124.0 jit_solution(11765625856595349737)
XLA Ops:
  0.6 1.2 collective-permute-start.2
  1.8 5.9 %collective-permute-start.3 = (bf16[512,128]{1,0:T(8,128)(2,1)}, bf16[512,128]{1,0:T(8,128)(2,1)S(1)}, u32[]{:S(2)}, u32[]{:S(2)}) collective-permute-start(bf16[512,128]{1,0:T(8,128)(2,1)} %refs_3_.1), channel_id=1, source_target_pairs={{0,5},{1,4},{2,7},{3,6},{8,13},{9,12},{10,15},{11,14},{16,21},{17,... | collective-permute-start | bytes 393224 | tf_op jit(solution)/shard_map/ppermute | solution.py:263
  7.8 1.6 %collective-permute-start.5 = (bf16[512,128]{1,0:T(8,128)(2,1)}, bf16[512,128]{1,0:T(8,128)(2,1)S(1)}, u32[]{:S(2)}, u32[]{:S(2)}) collective-permute-start(bf16[512,128]{1,0:T(8,128)(2,1)} %refs_5_.1), channel_id=1, source_target_pairs={{0,8},{8,16},{16,24},{24,32},{32,40},{40,48},{48,56},{56,64},{64,7... | collective-permute-start | bytes 393224 | tf_op jit(solution)/shard_map/ppermute | solution.py:271
  9.4 1.3 %collective-permute-start.6 = (bf16[512,128]{1,0:T(8,128)(2,1)}, bf16[512,128]{1,0:T(8,128)(2,1)S(1)}, u32[]{:S(2)}, u32[]{:S(2)}) collective-permute-start(bf16[512,128]{1,0:T(8,128)(2,1)} %refs_5_.1), channel_id=1, source_target_pairs={{0,5},{1,4},{2,7},{3,6},{8,13},{9,12},{10,15},{11,14},{16,21},{17,... | collective-permute-start | bytes 393224 | tf_op jit(solution)/shard_map/ppermute | solution.py:263
  10.8 1.6 %collective-permute-start.10 = (bf16[512,128]{1,0:T(8,128)(2,1)S(1)}, bf16[512,128]{1,0:T(8,128)(2,1)S(1)}, u32[]{:S(2)}, u32[]{:S(2)}) collective-permute-start(bf16[512,128]{1,0:T(8,128)(2,1)S(1)} %collective-permute-done.2.refs_11_), channel_id=1, source_target_pairs={{0,8},{8,16},{16,24},{24,32},{32,40},{40,48},{48,56},{56,64},{64,7... | collective-permute-start | bytes 393224 | tf_op jit(solution)/shard_map/ppermute | solution.py:271
  12.4 3.4 %collective-permute-start.11 = (bf16[512,128]{1,0:T(8,128)(2,1)S(1)}, bf16[512,128]{1,0:T(8,128)(2,1)S(1)}, u32[]{:S(2)}, u32[]{:S(2)}) collective-permute-start(bf16[512,128]{1,0:T(8,128)(2,1)S(1)} %collective-permute-done.2.refs_11_), channel_id=1, source_target_pairs={{0,5},{1,4},{4,1},{5,0},{2,7},{3,6},{6,3},{7,2},{8,13},{9,12},{12,... | collective-permute-start | bytes 393224 | tf_op jit(solution)/shard_map/ppermute | solution.py:263
  15.9 2.0 %collective-permute-start.13 = (bf16[512,128]{1,0:T(8,128)(2,1)S(1)}, bf16[512,128]{1,0:T(8,128)(2,1)S(1)}, u32[]{:S(2)}, u32[]{:S(2)}) collective-permute-start(bf16[512,128]{1,0:T(8,128)(2,1)S(1)} %collective-permute-done.5.refs_13_), channel_id=1, source_target_pairs={{0,8},{8,16},{16,24},{24,32},{32,40},{40,48},{48,56},{56,64},{64,7... | collective-permute-start | bytes 393224 | tf_op jit(solution)/shard_map/ppermute | solution.py:271
  17.9 0.8 collective-permute-start.14
  18.7 0.5 collective-permute-start.1
  19.2 0.4 collective-permute-done.11.refs_15_
  19.6 1.3 %collective-permute-done.13.refs_21_ = bf16[512,128]{1,0:T(8,128)(2,1)S(1)} collective-permute-done((bf16[512,128]{1,0:T(8,128)(2,1)S(1)}, bf16[512,128]{1,0:T(8,128)(2,1)S(1)}, u32[]{:S(2)}, u32[]{:S(2)}) %collective-permute-start.13) | collective-permute-done | bytes 131104 | tf_op jit(solution)/shard_map/ppermute | solution.py:271
  20.9 3.1 %collective-permute-done.14.refs_17_ = bf16[512,128]{1,0:T(8,128)(2,1)S(1)} collective-permute-done((bf16[512,128]{1,0:T(8,128)(2,1)S(1)}, bf16[512,128]{1,0:T(8,128)(2,1)S(1)}, u32[]{:S(2)}, u32[]{:S(2)}) %collective-permute-start.14) | collective-permute-done | bytes 131104 | tf_op jit(solution)/shard_map/ppermute | solution.py:263
  24.1 0.5 collective-permute-start.7
  24.6 1.3 %collective-permute-start.18 = (bf16[512,128]{1,0:T(8,128)(2,1)S(1)}, bf16[512,128]{1,0:T(8,128)(2,1)S(1)}, u32[]{:S(2)}, u32[]{:S(2)}) collective-permute-start(bf16[512,128]{1,0:T(8,128)(2,1)S(1)} %collective-permute-done.10.refs_19_), channel_id=1, source_target_pairs={{4,1},{5,0},{6,3},{7,2},{12,9},{13,8},{14,11},{15,10},{20,17},{21,... | collective-permute-start | bytes 393224 | tf_op jit(solution)/shard_map/ppermute | solution.py:263
  25.9 1.3 %collective-permute-start.20 = (bf16[512,128]{1,0:T(8,128)(2,1)S(1)}, bf16[512,128]{1,0:T(8,128)(2,1)S(1)}, u32[]{:S(2)}, u32[]{:S(2)}) collective-permute-start(bf16[512,128]{1,0:T(8,128)(2,1)S(1)} %collective-permute-done.13.refs_21_), channel_id=1, source_target_pairs={{4,1},{5,0},{6,3},{7,2},{12,9},{13,8},{14,11},{15,10},{20,17},{21,... | collective-permute-start | bytes 393224 | tf_op jit(solution)/shard_map/ppermute | solution.py:263
  27.2 0.2 collective-permute-start.16
  27.4 0.4 collective-permute-start.17
  27.8 0.1 collective-permute-start.12
  27.9 6.1 %collective-permute-done.18.refs_23_ = bf16[512,128]{1,0:T(8,128)(2,1)S(1)} collective-permute-done((bf16[512,128]{1,0:T(8,128)(2,1)S(1)}, bf16[512,128]{1,0:T(8,128)(2,1)S(1)}, u32[]{:S(2)}, u32[]{:S(2)}) %collective-permute-start.18) | collective-permute-done | bytes 131104 | tf_op jit(solution)/shard_map/ppermute | solution.py:263
  34.0 2.0 %collective-permute-done.20.refs_25_ = bf16[512,128]{1,0:T(8,128)(2,1)S(1)} collective-permute-done((bf16[512,128]{1,0:T(8,128)(2,1)S(1)}, bf16[512,128]{1,0:T(8,128)(2,1)S(1)}, u32[]{:S(2)}, u32[]{:S(2)}) %collective-permute-start.20) | collective-permute-done | bytes 131104 | tf_op jit(solution)/shard_map/ppermute | solution.py:263
  36.0 0.5 collective-permute-start.21
  36.5 0.8 collective-permute-done.19.refs_24_
  37.3 0.2 collective-permute-done.21.refs_26_
  37.7 0.3 copy-done.22
  38.0 0.7 copy-done.23
  38.6 47.7 %attention.1 = (bf16[4,512,128]{2,1,0:T(8,128)(2,1)}, bf16[4,512,128]{2,1,0:T(8,128)(2,1)}, bf16[3,2,512,128]{3,2,1,0:T(8,128)(2,1)}, bf16[3,2,512,128]{3,2,1,0:...) custom-call(s32[16]{0:T(128)} %refs_0_.1, bf16[4,512,128]{2,1,0:T(8,128)(2,1)} %refs_1_.1, ...), custom_call_target="tpu_custom_call" | custom-call | flops 8589934592 | bytes 16777216 | tf_op jit(solution)/shard_map/attention/pallas_call | solution.py:230
  86.4 0.1 collective-permute-start.28
  86.5 0.5 collective-permute-start.22
  87.0 2.0 %collective-permute-done.28 = bf16[3,2,512,128]{3,2,1,0:T(8,128)(2,1)S(1)} collective-permute-done((bf16[3,2,512,128]{3,2,1,0:T(8,128)(2,1)}, bf16[3,2,512,128]{3,2,1,0:T(8,128)(2,1)S(1)}, u32[]{:S(2)}, u32[]{:S(2)}) %collective-permute-start.28) | collective-permute-done | bytes 786464 | tf_op jit(solution)/shard_map/ppermute | solution.py:258
  89.0 1.1 fusion.13
  90.1 0.1 collective-permute-start.29
  90.2 3.2 %collective-permute-start.30 = (bf16[512,128]{1,0:T(8,128)(2,1)S(1)}, bf16[512,128]{1,0:T(8,128)(2,1)S(1)}, u32[]{:S(2)}, u32[]{:S(2)}) collective-permute-start(bf16[512,128]{1,0:T(8,128)(2,1)S(1)} %get-tuple-element.32), channel_id=1, source_target_pairs={{0,5},{1,4},{4,1},{5,0},{2,7},{3,6},{6,3},{7,2},{8,13},{9,12},{12,... | collective-permute-start | bytes 393224 | tf_op jit(solution)/shard_map/ppermute | solution.py:263
  93.4 0.1 fusion.11
  93.6 0.2 collective-permute-start.23
  93.7 3.1 %collective-permute-start.24 = (bf16[512,128]{1,0:T(8,128)(2,1)S(1)}, bf16[512,128]{1,0:T(8,128)(2,1)S(1)}, u32[]{:S(2)}, u32[]{:S(2)}) collective-permute-start(bf16[512,128]{1,0:T(8,128)(2,1)S(1)} %get-tuple-element.34), channel_id=1, source_target_pairs={{0,5},{1,4},{4,1},{5,0},{2,7},{3,6},{6,3},{7,2},{8,13},{9,12},{12,... | collective-permute-start | bytes 393224 | tf_op jit(solution)/shard_map/ppermute | solution.py:263
  96.9 0.9 collective-permute-done.29
  97.9 5.5 %collective-permute-done.23 = bf16[512,128]{1,0:T(8,128)(2,1)S(1)} collective-permute-done((bf16[512,128]{1,0:T(8,128)(2,1)S(1)}, bf16[512,128]{1,0:T(8,128)(2,1)S(1)}, u32[]{:S(2)}, u32[]{:S(2)}) %collective-permute-start.23) | collective-permute-done | bytes 131104 | tf_op jit(solution)/shard_map/ppermute | solution.py:263
  103.5 1.4 %collective-permute-done.31 = bf16[512,128]{1,0:T(8,128)(2,1)S(1)} collective-permute-done((bf16[512,128]{1,0:T(8,128)(2,1)S(1)}, bf16[512,128]{1,0:T(8,128)(2,1)S(1)}, u32[]{:S(2)}, u32[]{:S(2)}) %collective-permute-start.31) | collective-permute-done | bytes 131104 | tf_op jit(solution)/shard_map/ppermute | solution.py:271
  105.1 0.3 collective-permute-done.24
  105.4 5.6 %collective-permute-done.25 = bf16[512,128]{1,0:T(8,128)(2,1)S(1)} collective-permute-done((bf16[512,128]{1,0:T(8,128)(2,1)S(1)}, bf16[512,128]{1,0:T(8,128)(2,1)S(1)}, u32[]{:S(2)}, u32[]{:S(2)}) %collective-permute-start.25) | collective-permute-done | bytes 131104 | tf_op jit(solution)/shard_map/ppermute | solution.py:271
  111.1 1.2 %collective-permute-done.32 = bf16[512,128]{1,0:T(8,128)(2,1)S(1)} collective-permute-done((bf16[512,128]{1,0:T(8,128)(2,1)S(1)}, bf16[512,128]{1,0:T(8,128)(2,1)S(1)}, u32[]{:S(2)}, u32[]{:S(2)}) %collective-permute-start.32) | collective-permute-done | bytes 131104 | tf_op jit(solution)/shard_map/ppermute | solution.py:271
  112.4 0.1 collective-permute-start.33
  112.5 5.6 %collective-permute-done.26 = bf16[512,128]{1,0:T(8,128)(2,1)S(1)} collective-permute-done((bf16[512,128]{1,0:T(8,128)(2,1)S(1)}, bf16[512,128]{1,0:T(8,128)(2,1)S(1)}, u32[]{:S(2)}, u32[]{:S(2)}) %collective-permute-start.26) | collective-permute-done | bytes 131104 | tf_op jit(solution)/shard_map/ppermute | solution.py:271
  118.2 0.1 fusion.9
  118.2 0.1 collective-permute-start.27
  118.4 0.7 add_convert_fusion
  119.0 4.2 %collective-permute-done.27 = bf16[512,128]{1,0:T(8,128)(2,1)S(1)} collective-permute-done((bf16[512,128]{1,0:T(8,128)(2,1)S(1)}, bf16[512,128]{1,0:T(8,128)(2,1)S(1)}, u32[]{:S(2)}, u32[]{:S(2)}) %collective-permute-start.27) | collective-permute-done | bytes 131104 | tf_op jit(solution)/shard_map/ppermute | solution.py:267
  123.3 0.7 add_convert_fusion.3
  (79 shorter events, 0.8 us)
Async XLA Ops:
  0.6 10.1 %collective-permute-start.2 = (bf16[512,128]{1,0:T(8,128)(2,1)}, bf16[512,128]{1,0:T(8,128)(2,1)S(1)}, u32[]{:S(2)}, u32[]{:S(2)}) collective-permute-start(bf16[512,128]{1,0:T(8,128)(2,1)} %refs_3_.1), channel_id=1, source_target_pairs={{0,8},{8,16},{16,24},{24,32},{32,40},{40,48},{48,56},{56,64},{64,7... | collective-permute-start | bytes 393224 | tf_op jit(solution)/shard_map/ppermute | solution.py:271
  1.8 8.9 %collective-permute-start.3 = (bf16[512,128]{1,0:T(8,128)(2,1)}, bf16[512,128]{1,0:T(8,128)(2,1)S(1)}, u32[]{:S(2)}, u32[]{:S(2)}) collective-permute-start(bf16[512,128]{1,0:T(8,128)(2,1)} %refs_3_.1), channel_id=1, source_target_pairs={{0,5},{1,4},{2,7},{3,6},{8,13},{9,12},{10,15},{11,14},{16,21},{17,... | collective-permute-start | bytes 393224 | tf_op jit(solution)/shard_map/ppermute | solution.py:263
  7.8 8.1 %collective-permute-start.5 = (bf16[512,128]{1,0:T(8,128)(2,1)}, bf16[512,128]{1,0:T(8,128)(2,1)S(1)}, u32[]{:S(2)}, u32[]{:S(2)}) collective-permute-start(bf16[512,128]{1,0:T(8,128)(2,1)} %refs_5_.1), channel_id=1, source_target_pairs={{0,8},{8,16},{16,24},{24,32},{32,40},{40,48},{48,56},{56,64},{64,7... | collective-permute-start | bytes 393224 | tf_op jit(solution)/shard_map/ppermute | solution.py:271
  9.4 6.4 %collective-permute-start.6 = (bf16[512,128]{1,0:T(8,128)(2,1)}, bf16[512,128]{1,0:T(8,128)(2,1)S(1)}, u32[]{:S(2)}, u32[]{:S(2)}) collective-permute-start(bf16[512,128]{1,0:T(8,128)(2,1)} %refs_5_.1), channel_id=1, source_target_pairs={{0,5},{1,4},{2,7},{3,6},{8,13},{9,12},{10,15},{11,14},{16,21},{17,... | collective-permute-start | bytes 393224 | tf_op jit(solution)/shard_map/ppermute | solution.py:263
  10.7 26.8 %copy-start.2 = (bf16[512,128]{1,0:T(8,128)(2,1)}, bf16[512,128]{1,0:T(8,128)(2,1)S(1)}, u32[]{:S(2)}) copy-start(bf16[512,128]{1,0:T(8,128)(2,1)S(1)} %collective-permute-done.2.refs_11_) | copy-start | bytes 393220
  10.8 26.8 %copy-start.3 = (bf16[512,128]{1,0:T(8,128)(2,1)}, bf16[512,128]{1,0:T(8,128)(2,1)S(1)}, u32[]{:S(2)}) copy-start(bf16[512,128]{1,0:T(8,128)(2,1)S(1)} %collective-permute-done.3.refs_7_) | copy-start | bytes 393220
  10.8 7.9 %collective-permute-start.10 = (bf16[512,128]{1,0:T(8,128)(2,1)S(1)}, bf16[512,128]{1,0:T(8,128)(2,1)S(1)}, u32[]{:S(2)}, u32[]{:S(2)}) collective-permute-start(bf16[512,128]{1,0:T(8,128)(2,1)S(1)} %collective-permute-done.2.refs_11_), channel_id=1, source_target_pairs={{0,8},{8,16},{16,24},{24,32},{32,40},{40,48},{48,56},{56,64},{64,7... | collective-permute-start | bytes 393224 | tf_op jit(solution)/shard_map/ppermute | solution.py:271
  12.4 7.2 %collective-permute-start.11 = (bf16[512,128]{1,0:T(8,128)(2,1)S(1)}, bf16[512,128]{1,0:T(8,128)(2,1)S(1)}, u32[]{:S(2)}, u32[]{:S(2)}) collective-permute-start(bf16[512,128]{1,0:T(8,128)(2,1)S(1)} %collective-permute-done.2.refs_11_), channel_id=1, source_target_pairs={{0,5},{1,4},{4,1},{5,0},{2,7},{3,6},{6,3},{7,2},{8,13},{9,12},{12,... | collective-permute-start | bytes 393224 | tf_op jit(solution)/shard_map/ppermute | solution.py:263
  15.9 21.7 %copy-start.4 = (bf16[512,128]{1,0:T(8,128)(2,1)}, bf16[512,128]{1,0:T(8,128)(2,1)S(1)}, u32[]{:S(2)}) copy-start(bf16[512,128]{1,0:T(8,128)(2,1)S(1)} %collective-permute-done.5.refs_13_) | copy-start | bytes 393220
  15.9 21.6 %copy-start.5 = (bf16[512,128]{1,0:T(8,128)(2,1)}, bf16[512,128]{1,0:T(8,128)(2,1)S(1)}, u32[]{:S(2)}) copy-start(bf16[512,128]{1,0:T(8,128)(2,1)S(1)} %collective-permute-done.6.refs_9_) | copy-start | bytes 393220
  15.9 5.0 %collective-permute-start.13 = (bf16[512,128]{1,0:T(8,128)(2,1)S(1)}, bf16[512,128]{1,0:T(8,128)(2,1)S(1)}, u32[]{:S(2)}, u32[]{:S(2)}) collective-permute-start(bf16[512,128]{1,0:T(8,128)(2,1)S(1)} %collective-permute-done.5.refs_13_), channel_id=1, source_target_pairs={{0,8},{8,16},{16,24},{24,32},{32,40},{40,48},{48,56},{56,64},{64,7... | collective-permute-start | bytes 393224 | tf_op jit(solution)/shard_map/ppermute | solution.py:271
  17.9 6.2 %collective-permute-start.14 = (bf16[512,128]{1,0:T(8,128)(2,1)S(1)}, bf16[512,128]{1,0:T(8,128)(2,1)S(1)}, u32[]{:S(2)}, u32[]{:S(2)}) collective-permute-start(bf16[512,128]{1,0:T(8,128)(2,1)S(1)} %collective-permute-done.5.refs_13_), channel_id=1, source_target_pairs={{0,5},{1,4},{4,1},{5,0},{2,7},{3,6},{6,3},{7,2},{8,13},{9,12},{12,... | collective-permute-start | bytes 393224 | tf_op jit(solution)/shard_map/ppermute | solution.py:263
  18.7 5.4 %collective-permute-start = (bf16[512,128]{1,0:T(8,128)(2,1)}, bf16[512,128]{1,0:T(8,128)(2,1)S(1)}, u32[]{:S(2)}, u32[]{:S(2)}) collective-permute-start(bf16[512,128]{1,0:T(8,128)(2,1)} %refs_3_.1), channel_id=1, source_target_pairs={{0,2},{2,0},{1,3},{3,1},{4,6},{6,4},{5,7},{7,5},{8,10},{10,8},{9,1... | collective-permute-start | bytes 393224 | tf_op jit(solution)/shard_map/ppermute | solution.py:258
  18.7 18.9 %copy-start.6 = (bf16[512,128]{1,0:T(8,128)(2,1)}, bf16[512,128]{1,0:T(8,128)(2,1)S(1)}, u32[]{:S(2)}) copy-start(bf16[512,128]{1,0:T(8,128)(2,1)S(1)} %collective-permute-done.10.refs_19_) | copy-start | bytes 393220
  18.7 5.9 %collective-permute-start.1 = (bf16[512,128]{1,0:T(8,128)(2,1)}, bf16[512,128]{1,0:T(8,128)(2,1)S(1)}, u32[]{:S(2)}, u32[]{:S(2)}) collective-permute-start(bf16[512,128]{1,0:T(8,128)(2,1)} %refs_5_.1), channel_id=1, source_target_pairs={{0,2},{2,0},{1,3},{3,1},{4,6},{6,4},{5,7},{7,5},{8,10},{10,8},{9,1... | collective-permute-start | bytes 393224 | tf_op jit(solution)/shard_map/ppermute | solution.py:258
  19.6 17.9 %copy-start.7 = (bf16[512,128]{1,0:T(8,128)(2,1)}, bf16[512,128]{1,0:T(8,128)(2,1)S(1)}, u32[]{:S(2)}) copy-start(bf16[512,128]{1,0:T(8,128)(2,1)S(1)} %collective-permute-done.11.refs_15_) | copy-start | bytes 393220
  19.6 6.3 %collective-permute-start.8 = (bf16[512,128]{1,0:T(8,128)(2,1)S(1)}, bf16[512,128]{1,0:T(8,128)(2,1)S(1)}, u32[]{:S(2)}, u32[]{:S(2)}) collective-permute-start(bf16[512,128]{1,0:T(8,128)(2,1)S(1)} %collective-permute-done.2.refs_11_), channel_id=1, source_target_pairs={{0,2},{2,0},{1,3},{3,1},{4,6},{6,4},{5,7},{7,5},{8,10},{10,8},{9,1... | collective-permute-start | bytes 393224 | tf_op jit(solution)/shard_map/ppermute | solution.py:258
  20.9 16.6 %copy-start.8 = (bf16[512,128]{1,0:T(8,128)(2,1)}, bf16[512,128]{1,0:T(8,128)(2,1)S(1)}, u32[]{:S(2)}) copy-start(bf16[512,128]{1,0:T(8,128)(2,1)S(1)} %collective-permute-done.13.refs_21_) | copy-start | bytes 393220
  20.9 6.3 %collective-permute-start.9 = (bf16[512,128]{1,0:T(8,128)(2,1)S(1)}, bf16[512,128]{1,0:T(8,128)(2,1)S(1)}, u32[]{:S(2)}, u32[]{:S(2)}) collective-permute-start(bf16[512,128]{1,0:T(8,128)(2,1)S(1)} %collective-permute-done.5.refs_13_), channel_id=1, source_target_pairs={{0,2},{2,0},{1,3},{3,1},{4,6},{6,4},{5,7},{7,5},{8,10},{10,8},{9,1... | collective-permute-start | bytes 393224 | tf_op jit(solution)/shard_map/ppermute | solution.py:258
  24.0 13.5 %copy-start.9 = (bf16[512,128]{1,0:T(8,128)(2,1)}, bf16[512,128]{1,0:T(8,128)(2,1)S(1)}, u32[]{:S(2)}) copy-start(bf16[512,128]{1,0:T(8,128)(2,1)S(1)} %collective-permute-done.14.refs_17_) | copy-start | bytes 393220
  24.1 3.3 %collective-permute-start.4 = (bf16[512,128]{1,0:T(8,128)(2,1)S(1)}, bf16[512,128]{1,0:T(8,128)(2,1)S(1)}, u32[]{:S(2)}, u32[]{:S(2)}) collective-permute-start(bf16[512,128]{1,0:T(8,128)(2,1)S(1)} %collective-permute-done.3.refs_7_), channel_id=1, source_target_pairs={{0,2},{2,0},{1,3},{3,1},{4,6},{6,4},{5,7},{7,5},{8,10},{10,8},{9,1... | collective-permute-start | bytes 393224 | tf_op jit(solution)/shard_map/ppermute | solution.py:258
  24.1 13.5 %copy-start.10 = (bf16[512,128]{1,0:T(8,128)(2,1)}, bf16[512,128]{1,0:T(8,128)(2,1)S(1)}, u32[]{:S(2)}) copy-start(bf16[512,128]{1,0:T(8,128)(2,1)S(1)} %collective-permute-done.refs_4_) | copy-start | bytes 393220
  24.1 3.7 %collective-permute-start.7 = (bf16[512,128]{1,0:T(8,128)(2,1)S(1)}, bf16[512,128]{1,0:T(8,128)(2,1)S(1)}, u32[]{:S(2)}, u32[]{:S(2)}) collective-permute-start(bf16[512,128]{1,0:T(8,128)(2,1)S(1)} %collective-permute-done.6.refs_9_), channel_id=1, source_target_pairs={{0,2},{2,0},{1,3},{3,1},{4,6},{6,4},{5,7},{7,5},{8,10},{10,8},{9,1... | collective-permute-start | bytes 393224 | tf_op jit(solution)/shard_map/ppermute | solution.py:258
  24.6 13.0 %copy-start.11 = (bf16[512,128]{1,0:T(8,128)(2,1)}, bf16[512,128]{1,0:T(8,128)(2,1)S(1)}, u32[]{:S(2)}) copy-start(bf16[512,128]{1,0:T(8,128)(2,1)S(1)} %collective-permute-done.1.refs_6_) | copy-start | bytes 393220
  24.6 9.4 %collective-permute-start.18 = (bf16[512,128]{1,0:T(8,128)(2,1)S(1)}, bf16[512,128]{1,0:T(8,128)(2,1)S(1)}, u32[]{:S(2)}, u32[]{:S(2)}) collective-permute-start(bf16[512,128]{1,0:T(8,128)(2,1)S(1)} %collective-permute-done.10.refs_19_), channel_id=1, source_target_pairs={{4,1},{5,0},{6,3},{7,2},{12,9},{13,8},{14,11},{15,10},{20,17},{21,... | collective-permute-start | bytes 393224 | tf_op jit(solution)/shard_map/ppermute | solution.py:263
  25.9 11.7 %copy-start.12 = (bf16[512,128]{1,0:T(8,128)(2,1)}, bf16[512,128]{1,0:T(8,128)(2,1)S(1)}, u32[]{:S(2)}) copy-start(bf16[512,128]{1,0:T(8,128)(2,1)S(1)} %collective-permute-done.8.refs_12_) | copy-start | bytes 393220
  25.9 10.1 %collective-permute-start.20 = (bf16[512,128]{1,0:T(8,128)(2,1)S(1)}, bf16[512,128]{1,0:T(8,128)(2,1)S(1)}, u32[]{:S(2)}, u32[]{:S(2)}) collective-permute-start(bf16[512,128]{1,0:T(8,128)(2,1)S(1)} %collective-permute-done.13.refs_21_), channel_id=1, source_target_pairs={{4,1},{5,0},{6,3},{7,2},{12,9},{13,8},{14,11},{15,10},{20,17},{21,... | collective-permute-start | bytes 393224 | tf_op jit(solution)/shard_map/ppermute | solution.py:263
  27.2 10.4 %copy-start.13 = (bf16[512,128]{1,0:T(8,128)(2,1)}, bf16[512,128]{1,0:T(8,128)(2,1)S(1)}, u32[]{:S(2)}) copy-start(bf16[512,128]{1,0:T(8,128)(2,1)S(1)} %collective-permute-done.9.refs_14_) | copy-start | bytes 393220
  27.2 8.8 %collective-permute-start.16 = (bf16[512,128]{1,0:T(8,128)(2,1)S(1)}, bf16[512,128]{1,0:T(8,128)(2,1)S(1)}, u32[]{:S(2)}, u32[]{:S(2)}) collective-permute-start(bf16[512,128]{1,0:T(8,128)(2,1)S(1)} %collective-permute-done.10.refs_19_), channel_id=1, source_target_pairs={{0,2},{2,0},{1,3},{3,1},{4,6},{6,4},{5,7},{7,5},{8,10},{10,8},{9,1... | collective-permute-start | bytes 393224 | tf_op jit(solution)/shard_map/ppermute | solution.py:258
  27.4 10.2 %copy-start.14 = (bf16[512,128]{1,0:T(8,128)(2,1)}, bf16[512,128]{1,0:T(8,128)(2,1)S(1)}, u32[]{:S(2)}) copy-start(bf16[512,128]{1,0:T(8,128)(2,1)S(1)} %collective-permute-done.4.refs_8_) | copy-start | bytes 393220
  27.4 9.1 %collective-permute-start.17 = (bf16[512,128]{1,0:T(8,128)(2,1)S(1)}, bf16[512,128]{1,0:T(8,128)(2,1)S(1)}, u32[]{:S(2)}, u32[]{:S(2)}) collective-permute-start(bf16[512,128]{1,0:T(8,128)(2,1)S(1)} %collective-permute-done.13.refs_21_), channel_id=1, source_target_pairs={{0,2},{2,0},{1,3},{3,1},{4,6},{6,4},{5,7},{7,5},{8,10},{10,8},{9,1... | collective-permute-start | bytes 393224 | tf_op jit(solution)/shard_map/ppermute | solution.py:258
  27.8 9.8 %copy-start.15 = (bf16[512,128]{1,0:T(8,128)(2,1)}, bf16[512,128]{1,0:T(8,128)(2,1)S(1)}, u32[]{:S(2)}) copy-start(bf16[512,128]{1,0:T(8,128)(2,1)S(1)} %collective-permute-done.7.refs_10_) | copy-start | bytes 393220
  27.8 8.7 %collective-permute-start.12 = (bf16[512,128]{1,0:T(8,128)(2,1)S(1)}, bf16[512,128]{1,0:T(8,128)(2,1)S(1)}, u32[]{:S(2)}, u32[]{:S(2)}) collective-permute-start(bf16[512,128]{1,0:T(8,128)(2,1)S(1)} %collective-permute-done.11.refs_15_), channel_id=1, source_target_pairs={{0,2},{2,0},{1,3},{3,1},{4,6},{6,4},{5,7},{7,5},{8,10},{10,8},{9,1... | collective-permute-start | bytes 393224 | tf_op jit(solution)/shard_map/ppermute | solution.py:258
  34.0 2.5 %collective-permute-start.15 = (bf16[512,128]{1,0:T(8,128)(2,1)S(1)}, bf16[512,128]{1,0:T(8,128)(2,1)S(1)}, u32[]{:S(2)}, u32[]{:S(2)}) collective-permute-start(bf16[512,128]{1,0:T(8,128)(2,1)S(1)} %collective-permute-done.14.refs_17_), channel_id=1, source_target_pairs={{0,2},{2,0},{1,3},{3,1},{4,6},{6,4},{5,7},{7,5},{8,10},{10,8},{9,1... | collective-permute-start | bytes 393224 | tf_op jit(solution)/shard_map/ppermute | solution.py:258
  36.0 1.3 %collective-permute-start.19 = (bf16[512,128]{1,0:T(8,128)(2,1)S(1)}, bf16[512,128]{1,0:T(8,128)(2,1)S(1)}, u32[]{:S(2)}, u32[]{:S(2)}) collective-permute-start(bf16[512,128]{1,0:T(8,128)(2,1)S(1)} %collective-permute-done.18.refs_23_), channel_id=1, source_target_pairs={{0,2},{2,0},{1,3},{3,1},{4,6},{6,4},{5,7},{7,5},{8,10},{10,8},{9,1... | collective-permute-start | bytes 393224 | tf_op jit(solution)/shard_map/ppermute | solution.py:258
  36.0 1.5 %collective-permute-start.21 = (bf16[512,128]{1,0:T(8,128)(2,1)S(1)}, bf16[512,128]{1,0:T(8,128)(2,1)S(1)}, u32[]{:S(2)}, u32[]{:S(2)}) collective-permute-start(bf16[512,128]{1,0:T(8,128)(2,1)S(1)} %collective-permute-done.20.refs_25_), channel_id=1, source_target_pairs={{0,2},{2,0},{1,3},{3,1},{4,6},{6,4},{5,7},{7,5},{8,10},{10,8},{9,1... | collective-permute-start | bytes 393224 | tf_op jit(solution)/shard_map/ppermute | solution.py:258
  86.4 2.6 %collective-permute-start.28 = (bf16[3,2,512,128]{3,2,1,0:T(8,128)(2,1)}, bf16[3,2,512,128]{3,2,1,0:T(8,128)(2,1)S(1)}, u32[]{:S(2)}, u32[]{:S(2)}) collective-permute-start(bf16[3,2,512,128]{3,2,1,0:T(8,128)(2,1)} %get-tuple-element.31), channel_id=1, source_target_pairs={{0,2},{2,0},{1,3},{3,1},{4,6},{6,4},{5,7},{7,5},{8,10},{10,8},{9,1... | collective-permute-start | bytes 2359304 | tf_op jit(solution)/shard_map/ppermute | solution.py:258
  86.5 7.0 %collective-permute-start.22 = (bf16[3,2,512,128]{3,2,1,0:T(8,128)(2,1)}, bf16[3,2,512,128]{3,2,1,0:T(8,128)(2,1)S(1)}, u32[]{:S(2)}, u32[]{:S(2)}) collective-permute-start(bf16[3,2,512,128]{3,2,1,0:T(8,128)(2,1)} %get-tuple-element.29), channel_id=1, source_target_pairs={{0,2},{2,0},{1,3},{3,1},{4,6},{6,4},{5,7},{7,5},{8,10},{10,8},{9,1... | collective-permute-start | bytes 2359304 | tf_op jit(solution)/shard_map/ppermute | solution.py:258
  90.1 7.6 %collective-permute-start.29 = (bf16[512,128]{1,0:T(8,128)(2,1)S(1)}, bf16[512,128]{1,0:T(8,128)(2,1)S(1)}, u32[]{:S(2)}, u32[]{:S(2)}) collective-permute-start(bf16[512,128]{1,0:T(8,128)(2,1)S(1)} %get-tuple-element.33), channel_id=1, source_target_pairs={{0,5},{1,4},{4,1},{5,0},{2,7},{3,6},{6,3},{7,2},{8,13},{9,12},{12,... | collective-permute-start | bytes 393224 | tf_op jit(solution)/shard_map/ppermute | solution.py:263
  90.2 13.3 %collective-permute-start.30 = (bf16[512,128]{1,0:T(8,128)(2,1)S(1)}, bf16[512,128]{1,0:T(8,128)(2,1)S(1)}, u32[]{:S(2)}, u32[]{:S(2)}) collective-permute-start(bf16[512,128]{1,0:T(8,128)(2,1)S(1)} %get-tuple-element.32), channel_id=1, source_target_pairs={{0,5},{1,4},{4,1},{5,0},{2,7},{3,6},{6,3},{7,2},{8,13},{9,12},{12,... | collective-permute-start | bytes 393224 | tf_op jit(solution)/shard_map/ppermute | solution.py:263
  93.6 9.8 %collective-permute-start.23 = (bf16[512,128]{1,0:T(8,128)(2,1)S(1)}, bf16[512,128]{1,0:T(8,128)(2,1)S(1)}, u32[]{:S(2)}, u32[]{:S(2)}) collective-permute-start(bf16[512,128]{1,0:T(8,128)(2,1)S(1)} %get-tuple-element.35), channel_id=1, source_target_pairs={{0,5},{1,4},{4,1},{5,0},{2,7},{3,6},{6,3},{7,2},{8,13},{9,12},{12,... | collective-permute-start | bytes 393224 | tf_op jit(solution)/shard_map/ppermute | solution.py:263
  93.7 11.6 %collective-permute-start.24 = (bf16[512,128]{1,0:T(8,128)(2,1)S(1)}, bf16[512,128]{1,0:T(8,128)(2,1)S(1)}, u32[]{:S(2)}, u32[]{:S(2)}) collective-permute-start(bf16[512,128]{1,0:T(8,128)(2,1)S(1)} %get-tuple-element.34), channel_id=1, source_target_pairs={{0,5},{1,4},{4,1},{5,0},{2,7},{3,6},{6,3},{7,2},{8,13},{9,12},{12,... | collective-permute-start | bytes 393224 | tf_op jit(solution)/shard_map/ppermute | solution.py:263
  97.8 7.1 %collective-permute-start.31 = (bf16[512,128]{1,0:T(8,128)(2,1)S(1)}, bf16[512,128]{1,0:T(8,128)(2,1)S(1)}, u32[]{:S(2)}, u32[]{:S(2)}) collective-permute-start(bf16[512,128]{1,0:T(8,128)(2,1)S(1)} %fusion), channel_id=1, source_target_pairs={{0,120},{8,0},{16,8},{24,16},{32,24},{40,32},{48,40},{56,48},{64,5... | collective-permute-start | bytes 393224 | tf_op jit(solution)/shard_map/ppermute | solution.py:271
  103.4 7.5 %collective-permute-start.25 = (bf16[512,128]{1,0:T(8,128)(2,1)S(1)}, bf16[512,128]{1,0:T(8,128)(2,1)S(1)}, u32[]{:S(2)}, u32[]{:S(2)}) collective-permute-start(bf16[512,128]{1,0:T(8,128)(2,1)S(1)} %fusion.5), channel_id=1, source_target_pairs={{0,120},{8,0},{16,8},{24,16},{32,24},{40,32},{48,40},{56,48},{64,5... | collective-permute-start | bytes 393224 | tf_op jit(solution)/shard_map/ppermute | solution.py:271
  105.0 7.3 %collective-permute-start.32 = (bf16[512,128]{1,0:T(8,128)(2,1)S(1)}, bf16[512,128]{1,0:T(8,128)(2,1)S(1)}, u32[]{:S(2)}, u32[]{:S(2)}) collective-permute-start(bf16[512,128]{1,0:T(8,128)(2,1)S(1)} %fusion.2), channel_id=1, source_target_pairs={{0,120},{8,0},{16,8},{24,16},{32,24},{40,32},{48,40},{56,48},{64,5... | collective-permute-start | bytes 393224 | tf_op jit(solution)/shard_map/ppermute | solution.py:271
  111.0 7.1 %collective-permute-start.26 = (bf16[512,128]{1,0:T(8,128)(2,1)S(1)}, bf16[512,128]{1,0:T(8,128)(2,1)S(1)}, u32[]{:S(2)}, u32[]{:S(2)}) collective-permute-start(bf16[512,128]{1,0:T(8,128)(2,1)S(1)} %fusion.7), channel_id=1, source_target_pairs={{0,120},{8,0},{16,8},{24,16},{32,24},{40,32},{48,40},{56,48},{64,5... | collective-permute-start | bytes 393224 | tf_op jit(solution)/shard_map/ppermute | solution.py:271
  112.4 5.9 %collective-permute-start.33 = (bf16[512,128]{1,0:T(8,128)(2,1)S(1)}, bf16[512,128]{1,0:T(8,128)(2,1)S(1)}, u32[]{:S(2)}, u32[]{:S(2)}) collective-permute-start(bf16[512,128]{1,0:T(8,128)(2,1)S(1)} %fusion.4), channel_id=1, source_target_pairs={{0,1},{1,0},{2,3},{3,2},{4,5},{5,4},{6,7},{7,6},{8,9},{9,8},{10,11... | collective-permute-start | bytes 393224 | tf_op jit(solution)/shard_map/ppermute | solution.py:267
  118.2 5.0 %collective-permute-start.27 = (bf16[512,128]{1,0:T(8,128)(2,1)S(1)}, bf16[512,128]{1,0:T(8,128)(2,1)S(1)}, u32[]{:S(2)}, u32[]{:S(2)}) collective-permute-start(bf16[512,128]{1,0:T(8,128)(2,1)S(1)} %fusion.9), channel_id=1, source_target_pairs={{0,1},{1,0},{2,3},{3,2},{4,5},{5,4},{6,7},{7,6},{8,9},{9,8},{10,11... | collective-permute-start | bytes 393224 | tf_op jit(solution)/shard_map/ppermute | solution.py:267
  (10 other events, 26.5 us)

commit v3 on v2

v3 whole, which is shorter than its diff:
```python
import math

import jax
import jax.numpy as jnp
from jax import lax
from jax.experimental import pallas as pl
from jax.experimental.pallas import tpu as pltpu
from jax.sharding import Mesh, PartitionSpec as P

NEGATIVE = -1e30
BLK = 512
HEADS = 4
HD = 128
NQ = HEADS * BLK
HALF = BLK // 2
ROWS = 3
SLOTS = 4 * ROWS
SCALE = HD ** -0.5
LOG2 = SCALE * math.log2(math.e)
BOUND = 64.0
F32 = jnp.float32
BF16 = jnp.bfloat16
SEQ = ("x", "y", "zh", "core")
VMEM = pl.BlockSpec(memory_space=pltpu.VMEM)
SMEM = pl.BlockSpec(memory_space=pltpu.SMEM)
ANY = pl.BlockSpec(memory_space=pl.ANY)
DMA = pltpu.SemaphoreType.DMA
NEAR = [(dz, dc) for dz in range(2) for dc in range(2)]


def shape(dims, dtype):
    return jax.ShapeDtypeStruct(dims, dtype)


def params(flops):
    return dict(
        compiler_params=pltpu.CompilerParams(vmem_limit_bytes=56 << 20),
        cost_estimate=pl.CostEstimate(flops=flops, bytes_accessed=16 << 20, transcendentals=4 << 20),
    )


def dot(a, b):
    return lax.dot_general(a, b, (((1,), (0,)), ((), ())), preferred_element_type=F32)


class Place:
    def __init__(self, len_ref):
        row = lax.axis_index("x") * 4 + lax.axis_index("y")
        self.zh = lax.axis_index("zh")
        self.core = lax.axis_index("core")
        place = self.zh * 2 + self.core
        base = (row - 2) * (4 * BLK)
        first = base + (8 + place) * BLK
        self.q_pos = lax.broadcasted_iota(jnp.int32, (1, BLK), 1) + (8 + place) * BLK
        starts = jnp.zeros((1, BLK), jnp.int32) - base
        first_start = -base
        last_start = -base
        end = jnp.int32(0)
        for c in range(16):
            end = end + len_ref[c]
            rel = end - base
            starts = jnp.where(self.q_pos >= rel, rel, starts)
            first_start = jnp.where(end <= first, rel, first_start)
            last_start = jnp.where(end <= first + BLK - 1, rel, last_start)
        self.starts = starts
        self.last_start = last_start
        self.lo = first_start // BLK
        self.hi = 8 + place

    def slot(self, j, dz, dc):
        return (2 - j) * 4 + (1 - self.zh if dz else self.zh) * 2 + (1 - self.core if dc else self.core)

    def span(self, rows):
        return jnp.maximum(self.lo, (2 - max(rows)) * 4), jnp.minimum(self.hi + 1, (3 - min(rows)) * 4)

    def mask(self, t):
        k_pos = lax.broadcasted_iota(jnp.int32, (BLK, BLK), 0) + t * BLK
        return (k_pos >= self.starts) & (k_pos <= self.q_pos)


class Fetch:
    def __init__(self, at, rows, refs, kvs, sem, base):
        order = [(j, dz, dc) for j in rows for dz, dc in NEAR]
        self.copies = [
            pltpu.make_async_copy(refs[n], kvs.at[at.slot(*where) - base], sem.at[n]) for n, where in enumerate(order)
        ]
        for copy in self.copies:
            copy.start()

    def wait(self):
        for copy in self.copies:
            copy.wait()


def transposed(q_ref, qt):
    for h in range(HEADS):
        qt[:, h * BLK:(h + 1) * BLK] = q_ref[h].T


def forward_rows(at, begin, end, base, kvs, qt, probs, row_max, total, acc, norms, finish=None, settle=None):
    def forward(t, masked):
        k = kvs[t - base, 0]
        v_t = kvs[t - base, 1].T
        squares = dot(jnp.square(k.astype(F32)).astype(BF16), jnp.ones((HD, HD), BF16))
        norms[...] = jnp.maximum(norms[...], jnp.max(squares.reshape(BLK // 8, 8, HD), axis=0))
        if masked:
            allowed = at.mask(t)

        def score(h):
            s = dot(k, qt[:, h * HALF:(h + 1) * HALF])
            return jnp.where(allowed[:, (h % 2) * HALF:(h % 2 + 1) * HALF], s, NEGATIVE) if masked else s

        def soft(h, s):
            cols = slice(h * HALF, (h + 1) * HALF)
            p = jnp.exp2(s * LOG2 - row_max[:, cols])
            total[:, cols] += jnp.sum(p, axis=0, keepdims=True)
            p = p.astype(BF16)
            probs[t - base, :, cols] = p
            return p

        def product(h, p):
            acc[:, h * HALF:(h + 1) * HALF] += dot(v_t, p)

        weights = soft(0, score(0))
        s = score(1)
        for h in range(1, 2 * HEADS):
            held, weights = weights, soft(h, s)
            if h + 1 < 2 * HEADS:
                s = score(h + 1)
            product(h - 1, held)
        product(2 * HEADS - 1, weights)

    def step(t, carry):
        masked = (t * BLK < at.last_start) | (t == at.hi)

        @pl.when(masked)
        def _():
            forward(t, True)

        @pl.when(jnp.logical_not(masked))
        def _():
            forward(t, False)

        if finish is not None:
            finish(t)
        return carry

    def run():
        total[...] = jnp.zeros((1, NQ), F32)
        acc[...] = jnp.zeros((HD, NQ), F32)
        lax.fori_loop(begin, end, step, 0)

    def max_step(t, carry):
        allowed = at.mask(t)
        for h in range(HEADS):
            cols = slice(h * BLK, (h + 1) * BLK)
            s = jnp.where(allowed, dot(kvs[t - base, 0], qt[:, cols]), NEGATIVE)
            row_max[:, cols] = jnp.maximum(row_max[:, cols], jnp.max(s, axis=0, keepdims=True))
        return carry

    q_norm = jnp.max(dot(jnp.ones((8, HD), BF16), jnp.square(qt[...].astype(F32)).astype(BF16)))
    norms[...] = jnp.zeros((8, HD), F32)
    row_max[...] = jnp.zeros((1, NQ), F32)
    run()

    @pl.when(q_norm * jnp.max(norms[...]) > 0.98 * (BOUND / LOG2) ** 2)
    def _():
        if settle is not None:
            settle()
        row_max[...] = jnp.full((1, NQ), NEGATIVE, F32)
        lax.fori_loop(begin, end, max_step, 0)
        row_max[...] = row_max[...] * LOG2
        run()


def backward_rows(at, begin, end, base, rows, kvs, q_ref, dot_t, do_s, delta, probs, stage, dq_acc, dkvs, out_refs, out_sem, ready=None):
    order = [(j, dz, dc) for j in rows for dz, dc in NEAR]
    spare = 4 * len(rows)

    def out_copy(n, t):
        j, dz, dc = order[n]
        return pltpu.make_async_copy(dkvs.at[t - base], out_refs[dc].at[rows.index(j), dz], out_sem.at[n])

    dkvs[spare] = jnp.zeros((2, BLK, HD), BF16)
    for n, where in enumerate(order):
        slot = at.slot(*where)

        @pl.when((slot < begin) | (slot >= end))
        def _():
            out_copy(n, base + spare).start()

    def step(t, carry):
        if ready is not None:
            ready(t)
        k_t = kvs[t - base, 0].T
        v = kvs[t - base, 1]

        def dp_of(h):
            return dot(v, dot_t[:, h * BLK:(h + 1) * BLK])

        def ds_of(h, dp):
            cols = slice(h * BLK, (h + 1) * BLK)
            ds = (probs[t - base, :, cols].astype(F32) * (dp - delta[:, cols])).astype(BF16)
            stage[:, cols] = ds
            return ds

        def dq_of(h, ds):
            dq_acc[:, h * BLK:(h + 1) * BLK] += dot(k_t, ds)

        d0 = dp_of(0)
        d1 = dp_of(1)
        s0 = ds_of(0, d0)
        dkvs[t - base, 1] = dot(probs[t - base], do_s[...]).astype(BF16)
        d2 = dp_of(2)
        dq_of(0, s0)
        s1 = ds_of(1, d1)
        d3 = dp_of(3)
        dq_of(1, s1)
        s2 = ds_of(2, d2)
        dq_of(2, s2)
        s3 = ds_of(3, d3)
        dq_of(3, s3)
        dkvs[t - base, 0] = (dot(stage[...], q_ref[...].reshape(NQ, HD)) * SCALE).astype(BF16)
        for n, where in enumerate(order):
            @pl.when(at.slot(*where) == t)
            def _():
                out_copy(n, t).start()

        return carry

    lax.fori_loop(begin, end, step, 0)

    def wait():
        for n in range(len(order)):
            out_copy(n, base).wait()

    return wait


def forward_kernel(*refs):
    len_ref, q_ref = refs[:2]
    kv_refs = refs[2:10]
    p_out, row_max, total, acc = refs[10:14]
    kvs, qt, probs, norms, in_sem, out_sem = refs[14:]
    at = Place(len_ref)
    fetch = Fetch(at, (0, 1), kv_refs, kvs, in_sem, 4)
    transposed(q_ref, qt)
    begin, end = at.span((0, 1))

    def out_copy(t):
        return pltpu.make_async_copy(probs.at[t - 4], p_out.at[t - 4], out_sem.at[t - 4])

    def settle():
        def wait(t, carry):
            out_copy(t).wait()
            return carry

        lax.fori_loop(begin, end, wait, 0)

    fetch.wait()
    forward_rows(
        at, begin, end, 4, kvs, qt, probs, row_max, total, acc, norms, lambda t: out_copy(t).start(), settle
    )
    settle()


def forward_call(seq_lengths, queries, blocks):
    return pl.pallas_call(
        forward_kernel,
        out_shape=(shape((8, BLK, NQ), BF16), shape((1, NQ), F32), shape((1, NQ), F32), shape((HD, NQ), F32)),
        in_specs=[SMEM, VMEM] + [ANY] * 8,
        out_specs=[ANY, VMEM, VMEM, VMEM],
        scratch_shapes=[
            pltpu.VMEM((8, 2, BLK, HD), BF16),
            pltpu.VMEM((HD, NQ), BF16),
            pltpu.VMEM((8, BLK, NQ), BF16),
            pltpu.VMEM((8, HD), F32),
            DMA((8,)),
            DMA((8,)),
        ],
        name="forward_near",
        **params(3 << 30),
    )(seq_lengths, queries, *blocks)


def middle_kernel(*refs):
    len_ref, q_ref, do_ref, max_near, total_near, acc_near = refs[:6]
    kv_refs = refs[6:10]
    o_ref, dot_t, do_s, delta, dq_acc = refs[10:15]
    out_refs = refs[15:17]
    kvs, dkvs, qt, probs, row_max, total, acc, norms, far_dot_t, far_do_s, far_delta, stage, in_sem, out_sem = refs[17:]
    at = Place(len_ref)
    fetch = Fetch(at, (2,), kv_refs, kvs, in_sem, 0)
    transposed(q_ref, qt)
    begin, end = at.span((2,))
    fetch.wait()
    forward_rows(at, begin, end, 0, kvs, qt, probs, row_max, total, acc, norms)
    for h in range(HEADS):
        cols = slice(h * BLK, (h + 1) * BLK)
        top = jnp.maximum(row_max[:, cols], max_near[:, cols])
        far = jnp.exp2(row_max[:, cols] - top)
        near = jnp.exp2(max_near[:, cols] - top)
        inverse = 1.0 / (far * total[:, cols] + near * total_near[:, cols])
        far = far * inverse
        near = near * inverse
        o = (acc[:, cols] * far + acc_near[:, cols] * near).astype(BF16)
        o_ref[h] = o.T
        o = o.astype(F32)
        grad = do_ref[h].T.astype(F32)
        for factor, t_ref, n_ref, d_ref in ((near, dot_t, do_s, delta), (far, far_dot_t, far_do_s, far_delta)):
            scaled = (grad * factor).astype(BF16)
            t_ref[:, cols] = scaled
            n_ref[h * BLK:(h + 1) * BLK] = scaled.T
            d_ref[:, cols] = jnp.sum(o * scaled.astype(F32), axis=0, keepdims=True)
    dq_acc[...] = jnp.zeros((HD, NQ), F32)
    wait = backward_rows(
        at, begin, end, 0, (2,), kvs, q_ref, far_dot_t, far_do_s, far_delta, probs, stage, dq_acc, dkvs, out_refs, out_sem
    )
    wait()


def middle_call(seq_lengths, queries, d_out, row_max, total, acc, blocks):
    grads = shape((1, 2, 2, BLK, HD), BF16)
    return pl.pallas_call(
        middle_kernel,
        out_shape=(
            shape((HEADS, BLK, HD), BF16),
            shape((HD, NQ), BF16),
            shape((NQ, HD), BF16),
            shape((1, NQ), F32),
            shape((HD, NQ), F32),
            grads,
            grads,
        ),
        in_specs=[SMEM] + [VMEM] * 5 + [ANY] * 4,
        out_specs=[VMEM] * 5 + [ANY] * 2,
        scratch_shapes=[
            pltpu.VMEM((4, 2, BLK, HD), BF16),
            pltpu.VMEM((5, 2, BLK, HD), BF16),
            pltpu.VMEM((HD, NQ), BF16),
            pltpu.VMEM((4, BLK, NQ), BF16),
            pltpu.VMEM((1, NQ), F32),
            pltpu.VMEM((1, NQ), F32),
            pltpu.VMEM((HD, NQ), F32),
            pltpu.VMEM((8, HD), F32),
            pltpu.VMEM((HD, NQ), BF16),
            pltpu.VMEM((NQ, HD), BF16),
            pltpu.VMEM((1, NQ), F32),
            pltpu.VMEM((BLK, NQ), BF16),
            DMA((4,)),
            DMA((4,)),
        ],
        name="middle_far",
        **params(5 << 30),
    )(seq_lengths, queries, d_out, row_max, total, acc, *blocks)


def backward_call(seq_lengths, queries, dot_t, do_s, delta, dq_in, probs, blocks, rows, last):
    count = 4 * len(rows)
    base = (2 - max(rows)) * 4

    def kernel(*refs):
        len_ref, q_ref, dot_ref, do_ref, delta_ref, dq_ref, p_in = refs[:7]
        kv_refs = refs[7:7 + count]
        dq_out = refs[7 + count]
        out_refs = refs[8 + count:10 + count]
        kvs, dkvs, tiles, stage, dq_acc, in_sem, p_sem, out_sem = refs[10 + count:]
        at = Place(len_ref)
        fetch = Fetch(at, rows, kv_refs, kvs, in_sem, base)
        begin, end = at.span(rows)

        def p_copy(t):
            return pltpu.make_async_copy(p_in.at[t - 4], tiles.at[t - base], p_sem.at[t - base])

        def start(t, carry):
            p_copy(t).start()
            return carry

        lax.fori_loop(begin, end, start, 0)
        dq_acc[...] = dq_ref[...]
        fetch.wait()
        wait = backward_rows(
            at, begin, end, base, rows, kvs, q_ref, dot_ref, do_ref, delta_ref, tiles, stage, dq_acc, dkvs, out_refs,
            out_sem, lambda t: p_copy(t).wait()
        )
        if last:
            for h in range(HEADS):
                dq_out[h] = (dq_acc[:, h * BLK:(h + 1) * BLK] * SCALE).astype(BF16).T
        else:
            dq_out[...] = dq_acc[...]
        wait()

    grads = shape((len(rows), 2, 2, BLK, HD), BF16)
    return pl.pallas_call(
        kernel,
        out_shape=(shape((HEADS, BLK, HD), BF16) if last else shape((HD, NQ), F32), grads, grads),
        in_specs=[SMEM] + [VMEM] * 5 + [ANY] * (1 + count),
        out_specs=[VMEM, ANY, ANY],
        scratch_shapes=[
            pltpu.VMEM((count, 2, BLK, HD), BF16),
            pltpu.VMEM((count + 1, 2, BLK, HD), BF16),
            pltpu.VMEM((count, BLK, NQ), BF16),
            pltpu.VMEM((BLK, NQ), BF16),
            pltpu.VMEM((HD, NQ), F32),
            DMA((count,)),
            DMA((count,)),
            DMA((count,)),
        ],
        name="backward_rows",
        **params(3 << 30),
    )(seq_lengths, queries, dot_t, do_s, delta, dq_in, probs, *blocks)


def swap_core(value):
    return lax.ppermute(value, "core", [(0, 1), (1, 0)])


def swap_z(value, sources=(0, 1)):
    pairs = [(2 * zh + zl, 2 * (1 - zh) + (1 - zl)) for zh in sources for zl in range(2)]
    return lax.ppermute(value, ("zh", "zl"), pairs)


def swap_head(value):
    return lax.ppermute(value, "zl", [(0, 1), (1, 0)])


def shift_row(value, by):
    return lax.ppermute(value, ("x", "y"), [(r, (r + by) % 16) for r in range(16)])


def added(*values):
    total = values[0].astype(F32)
    for value in values[1:]:
        total = total + value.astype(F32)
    return total.astype(BF16)


def on_device(queries, key_rows, value_rows, d_out, seq_lengths):
    own = jnp.stack([key_rows, value_rows])
    row1 = shift_row(own, 1)
    side0 = swap_z(own, (0,))
    row1, side0 = lax.optimization_barrier((row1, side0))
    row2 = shift_row(row1, 1)
    side1 = swap_z(row1)
    side2 = swap_z(row2, (1,))
    near = []
    for block in (own, side0, row1, side1):
        near += [block, swap_core(block)]
    far = []
    for block in (row2, side2):
        far += [block, swap_core(block)]
    probs, row_max, total, acc = forward_call(seq_lengths, queries, near)
    attended, dot_t, do_s, delta, dq, keep2, send2 = middle_call(
        seq_lengths, queries, d_out, row_max, total, acc, far
    )
    given = swap_core(send2)
    here2, there2 = (added(keep2[0, dz], given[0, dz]) for dz in range(2))
    dq, here2, there2 = lax.optimization_barrier((dq, here2, there2))
    side2 = swap_z(there2, (0,))
    dq, keep1, send1 = backward_call(seq_lengths, queries, dot_t, do_s, delta, dq, probs, near[4:], (1,), False)
    given = swap_core(send1)
    here1, there1 = ([added(keep1[0, dz, part], given[0, dz, part]) for part in range(2)] for dz in range(2))
    sum2 = added(here2, side2)
    dq, here1, there1, sum2 = lax.optimization_barrier((dq, here1, there1, sum2))
    back2 = shift_row(sum2, -1)
    side1 = [swap_z(there) for there in there1]
    dq, keep0, send0 = backward_call(seq_lengths, queries, dot_t, do_s, delta, dq, probs, near[:4], (0,), True)
    given = swap_core(send0)
    outs = []
    for part in range(2):
        here0, there0 = (added(keep0[0, dz, part], given[0, dz, part]) for dz in range(2))
        back1 = shift_row(added(here1[part], side1[part], back2[part]), -1)
        half = added(here0, swap_z(there0, (1,)), back1)
        outs.append(added(half, swap_head(half)))
    return attended, dq, outs[0], outs[1]


def solution(mesh):
    fine = Mesh(mesh.devices.reshape(4, 4, 2, 2, 2), ("x", "y", "zh", "core", "zl"))
    tokens = P("zl", SEQ, None)
    rows = P(SEQ, None)
    return jax.shard_map(
        on_device,
        mesh=fine,
        in_specs=(tokens, rows, rows, tokens, P()),
        out_specs=(tokens, tokens, rows, rows),
        check_vma=False,
    )
```

time: 124 us -> 161 us (1.30)
  the two profiles are of different devices: /device:TPU:26 before, /device:TPU:6 now
where the time goes in v3:
time: 161 us; the launch traced here: 159 us
  starting transfers between devices  65.7 us (41%)
  waiting for transfers between devices  47.9 us (30%)
  Pallas kernels  35.5 us (22%)
  other arithmetic  7.11 us (4%)
  local copies, waits for them, and re-layouts  2.21 us (1%)
    ppermute x5, starting transfers between devices, shift_row(): lax.ppermute(value, ('x', 'y'), [(r, (r + by) % 16) for r in range(16)])  29.9 us
    ppermute x8, waiting for transfers between devices, swap_z(): return lax.ppermute(value, ('zh', 'zl'), pairs)  29.9 us
    ppermute x8, starting transfers between devices, swap_z(): return lax.ppermute(value, ('zh', 'zl'), pairs)  26.7 us
    pallas_call x2, Pallas kernels, backward_call(): pl.pallas_call(kernel, out_shape=(shape((HEADS, BLK, HD), BF16) if last e...  14.9 us
    pallas_call x1, Pallas kernels, forward_call(): pl.pallas_call(forward_kernel, out_shape=(shape((8, BLK, NQ), BF16), shap...  14.6 us
    ppermute x5, waiting for transfers between devices, shift_row(): lax.ppermute(value, ('x', 'y'), [(r, (r + by) % 16) for r in range(16)])  12.6 us
    ppermute x9, starting transfers between devices, swap_core(): return lax.ppermute(value, 'core', [(0, 1), (1, 0)])  7.07 us
    convert_element_type x8, other arithmetic, added(): return total.astype(BF16)  6.11 us
  transfers between devices with their start and end apart: 24, of which 13 were waited for; matrix products, arithmetic and copies ran while one was open for 1% of the time, Pallas kernels for 9%

profile of v3, /device:TPU:6, one launch (start us, length us, event | category | flops | bytes accessed | tf_op | source)
XLA Modules:
  0.0 159.4 jit_solution(13896233470709348143)
XLA Ops:
  0.6 1.0 pad_maximum_fusion.refs_2_.refs_7_
  1.6 6.0 %collective-permute-start.2 = (bf16[2,512,128]{2,1,0:T(8,128)(2,1)S(1)}, bf16[2,512,128]{2,1,0:T(8,128)(2,1)S(1)}, u32[]{:S(2)}, u32[]{:S(2)}) collective-permute-start(bf16[2,512,128]{2,1,0:T(8,128)(2,1)S(1)} %pad_maximum_fusion.refs_2_.refs_7_), channel_id=1, source_target_pairs={{0,5},{1,4},{2,7},{3,6},{8,13},{9,12},{10,15},{11,14},{16,21},{17,... | collective-permute-start | bytes 786440 | tf_op jit(solution)/shard_map/ppermute | solution.py:420
  7.6 1.6 %collective-permute-start.1 = (bf16[2,512,128]{2,1,0:T(8,128)(2,1)S(1)}, bf16[2,512,128]{2,1,0:T(8,128)(2,1)S(1)}, u32[]{:S(2)}, u32[]{:S(2)}) collective-permute-start(bf16[2,512,128]{2,1,0:T(8,128)(2,1)S(1)} %pad_maximum_fusion.refs_2_.refs_7_), channel_id=1, source_target_pairs={{0,8},{8,16},{16,24},{24,32},{32,40},{40,48},{48,56},{56,64},{64,7... | collective-permute-start | bytes 786440 | tf_op jit(solution)/shard_map/ppermute | solution.py:428
  9.2 3.9 %collective-permute-done.2.refs_4_.refs_9_ = bf16[2,512,128]{2,1,0:T(8,128)(2,1)S(1)} collective-permute-done((bf16[2,512,128]{2,1,0:T(8,128)(2,1)S(1)}, bf16[2,512,128]{2,1,0:T(8,128)(2,1)S(1)}, u32[]{:S(2)}, u32[]{:S(2)}) %collective-permute-start.2) | collective-permute-done | bytes 262176 | tf_op jit(solution)/shard_map/ppermute | solution.py:420
  13.1 4.4 %collective-permute-done.1.refs_6_.refs_7_ = bf16[2,512,128]{2,1,0:T(8,128)(2,1)S(1)} collective-permute-done((bf16[2,512,128]{2,1,0:T(8,128)(2,1)S(1)}, bf16[2,512,128]{2,1,0:T(8,128)(2,1)S(1)}, u32[]{:S(2)}, u32[]{:S(2)}) %collective-permute-start.1) | collective-permute-done | bytes 262176 | tf_op jit(solution)/shard_map/ppermute | solution.py:428
  17.6 0.9 collective-permute-start.5
  18.5 0.5 collective-permute-start.4
  19.0 7.5 %collective-permute-done.7.refs_6_ = bf16[2,512,128]{2,1,0:T(8,128)(2,1)S(1)} collective-permute-done((bf16[2,512,128]{2,1,0:T(8,128)(2,1)S(1)}, bf16[2,512,128]{2,1,0:T(8,128)(2,1)S(1)}, u32[]{:S(2)}, u32[]{:S(2)}) %collective-permute-start.7) | collective-permute-done | bytes 262176 | tf_op jit(solution)/shard_map/ppermute | solution.py:428
  26.5 1.3 collective-permute-start.9
  27.9 0.5 collective-permute-start.6
  28.4 0.1 collective-permute-start.8
  28.5 7.5 %collective-permute-done.9.refs_8_ = bf16[2,512,128]{2,1,0:T(8,128)(2,1)S(1)} collective-permute-done((bf16[2,512,128]{2,1,0:T(8,128)(2,1)S(1)}, bf16[2,512,128]{2,1,0:T(8,128)(2,1)S(1)}, u32[]{:S(2)}, u32[]{:S(2)}) %collective-permute-start.9) | collective-permute-done | bytes 262176 | tf_op jit(solution)/shard_map/ppermute | solution.py:420
  36.1 0.6 copy-done.3
  36.7 0.1 copy-done.6
  36.8 0.7 copy-done.7
  37.5 14.6 %forward_near.1 = (bf16[8,512,2048]{2,1,0:T(8,128)(2,1)}, f32[1,2048]{1,0:T(1,128)}, f32[1,2048]{1,0:T(1,128)}, f32[128,2048]{1,0:T(8,128)}) custom-call(s32[16]{0:T(128)} %refs_0_.7, bf16[4,512,128]{2,1,0:T(8,128)(2,1)} %refs_1_.7, bf16[2,512,128]{2,1,0:T(8,128)(2,1)} %copy-done, bf16[2,512,128]{2,1,0:T(8,128)(2,1)} %copy-done.2, ...), custom_call_target="tpu_custom_call" | custom-call | flops 3221225472 | bytes 16777216 | tf_op jit(solution)/shard_map/forward_near/pallas_call | solution.py:268
  52.2 0.7 copy-done.10
  52.9 6.0 %middle_far.1 = (bf16[4,512,128]{2,1,0:T(8,128)(2,1)}, bf16[128,2048]{1,0:T(8,128)(2,1)}, bf16[2048,128]{1,0:T(8,128)(2,1)}, f32[1,2048]{1,0:T(1,128)}, f32[128,...) custom-call(s32[16]{0:T(128)} %refs_0_.7, bf16[4,512,128]{2,1,0:T(8,128)(2,1)} %refs_1_.7, ...), custom_call_target="tpu_custom_call" | custom-call | flops 5368709120 | bytes 16777216 | tf_op jit(solution)/shard_map/middle_far/pallas_call | solution.py:324
  59.0 3.9 %collective-permute-start.11 = (bf16[1,2,2,512,128]{4,3,2,1,0:T(8,128)(2,1)}, bf16[1,2,2,512,128]{4,3,2,1,0:T(8,128)(2,1)S(1)}, u32[]{:S(2)}, u32[]{:S(2)}) collective-permute-start(bf16[1,2,2,512,128]{4,3,2,1,0:T(8,128)(2,1)} %get-tuple-element.43), channel_id=1, source_target_pairs={{0,2},{2,0},{1,3},{3,1},{4,6},{6,4},{5,7},{7,5},{8,10},{10,8},{9,1... | collective-permute-start | bytes 1572872 | tf_op jit(solution)/shard_map/ppermute | solution.py:415
  62.9 1.7 %collective-permute-done.11 = bf16[1,2,2,512,128]{4,3,2,1,0:T(8,128)(2,1)S(1)} collective-permute-done((bf16[1,2,2,512,128]{4,3,2,1,0:T(8,128)(2,1)}, bf16[1,2,2,512,128]{4,3,2,1,0:T(8,128)(2,1)S(1)}, u32[]{:S(2)}, u32[]{:S(2)}) %collective-permute-start.11) | collective-permute-done | bytes 524320 | tf_op jit(solution)/shard_map/ppermute | solution.py:415
  64.6 1.2 fusion.1
  65.8 7.5 %backward_rows.2 = (f32[128,2048]{1,0:T(8,128)}, bf16[1,2,2,512,128]{4,3,2,1,0:T(8,128)(2,1)}, bf16[1,2,2,512,128]{4,3,2,1,0:T(8,128)(2,1)}) custom-call(s32[16]{0:T(128)} %refs_0_.7, bf16[4,512,128]{2,1,0:T(8,128)(2,1)} %refs_1_.7, bf16[128,2048]{1,0:T(8,128)(2,1)} %get-tuple-element.38.refs_2_, bf16[2048,128]{1,0:T(8,128)(2,1)} %get-tuple-element.39.refs_3_, ...), custom_call_target="tpu_custom_call" | custom-call | flops 3221225472 | bytes 16777216 | tf_op jit(solution)/shard_map/backward_rows/pallas_call | solution.py:394
  73.4 0.5 collective-permute-start.12
  73.8 8.1 %collective-permute-start.13 = (bf16[2,512,128]{2,1,0:T(8,128)(2,1)S(1)}, bf16[2,512,128]{2,1,0:T(8,128)(2,1)S(1)}, u32[]{:S(2)}, u32[]{:S(2)}) collective-permute-start(bf16[2,512,128]{2,1,0:T(8,128)(2,1)S(1)} %get-tuple-element.50), channel_id=1, source_target_pairs={{0,5},{1,4},{2,7},{3,6},{8,13},{9,12},{10,15},{11,14},{16,21},{17,... | collective-permute-start | bytes 786440 | tf_op jit(solution)/shard_map/ppermute | solution.py:420
  81.9 5.6 %collective-permute-done.13 = bf16[2,512,128]{2,1,0:T(8,128)(2,1)S(1)} collective-permute-done((bf16[2,512,128]{2,1,0:T(8,128)(2,1)S(1)}, bf16[2,512,128]{2,1,0:T(8,128)(2,1)S(1)}, u32[]{:S(2)}, u32[]{:S(2)}) %collective-permute-start.13) | collective-permute-done | bytes 262176 | tf_op jit(solution)/shard_map/ppermute | solution.py:420
  87.7 1.2 fusion.11
  88.9 7.4 %backward_rows.3 = (bf16[4,512,128]{2,1,0:T(8,128)(2,1)}, bf16[1,2,2,512,128]{4,3,2,1,0:T(8,128)(2,1)}, bf16[1,2,2,512,128]{4,3,2,1,0:T(8,128)(2,1)}) custom-call(s32[16]{0:T(128)} %refs_0_.7, bf16[4,512,128]{2,1,0:T(8,128)(2,1)} %refs_1_.7, bf16[128,2048]{1,0:T(8,128)(2,1)} %get-tuple-element.38.refs_2_, bf16[2048,128]{1,0:T(8,128)(2,1)} %get-tuple-element.39.refs_3_, ...), custom_call_target="tpu_custom_call" | custom-call | flops 3221225472 | bytes 16777216 | tf_op jit(solution)/shard_map/backward_rows/pallas_call | solution.py:394
  96.3 1.5 collective-permute-start.14
  97.8 25.5 %collective-permute-start.17 = (bf16[2,512,128]{2,1,0:T(8,128)(2,1)S(1)}, bf16[2,512,128]{2,1,0:T(8,128)(2,1)S(1)}, u32[]{:S(2)}, u32[]{:S(2)}) collective-permute-start(bf16[2,512,128]{2,1,0:T(8,128)(2,1)S(1)} %add_convert_fusion), channel_id=1, source_target_pairs={{0,120},{8,0},{16,8},{24,16},{32,24},{40,32},{48,40},{56,48},{64,5... | collective-permute-start | bytes 786440 | tf_op jit(solution)/shard_map/ppermute | solution.py:428
  123.3 7.8 %collective-permute-start.16 = (bf16[512,128]{1,0:T(8,128)(2,1)S(1)}, bf16[512,128]{1,0:T(8,128)(2,1)S(1)}, u32[]{:S(2)}, u32[]{:S(2)}) collective-permute-start(bf16[512,128]{1,0:T(8,128)(2,1)S(1)} %get-tuple-element.56), channel_id=1, source_target_pairs={{0,5},{1,4},{4,1},{5,0},{2,7},{3,6},{6,3},{7,2},{8,13},{9,12},{12,... | collective-permute-start | bytes 393224 | tf_op jit(solution)/shard_map/ppermute | solution.py:420
  131.1 3.9 %collective-permute-done.16 = bf16[512,128]{1,0:T(8,128)(2,1)S(1)} collective-permute-done((bf16[512,128]{1,0:T(8,128)(2,1)S(1)}, bf16[512,128]{1,0:T(8,128)(2,1)S(1)}, u32[]{:S(2)}, u32[]{:S(2)}) %collective-permute-start.16) | collective-permute-done | bytes 131104 | tf_op jit(solution)/shard_map/ppermute | solution.py:420
  135.0 2.4 %collective-permute-done.21 = bf16[512,128]{1,0:T(8,128)(2,1)S(1)} collective-permute-done((bf16[512,128]{1,0:T(8,128)(2,1)S(1)}, bf16[512,128]{1,0:T(8,128)(2,1)S(1)}, u32[]{:S(2)}, u32[]{:S(2)}) %collective-permute-start.21) | collective-permute-done | bytes 131104 | tf_op jit(solution)/shard_map/ppermute | solution.py:420
  137.4 0.1 fusion.2
  137.5 0.4 collective-permute-start.22
  137.9 2.3 %collective-permute-start.18 = (bf16[512,128]{1,0:T(8,128)(2,1)S(1)}, bf16[512,128]{1,0:T(8,128)(2,1)S(1)}, u32[]{:S(2)}, u32[]{:S(2)}) collective-permute-start(bf16[512,128]{1,0:T(8,128)(2,1)S(1)} %get-tuple-element.71), channel_id=1, source_target_pairs={{0,120},{8,0},{16,8},{24,16},{32,24},{40,32},{48,40},{56,48},{64,5... | collective-permute-start | bytes 393224 | tf_op jit(solution)/shard_map/ppermute | solution.py:428
  140.2 1.0 fusion.15
  141.2 1.3 collective-permute-start.20
  142.5 1.3 collective-permute-start.15
  143.8 0.7 collective-permute-done.18
  144.5 5.2 %collective-permute-done.20 = bf16[512,128]{1,0:T(8,128)(2,1)S(1)} collective-permute-done((bf16[512,128]{1,0:T(8,128)(2,1)S(1)}, bf16[512,128]{1,0:T(8,128)(2,1)S(1)}, u32[]{:S(2)}, u32[]{:S(2)}) %collective-permute-start.20) | collective-permute-done | bytes 131104 | tf_op jit(solution)/shard_map/ppermute | solution.py:420
  149.7 1.4 collective-permute-done.15
  151.1 1.1 fusion.4
  152.2 0.1 collective-permute-start.23
  152.3 2.0 %collective-permute-start.19 = (bf16[512,128]{1,0:T(8,128)(2,1)S(1)}, bf16[512,128]{1,0:T(8,128)(2,1)S(1)}, u32[]{:S(2)}, u32[]{:S(2)}) collective-permute-start(bf16[512,128]{1,0:T(8,128)(2,1)S(1)} %get-tuple-element.61), channel_id=1, source_target_pairs={{0,1},{1,0},{2,3},{3,2},{4,5},{5,4},{6,7},{7,6},{8,9},{9,8},{10,11... | collective-permute-start | bytes 393224 | tf_op jit(solution)/shard_map/ppermute | solution.py:424
  154.4 2.9 %collective-permute-done.23 = bf16[512,128]{1,0:T(8,128)(2,1)S(1)} collective-permute-done((bf16[512,128]{1,0:T(8,128)(2,1)S(1)}, bf16[512,128]{1,0:T(8,128)(2,1)S(1)}, u32[]{:S(2)}, u32[]{:S(2)}) %collective-permute-start.23) | collective-permute-done | bytes 131104 | tf_op jit(solution)/shard_map/ppermute | solution.py:424
  157.3 0.7 add_convert_fusion.3
  158.0 0.7 collective-permute-done.19
  158.7 0.7 add_convert_fusion.6
  (37 shorter events, 0.3 us)
Async XLA Ops:
  1.6 34.4 %copy-start = (bf16[2,512,128]{2,1,0:T(8,128)(2,1)}, bf16[2,512,128]{2,1,0:T(8,128)(2,1)S(1)}, u32[]{:S(2)}) copy-start(bf16[2,512,128]{2,1,0:T(8,128)(2,1)S(1)} %pad_maximum_fusion.refs_2_.refs_7_) | copy-start | bytes 786436
  1.6 11.5 %collective-permute-start.2 = (bf16[2,512,128]{2,1,0:T(8,128)(2,1)S(1)}, bf16[2,512,128]{2,1,0:T(8,128)(2,1)S(1)}, u32[]{:S(2)}, u32[]{:S(2)}) collective-permute-start(bf16[2,512,128]{2,1,0:T(8,128)(2,1)S(1)} %pad_maximum_fusion.refs_2_.refs_7_), channel_id=1, source_target_pairs={{0,5},{1,4},{2,7},{3,6},{8,13},{9,12},{10,15},{11,14},{16,21},{17,... | collective-permute-start | bytes 786440 | tf_op jit(solution)/shard_map/ppermute | solution.py:420
  7.6 9.9 %collective-permute-start.1 = (bf16[2,512,128]{2,1,0:T(8,128)(2,1)S(1)}, bf16[2,512,128]{2,1,0:T(8,128)(2,1)S(1)}, u32[]{:S(2)}, u32[]{:S(2)}) collective-permute-start(bf16[2,512,128]{2,1,0:T(8,128)(2,1)S(1)} %pad_maximum_fusion.refs_2_.refs_7_), channel_id=1, source_target_pairs={{0,8},{8,16},{16,24},{24,32},{32,40},{40,48},{48,56},{56,64},{64,7... | collective-permute-start | bytes 786440 | tf_op jit(solution)/shard_map/ppermute | solution.py:428
  13.1 22.9 %copy-start.1 = (bf16[2,512,128]{2,1,0:T(8,128)(2,1)}, bf16[2,512,128]{2,1,0:T(8,128)(2,1)S(1)}, u32[]{:S(2)}) copy-start(bf16[2,512,128]{2,1,0:T(8,128)(2,1)S(1)} %collective-permute-done.2.refs_4_.refs_9_) | copy-start | bytes 786436
  17.5 18.5 %copy-start.4 = (bf16[2,512,128]{2,1,0:T(8,128)(2,1)}, bf16[2,512,128]{2,1,0:T(8,128)(2,1)S(1)}, u32[]{:S(2)}) copy-start(bf16[2,512,128]{2,1,0:T(8,128)(2,1)S(1)} %collective-permute-done.1.refs_6_.refs_7_) | copy-start | bytes 786436
  17.6 9.0 %collective-permute-start.7 = (bf16[2,512,128]{2,1,0:T(8,128)(2,1)S(1)}, bf16[2,512,128]{2,1,0:T(8,128)(2,1)S(1)}, u32[]{:S(2)}, u32[]{:S(2)}) collective-permute-start(bf16[2,512,128]{2,1,0:T(8,128)(2,1)S(1)} %collective-permute-done.1.refs_6_.refs_7_), channel_id=1, source_target_pairs={{0,8},{8,16},{16,24},{24,32},{32,40},{40,48},{48,56},{56,64},{64,7... | collective-permute-start | bytes 786440 | tf_op jit(solution)/shard_map/ppermute | solution.py:428
  17.6 10.3 %collective-permute-start.5 = (bf16[2,512,128]{2,1,0:T(8,128)(2,1)S(1)}, bf16[2,512,128]{2,1,0:T(8,128)(2,1)S(1)}, u32[]{:S(2)}, u32[]{:S(2)}) collective-permute-start(bf16[2,512,128]{2,1,0:T(8,128)(2,1)S(1)} %collective-permute-done.1.refs_6_.refs_7_), channel_id=1, source_target_pairs={{0,5},{1,4},{4,1},{5,0},{2,7},{3,6},{6,3},{7,2},{8,13},{9,12},{12,... | collective-permute-start | bytes 786440 | tf_op jit(solution)/shard_map/ppermute | solution.py:420
  18.5 9.9 %collective-permute-start = (bf16[2,512,128]{2,1,0:T(8,128)(2,1)S(1)}, bf16[2,512,128]{2,1,0:T(8,128)(2,1)S(1)}, u32[]{:S(2)}, u32[]{:S(2)}) collective-permute-start(bf16[2,512,128]{2,1,0:T(8,128)(2,1)S(1)} %pad_maximum_fusion.refs_2_.refs_7_), channel_id=1, source_target_pairs={{0,2},{2,0},{1,3},{3,1},{4,6},{6,4},{5,7},{7,5},{8,10},{10,8},{9,1... | collective-permute-start | bytes 786440 | tf_op jit(solution)/shard_map/ppermute | solution.py:415
  18.5 17.5 %collective-permute-start.4 = (bf16[2,512,128]{2,1,0:T(8,128)(2,1)S(1)}, bf16[2,512,128]{2,1,0:T(8,128)(2,1)S(1)}, u32[]{:S(2)}, u32[]{:S(2)}) collective-permute-start(bf16[2,512,128]{2,1,0:T(8,128)(2,1)S(1)} %collective-permute-done.1.refs_6_.refs_7_), channel_id=1, source_target_pairs={{0,2},{2,0},{1,3},{3,1},{4,6},{6,4},{5,7},{7,5},{8,10},{10,8},{9,1... | collective-permute-start | bytes 786440 | tf_op jit(solution)/shard_map/ppermute | solution.py:415
  26.5 25.6 %copy-start.8 = (bf16[2,512,128]{2,1,0:T(8,128)(2,1)}, bf16[2,512,128]{2,1,0:T(8,128)(2,1)S(1)}, u32[]{:S(2)}) copy-start(bf16[2,512,128]{2,1,0:T(8,128)(2,1)S(1)} %collective-permute-done.7.refs_6_) | copy-start | bytes 786436
  26.5 9.5 %collective-permute-start.9 = (bf16[2,512,128]{2,1,0:T(8,128)(2,1)S(1)}, bf16[2,512,128]{2,1,0:T(8,128)(2,1)S(1)}, u32[]{:S(2)}, u32[]{:S(2)}) collective-permute-start(bf16[2,512,128]{2,1,0:T(8,128)(2,1)S(1)} %collective-permute-done.7.refs_6_), channel_id=1, source_target_pairs={{4,1},{5,0},{6,3},{7,2},{12,9},{13,8},{14,11},{15,10},{20,17},{21,... | collective-permute-start | bytes 786440 | tf_op jit(solution)/shard_map/ppermute | solution.py:420
  27.8 8.2 %collective-permute-start.3 = (bf16[2,512,128]{2,1,0:T(8,128)(2,1)S(1)}, bf16[2,512,128]{2,1,0:T(8,128)(2,1)S(1)}, u32[]{:S(2)}, u32[]{:S(2)}) collective-permute-start(bf16[2,512,128]{2,1,0:T(8,128)(2,1)S(1)} %collective-permute-done.2.refs_4_.refs_9_), channel_id=1, source_target_pairs={{0,2},{2,0},{1,3},{3,1},{4,6},{6,4},{5,7},{7,5},{8,10},{10,8},{9,1... | collective-permute-start | bytes 786440 | tf_op jit(solution)/shard_map/ppermute | solution.py:415
  27.9 8.2 %copy-start.5 = (bf16[2,512,128]{2,1,0:T(8,128)(2,1)}, bf16[2,512,128]{2,1,0:T(8,128)(2,1)S(1)}, u32[]{:S(2)}) copy-start(bf16[2,512,128]{2,1,0:T(8,128)(2,1)S(1)} %collective-permute-done.5.refs_8_.refs_9_) | copy-start | bytes 786436
  27.9 8.1 %collective-permute-start.6 = (bf16[2,512,128]{2,1,0:T(8,128)(2,1)S(1)}, bf16[2,512,128]{2,1,0:T(8,128)(2,1)S(1)}, u32[]{:S(2)}, u32[]{:S(2)}) collective-permute-start(bf16[2,512,128]{2,1,0:T(8,128)(2,1)S(1)} %collective-permute-done.5.refs_8_.refs_9_), channel_id=1, source_target_pairs={{0,2},{2,0},{1,3},{3,1},{4,6},{6,4},{5,7},{7,5},{8,10},{10,8},{9,1... | collective-permute-start | bytes 786440 | tf_op jit(solution)/shard_map/ppermute | solution.py:415
  28.4 7.7 %copy-start.2 = (bf16[2,512,128]{2,1,0:T(8,128)(2,1)}, bf16[2,512,128]{2,1,0:T(8,128)(2,1)S(1)}, u32[]{:S(2)}) copy-start(bf16[2,512,128]{2,1,0:T(8,128)(2,1)S(1)} %collective-permute-done.refs_3_.refs_8_) | copy-start | bytes 786436
  28.4 23.7 %collective-permute-start.8 = (bf16[2,512,128]{2,1,0:T(8,128)(2,1)S(1)}, bf16[2,512,128]{2,1,0:T(8,128)(2,1)S(1)}, u32[]{:S(2)}, u32[]{:S(2)}) collective-permute-start(bf16[2,512,128]{2,1,0:T(8,128)(2,1)S(1)} %collective-permute-done.7.refs_6_), channel_id=1, source_target_pairs={{0,2},{2,0},{1,3},{3,1},{4,6},{6,4},{5,7},{7,5},{8,10},{10,8},{9,1... | collective-permute-start | bytes 786440 | tf_op jit(solution)/shard_map/ppermute | solution.py:415
  36.0 16.2 %copy-start.9 = (bf16[2,512,128]{2,1,0:T(8,128)(2,1)}, bf16[2,512,128]{2,1,0:T(8,128)(2,1)S(1)}, u32[]{:S(2)}) copy-start(bf16[2,512,128]{2,1,0:T(8,128)(2,1)S(1)} %collective-permute-done.9.refs_8_) | copy-start | bytes 786436
  36.0 16.1 %collective-permute-start.10 = (bf16[2,512,128]{2,1,0:T(8,128)(2,1)S(1)}, bf16[2,512,128]{2,1,0:T(8,128)(2,1)S(1)}, u32[]{:S(2)}, u32[]{:S(2)}) collective-permute-start(bf16[2,512,128]{2,1,0:T(8,128)(2,1)S(1)} %collective-permute-done.9.refs_8_), channel_id=1, source_target_pairs={{0,2},{2,0},{1,3},{3,1},{4,6},{6,4},{5,7},{7,5},{8,10},{10,8},{9,1... | collective-permute-start | bytes 786440 | tf_op jit(solution)/shard_map/ppermute | solution.py:415
  36.0 0.7 copy-start.3
  36.0 0.8 copy-start.6
  36.8 0.7 copy-start.7
  52.1 0.7 copy-start.10
  52.1 0.8 copy-start.11
  59.0 5.7 %collective-permute-start.11 = (bf16[1,2,2,512,128]{4,3,2,1,0:T(8,128)(2,1)}, bf16[1,2,2,512,128]{4,3,2,1,0:T(8,128)(2,1)S(1)}, u32[]{:S(2)}, u32[]{:S(2)}) collective-permute-start(bf16[1,2,2,512,128]{4,3,2,1,0:T(8,128)(2,1)} %get-tuple-element.43), channel_id=1, source_target_pairs={{0,2},{2,0},{1,3},{3,1},{4,6},{6,4},{5,7},{7,5},{8,10},{10,8},{9,1... | collective-permute-start | bytes 1572872 | tf_op jit(solution)/shard_map/ppermute | solution.py:415
  73.4 14.3 %collective-permute-start.12 = (bf16[1,2,2,512,128]{4,3,2,1,0:T(8,128)(2,1)}, bf16[1,2,2,512,128]{4,3,2,1,0:T(8,128)(2,1)S(1)}, u32[]{:S(2)}, u32[]{:S(2)}) collective-permute-start(bf16[1,2,2,512,128]{4,3,2,1,0:T(8,128)(2,1)} %get-tuple-element.48), channel_id=1, source_target_pairs={{0,2},{2,0},{1,3},{3,1},{4,6},{6,4},{5,7},{7,5},{8,10},{10,8},{9,1... | collective-permute-start | bytes 1572872 | tf_op jit(solution)/shard_map/ppermute | solution.py:415
  73.8 13.7 %collective-permute-start.13 = (bf16[2,512,128]{2,1,0:T(8,128)(2,1)S(1)}, bf16[2,512,128]{2,1,0:T(8,128)(2,1)S(1)}, u32[]{:S(2)}, u32[]{:S(2)}) collective-permute-start(bf16[2,512,128]{2,1,0:T(8,128)(2,1)S(1)} %get-tuple-element.50), channel_id=1, source_target_pairs={{0,5},{1,4},{2,7},{3,6},{8,13},{9,12},{10,15},{11,14},{16,21},{17,... | collective-permute-start | bytes 786440 | tf_op jit(solution)/shard_map/ppermute | solution.py:420
  96.3 43.9 %collective-permute-start.14 = (bf16[1,2,2,512,128]{4,3,2,1,0:T(8,128)(2,1)}, bf16[1,2,2,512,128]{4,3,2,1,0:T(8,128)(2,1)S(1)}, u32[]{:S(2)}, u32[]{:S(2)}) collective-permute-start(bf16[1,2,2,512,128]{4,3,2,1,0:T(8,128)(2,1)} %get-tuple-element.54), channel_id=1, source_target_pairs={{0,2},{2,0},{1,3},{3,1},{4,6},{6,4},{5,7},{7,5},{8,10},{10,8},{9,1... | collective-permute-start | bytes 1572872 | tf_op jit(solution)/shard_map/ppermute | solution.py:415
  97.8 39.6 %collective-permute-start.17 = (bf16[2,512,128]{2,1,0:T(8,128)(2,1)S(1)}, bf16[2,512,128]{2,1,0:T(8,128)(2,1)S(1)}, u32[]{:S(2)}, u32[]{:S(2)}) collective-permute-start(bf16[2,512,128]{2,1,0:T(8,128)(2,1)S(1)} %add_convert_fusion), channel_id=1, source_target_pairs={{0,120},{8,0},{16,8},{24,16},{32,24},{40,32},{48,40},{56,48},{64,5... | collective-permute-start | bytes 786440 | tf_op jit(solution)/shard_map/ppermute | solution.py:428
  123.3 11.7 %collective-permute-start.16 = (bf16[512,128]{1,0:T(8,128)(2,1)S(1)}, bf16[512,128]{1,0:T(8,128)(2,1)S(1)}, u32[]{:S(2)}, u32[]{:S(2)}) collective-permute-start(bf16[512,128]{1,0:T(8,128)(2,1)S(1)} %get-tuple-element.56), channel_id=1, source_target_pairs={{0,5},{1,4},{4,1},{5,0},{2,7},{3,6},{6,3},{7,2},{8,13},{9,12},{12,... | collective-permute-start | bytes 393224 | tf_op jit(solution)/shard_map/ppermute | solution.py:420
  131.1 6.3 %collective-permute-start.21 = (bf16[512,128]{1,0:T(8,128)(2,1)S(1)}, bf16[512,128]{1,0:T(8,128)(2,1)S(1)}, u32[]{:S(2)}, u32[]{:S(2)}) collective-permute-start(bf16[512,128]{1,0:T(8,128)(2,1)S(1)} %get-tuple-element.59), channel_id=1, source_target_pairs={{0,5},{1,4},{4,1},{5,0},{2,7},{3,6},{6,3},{7,2},{8,13},{9,12},{12,... | collective-permute-start | bytes 393224 | tf_op jit(solution)/shard_map/ppermute | solution.py:420
  137.5 6.4 %collective-permute-start.22 = (bf16[512,128]{1,0:T(8,128)(2,1)S(1)}, bf16[512,128]{1,0:T(8,128)(2,1)S(1)}, u32[]{:S(2)}, u32[]{:S(2)}) collective-permute-start(bf16[512,128]{1,0:T(8,128)(2,1)S(1)} %get-tuple-element.70), channel_id=1, source_target_pairs={{0,120},{8,0},{16,8},{24,16},{32,24},{40,32},{48,40},{56,48},{64,5... | collective-permute-start | bytes 393224 | tf_op jit(solution)/shard_map/ppermute | solution.py:428
  137.9 6.6 %collective-permute-start.18 = (bf16[512,128]{1,0:T(8,128)(2,1)S(1)}, bf16[512,128]{1,0:T(8,128)(2,1)S(1)}, u32[]{:S(2)}, u32[]{:S(2)}) collective-permute-start(bf16[512,128]{1,0:T(8,128)(2,1)S(1)} %get-tuple-element.71), channel_id=1, source_target_pairs={{0,120},{8,0},{16,8},{24,16},{32,24},{40,32},{48,40},{56,48},{64,5... | collective-permute-start | bytes 393224 | tf_op jit(solution)/shard_map/ppermute | solution.py:428
  141.2 8.5 %collective-permute-start.20 = (bf16[512,128]{1,0:T(8,128)(2,1)S(1)}, bf16[512,128]{1,0:T(8,128)(2,1)S(1)}, u32[]{:S(2)}, u32[]{:S(2)}) collective-permute-start(bf16[512,128]{1,0:T(8,128)(2,1)S(1)} %get-tuple-element.62), channel_id=1, source_target_pairs={{4,1},{5,0},{6,3},{7,2},{12,9},{13,8},{14,11},{15,10},{20,17},{21,... | collective-permute-start | bytes 393224 | tf_op jit(solution)/shard_map/ppermute | solution.py:420
  142.5 8.6 %collective-permute-start.15 = (bf16[512,128]{1,0:T(8,128)(2,1)S(1)}, bf16[512,128]{1,0:T(8,128)(2,1)S(1)}, u32[]{:S(2)}, u32[]{:S(2)}) collective-permute-start(bf16[512,128]{1,0:T(8,128)(2,1)S(1)} %get-tuple-element.63), channel_id=1, source_target_pairs={{4,1},{5,0},{6,3},{7,2},{12,9},{13,8},{14,11},{15,10},{20,17},{21,... | collective-permute-start | bytes 393224 | tf_op jit(solution)/shard_map/ppermute | solution.py:420
  152.2 5.0 %collective-permute-start.23 = (bf16[512,128]{1,0:T(8,128)(2,1)S(1)}, bf16[512,128]{1,0:T(8,128)(2,1)S(1)}, u32[]{:S(2)}, u32[]{:S(2)}) collective-permute-start(bf16[512,128]{1,0:T(8,128)(2,1)S(1)} %get-tuple-element.60), channel_id=1, source_target_pairs={{0,1},{1,0},{2,3},{3,2},{4,5},{5,4},{6,7},{7,6},{8,9},{9,8},{10,11... | collective-permute-start | bytes 393224 | tf_op jit(solution)/shard_map/ppermute | solution.py:424
  152.3 6.4 %collective-permute-start.19 = (bf16[512,128]{1,0:T(8,128)(2,1)S(1)}, bf16[512,128]{1,0:T(8,128)(2,1)S(1)}, u32[]{:S(2)}, u32[]{:S(2)}) collective-permute-start(bf16[512,128]{1,0:T(8,128)(2,1)S(1)} %get-tuple-element.61), channel_id=1, source_target_pairs={{0,1},{1,0},{2,3},{3,2},{4,5},{5,4},{6,7},{7,6},{8,9},{9,8},{10,11... | collective-permute-start | bytes 393224 | tf_op jit(solution)/shard_map/ppermute | solution.py:424

commit v4 on v2

v4 whole, which is shorter than its diff:
```python
import math

import jax
import jax.numpy as jnp
from jax import lax
from jax.experimental import pallas as pl
from jax.experimental.pallas import tpu as pltpu
from jax.sharding import Mesh, PartitionSpec as P

NEGATIVE = -1e30
BLK = 512
HEADS = 4
HD = 128
NQ = HEADS * BLK
HALF = BLK // 2
ROWS = 3
SLOTS = 4 * ROWS
SPAN = 9
SCALE = HD ** -0.5
LOG2 = SCALE * math.log2(math.e)
BOUND = 64.0
F32 = jnp.float32
BF16 = jnp.bfloat16
SEQ = ("x", "y", "zh", "core")
VMEM = pl.BlockSpec(memory_space=pltpu.VMEM)
SMEM = pl.BlockSpec(memory_space=pltpu.SMEM)
ANY = pl.BlockSpec(memory_space=pl.ANY)
DMA = pltpu.SemaphoreType.DMA
NEAR = [(dz, dc) for dz in range(2) for dc in range(2)]


def shape(dims, dtype):
    return jax.ShapeDtypeStruct(dims, dtype)


def dot(a, b):
    return lax.dot_general(a, b, (((1,), (0,)), ((), ())), preferred_element_type=F32)


class Place:
    def __init__(self, len_ref):
        row = lax.axis_index("x") * 4 + lax.axis_index("y")
        self.zh = lax.axis_index("zh")
        self.core = lax.axis_index("core")
        place = self.zh * 2 + self.core
        base = (row - 2) * (4 * BLK)
        first = base + (8 + place) * BLK
        self.q_pos = lax.broadcasted_iota(jnp.int32, (1, BLK), 1) + (8 + place) * BLK
        starts = jnp.zeros((1, BLK), jnp.int32) - base
        first_start = -base
        last_start = -base
        end = jnp.int32(0)
        for c in range(16):
            end = end + len_ref[c]
            rel = end - base
            starts = jnp.where(self.q_pos >= rel, rel, starts)
            first_start = jnp.where(end <= first, rel, first_start)
            last_start = jnp.where(end <= first + BLK - 1, rel, last_start)
        self.starts = starts
        self.last_start = last_start
        self.lo = first_start // BLK
        self.hi = 8 + place

    def slot(self, j, dz, dc):
        return (2 - j) * 4 + (1 - self.zh if dz else self.zh) * 2 + (1 - self.core if dc else self.core)

    def mask(self, t):
        k_pos = lax.broadcasted_iota(jnp.int32, (BLK, BLK), 0) + t * BLK
        return (k_pos >= self.starts) & (k_pos <= self.q_pos)


def attention_kernel(*refs):
    len_ref, q_ref, do_ref = refs[:3]
    kv_refs = refs[3:15]
    o_ref, dq_ref = refs[15:17]
    out_refs = refs[17:21]
    kvs, dkvs, qt, dot_t, do_s, probs, row_max, total, acc, dq_acc, stage, delta, norms, in_sem, out_sem = refs[21:]
    at = Place(len_ref)
    order = [(j, dz, dc) for j in range(ROWS) for dz, dc in NEAR]
    for n, where in enumerate(order):
        slot = at.slot(*where)
        pltpu.make_async_copy(kv_refs[n], kvs.at[slot], in_sem.at[slot]).start()

    def arrived(t):
        pltpu.make_async_copy(kv_refs[0], kvs.at[t], in_sem.at[t]).wait()

    def out_copy(n, part, t):
        j, dz, dc = order[n]
        return pltpu.make_async_copy(dkvs.at[t, part], out_refs[part * 2 + dc].at[j, dz], out_sem.at[n, part])

    begin, end = at.lo, at.hi + 1
    dkvs[SLOTS] = jnp.zeros((2, BLK, HD), BF16)
    for n, where in enumerate(order):
        slot = at.slot(*where)

        @pl.when((slot < begin) | (slot >= end))
        def _():
            for part in range(2):
                out_copy(n, part, SLOTS).start()

    for h in range(HEADS):
        cols = slice(h * BLK, (h + 1) * BLK)
        qt[:, cols] = q_ref[h].T
        dot_t[:, cols] = do_ref[h].T
    dq_acc[...] = jnp.zeros((HD, NQ), F32)
    norms[...] = jnp.zeros((8, HD), F32)

    def forward(t, masked, shift):
        k = kvs[t, 0]
        v_t = kvs[t, 1].T
        if not shift:
            squares = dot(jnp.square(k.astype(F32)).astype(BF16), jnp.ones((HD, HD), BF16))
            norms[...] = jnp.maximum(norms[...], jnp.max(squares.reshape(BLK // 8, 8, HD), axis=0))
        if masked:
            allowed = at.mask(t)

        def score(h):
            s = dot(k, qt[:, h * HALF:(h + 1) * HALF])
            return jnp.where(allowed[:, (h % 2) * HALF:(h % 2 + 1) * HALF], s, NEGATIVE) if masked else s

        def soft(h, s):
            cols = slice(h * HALF, (h + 1) * HALF)
            p = jnp.exp2(s * LOG2 - row_max[:, cols] if shift else s * LOG2)
            total[:, cols] += jnp.sum(p, axis=0, keepdims=True)
            p = p.astype(BF16)
            probs[t - begin, :, cols] = p
            return p

        def product(h, p):
            acc[:, h * HALF:(h + 1) * HALF] += dot(v_t, p)

        weights = soft(0, score(0))
        s = score(1)
        for h in range(1, 2 * HEADS):
            held, weights = weights, soft(h, s)
            if h + 1 < 2 * HEADS:
                s = score(h + 1)
            product(h - 1, held)
        product(2 * HEADS - 1, weights)

    def clear():
        total[...] = jnp.zeros((1, NQ), F32)
        acc[...] = jnp.zeros((HD, NQ), F32)

    def fast_step(t, carry):
        arrived(t)
        masked = (t * BLK < at.last_start) | (t == at.hi)

        @pl.when(masked)
        def _():
            forward(t, True, False)

        @pl.when(jnp.logical_not(masked))
        def _():
            forward(t, False, False)

        return carry

    def max_step(t, carry):
        allowed = at.mask(t)
        for h in range(HEADS):
            cols = slice(h * BLK, (h + 1) * BLK)
            s = jnp.where(allowed, dot(kvs[t, 0], qt[:, cols]), NEGATIVE)
            row_max[:, cols] = jnp.maximum(row_max[:, cols], jnp.max(s, axis=0, keepdims=True))
        return carry

    def slow_step(t, carry):
        forward(t, True, True)
        return carry

    clear()
    lax.fori_loop(begin, end, fast_step, 0)
    q_norm = jnp.max(dot(jnp.ones((8, HD), BF16), jnp.square(qt[...].astype(F32)).astype(BF16)))

    @pl.when(q_norm * jnp.max(norms[...]) > 0.98 * (BOUND / LOG2) ** 2)
    def _():
        clear()
        row_max[...] = jnp.full((1, NQ), NEGATIVE, F32)
        lax.fori_loop(begin, end, max_step, 0)
        row_max[...] = row_max[...] * LOG2
        lax.fori_loop(begin, end, slow_step, 0)

    for h in range(HEADS):
        cols = slice(h * BLK, (h + 1) * BLK)
        inverse = 1.0 / total[:, cols]
        o = (acc[:, cols] * inverse).astype(BF16)
        o_ref[h] = o.T
        scaled = (dot_t[:, cols].astype(F32) * inverse).astype(BF16)
        dot_t[:, cols] = scaled
        do_s[h * BLK:(h + 1) * BLK] = scaled.T
        delta[:, cols] = jnp.sum(o.astype(F32) * scaled.astype(F32), axis=0, keepdims=True)

    def backward_step(t, carry):
        k_t = kvs[t, 0].T
        v = kvs[t, 1]

        def dp_of(h):
            return dot(v, dot_t[:, h * BLK:(h + 1) * BLK])

        def ds_of(h, dp):
            cols = slice(h * BLK, (h + 1) * BLK)
            ds = (probs[t - begin, :, cols].astype(F32) * (dp - delta[:, cols])).astype(BF16)
            stage[:, cols] = ds
            return ds

        def dq_of(h, ds):
            dq_acc[:, h * BLK:(h + 1) * BLK] += dot(k_t, ds)

        d0 = dp_of(0)
        d1 = dp_of(1)
        s0 = ds_of(0, d0)
        dkvs[t, 1] = dot(probs[t - begin], do_s[...]).astype(BF16)
        d2 = dp_of(2)
        dq_of(0, s0)
        s1 = ds_of(1, d1)
        d3 = dp_of(3)
        dq_of(1, s1)
        s2 = ds_of(2, d2)
        dq_of(2, s2)
        s3 = ds_of(3, d3)
        dq_of(3, s3)
        dkvs[t, 0] = (dot(stage[...], q_ref[...].reshape(NQ, HD)) * SCALE).astype(BF16)

        for n, where in enumerate(order):
            @pl.when(at.slot(*where) == t)
            def _():
                for part in range(2):
                    out_copy(n, part, t).start()

        return carry

    lax.fori_loop(begin, end, backward_step, 0)
    for h in range(HEADS):
        dq_ref[h] = (dq_acc[:, h * BLK:(h + 1) * BLK] * SCALE).astype(BF16).T

    def rest(t, carry):
        arrived(t)
        return carry

    lax.fori_loop(0, begin, rest, 0)
    lax.fori_loop(end, SLOTS, rest, 0)
    for n in range(len(order)):
        for part in range(2):
            out_copy(n, part, 0).wait()


def attention(seq_lengths, queries, d_out, blocks):
    rows = shape((HEADS, BLK, HD), BF16)
    grads = shape((ROWS, 2, BLK, HD), BF16)
    return pl.pallas_call(
        attention_kernel,
        out_shape=(rows, rows) + (grads,) * 4,
        in_specs=[SMEM, VMEM, VMEM] + [ANY] * SLOTS,
        out_specs=[VMEM, VMEM] + [ANY] * 4,
        scratch_shapes=[
            pltpu.VMEM((SLOTS, 2, BLK, HD), BF16),
            pltpu.VMEM((SLOTS + 1, 2, BLK, HD), BF16),
            pltpu.VMEM((HD, NQ), BF16),
            pltpu.VMEM((HD, NQ), BF16),
            pltpu.VMEM((NQ, HD), BF16),
            pltpu.VMEM((SPAN, BLK, NQ), BF16),
            pltpu.VMEM((1, NQ), F32),
            pltpu.VMEM((1, NQ), F32),
            pltpu.VMEM((HD, NQ), F32),
            pltpu.VMEM((HD, NQ), F32),
            pltpu.VMEM((BLK, NQ), BF16),
            pltpu.VMEM((1, NQ), F32),
            pltpu.VMEM((8, HD), F32),
            DMA((SLOTS,)),
            DMA((SLOTS, 2)),
        ],
        compiler_params=pltpu.CompilerParams(vmem_limit_bytes=56 << 20),
        cost_estimate=pl.CostEstimate(flops=8 << 30, bytes_accessed=16 << 20, transcendentals=9 << 20),
        name="attention",
    )(seq_lengths, queries, d_out, *blocks)


def swap_core(value):
    return lax.ppermute(value, "core", [(0, 1), (1, 0)])


def swap_z(value, sources=(0, 1)):
    pairs = [(2 * zh + zl, 2 * (1 - zh) + (1 - zl)) for zh in sources for zl in range(2)]
    return lax.ppermute(value, ("zh", "zl"), pairs)


def swap_head(value):
    return lax.ppermute(value, "zl", [(0, 1), (1, 0)])


def shift_row(value, by):
    return lax.ppermute(value, ("x", "y"), [(r, (r + by) % 16) for r in range(16)])


def added(*values):
    total = values[0].astype(F32)
    for value in values[1:]:
        total = total + value.astype(F32)
    return total.astype(BF16)


def returned(keep, send):
    first = lax.axis_index("zh") == 0
    given = swap_core(send)
    outer = swap_z(added(jnp.where(first, keep[2, 1], keep[0, 1]), jnp.where(first, given[2, 1], given[0, 1])))
    middle = swap_z(added(keep[1, 1], given[1, 1]))
    zero = jnp.zeros((), BF16)
    back = shift_row(added(keep[2, 0], given[2, 0], jnp.where(first, zero, outer)), -1)
    back = shift_row(added(keep[1, 0], given[1, 0], middle, back), -1)
    half = added(keep[0, 0], given[0, 0], jnp.where(first, outer, zero), back)
    return added(half, swap_head(half))


def on_device(queries, key_rows, value_rows, d_out, seq_lengths):
    own = jnp.stack([key_rows, value_rows])
    row1 = shift_row(own, 1)
    side0 = swap_z(own, (0,))
    row1, side0 = lax.optimization_barrier((row1, side0))
    row2 = shift_row(row1, 1)
    side1 = swap_z(row1)
    row2, side1 = lax.optimization_barrier((row2, side1))
    side2 = swap_z(row2, (1,))
    blocks = []
    for block in (own, side0, row1, side1, row2, side2):
        blocks += [block, swap_core(block)]
    attended, grad_queries, *parts = attention(seq_lengths, queries, d_out, blocks)
    return attended, grad_queries, returned(*parts[:2]), returned(*parts[2:])


def solution(mesh):
    fine = Mesh(mesh.devices.reshape(4, 4, 2, 2, 2), ("x", "y", "zh", "core", "zl"))
    tokens = P("zl", SEQ, None)
    rows = P(SEQ, None)
    return jax.shard_map(
        on_device,
        mesh=fine,
        in_specs=(tokens, rows, rows, tokens, P()),
        out_specs=(tokens, tokens, rows, rows),
        check_vma=False,
    )
```

time: 124 us -> 129 us (1.040)
  the two profiles are of different devices: /device:TPU:26 before, /device:TPU:28 now
where the time goes in v4:
time: 129 us; the launch traced here: 130 us
  starting transfers between devices  52.7 us (41%)
  waiting for transfers between devices  36.8 us (29%)
  Pallas kernels  34.7 us (27%)
  other arithmetic  4.06 us (3%)
    pallas_call x1, Pallas kernels, attention(): pl.pallas_call(attention_kernel, out_shape=(rows, rows) + (grads,) * 4, i...  34.7 us
    ppermute x7, starting transfers between devices, swap_z(): return lax.ppermute(value, ('zh', 'zl'), pairs)  25.3 us
    ppermute x6, starting transfers between devices, shift_row(): lax.ppermute(value, ('x', 'y'), [(r, (r + by) % 16) for r in range(16)])  20.2 us
    ppermute x7, waiting for transfers between devices, swap_z(): return lax.ppermute(value, ('zh', 'zl'), pairs)  14.7 us
    ppermute x6, waiting for transfers between devices, shift_row(): lax.ppermute(value, ('x', 'y'), [(r, (r + by) % 16) for r in range(16)])  14.3 us
    ppermute x8, starting transfers between devices, swap_core(): return lax.ppermute(value, 'core', [(0, 1), (1, 0)])  6.99 us
    ppermute x2, waiting for transfers between devices, swap_head(): return lax.ppermute(value, 'zl', [(0, 1), (1, 0)])  4.26 us
    ppermute x8, waiting for transfers between devices, swap_core(): return lax.ppermute(value, 'core', [(0, 1), (1, 0)])  3.5 us
  transfers between devices with their start and end apart: 23, of which 13 were waited for; matrix products, arithmetic and copies ran while one was open for 2% of the time, Pallas kernels for 0%

profile of v4, /device:TPU:28, one launch (start us, length us, event | category | flops | bytes accessed | tf_op | source)
XLA Modules:
  0.0 129.9 jit_solution(18057589161789962102)
XLA Ops:
  0.6 1.0 pad_maximum_fusion.refs_3_
  1.6 0.9 collective-permute-start.1
  2.6 5.9 %collective-permute-start.2 = (bf16[2,512,128]{2,1,0:T(8,128)(2,1)S(1)}, bf16[2,512,128]{2,1,0:T(8,128)(2,1)S(1)}, u32[]{:S(2)}, u32[]{:S(2)}) collective-permute-start(bf16[2,512,128]{2,1,0:T(8,128)(2,1)S(1)} %pad_maximum_fusion.refs_3_), channel_id=1, source_target_pairs={{0,5},{1,4},{2,7},{3,6},{8,13},{9,12},{10,15},{11,14},{16,21},{17,... | collective-permute-start | bytes 786440 | tf_op jit(solution)/shard_map/ppermute | solution.py:284
  8.5 1.2 collective-permute-done.1.refs_7_
  9.8 4.0 %collective-permute-done.2.refs_5_ = bf16[2,512,128]{2,1,0:T(8,128)(2,1)S(1)} collective-permute-done((bf16[2,512,128]{2,1,0:T(8,128)(2,1)S(1)}, bf16[2,512,128]{2,1,0:T(8,128)(2,1)S(1)}, u32[]{:S(2)}, u32[]{:S(2)}) %collective-permute-start.2) | collective-permute-done | bytes 262176 | tf_op jit(solution)/shard_map/ppermute | solution.py:284
  13.8 1.6 %collective-permute-start.5 = (bf16[2,512,128]{2,1,0:T(8,128)(2,1)S(1)}, bf16[2,512,128]{2,1,0:T(8,128)(2,1)S(1)}, u32[]{:S(2)}, u32[]{:S(2)}) collective-permute-start(bf16[2,512,128]{2,1,0:T(8,128)(2,1)S(1)} %collective-permute-done.1.refs_7_), channel_id=1, source_target_pairs={{0,8},{8,16},{16,24},{24,32},{32,40},{40,48},{48,56},{56,64},{64,7... | collective-permute-start | bytes 786440 | tf_op jit(solution)/shard_map/ppermute | solution.py:292
  15.3 3.7 %collective-permute-start.6 = (bf16[2,512,128]{2,1,0:T(8,128)(2,1)S(1)}, bf16[2,512,128]{2,1,0:T(8,128)(2,1)S(1)}, u32[]{:S(2)}, u32[]{:S(2)}) collective-permute-start(bf16[2,512,128]{2,1,0:T(8,128)(2,1)S(1)} %collective-permute-done.1.refs_7_), channel_id=1, source_target_pairs={{0,5},{1,4},{4,1},{5,0},{2,7},{3,6},{6,3},{7,2},{8,13},{9,12},{12,... | collective-permute-start | bytes 786440 | tf_op jit(solution)/shard_map/ppermute | solution.py:284
  19.0 1.6 %collective-permute-done.5.refs_11_ = bf16[2,512,128]{2,1,0:T(8,128)(2,1)S(1)} collective-permute-done((bf16[2,512,128]{2,1,0:T(8,128)(2,1)S(1)}, bf16[2,512,128]{2,1,0:T(8,128)(2,1)S(1)}, u32[]{:S(2)}, u32[]{:S(2)}) %collective-permute-start.5) | collective-permute-done | bytes 262176 | tf_op jit(solution)/shard_map/ppermute | solution.py:292
  20.6 3.2 %collective-permute-done.6.refs_9_ = bf16[2,512,128]{2,1,0:T(8,128)(2,1)S(1)} collective-permute-done((bf16[2,512,128]{2,1,0:T(8,128)(2,1)S(1)}, bf16[2,512,128]{2,1,0:T(8,128)(2,1)S(1)}, u32[]{:S(2)}, u32[]{:S(2)}) %collective-permute-start.6) | collective-permute-done | bytes 262176 | tf_op jit(solution)/shard_map/ppermute | solution.py:284
  23.9 1.3 collective-permute-start.9
  25.2 0.1 collective-permute-start.4
  25.3 0.5 collective-permute-start.3
  25.8 0.1 collective-permute-start.8
  25.8 0.0 collective-permute-done.refs_4_
  25.9 0.4 collective-permute-start.7
  26.3 7.1 %collective-permute-done.9.refs_13_ = bf16[2,512,128]{2,1,0:T(8,128)(2,1)S(1)} collective-permute-done((bf16[2,512,128]{2,1,0:T(8,128)(2,1)S(1)}, bf16[2,512,128]{2,1,0:T(8,128)(2,1)S(1)}, u32[]{:S(2)}, u32[]{:S(2)}) %collective-permute-start.9) | collective-permute-done | bytes 262176 | tf_op jit(solution)/shard_map/ppermute | solution.py:284
  33.4 1.5 %collective-permute-done.10.refs_14_ = bf16[2,512,128]{2,1,0:T(8,128)(2,1)S(1)} collective-permute-done((bf16[2,512,128]{2,1,0:T(8,128)(2,1)S(1)}, bf16[2,512,128]{2,1,0:T(8,128)(2,1)S(1)}, u32[]{:S(2)}, u32[]{:S(2)}) %collective-permute-start.10) | collective-permute-done | bytes 262176 | tf_op jit(solution)/shard_map/ppermute | solution.py:279
  35.0 0.7 copy-done.13
  35.7 34.7 %attention.1 = (bf16[4,512,128]{2,1,0:T(8,128)(2,1)}, bf16[4,512,128]{2,1,0:T(8,128)(2,1)}, bf16[3,2,512,128]{3,2,1,0:T(8,128)(2,1)}, bf16[3,2,512,128]{3,2,1,0:...) custom-call(s32[16]{0:T(128)} %refs_0_.1, bf16[4,512,128]{2,1,0:T(8,128)(2,1)} %refs_1_.1, ...), custom_call_target="tpu_custom_call" | custom-call | flops 8589934592 | bytes 16777216 | tf_op jit(solution)/shard_map/attention/pallas_call | solution.py:250
  70.4 5.8 %collective-permute-start.17 = (bf16[3,2,512,128]{3,2,1,0:T(8,128)(2,1)}, bf16[3,2,512,128]{3,2,1,0:T(8,128)(2,1)S(1)}, u32[]{:S(2)}, u32[]{:S(2)}) collective-permute-start(bf16[3,2,512,128]{3,2,1,0:T(8,128)(2,1)} %get-tuple-element.23), channel_id=1, source_target_pairs={{0,2},{2,0},{1,3},{3,1},{4,6},{6,4},{5,7},{7,5},{8,10},{10,8},{9,1... | collective-permute-start | bytes 2359304 | tf_op jit(solution)/shard_map/ppermute | solution.py:279
  76.2 0.1 collective-permute-start.11
  76.3 2.0 %collective-permute-done.17 = bf16[3,2,512,128]{3,2,1,0:T(8,128)(2,1)S(1)} collective-permute-done((bf16[3,2,512,128]{3,2,1,0:T(8,128)(2,1)}, bf16[3,2,512,128]{3,2,1,0:T(8,128)(2,1)S(1)}, u32[]{:S(2)}, u32[]{:S(2)}) %collective-permute-start.17) | collective-permute-done | bytes 786464 | tf_op jit(solution)/shard_map/ppermute | solution.py:279
  78.3 1.1 fusion.13
  79.5 10.8 %collective-permute-start.18 = (bf16[512,128]{1,0:T(8,128)(2,1)S(1)}, bf16[512,128]{1,0:T(8,128)(2,1)S(1)}, u32[]{:S(2)}, u32[]{:S(2)}) collective-permute-start(bf16[512,128]{1,0:T(8,128)(2,1)S(1)} %get-tuple-element.25), channel_id=1, source_target_pairs={{0,5},{1,4},{4,1},{5,0},{2,7},{3,6},{6,3},{7,2},{8,13},{9,12},{12,... | collective-permute-start | bytes 393224 | tf_op jit(solution)/shard_map/ppermute | solution.py:284
  90.3 0.3 collective-permute-start.19
  90.6 0.1 fusion.11
  90.7 3.0 %collective-permute-start.12 = (bf16[512,128]{1,0:T(8,128)(2,1)S(1)}, bf16[512,128]{1,0:T(8,128)(2,1)S(1)}, u32[]{:S(2)}, u32[]{:S(2)}) collective-permute-start(bf16[512,128]{1,0:T(8,128)(2,1)S(1)} %get-tuple-element.27), channel_id=1, source_target_pairs={{0,5},{1,4},{4,1},{5,0},{2,7},{3,6},{6,3},{7,2},{8,13},{9,12},{12,... | collective-permute-start | bytes 393224 | tf_op jit(solution)/shard_map/ppermute | solution.py:284
  93.7 0.3 collective-permute-start.13
  94.0 0.4 collective-permute-done.18
  94.4 0.1 fusion
  94.5 11.7 %collective-permute-start.20 = (bf16[512,128]{1,0:T(8,128)(2,1)S(1)}, bf16[512,128]{1,0:T(8,128)(2,1)S(1)}, u32[]{:S(2)}, u32[]{:S(2)}) collective-permute-start(bf16[512,128]{1,0:T(8,128)(2,1)S(1)} %fusion), channel_id=1, source_target_pairs={{0,120},{8,0},{16,8},{24,16},{32,24},{40,32},{48,40},{56,48},{64,5... | collective-permute-start | bytes 393224 | tf_op jit(solution)/shard_map/ppermute | solution.py:292
  106.1 0.1 fusion.5
  106.2 5.5 %collective-permute-start.14 = (bf16[512,128]{1,0:T(8,128)(2,1)S(1)}, bf16[512,128]{1,0:T(8,128)(2,1)S(1)}, u32[]{:S(2)}, u32[]{:S(2)}) collective-permute-start(bf16[512,128]{1,0:T(8,128)(2,1)S(1)} %fusion.5), channel_id=1, source_target_pairs={{0,120},{8,0},{16,8},{24,16},{32,24},{40,32},{48,40},{56,48},{64,5... | collective-permute-start | bytes 393224 | tf_op jit(solution)/shard_map/ppermute | solution.py:292
  111.8 0.1 fusion.2
  111.8 0.1 collective-permute-start.21
  111.9 5.0 %collective-permute-done.14 = bf16[512,128]{1,0:T(8,128)(2,1)S(1)} collective-permute-done((bf16[512,128]{1,0:T(8,128)(2,1)S(1)}, bf16[512,128]{1,0:T(8,128)(2,1)S(1)}, u32[]{:S(2)}, u32[]{:S(2)}) %collective-permute-start.14) | collective-permute-done | bytes 131104 | tf_op jit(solution)/shard_map/ppermute | solution.py:292
  116.9 0.1 fusion.7
  117.0 0.4 collective-permute-start.15
  117.4 2.3 %collective-permute-done.21 = bf16[512,128]{1,0:T(8,128)(2,1)S(1)} collective-permute-done((bf16[512,128]{1,0:T(8,128)(2,1)S(1)}, bf16[512,128]{1,0:T(8,128)(2,1)S(1)}, u32[]{:S(2)}, u32[]{:S(2)}) %collective-permute-start.21) | collective-permute-done | bytes 131104 | tf_op jit(solution)/shard_map/ppermute | solution.py:292
  119.7 0.1 fusion.4
  119.8 0.1 collective-permute-start.22
  119.9 4.3 %collective-permute-done.15 = bf16[512,128]{1,0:T(8,128)(2,1)S(1)} collective-permute-done((bf16[512,128]{1,0:T(8,128)(2,1)S(1)}, bf16[512,128]{1,0:T(8,128)(2,1)S(1)}, u32[]{:S(2)}, u32[]{:S(2)}) %collective-permute-start.15) | collective-permute-done | bytes 131104 | tf_op jit(solution)/shard_map/ppermute | solution.py:292
  124.1 0.1 fusion.9
  124.2 0.1 collective-permute-start.16
  124.3 1.5 %collective-permute-done.22 = bf16[512,128]{1,0:T(8,128)(2,1)S(1)} collective-permute-done((bf16[512,128]{1,0:T(8,128)(2,1)S(1)}, bf16[512,128]{1,0:T(8,128)(2,1)S(1)}, u32[]{:S(2)}, u32[]{:S(2)}) %collective-permute-start.22) | collective-permute-done | bytes 131104 | tf_op jit(solution)/shard_map/ppermute | solution.py:288
  125.8 0.7 add_convert_fusion
  126.5 2.8 %collective-permute-done.16 = bf16[512,128]{1,0:T(8,128)(2,1)S(1)} collective-permute-done((bf16[512,128]{1,0:T(8,128)(2,1)S(1)}, bf16[512,128]{1,0:T(8,128)(2,1)S(1)}, u32[]{:S(2)}, u32[]{:S(2)}) %collective-permute-start.16) | collective-permute-done | bytes 131104 | tf_op jit(solution)/shard_map/ppermute | solution.py:288
  129.2 0.7 add_convert_fusion.3
  (38 shorter events, 0.1 us)
Async XLA Ops:
  1.6 33.3 %copy-start.2 = (bf16[2,512,128]{2,1,0:T(8,128)(2,1)}, bf16[2,512,128]{2,1,0:T(8,128)(2,1)S(1)}, u32[]{:S(2)}) copy-start(bf16[2,512,128]{2,1,0:T(8,128)(2,1)S(1)} %pad_maximum_fusion.refs_3_) | copy-start | bytes 786436
  1.6 8.1 %collective-permute-start.1 = (bf16[2,512,128]{2,1,0:T(8,128)(2,1)S(1)}, bf16[2,512,128]{2,1,0:T(8,128)(2,1)S(1)}, u32[]{:S(2)}, u32[]{:S(2)}) collective-permute-start(bf16[2,512,128]{2,1,0:T(8,128)(2,1)S(1)} %pad_maximum_fusion.refs_3_), channel_id=1, source_target_pairs={{0,8},{8,16},{16,24},{24,32},{32,40},{40,48},{48,56},{56,64},{64,7... | collective-permute-start | bytes 786440 | tf_op jit(solution)/shard_map/ppermute | solution.py:292
  2.6 11.2 %collective-permute-start.2 = (bf16[2,512,128]{2,1,0:T(8,128)(2,1)S(1)}, bf16[2,512,128]{2,1,0:T(8,128)(2,1)S(1)}, u32[]{:S(2)}, u32[]{:S(2)}) collective-permute-start(bf16[2,512,128]{2,1,0:T(8,128)(2,1)S(1)} %pad_maximum_fusion.refs_3_), channel_id=1, source_target_pairs={{0,5},{1,4},{2,7},{3,6},{8,13},{9,12},{10,15},{11,14},{16,21},{17,... | collective-permute-start | bytes 786440 | tf_op jit(solution)/shard_map/ppermute | solution.py:284
  9.8 25.1 %copy-start.3 = (bf16[2,512,128]{2,1,0:T(8,128)(2,1)}, bf16[2,512,128]{2,1,0:T(8,128)(2,1)S(1)}, u32[]{:S(2)}) copy-start(bf16[2,512,128]{2,1,0:T(8,128)(2,1)S(1)} %collective-permute-done.1.refs_7_) | copy-start | bytes 786436
  13.8 21.1 %copy-start.4 = (bf16[2,512,128]{2,1,0:T(8,128)(2,1)}, bf16[2,512,128]{2,1,0:T(8,128)(2,1)S(1)}, u32[]{:S(2)}) copy-start(bf16[2,512,128]{2,1,0:T(8,128)(2,1)S(1)} %collective-permute-done.2.refs_5_) | copy-start | bytes 786436
  13.8 6.9 %collective-permute-start.5 = (bf16[2,512,128]{2,1,0:T(8,128)(2,1)S(1)}, bf16[2,512,128]{2,1,0:T(8,128)(2,1)S(1)}, u32[]{:S(2)}, u32[]{:S(2)}) collective-permute-start(bf16[2,512,128]{2,1,0:T(8,128)(2,1)S(1)} %collective-permute-done.1.refs_7_), channel_id=1, source_target_pairs={{0,8},{8,16},{16,24},{24,32},{32,40},{40,48},{48,56},{56,64},{64,7... | collective-permute-start | bytes 786440 | tf_op jit(solution)/shard_map/ppermute | solution.py:292
  15.3 8.5 %collective-permute-start.6 = (bf16[2,512,128]{2,1,0:T(8,128)(2,1)S(1)}, bf16[2,512,128]{2,1,0:T(8,128)(2,1)S(1)}, u32[]{:S(2)}, u32[]{:S(2)}) collective-permute-start(bf16[2,512,128]{2,1,0:T(8,128)(2,1)S(1)} %collective-permute-done.1.refs_7_), channel_id=1, source_target_pairs={{0,5},{1,4},{4,1},{5,0},{2,7},{3,6},{6,3},{7,2},{8,13},{9,12},{12,... | collective-permute-start | bytes 786440 | tf_op jit(solution)/shard_map/ppermute | solution.py:284
  19.0 6.8 %collective-permute-start = (bf16[2,512,128]{2,1,0:T(8,128)(2,1)S(1)}, bf16[2,512,128]{2,1,0:T(8,128)(2,1)S(1)}, u32[]{:S(2)}, u32[]{:S(2)}) collective-permute-start(bf16[2,512,128]{2,1,0:T(8,128)(2,1)S(1)} %pad_maximum_fusion.refs_3_), channel_id=1, source_target_pairs={{0,2},{2,0},{1,3},{3,1},{4,6},{6,4},{5,7},{7,5},{8,10},{10,8},{9,1... | collective-permute-start | bytes 786440 | tf_op jit(solution)/shard_map/ppermute | solution.py:279
  20.6 14.3 %copy-start.5 = (bf16[2,512,128]{2,1,0:T(8,128)(2,1)}, bf16[2,512,128]{2,1,0:T(8,128)(2,1)S(1)}, u32[]{:S(2)}) copy-start(bf16[2,512,128]{2,1,0:T(8,128)(2,1)S(1)} %collective-permute-done.5.refs_11_) | copy-start | bytes 786436
  23.9 11.0 %copy-start.6 = (bf16[2,512,128]{2,1,0:T(8,128)(2,1)}, bf16[2,512,128]{2,1,0:T(8,128)(2,1)S(1)}, u32[]{:S(2)}) copy-start(bf16[2,512,128]{2,1,0:T(8,128)(2,1)S(1)} %collective-permute-done.6.refs_9_) | copy-start | bytes 786436
  23.9 9.5 %collective-permute-start.9 = (bf16[2,512,128]{2,1,0:T(8,128)(2,1)S(1)}, bf16[2,512,128]{2,1,0:T(8,128)(2,1)S(1)}, u32[]{:S(2)}, u32[]{:S(2)}) collective-permute-start(bf16[2,512,128]{2,1,0:T(8,128)(2,1)S(1)} %collective-permute-done.5.refs_11_), channel_id=1, source_target_pairs={{4,1},{5,0},{6,3},{7,2},{12,9},{13,8},{14,11},{15,10},{20,17},{21,... | collective-permute-start | bytes 786440 | tf_op jit(solution)/shard_map/ppermute | solution.py:284
  25.2 8.2 %collective-permute-start.4 = (bf16[2,512,128]{2,1,0:T(8,128)(2,1)S(1)}, bf16[2,512,128]{2,1,0:T(8,128)(2,1)S(1)}, u32[]{:S(2)}, u32[]{:S(2)}) collective-permute-start(bf16[2,512,128]{2,1,0:T(8,128)(2,1)S(1)} %collective-permute-done.1.refs_7_), channel_id=1, source_target_pairs={{0,2},{2,0},{1,3},{3,1},{4,6},{6,4},{5,7},{7,5},{8,10},{10,8},{9,1... | collective-permute-start | bytes 786440 | tf_op jit(solution)/shard_map/ppermute | solution.py:279
  25.3 8.1 %collective-permute-start.3 = (bf16[2,512,128]{2,1,0:T(8,128)(2,1)S(1)}, bf16[2,512,128]{2,1,0:T(8,128)(2,1)S(1)}, u32[]{:S(2)}, u32[]{:S(2)}) collective-permute-start(bf16[2,512,128]{2,1,0:T(8,128)(2,1)S(1)} %collective-permute-done.2.refs_5_), channel_id=1, source_target_pairs={{0,2},{2,0},{1,3},{3,1},{4,6},{6,4},{5,7},{7,5},{8,10},{10,8},{9,1... | collective-permute-start | bytes 786440 | tf_op jit(solution)/shard_map/ppermute | solution.py:279
  25.8 7.6 %collective-permute-start.8 = (bf16[2,512,128]{2,1,0:T(8,128)(2,1)S(1)}, bf16[2,512,128]{2,1,0:T(8,128)(2,1)S(1)}, u32[]{:S(2)}, u32[]{:S(2)}) collective-permute-start(bf16[2,512,128]{2,1,0:T(8,128)(2,1)S(1)} %collective-permute-done.5.refs_11_), channel_id=1, source_target_pairs={{0,2},{2,0},{1,3},{3,1},{4,6},{6,4},{5,7},{7,5},{8,10},{10,8},{9,1... | collective-permute-start | bytes 786440 | tf_op jit(solution)/shard_map/ppermute | solution.py:279
  25.8 9.1 %copy-start.7 = (bf16[2,512,128]{2,1,0:T(8,128)(2,1)}, bf16[2,512,128]{2,1,0:T(8,128)(2,1)S(1)}, u32[]{:S(2)}) copy-start(bf16[2,512,128]{2,1,0:T(8,128)(2,1)S(1)} %collective-permute-done.refs_4_) | copy-start | bytes 786436
  25.9 7.6 %collective-permute-start.7 = (bf16[2,512,128]{2,1,0:T(8,128)(2,1)S(1)}, bf16[2,512,128]{2,1,0:T(8,128)(2,1)S(1)}, u32[]{:S(2)}, u32[]{:S(2)}) collective-permute-start(bf16[2,512,128]{2,1,0:T(8,128)(2,1)S(1)} %collective-permute-done.6.refs_9_), channel_id=1, source_target_pairs={{0,2},{2,0},{1,3},{3,1},{4,6},{6,4},{5,7},{7,5},{8,10},{10,8},{9,1... | collective-permute-start | bytes 786440 | tf_op jit(solution)/shard_map/ppermute | solution.py:279
  33.3 1.6 %copy-start.8 = (bf16[2,512,128]{2,1,0:T(8,128)(2,1)}, bf16[2,512,128]{2,1,0:T(8,128)(2,1)S(1)}, u32[]{:S(2)}) copy-start(bf16[2,512,128]{2,1,0:T(8,128)(2,1)S(1)} %collective-permute-done.9.refs_13_) | copy-start | bytes 786436
  33.3 1.5 %collective-permute-start.10 = (bf16[2,512,128]{2,1,0:T(8,128)(2,1)S(1)}, bf16[2,512,128]{2,1,0:T(8,128)(2,1)S(1)}, u32[]{:S(2)}, u32[]{:S(2)}) collective-permute-start(bf16[2,512,128]{2,1,0:T(8,128)(2,1)S(1)} %collective-permute-done.9.refs_13_), channel_id=1, source_target_pairs={{0,2},{2,0},{1,3},{3,1},{4,6},{6,4},{5,7},{7,5},{8,10},{10,8},{9,1... | collective-permute-start | bytes 786440 | tf_op jit(solution)/shard_map/ppermute | solution.py:279
  33.4 1.6 %copy-start.9 = (bf16[2,512,128]{2,1,0:T(8,128)(2,1)}, bf16[2,512,128]{2,1,0:T(8,128)(2,1)S(1)}, u32[]{:S(2)}) copy-start(bf16[2,512,128]{2,1,0:T(8,128)(2,1)S(1)} %collective-permute-done.4.refs_8_) | copy-start | bytes 786436
  33.4 1.6 %copy-start.10 = (bf16[2,512,128]{2,1,0:T(8,128)(2,1)}, bf16[2,512,128]{2,1,0:T(8,128)(2,1)S(1)}, u32[]{:S(2)}) copy-start(bf16[2,512,128]{2,1,0:T(8,128)(2,1)S(1)} %collective-permute-done.3.refs_6_) | copy-start | bytes 786436
  33.4 1.6 %copy-start.11 = (bf16[2,512,128]{2,1,0:T(8,128)(2,1)}, bf16[2,512,128]{2,1,0:T(8,128)(2,1)S(1)}, u32[]{:S(2)}) copy-start(bf16[2,512,128]{2,1,0:T(8,128)(2,1)S(1)} %collective-permute-done.8.refs_12_) | copy-start | bytes 786436
  33.4 1.5 %copy-start.12 = (bf16[2,512,128]{2,1,0:T(8,128)(2,1)}, bf16[2,512,128]{2,1,0:T(8,128)(2,1)S(1)}, u32[]{:S(2)}) copy-start(bf16[2,512,128]{2,1,0:T(8,128)(2,1)S(1)} %collective-permute-done.7.refs_10_) | copy-start | bytes 786436
  35.0 0.7 copy-start.13
  70.4 20.2 %copy-start = (bf16[3,2,512,128]{3,2,1,0:T(8,128)(2,1)S(1)}, bf16[3,2,512,128]{3,2,1,0:T(8,128)(2,1)}, u32[]{:S(2)}) copy-start(bf16[3,2,512,128]{3,2,1,0:T(8,128)(2,1)} %get-tuple-element.20) | copy-start | bytes 2359300
  70.4 7.9 %collective-permute-start.17 = (bf16[3,2,512,128]{3,2,1,0:T(8,128)(2,1)}, bf16[3,2,512,128]{3,2,1,0:T(8,128)(2,1)S(1)}, u32[]{:S(2)}, u32[]{:S(2)}) collective-permute-start(bf16[3,2,512,128]{3,2,1,0:T(8,128)(2,1)} %get-tuple-element.23), channel_id=1, source_target_pairs={{0,2},{2,0},{1,3},{3,1},{4,6},{6,4},{5,7},{7,5},{8,10},{10,8},{9,1... | collective-permute-start | bytes 2359304 | tf_op jit(solution)/shard_map/ppermute | solution.py:279
  76.2 14.4 %collective-permute-start.11 = (bf16[3,2,512,128]{3,2,1,0:T(8,128)(2,1)}, bf16[3,2,512,128]{3,2,1,0:T(8,128)(2,1)S(1)}, u32[]{:S(2)}, u32[]{:S(2)}) collective-permute-start(bf16[3,2,512,128]{3,2,1,0:T(8,128)(2,1)} %get-tuple-element.21), channel_id=1, source_target_pairs={{0,2},{2,0},{1,3},{3,1},{4,6},{6,4},{5,7},{7,5},{8,10},{10,8},{9,1... | collective-permute-start | bytes 2359304 | tf_op jit(solution)/shard_map/ppermute | solution.py:279
  79.5 14.9 %copy-start.1 = (bf16[3,2,512,128]{3,2,1,0:T(8,128)(2,1)S(1)}, bf16[3,2,512,128]{3,2,1,0:T(8,128)(2,1)}, u32[]{:S(2)}) copy-start(bf16[3,2,512,128]{3,2,1,0:T(8,128)(2,1)} %get-tuple-element.22) | copy-start | bytes 2359300
  79.5 14.9 %collective-permute-start.18 = (bf16[512,128]{1,0:T(8,128)(2,1)S(1)}, bf16[512,128]{1,0:T(8,128)(2,1)S(1)}, u32[]{:S(2)}, u32[]{:S(2)}) collective-permute-start(bf16[512,128]{1,0:T(8,128)(2,1)S(1)} %get-tuple-element.25), channel_id=1, source_target_pairs={{0,5},{1,4},{4,1},{5,0},{2,7},{3,6},{6,3},{7,2},{8,13},{9,12},{12,... | collective-permute-start | bytes 393224 | tf_op jit(solution)/shard_map/ppermute | solution.py:284
  90.3 21.4 %collective-permute-start.19 = (bf16[512,128]{1,0:T(8,128)(2,1)S(1)}, bf16[512,128]{1,0:T(8,128)(2,1)S(1)}, u32[]{:S(2)}, u32[]{:S(2)}) collective-permute-start(bf16[512,128]{1,0:T(8,128)(2,1)S(1)} %get-tuple-element.24), channel_id=1, source_target_pairs={{0,5},{1,4},{4,1},{5,0},{2,7},{3,6},{6,3},{7,2},{8,13},{9,12},{12,... | collective-permute-start | bytes 393224 | tf_op jit(solution)/shard_map/ppermute | solution.py:284
  90.7 15.4 %collective-permute-start.12 = (bf16[512,128]{1,0:T(8,128)(2,1)S(1)}, bf16[512,128]{1,0:T(8,128)(2,1)S(1)}, u32[]{:S(2)}, u32[]{:S(2)}) collective-permute-start(bf16[512,128]{1,0:T(8,128)(2,1)S(1)} %get-tuple-element.27), channel_id=1, source_target_pairs={{0,5},{1,4},{4,1},{5,0},{2,7},{3,6},{6,3},{7,2},{8,13},{9,12},{12,... | collective-permute-start | bytes 393224 | tf_op jit(solution)/shard_map/ppermute | solution.py:284
  93.7 18.2 %collective-permute-start.13 = (bf16[512,128]{1,0:T(8,128)(2,1)S(1)}, bf16[512,128]{1,0:T(8,128)(2,1)S(1)}, u32[]{:S(2)}, u32[]{:S(2)}) collective-permute-start(bf16[512,128]{1,0:T(8,128)(2,1)S(1)} %get-tuple-element.26), channel_id=1, source_target_pairs={{0,5},{1,4},{4,1},{5,0},{2,7},{3,6},{6,3},{7,2},{8,13},{9,12},{12,... | collective-permute-start | bytes 393224 | tf_op jit(solution)/shard_map/ppermute | solution.py:284
  94.5 17.3 %collective-permute-start.20 = (bf16[512,128]{1,0:T(8,128)(2,1)S(1)}, bf16[512,128]{1,0:T(8,128)(2,1)S(1)}, u32[]{:S(2)}, u32[]{:S(2)}) collective-permute-start(bf16[512,128]{1,0:T(8,128)(2,1)S(1)} %fusion), channel_id=1, source_target_pairs={{0,120},{8,0},{16,8},{24,16},{32,24},{40,32},{48,40},{56,48},{64,5... | collective-permute-start | bytes 393224 | tf_op jit(solution)/shard_map/ppermute | solution.py:292
  106.2 10.7 %collective-permute-start.14 = (bf16[512,128]{1,0:T(8,128)(2,1)S(1)}, bf16[512,128]{1,0:T(8,128)(2,1)S(1)}, u32[]{:S(2)}, u32[]{:S(2)}) collective-permute-start(bf16[512,128]{1,0:T(8,128)(2,1)S(1)} %fusion.5), channel_id=1, source_target_pairs={{0,120},{8,0},{16,8},{24,16},{32,24},{40,32},{48,40},{56,48},{64,5... | collective-permute-start | bytes 393224 | tf_op jit(solution)/shard_map/ppermute | solution.py:292
  111.8 7.8 %collective-permute-start.21 = (bf16[512,128]{1,0:T(8,128)(2,1)S(1)}, bf16[512,128]{1,0:T(8,128)(2,1)S(1)}, u32[]{:S(2)}, u32[]{:S(2)}) collective-permute-start(bf16[512,128]{1,0:T(8,128)(2,1)S(1)} %fusion.2), channel_id=1, source_target_pairs={{0,120},{8,0},{16,8},{24,16},{32,24},{40,32},{48,40},{56,48},{64,5... | collective-permute-start | bytes 393224 | tf_op jit(solution)/shard_map/ppermute | solution.py:292
  117.0 7.1 %collective-permute-start.15 = (bf16[512,128]{1,0:T(8,128)(2,1)S(1)}, bf16[512,128]{1,0:T(8,128)(2,1)S(1)}, u32[]{:S(2)}, u32[]{:S(2)}) collective-permute-start(bf16[512,128]{1,0:T(8,128)(2,1)S(1)} %fusion.7), channel_id=1, source_target_pairs={{0,120},{8,0},{16,8},{24,16},{32,24},{40,32},{48,40},{56,48},{64,5... | collective-permute-start | bytes 393224 | tf_op jit(solution)/shard_map/ppermute | solution.py:292
  119.8 6.0 %collective-permute-start.22 = (bf16[512,128]{1,0:T(8,128)(2,1)S(1)}, bf16[512,128]{1,0:T(8,128)(2,1)S(1)}, u32[]{:S(2)}, u32[]{:S(2)}) collective-permute-start(bf16[512,128]{1,0:T(8,128)(2,1)S(1)} %fusion.4), channel_id=1, source_target_pairs={{0,1},{1,0},{2,3},{3,2},{4,5},{5,4},{6,7},{7,6},{8,9},{9,8},{10,11... | collective-permute-start | bytes 393224 | tf_op jit(solution)/shard_map/ppermute | solution.py:288
  124.2 5.0 %collective-permute-start.16 = (bf16[512,128]{1,0:T(8,128)(2,1)S(1)}, bf16[512,128]{1,0:T(8,128)(2,1)S(1)}, u32[]{:S(2)}, u32[]{:S(2)}) collective-permute-start(bf16[512,128]{1,0:T(8,128)(2,1)S(1)} %fusion.9), channel_id=1, source_target_pairs={{0,1},{1,0},{2,3},{3,2},{4,5},{5,4},{6,7},{7,6},{8,9},{9,8},{10,11... | collective-permute-start | bytes 393224 | tf_op jit(solution)/shard_map/ppermute | solution.py:288

commit v5 on v4

--- a/solution.py
+++ b/solution.py
@@ -301,30 +301,35 @@
 
 def returned(keep, send):
     first = lax.axis_index("zh") == 0
-    given = swap_core(send)
-    outer = swap_z(added(jnp.where(first, keep[2, 1], keep[0, 1]), jnp.where(first, given[2, 1], given[0, 1])))
-    middle = swap_z(added(keep[1, 1], given[1, 1]))
     zero = jnp.zeros((), BF16)
-    back = shift_row(added(keep[2, 0], given[2, 0], jnp.where(first, zero, outer)), -1)
-    back = shift_row(added(keep[1, 0], given[1, 0], middle, back), -1)
-    half = added(keep[0, 0], given[0, 0], jnp.where(first, outer, zero), back)
-    return added(half, swap_head(half))
+    given = [swap_core(part) for part in send]
+    outer, middle = [], []
+    for a, b in zip(keep, given):
+        outer.append(added(jnp.where(first, a[2, 1], a[0, 1]), jnp.where(first, b[2, 1], b[0, 1])))
+        middle.append(added(a[1, 1], b[1, 1]))
+    outer = [swap_z(value) for value in outer]
+    middle = [swap_z(lax.optimization_barrier(both)[0]) for both in zip(middle, outer)]
+    done = []
+    for a, b, far, near in zip(keep, given, outer, middle):
+        back = shift_row(added(a[2, 0], b[2, 0], jnp.where(first, zero, far)), -1)
+        back = shift_row(added(a[1, 0], b[1, 0], near, back), -1)
+        done.append(added(a[0, 0], b[0, 0], jnp.where(first, far, zero), back))
+    return [added(half, swap_head(half)) for half in done]
 
 
 def on_device(queries, key_rows, value_rows, d_out, seq_lengths):
     own = jnp.stack([key_rows, value_rows])
     row1 = shift_row(own, 1)
     side0 = swap_z(own, (0,))
-    row1, side0 = lax.optimization_barrier((row1, side0))
     row2 = shift_row(row1, 1)
-    side1 = swap_z(row1)
-    row2, side1 = lax.optimization_barrier((row2, side1))
+    side1 = swap_z(lax.optimization_barrier((row1, side0))[0])
     side2 = swap_z(row2, (1,))
     blocks = []
     for block in (own, side0, row1, side1, row2, side2):
         blocks += [block, swap_core(block)]
     attended, grad_queries, *parts = attention(seq_lengths, queries, d_out, blocks)
-    return attended, grad_queries, returned(*parts[:2]), returned(*parts[2:])
+    grad_keys, grad_values = returned(parts[::2], parts[1::2])
+    return attended, grad_queries, grad_keys, grad_values
 
 
 def solution(mesh):

time: 129 us -> 128 us (level)
  the two profiles are of different devices: /device:TPU:28 before, /device:TPU:30 now
where the time goes in v5:
time: 128 us; the launch traced here: 129 us
  waiting for transfers between devices  41.7 us (33%)
  Pallas kernels  40.8 us (32%)
  starting transfers between devices  40.6 us (32%)
  other arithmetic  4.06 us (3%)
    pallas_call x1, Pallas kernels, attention(): pl.pallas_call(attention_kernel, out_shape=(rows, rows) + (grads,) * 4, i...  40.8 us
    ppermute x7, starting transfers between devices, swap_z(): return lax.ppermute(value, ('zh', 'zl'), pairs)  29.3 us
    ppermute x6, waiting for transfers between devices, shift_row(): lax.ppermute(value, ('x', 'y'), [(r, (r + by) % 16) for r in range(16)])  19.8 us
    ppermute x7, waiting for transfers between devices, swap_z(): return lax.ppermute(value, ('zh', 'zl'), pairs)  14.2 us
    ppermute x8, starting transfers between devices, swap_core(): return lax.ppermute(value, 'core', [(0, 1), (1, 0)])  6.43 us
    ppermute x2, waiting for transfers between devices, swap_head(): return lax.ppermute(value, 'zl', [(0, 1), (1, 0)])  4.28 us
    ppermute x6, starting transfers between devices, shift_row(): lax.ppermute(value, ('x', 'y'), [(r, (r + by) % 16) for r in range(16)])  4.03 us
    ppermute x8, waiting for transfers between devices, swap_core(): return lax.ppermute(value, 'core', [(0, 1), (1, 0)])  3.5 us
  transfers between devices with their start and end apart: 23, of which 14 were waited for; matrix products, arithmetic and copies ran while one was open for 2% of the time, Pallas kernels for 0%

profile of v5, /device:TPU:30, one launch (start us, length us, event | category | flops | bytes accessed | tf_op | source)
XLA Modules:
  0.0 128.8 jit_solution(2826689302126420555)
XLA Ops:
  0.6 1.0 pad_maximum_fusion.refs_3_
  1.6 0.1 collective-permute-start.3
  1.8 6.0 %collective-permute-start.1 = (bf16[2,512,128]{2,1,0:T(8,128)(2,1)S(1)}, bf16[2,512,128]{2,1,0:T(8,128)(2,1)S(1)}, u32[]{:S(2)}, u32[]{:S(2)}) collective-permute-start(bf16[2,512,128]{2,1,0:T(8,128)(2,1)S(1)} %pad_maximum_fusion.refs_3_), channel_id=1, source_target_pairs={{0,5},{1,4},{2,7},{3,6},{8,13},{9,12},{10,15},{11,14},{16,21},{17,... | collective-permute-start | bytes 786440 | tf_op jit(solution)/shard_map/ppermute | solution.py:284
  7.8 2.0 %collective-permute-done.3.refs_7_ = bf16[2,512,128]{2,1,0:T(8,128)(2,1)S(1)} collective-permute-done((bf16[2,512,128]{2,1,0:T(8,128)(2,1)S(1)}, bf16[2,512,128]{2,1,0:T(8,128)(2,1)S(1)}, u32[]{:S(2)}, u32[]{:S(2)}) %collective-permute-start.3) | collective-permute-done | bytes 262176 | tf_op jit(solution)/shard_map/ppermute | solution.py:292
  9.8 3.6 %collective-permute-start.7 = (bf16[2,512,128]{2,1,0:T(8,128)(2,1)S(1)}, bf16[2,512,128]{2,1,0:T(8,128)(2,1)S(1)}, u32[]{:S(2)}, u32[]{:S(2)}) collective-permute-start(bf16[2,512,128]{2,1,0:T(8,128)(2,1)S(1)} %collective-permute-done.3.refs_7_), channel_id=1, source_target_pairs={{0,8},{8,16},{16,24},{24,32},{32,40},{40,48},{48,56},{56,64},{64,7... | collective-permute-start | bytes 786440 | tf_op jit(solution)/shard_map/ppermute | solution.py:292
  13.4 0.0 collective-permute-start
  13.4 4.1 %collective-permute-start.5 = (bf16[2,512,128]{2,1,0:T(8,128)(2,1)S(1)}, bf16[2,512,128]{2,1,0:T(8,128)(2,1)S(1)}, u32[]{:S(2)}, u32[]{:S(2)}) collective-permute-start(bf16[2,512,128]{2,1,0:T(8,128)(2,1)S(1)} %collective-permute-done.3.refs_7_), channel_id=1, source_target_pairs={{0,5},{1,4},{4,1},{5,0},{2,7},{3,6},{6,3},{7,2},{8,13},{9,12},{12,... | collective-permute-start | bytes 786440 | tf_op jit(solution)/shard_map/ppermute | solution.py:284
  17.5 0.8 collective-permute-done.7.refs_11_
  18.3 1.3 collective-permute-start.9
  19.6 0.1 collective-permute-start.4
  19.7 0.5 collective-permute-start.2
  20.2 0.1 collective-permute-start.8
  20.3 4.3 %collective-permute-done.5.refs_9_ = bf16[2,512,128]{2,1,0:T(8,128)(2,1)S(1)} collective-permute-done((bf16[2,512,128]{2,1,0:T(8,128)(2,1)S(1)}, bf16[2,512,128]{2,1,0:T(8,128)(2,1)S(1)}, u32[]{:S(2)}, u32[]{:S(2)}) %collective-permute-start.5) | collective-permute-done | bytes 262176 | tf_op jit(solution)/shard_map/ppermute | solution.py:284
  24.7 5.3 %collective-permute-done.9.refs_13_ = bf16[2,512,128]{2,1,0:T(8,128)(2,1)S(1)} collective-permute-done((bf16[2,512,128]{2,1,0:T(8,128)(2,1)S(1)}, bf16[2,512,128]{2,1,0:T(8,128)(2,1)S(1)}, u32[]{:S(2)}, u32[]{:S(2)}) %collective-permute-start.9) | collective-permute-done | bytes 262176 | tf_op jit(solution)/shard_map/ppermute | solution.py:284
  30.1 1.5 %collective-permute-done.10.refs_14_ = bf16[2,512,128]{2,1,0:T(8,128)(2,1)S(1)} collective-permute-done((bf16[2,512,128]{2,1,0:T(8,128)(2,1)S(1)}, bf16[2,512,128]{2,1,0:T(8,128)(2,1)S(1)}, u32[]{:S(2)}, u32[]{:S(2)}) %collective-permute-start.10) | collective-permute-done | bytes 262176 | tf_op jit(solution)/shard_map/ppermute | solution.py:279
  31.6 0.7 copy-done.13
  32.3 40.8 %attention.1 = (bf16[4,512,128]{2,1,0:T(8,128)(2,1)}, bf16[4,512,128]{2,1,0:T(8,128)(2,1)}, bf16[3,2,512,128]{3,2,1,0:T(8,128)(2,1)}, bf16[3,2,512,128]{3,2,1,0:...) custom-call(s32[16]{0:T(128)} %refs_0_.1, bf16[4,512,128]{2,1,0:T(8,128)(2,1)} %refs_1_.1, ...), custom_call_target="tpu_custom_call" | custom-call | flops 8589934592 | bytes 16777216 | tf_op jit(solution)/shard_map/attention/pallas_call | solution.py:250
  73.1 5.7 %collective-permute-start.17 = (bf16[3,2,512,128]{3,2,1,0:T(8,128)(2,1)}, bf16[3,2,512,128]{3,2,1,0:T(8,128)(2,1)S(1)}, u32[]{:S(2)}, u32[]{:S(2)}) collective-permute-start(bf16[3,2,512,128]{3,2,1,0:T(8,128)(2,1)} %get-tuple-element.20), channel_id=1, source_target_pairs={{0,2},{2,0},{1,3},{3,1},{4,6},{6,4},{5,7},{7,5},{8,10},{10,8},{9,1... | collective-permute-start | bytes 2359304 | tf_op jit(solution)/shard_map/ppermute | solution.py:279
  78.8 0.1 collective-permute-start.11
  78.9 2.0 %collective-permute-done.17 = bf16[3,2,512,128]{3,2,1,0:T(8,128)(2,1)S(1)} collective-permute-done((bf16[3,2,512,128]{3,2,1,0:T(8,128)(2,1)}, bf16[3,2,512,128]{3,2,1,0:T(8,128)(2,1)S(1)}, u32[]{:S(2)}, u32[]{:S(2)}) %collective-permute-start.17) | collective-permute-done | bytes 786464 | tf_op jit(solution)/shard_map/ppermute | solution.py:279
  80.9 1.1 fusion.13
  82.0 12.1 %collective-permute-start.18 = (bf16[512,128]{1,0:T(8,128)(2,1)S(1)}, bf16[512,128]{1,0:T(8,128)(2,1)S(1)}, u32[]{:S(2)}, u32[]{:S(2)}) collective-permute-start(bf16[512,128]{1,0:T(8,128)(2,1)S(1)} %get-tuple-element.23), channel_id=1, source_target_pairs={{0,5},{1,4},{4,1},{5,0},{2,7},{3,6},{6,3},{7,2},{8,13},{9,12},{12,... | collective-permute-start | bytes 393224 | tf_op jit(solution)/shard_map/ppermute | solution.py:284
  94.2 0.1 fusion.11
  94.3 0.1 collective-permute-start.12
  94.4 3.8 %collective-permute-done.18 = bf16[512,128]{1,0:T(8,128)(2,1)S(1)} collective-permute-done((bf16[512,128]{1,0:T(8,128)(2,1)S(1)}, bf16[512,128]{1,0:T(8,128)(2,1)S(1)}, u32[]{:S(2)}, u32[]{:S(2)}) %collective-permute-start.18) | collective-permute-done | bytes 131104 | tf_op jit(solution)/shard_map/ppermute | solution.py:284
  98.2 3.5 %collective-permute-start.19 = (bf16[512,128]{1,0:T(8,128)(2,1)S(1)}, bf16[512,128]{1,0:T(8,128)(2,1)S(1)}, u32[]{:S(2)}, u32[]{:S(2)}) collective-permute-start(bf16[512,128]{1,0:T(8,128)(2,1)S(1)} %get-tuple-element.21), channel_id=1, source_target_pairs={{0,5},{1,4},{4,1},{5,0},{2,7},{3,6},{6,3},{7,2},{8,13},{9,12},{12,... | collective-permute-start | bytes 393224 | tf_op jit(solution)/shard_map/ppermute | solution.py:284
  101.7 0.1 fusion
  101.8 0.1 collective-permute-start.20
  101.9 2.1 %collective-permute-start.13 = (bf16[512,128]{1,0:T(8,128)(2,1)S(1)}, bf16[512,128]{1,0:T(8,128)(2,1)S(1)}, u32[]{:S(2)}, u32[]{:S(2)}) collective-permute-start(bf16[512,128]{1,0:T(8,128)(2,1)S(1)} %get-tuple-element.18), channel_id=1, source_target_pairs={{0,5},{1,4},{4,1},{5,0},{2,7},{3,6},{6,3},{7,2},{8,13},{9,12},{12,... | collective-permute-start | bytes 393224 | tf_op jit(solution)/shard_map/ppermute | solution.py:284
  104.0 0.1 fusion.5
  104.0 0.1 collective-permute-start.14
  104.1 0.7 collective-permute-done.19
  104.8 6.2 %collective-permute-done.20 = bf16[512,128]{1,0:T(8,128)(2,1)S(1)} collective-permute-done((bf16[512,128]{1,0:T(8,128)(2,1)S(1)}, bf16[512,128]{1,0:T(8,128)(2,1)S(1)}, u32[]{:S(2)}, u32[]{:S(2)}) %collective-permute-start.20) | collective-permute-done | bytes 131104 | tf_op jit(solution)/shard_map/ppermute | solution.py:292
  111.0 0.1 fusion.2
  111.1 0.1 collective-permute-start.21
  111.2 1.7 %collective-permute-done.14 = bf16[512,128]{1,0:T(8,128)(2,1)S(1)} collective-permute-done((bf16[512,128]{1,0:T(8,128)(2,1)S(1)}, bf16[512,128]{1,0:T(8,128)(2,1)S(1)}, u32[]{:S(2)}, u32[]{:S(2)}) %collective-permute-start.14) | collective-permute-done | bytes 131104 | tf_op jit(solution)/shard_map/ppermute | solution.py:292
  112.9 0.1 fusion.7
  113.0 0.1 collective-permute-start.15
  113.1 7.6 %collective-permute-done.21 = bf16[512,128]{1,0:T(8,128)(2,1)S(1)} collective-permute-done((bf16[512,128]{1,0:T(8,128)(2,1)S(1)}, bf16[512,128]{1,0:T(8,128)(2,1)S(1)}, u32[]{:S(2)}, u32[]{:S(2)}) %collective-permute-start.21) | collective-permute-done | bytes 131104 | tf_op jit(solution)/shard_map/ppermute | solution.py:292
  120.7 0.1 fusion.4
  120.8 0.1 collective-permute-start.22
  120.9 1.4 %collective-permute-done.15 = bf16[512,128]{1,0:T(8,128)(2,1)S(1)} collective-permute-done((bf16[512,128]{1,0:T(8,128)(2,1)S(1)}, bf16[512,128]{1,0:T(8,128)(2,1)S(1)}, u32[]{:S(2)}, u32[]{:S(2)}) %collective-permute-start.15) | collective-permute-done | bytes 131104 | tf_op jit(solution)/shard_map/ppermute | solution.py:292
  122.3 0.1 fusion.9
  122.4 0.8 collective-permute-start.16
  123.1 3.6 %collective-permute-done.22 = bf16[512,128]{1,0:T(8,128)(2,1)S(1)} collective-permute-done((bf16[512,128]{1,0:T(8,128)(2,1)S(1)}, bf16[512,128]{1,0:T(8,128)(2,1)S(1)}, u32[]{:S(2)}, u32[]{:S(2)}) %collective-permute-start.22) | collective-permute-done | bytes 131104 | tf_op jit(solution)/shard_map/ppermute | solution.py:288
  126.7 0.7 add_convert_fusion
  127.4 0.7 collective-permute-done.16
  128.1 0.7 add_convert_fusion.3
  (38 shorter events, 0.1 us)
Async XLA Ops:
  1.6 29.9 %copy-start.2 = (bf16[2,512,128]{2,1,0:T(8,128)(2,1)}, bf16[2,512,128]{2,1,0:T(8,128)(2,1)S(1)}, u32[]{:S(2)}) copy-start(bf16[2,512,128]{2,1,0:T(8,128)(2,1)S(1)} %pad_maximum_fusion.refs_3_) | copy-start | bytes 786436
  1.6 8.1 %collective-permute-start.3 = (bf16[2,512,128]{2,1,0:T(8,128)(2,1)S(1)}, bf16[2,512,128]{2,1,0:T(8,128)(2,1)S(1)}, u32[]{:S(2)}, u32[]{:S(2)}) collective-permute-start(bf16[2,512,128]{2,1,0:T(8,128)(2,1)S(1)} %pad_maximum_fusion.refs_3_), channel_id=1, source_target_pairs={{0,8},{8,16},{16,24},{24,32},{32,40},{40,48},{48,56},{56,64},{64,7... | collective-permute-start | bytes 786440 | tf_op jit(solution)/shard_map/ppermute | solution.py:292
  1.8 11.6 %collective-permute-start.1 = (bf16[2,512,128]{2,1,0:T(8,128)(2,1)S(1)}, bf16[2,512,128]{2,1,0:T(8,128)(2,1)S(1)}, u32[]{:S(2)}, u32[]{:S(2)}) collective-permute-start(bf16[2,512,128]{2,1,0:T(8,128)(2,1)S(1)} %pad_maximum_fusion.refs_3_), channel_id=1, source_target_pairs={{0,5},{1,4},{2,7},{3,6},{8,13},{9,12},{10,15},{11,14},{16,21},{17,... | collective-permute-start | bytes 786440 | tf_op jit(solution)/shard_map/ppermute | solution.py:284
  9.8 21.8 %copy-start.3 = (bf16[2,512,128]{2,1,0:T(8,128)(2,1)}, bf16[2,512,128]{2,1,0:T(8,128)(2,1)S(1)}, u32[]{:S(2)}) copy-start(bf16[2,512,128]{2,1,0:T(8,128)(2,1)S(1)} %collective-permute-done.3.refs_7_) | copy-start | bytes 786436
  9.8 8.6 %collective-permute-start.7 = (bf16[2,512,128]{2,1,0:T(8,128)(2,1)S(1)}, bf16[2,512,128]{2,1,0:T(8,128)(2,1)S(1)}, u32[]{:S(2)}, u32[]{:S(2)}) collective-permute-start(bf16[2,512,128]{2,1,0:T(8,128)(2,1)S(1)} %collective-permute-done.3.refs_7_), channel_id=1, source_target_pairs={{0,8},{8,16},{16,24},{24,32},{32,40},{40,48},{48,56},{56,64},{64,7... | collective-permute-start | bytes 786440 | tf_op jit(solution)/shard_map/ppermute | solution.py:292
  13.4 6.8 %collective-permute-start = (bf16[2,512,128]{2,1,0:T(8,128)(2,1)S(1)}, bf16[2,512,128]{2,1,0:T(8,128)(2,1)S(1)}, u32[]{:S(2)}, u32[]{:S(2)}) collective-permute-start(bf16[2,512,128]{2,1,0:T(8,128)(2,1)S(1)} %pad_maximum_fusion.refs_3_), channel_id=1, source_target_pairs={{0,2},{2,0},{1,3},{3,1},{4,6},{6,4},{5,7},{7,5},{8,10},{10,8},{9,1... | collective-permute-start | bytes 786440 | tf_op jit(solution)/shard_map/ppermute | solution.py:279
  13.4 18.2 %copy-start.4 = (bf16[2,512,128]{2,1,0:T(8,128)(2,1)}, bf16[2,512,128]{2,1,0:T(8,128)(2,1)S(1)}, u32[]{:S(2)}) copy-start(bf16[2,512,128]{2,1,0:T(8,128)(2,1)S(1)} %collective-permute-done.1.refs_5_) | copy-start | bytes 786436
  13.4 11.3 %collective-permute-start.5 = (bf16[2,512,128]{2,1,0:T(8,128)(2,1)S(1)}, bf16[2,512,128]{2,1,0:T(8,128)(2,1)S(1)}, u32[]{:S(2)}, u32[]{:S(2)}) collective-permute-start(bf16[2,512,128]{2,1,0:T(8,128)(2,1)S(1)} %collective-permute-done.3.refs_7_), channel_id=1, source_target_pairs={{0,5},{1,4},{4,1},{5,0},{2,7},{3,6},{6,3},{7,2},{8,13},{9,12},{12,... | collective-permute-start | bytes 786440 | tf_op jit(solution)/shard_map/ppermute | solution.py:284
  18.3 13.2 %copy-start.5 = (bf16[2,512,128]{2,1,0:T(8,128)(2,1)}, bf16[2,512,128]{2,1,0:T(8,128)(2,1)S(1)}, u32[]{:S(2)}) copy-start(bf16[2,512,128]{2,1,0:T(8,128)(2,1)S(1)} %collective-permute-done.7.refs_11_) | copy-start | bytes 786436
  18.3 11.7 %collective-permute-start.9 = (bf16[2,512,128]{2,1,0:T(8,128)(2,1)S(1)}, bf16[2,512,128]{2,1,0:T(8,128)(2,1)S(1)}, u32[]{:S(2)}, u32[]{:S(2)}) collective-permute-start(bf16[2,512,128]{2,1,0:T(8,128)(2,1)S(1)} %collective-permute-done.7.refs_11_), channel_id=1, source_target_pairs={{4,1},{5,0},{6,3},{7,2},{12,9},{13,8},{14,11},{15,10},{20,17},{21,... | collective-permute-start | bytes 786440 | tf_op jit(solution)/shard_map/ppermute | solution.py:284
  19.6 10.4 %collective-permute-start.4 = (bf16[2,512,128]{2,1,0:T(8,128)(2,1)S(1)}, bf16[2,512,128]{2,1,0:T(8,128)(2,1)S(1)}, u32[]{:S(2)}, u32[]{:S(2)}) collective-permute-start(bf16[2,512,128]{2,1,0:T(8,128)(2,1)S(1)} %collective-permute-done.3.refs_7_), channel_id=1, source_target_pairs={{0,2},{2,0},{1,3},{3,1},{4,6},{6,4},{5,7},{7,5},{8,10},{10,8},{9,1... | collective-permute-start | bytes 786440 | tf_op jit(solution)/shard_map/ppermute | solution.py:279
  19.7 10.3 %collective-permute-start.2 = (bf16[2,512,128]{2,1,0:T(8,128)(2,1)S(1)}, bf16[2,512,128]{2,1,0:T(8,128)(2,1)S(1)}, u32[]{:S(2)}, u32[]{:S(2)}) collective-permute-start(bf16[2,512,128]{2,1,0:T(8,128)(2,1)S(1)} %collective-permute-done.1.refs_5_), channel_id=1, source_target_pairs={{0,2},{2,0},{1,3},{3,1},{4,6},{6,4},{5,7},{7,5},{8,10},{10,8},{9,1... | collective-permute-start | bytes 786440 | tf_op jit(solution)/shard_map/ppermute | solution.py:279
  20.2 11.4 %copy-start.6 = (bf16[2,512,128]{2,1,0:T(8,128)(2,1)}, bf16[2,512,128]{2,1,0:T(8,128)(2,1)S(1)}, u32[]{:S(2)}) copy-start(bf16[2,512,128]{2,1,0:T(8,128)(2,1)S(1)} %collective-permute-done.refs_4_) | copy-start | bytes 786436
  20.2 9.9 %collective-permute-start.8 = (bf16[2,512,128]{2,1,0:T(8,128)(2,1)S(1)}, bf16[2,512,128]{2,1,0:T(8,128)(2,1)S(1)}, u32[]{:S(2)}, u32[]{:S(2)}) collective-permute-start(bf16[2,512,128]{2,1,0:T(8,128)(2,1)S(1)} %collective-permute-done.7.refs_11_), channel_id=1, source_target_pairs={{0,2},{2,0},{1,3},{3,1},{4,6},{6,4},{5,7},{7,5},{8,10},{10,8},{9,1... | collective-permute-start | bytes 786440 | tf_op jit(solution)/shard_map/ppermute | solution.py:279
  24.6 6.9 %copy-start.7 = (bf16[2,512,128]{2,1,0:T(8,128)(2,1)}, bf16[2,512,128]{2,1,0:T(8,128)(2,1)S(1)}, u32[]{:S(2)}) copy-start(bf16[2,512,128]{2,1,0:T(8,128)(2,1)S(1)} %collective-permute-done.5.refs_9_) | copy-start | bytes 786436
  24.6 5.4 %collective-permute-start.6 = (bf16[2,512,128]{2,1,0:T(8,128)(2,1)S(1)}, bf16[2,512,128]{2,1,0:T(8,128)(2,1)S(1)}, u32[]{:S(2)}, u32[]{:S(2)}) collective-permute-start(bf16[2,512,128]{2,1,0:T(8,128)(2,1)S(1)} %collective-permute-done.5.refs_9_), channel_id=1, source_target_pairs={{0,2},{2,0},{1,3},{3,1},{4,6},{6,4},{5,7},{7,5},{8,10},{10,8},{9,1... | collective-permute-start | bytes 786440 | tf_op jit(solution)/shard_map/ppermute | solution.py:279
  30.0 1.6 %copy-start.8 = (bf16[2,512,128]{2,1,0:T(8,128)(2,1)}, bf16[2,512,128]{2,1,0:T(8,128)(2,1)S(1)}, u32[]{:S(2)}) copy-start(bf16[2,512,128]{2,1,0:T(8,128)(2,1)S(1)} %collective-permute-done.9.refs_13_) | copy-start | bytes 786436
  30.0 1.5 %collective-permute-start.10 = (bf16[2,512,128]{2,1,0:T(8,128)(2,1)S(1)}, bf16[2,512,128]{2,1,0:T(8,128)(2,1)S(1)}, u32[]{:S(2)}, u32[]{:S(2)}) collective-permute-start(bf16[2,512,128]{2,1,0:T(8,128)(2,1)S(1)} %collective-permute-done.9.refs_13_), channel_id=1, source_target_pairs={{0,2},{2,0},{1,3},{3,1},{4,6},{6,4},{5,7},{7,5},{8,10},{10,8},{9,1... | collective-permute-start | bytes 786440 | tf_op jit(solution)/shard_map/ppermute | solution.py:279
  30.0 1.6 %copy-start.9 = (bf16[2,512,128]{2,1,0:T(8,128)(2,1)}, bf16[2,512,128]{2,1,0:T(8,128)(2,1)S(1)}, u32[]{:S(2)}) copy-start(bf16[2,512,128]{2,1,0:T(8,128)(2,1)S(1)} %collective-permute-done.4.refs_8_) | copy-start | bytes 786436
  30.0 1.6 %copy-start.10 = (bf16[2,512,128]{2,1,0:T(8,128)(2,1)}, bf16[2,512,128]{2,1,0:T(8,128)(2,1)S(1)}, u32[]{:S(2)}) copy-start(bf16[2,512,128]{2,1,0:T(8,128)(2,1)S(1)} %collective-permute-done.2.refs_6_) | copy-start | bytes 786436
  30.1 1.6 %copy-start.12 = (bf16[2,512,128]{2,1,0:T(8,128)(2,1)}, bf16[2,512,128]{2,1,0:T(8,128)(2,1)S(1)}, u32[]{:S(2)}) copy-start(bf16[2,512,128]{2,1,0:T(8,128)(2,1)S(1)} %collective-permute-done.6.refs_10_) | copy-start | bytes 786436
  30.1 1.5 %copy-start.11 = (bf16[2,512,128]{2,1,0:T(8,128)(2,1)}, bf16[2,512,128]{2,1,0:T(8,128)(2,1)S(1)}, u32[]{:S(2)}) copy-start(bf16[2,512,128]{2,1,0:T(8,128)(2,1)S(1)} %collective-permute-done.8.refs_12_) | copy-start | bytes 786436
  31.6 0.7 copy-start.13
  73.1 21.1 %copy-start = (bf16[3,2,512,128]{3,2,1,0:T(8,128)(2,1)S(1)}, bf16[3,2,512,128]{3,2,1,0:T(8,128)(2,1)}, u32[]{:S(2)}) copy-start(bf16[3,2,512,128]{3,2,1,0:T(8,128)(2,1)} %get-tuple-element.16) | copy-start | bytes 2359300
  73.1 7.8 %collective-permute-start.17 = (bf16[3,2,512,128]{3,2,1,0:T(8,128)(2,1)}, bf16[3,2,512,128]{3,2,1,0:T(8,128)(2,1)S(1)}, u32[]{:S(2)}, u32[]{:S(2)}) collective-permute-start(bf16[3,2,512,128]{3,2,1,0:T(8,128)(2,1)} %get-tuple-element.20), channel_id=1, source_target_pairs={{0,2},{2,0},{1,3},{3,1},{4,6},{6,4},{5,7},{7,5},{8,10},{10,8},{9,1... | collective-permute-start | bytes 2359304 | tf_op jit(solution)/shard_map/ppermute | solution.py:279
  78.8 15.4 %collective-permute-start.11 = (bf16[3,2,512,128]{3,2,1,0:T(8,128)(2,1)}, bf16[3,2,512,128]{3,2,1,0:T(8,128)(2,1)S(1)}, u32[]{:S(2)}, u32[]{:S(2)}) collective-permute-start(bf16[3,2,512,128]{3,2,1,0:T(8,128)(2,1)} %get-tuple-element.17), channel_id=1, source_target_pairs={{0,2},{2,0},{1,3},{3,1},{4,6},{6,4},{5,7},{7,5},{8,10},{10,8},{9,1... | collective-permute-start | bytes 2359304 | tf_op jit(solution)/shard_map/ppermute | solution.py:279
  82.0 19.7 %copy-start.1 = (bf16[3,2,512,128]{3,2,1,0:T(8,128)(2,1)S(1)}, bf16[3,2,512,128]{3,2,1,0:T(8,128)(2,1)}, u32[]{:S(2)}) copy-start(bf16[3,2,512,128]{3,2,1,0:T(8,128)(2,1)} %get-tuple-element.19) | copy-start | bytes 2359300
  82.0 16.1 %collective-permute-start.18 = (bf16[512,128]{1,0:T(8,128)(2,1)S(1)}, bf16[512,128]{1,0:T(8,128)(2,1)S(1)}, u32[]{:S(2)}, u32[]{:S(2)}) collective-permute-start(bf16[512,128]{1,0:T(8,128)(2,1)S(1)} %get-tuple-element.23), channel_id=1, source_target_pairs={{0,5},{1,4},{4,1},{5,0},{2,7},{3,6},{6,3},{7,2},{8,13},{9,12},{12,... | collective-permute-start | bytes 393224 | tf_op jit(solution)/shard_map/ppermute | solution.py:284
  94.3 7.6 %collective-permute-start.12 = (bf16[512,128]{1,0:T(8,128)(2,1)S(1)}, bf16[512,128]{1,0:T(8,128)(2,1)S(1)}, u32[]{:S(2)}, u32[]{:S(2)}) collective-permute-start(bf16[512,128]{1,0:T(8,128)(2,1)S(1)} %get-tuple-element.25), channel_id=1, source_target_pairs={{0,5},{1,4},{4,1},{5,0},{2,7},{3,6},{6,3},{7,2},{8,13},{9,12},{12,... | collective-permute-start | bytes 393224 | tf_op jit(solution)/shard_map/ppermute | solution.py:284
  98.2 6.6 %collective-permute-start.19 = (bf16[512,128]{1,0:T(8,128)(2,1)S(1)}, bf16[512,128]{1,0:T(8,128)(2,1)S(1)}, u32[]{:S(2)}, u32[]{:S(2)}) collective-permute-start(bf16[512,128]{1,0:T(8,128)(2,1)S(1)} %get-tuple-element.21), channel_id=1, source_target_pairs={{0,5},{1,4},{4,1},{5,0},{2,7},{3,6},{6,3},{7,2},{8,13},{9,12},{12,... | collective-permute-start | bytes 393224 | tf_op jit(solution)/shard_map/ppermute | solution.py:284
  101.8 9.3 %collective-permute-start.20 = (bf16[512,128]{1,0:T(8,128)(2,1)S(1)}, bf16[512,128]{1,0:T(8,128)(2,1)S(1)}, u32[]{:S(2)}, u32[]{:S(2)}) collective-permute-start(bf16[512,128]{1,0:T(8,128)(2,1)S(1)} %fusion), channel_id=1, source_target_pairs={{0,120},{8,0},{16,8},{24,16},{32,24},{40,32},{48,40},{56,48},{64,5... | collective-permute-start | bytes 393224 | tf_op jit(solution)/shard_map/ppermute | solution.py:292
  101.9 9.3 %collective-permute-start.13 = (bf16[512,128]{1,0:T(8,128)(2,1)S(1)}, bf16[512,128]{1,0:T(8,128)(2,1)S(1)}, u32[]{:S(2)}, u32[]{:S(2)}) collective-permute-start(bf16[512,128]{1,0:T(8,128)(2,1)S(1)} %get-tuple-element.18), channel_id=1, source_target_pairs={{0,5},{1,4},{4,1},{5,0},{2,7},{3,6},{6,3},{7,2},{8,13},{9,12},{12,... | collective-permute-start | bytes 393224 | tf_op jit(solution)/shard_map/ppermute | solution.py:284
  104.0 8.9 %collective-permute-start.14 = (bf16[512,128]{1,0:T(8,128)(2,1)S(1)}, bf16[512,128]{1,0:T(8,128)(2,1)S(1)}, u32[]{:S(2)}, u32[]{:S(2)}) collective-permute-start(bf16[512,128]{1,0:T(8,128)(2,1)S(1)} %fusion.5), channel_id=1, source_target_pairs={{0,120},{8,0},{16,8},{24,16},{32,24},{40,32},{48,40},{56,48},{64,5... | collective-permute-start | bytes 393224 | tf_op jit(solution)/shard_map/ppermute | solution.py:292
  111.1 9.6 %collective-permute-start.21 = (bf16[512,128]{1,0:T(8,128)(2,1)S(1)}, bf16[512,128]{1,0:T(8,128)(2,1)S(1)}, u32[]{:S(2)}, u32[]{:S(2)}) collective-permute-start(bf16[512,128]{1,0:T(8,128)(2,1)S(1)} %fusion.2), channel_id=1, source_target_pairs={{0,120},{8,0},{16,8},{24,16},{32,24},{40,32},{48,40},{56,48},{64,5... | collective-permute-start | bytes 393224 | tf_op jit(solution)/shard_map/ppermute | solution.py:292
  113.0 9.3 %collective-permute-start.15 = (bf16[512,128]{1,0:T(8,128)(2,1)S(1)}, bf16[512,128]{1,0:T(8,128)(2,1)S(1)}, u32[]{:S(2)}, u32[]{:S(2)}) collective-permute-start(bf16[512,128]{1,0:T(8,128)(2,1)S(1)} %fusion.7), channel_id=1, source_target_pairs={{0,120},{8,0},{16,8},{24,16},{32,24},{40,32},{48,40},{56,48},{64,5... | collective-permute-start | bytes 393224 | tf_op jit(solution)/shard_map/ppermute | solution.py:292
  120.8 5.9 %collective-permute-start.22 = (bf16[512,128]{1,0:T(8,128)(2,1)S(1)}, bf16[512,128]{1,0:T(8,128)(2,1)S(1)}, u32[]{:S(2)}, u32[]{:S(2)}) collective-permute-start(bf16[512,128]{1,0:T(8,128)(2,1)S(1)} %fusion.4), channel_id=1, source_target_pairs={{0,1},{1,0},{2,3},{3,2},{4,5},{5,4},{6,7},{7,6},{8,9},{9,8},{10,11... | collective-permute-start | bytes 393224 | tf_op jit(solution)/shard_map/ppermute | solution.py:288
  122.4 5.7 %collective-permute-start.16 = (bf16[512,128]{1,0:T(8,128)(2,1)S(1)}, bf16[512,128]{1,0:T(8,128)(2,1)S(1)}, u32[]{:S(2)}, u32[]{:S(2)}) collective-permute-start(bf16[512,128]{1,0:T(8,128)(2,1)S(1)} %fusion.9), channel_id=1, source_target_pairs={{0,1},{1,0},{2,3},{3,2},{4,5},{5,4},{6,7},{7,6},{8,9},{9,8},{10,11... | collective-permute-start | bytes 393224 | tf_op jit(solution)/shard_map/ppermute | solution.py:288

commit v6 on v5

--- a/solution.py
+++ b/solution.py
@@ -15,6 +15,7 @@
 HALF = BLK // 2
 ROWS = 3
 SLOTS = 4 * ROWS
+GROUP = 3
 SPAN = 9
 SCALE = HD ** -0.5
 LOG2 = SCALE * math.log2(math.e)
@@ -70,11 +71,15 @@
 
 
 def attention_kernel(*refs):
-    len_ref, q_ref, do_ref = refs[:3]
+    len_ref, q_hbm, do_hbm = refs[:3]
     kv_refs = refs[3:15]
-    o_ref, dq_ref = refs[15:17]
+    o_hbm, dq_hbm = refs[15:17]
     out_refs = refs[17:21]
-    kvs, dkvs, qt, dot_t, do_s, probs, row_max, total, acc, dq_acc, stage, delta, norms, in_sem, out_sem = refs[21:]
+    kvs, dkvs, qt, dot_t, do_s, probs, row_max, total, acc, dq_acc, stage, delta, norms, q_ref, do_ref, o_ref, dq_ref, row_sem, in_sem, out_sem = refs[21:]
+    loads = [[pltpu.make_async_copy(a.at[h], b.at[h], row_sem.at[n, h]) for n, (a, b) in enumerate(((q_hbm, q_ref), (do_hbm, do_ref)))] for h in range(HEADS)]
+    for pair in loads:
+        for copy in pair:
+            copy.start()
     at = Place(len_ref)
     order = [(j, dz, dc) for j in range(ROWS) for dz, dc in NEAR]
     for n, where in enumerate(order):
@@ -88,18 +93,23 @@
         j, dz, dc = order[n]
         return pltpu.make_async_copy(dkvs.at[t, part], out_refs[part * 2 + dc].at[j, dz], out_sem.at[n, part])
 
-    begin, end = at.lo, at.hi + 1
-    dkvs[SLOTS] = jnp.zeros((2, BLK, HD), BF16)
+    begin = at.lo
+    end = begin + (at.hi - begin + GROUP) // GROUP * GROUP
+    for spare in range(SLOTS, SLOTS + GROUP - 1):
+        kvs[spare] = jnp.zeros((2, BLK, HD), BF16)
+    dkvs[SLOTS + GROUP - 1] = jnp.zeros((2, BLK, HD), BF16)
     for n, where in enumerate(order):
         slot = at.slot(*where)
 
         @pl.when((slot < begin) | (slot >= end))
         def _():
             for part in range(2):
-                out_copy(n, part, SLOTS).start()
+                out_copy(n, part, SLOTS + GROUP - 1).start()
 
     for h in range(HEADS):
         cols = slice(h * BLK, (h + 1) * BLK)
+        for copy in loads[h]:
+            copy.wait()
         qt[:, cols] = q_ref[h].T
         dot_t[:, cols] = do_ref[h].T
     dq_acc[...] = jnp.zeros((HD, NQ), F32)
@@ -142,17 +152,16 @@
         total[...] = jnp.zeros((1, NQ), F32)
         acc[...] = jnp.zeros((HD, NQ), F32)
 
-    def fast_step(t, carry):
-        arrived(t)
-        masked = (t * BLK < at.last_start) | (t == at.hi)
-
-        @pl.when(masked)
-        def _():
-            forward(t, True, False)
-
-        @pl.when(jnp.logical_not(masked))
-        def _():
-            forward(t, False, False)
+    def fast_step(i, carry):
+        for u in range(GROUP):
+            t = begin + i * GROUP + u
+
+            @pl.when(t < SLOTS)
+            def _():
+                arrived(t)
+
+        for u in range(GROUP):
+            forward(begin + i * GROUP + u, True, False)
 
         return carry
 
@@ -169,7 +178,7 @@
         return carry
 
     clear()
-    lax.fori_loop(begin, end, fast_step, 0)
+    lax.fori_loop(0, (end - begin) // GROUP, fast_step, 0)
     q_norm = jnp.max(dot(jnp.ones((8, HD), BF16), jnp.square(qt[...].astype(F32)).astype(BF16)))
 
     @pl.when(q_norm * jnp.max(norms[...]) > 0.98 * (BOUND / LOG2) ** 2)
@@ -185,13 +194,13 @@
         inverse = 1.0 / total[:, cols]
         o = (acc[:, cols] * inverse).astype(BF16)
         o_ref[h] = o.T
+        pltpu.make_async_copy(o_ref.at[h], o_hbm.at[h], row_sem.at[2, h]).start()
         scaled = (dot_t[:, cols].astype(F32) * inverse).astype(BF16)
         dot_t[:, cols] = scaled
         do_s[h * BLK:(h + 1) * BLK] = scaled.T
         delta[:, cols] = jnp.sum(o.astype(F32) * scaled.astype(F32), axis=0, keepdims=True)
 
-    def backward_step(t, carry):
-        k_t = kvs[t, 0].T
+    def backward_tile(t, u):
         v = kvs[t, 1]
 
         def dp_of(h):
@@ -200,48 +209,55 @@
         def ds_of(h, dp):
             cols = slice(h * BLK, (h + 1) * BLK)
             ds = (probs[t - begin, :, cols].astype(F32) * (dp - delta[:, cols])).astype(BF16)
-            stage[:, cols] = ds
+            stage[u * BLK:(u + 1) * BLK, cols] = ds
             return ds
-
-        def dq_of(h, ds):
-            dq_acc[:, h * BLK:(h + 1) * BLK] += dot(k_t, ds)
 
         d0 = dp_of(0)
         d1 = dp_of(1)
-        s0 = ds_of(0, d0)
+        ds_of(0, d0)
         dkvs[t, 1] = dot(probs[t - begin], do_s[...]).astype(BF16)
         d2 = dp_of(2)
-        dq_of(0, s0)
-        s1 = ds_of(1, d1)
+        ds_of(1, d1)
         d3 = dp_of(3)
-        dq_of(1, s1)
-        s2 = ds_of(2, d2)
-        dq_of(2, s2)
-        s3 = ds_of(3, d3)
-        dq_of(3, s3)
-        dkvs[t, 0] = (dot(stage[...], q_ref[...].reshape(NQ, HD)) * SCALE).astype(BF16)
-
+        ds_of(2, d2)
+        ds_of(3, d3)
+        dkvs[t, 0] = (dot(stage[u * BLK:(u + 1) * BLK], q_ref[...].reshape(NQ, HD)) * SCALE).astype(BF16)
+
+    def backward_step(i, carry):
+        first = begin + i * GROUP
+        for u in range(GROUP):
+            backward_tile(first + u, u)
+        k_t = jnp.concatenate([kvs[first + u, 0].T for u in range(GROUP)], axis=1)
+        for h in range(HEADS):
+            cols = slice(h * BLK, (h + 1) * BLK)
+            dq_acc[:, cols] += dot(k_t, stage[:, cols])
         for n, where in enumerate(order):
-            @pl.when(at.slot(*where) == t)
+            slot = at.slot(*where)
+
+            @pl.when((slot >= first) & (slot < first + GROUP))
             def _():
                 for part in range(2):
-                    out_copy(n, part, t).start()
-
-        return carry
-
-    lax.fori_loop(begin, end, backward_step, 0)
+                    out_copy(n, part, slot).start()
+
+        return carry
+
+    lax.fori_loop(0, (end - begin) // GROUP, backward_step, 0)
     for h in range(HEADS):
         dq_ref[h] = (dq_acc[:, h * BLK:(h + 1) * BLK] * SCALE).astype(BF16).T
+        pltpu.make_async_copy(dq_ref.at[h], dq_hbm.at[h], row_sem.at[3, h]).start()
 
     def rest(t, carry):
         arrived(t)
         return carry
 
     lax.fori_loop(0, begin, rest, 0)
-    lax.fori_loop(end, SLOTS, rest, 0)
+    lax.fori_loop(jnp.minimum(end, SLOTS), SLOTS, rest, 0)
     for n in range(len(order)):
         for part in range(2):
             out_copy(n, part, 0).wait()
+    for h in range(HEADS):
+        pltpu.make_async_copy(o_ref.at[h], o_hbm.at[h], row_sem.at[2, h]).wait()
+        pltpu.make_async_copy(dq_ref.at[h], dq_hbm.at[h], row_sem.at[3, h]).wait()
 
 
 def attention(seq_lengths, queries, d_out, blocks):
@@ -250,11 +266,11 @@
     return pl.pallas_call(
         attention_kernel,
         out_shape=(rows, rows) + (grads,) * 4,
-        in_specs=[SMEM, VMEM, VMEM] + [ANY] * SLOTS,
-        out_specs=[VMEM, VMEM] + [ANY] * 4,
+        in_specs=[SMEM] + [ANY] * (2 + SLOTS),
+        out_specs=[ANY] * 6,
         scratch_shapes=[
-            pltpu.VMEM((SLOTS, 2, BLK, HD), BF16),
-            pltpu.VMEM((SLOTS + 1, 2, BLK, HD), BF16),
+            pltpu.VMEM((SLOTS + GROUP - 1, 2, BLK, HD), BF16),
+            pltpu.VMEM((SLOTS + GROUP, 2, BLK, HD), BF16),
             pltpu.VMEM((HD, NQ), BF16),
             pltpu.VMEM((HD, NQ), BF16),
             pltpu.VMEM((NQ, HD), BF16),
@@ -263,9 +279,14 @@
             pltpu.VMEM((1, NQ), F32),
             pltpu.VMEM((HD, NQ), F32),
             pltpu.VMEM((HD, NQ), F32),
-            pltpu.VMEM((BLK, NQ), BF16),
+            pltpu.VMEM((GROUP * BLK, NQ), BF16),
             pltpu.VMEM((1, NQ), F32),
             pltpu.VMEM((8, HD), F32),
+            pltpu.VMEM((HEADS, BLK, HD), BF16),
+            pltpu.VMEM((HEADS, BLK, HD), BF16),
+            pltpu.VMEM((HEADS, BLK, HD), BF16),
+            pltpu.VMEM((HEADS, BLK, HD), BF16),
+            DMA((4, HEADS)),
             DMA((SLOTS,)),
             DMA((SLOTS, 2)),
         ],

time: 128 us -> 126 us (0.984); the launches traced: 129 us -> 125 us
  starting transfers between devices: 40.6 us -> 22.1 us
  Pallas kernels: 40.8 us -> 55.4 us
    pallas_call x1, Pallas kernels: 40.8 us -> 55.4 us  [attention(): pl.pallas_call(attention_kernel, out_shape=(rows, rows) + (grads,) * 4, i...]
    ppermute x7, starting transfers between devices: 29.3 us -> 16.3 us  [swap_z(): return lax.ppermute(value, ('zh', 'zl'), pairs)]
    ppermute x8, starting transfers between devices: 6.43 us -> 1.27 us  [swap_core(): return lax.ppermute(value, 'core', [(0, 1), (1, 0)])]
    ppermute x7, waiting for transfers between devices: 14.2 us -> 19.3 us  [swap_z(): return lax.ppermute(value, ('zh', 'zl'), pairs)]
    ppermute x6, waiting for transfers between devices: 19.8 us -> 15.3 us  [shift_row(): lax.ppermute(value, ('x', 'y'), [(r, (r + by) % 16) for r in range(16)])]
  transfers between devices with their start and end apart: 23 -> 23, of which waited for: 14 -> 15; matrix products, arithmetic and copies ran while one was open for 2% -> 2% of each run, Pallas kernels for 0% -> 0%
where the time goes in v6:
time: 126 us; the launch traced here: 125 us
  Pallas kernels  55.4 us (44%)
  waiting for transfers between devices  42 us (33%)
  starting transfers between devices  22.1 us (18%)
  other arithmetic  4.07 us (3%)
    pallas_call x1, Pallas kernels, attention(): pl.pallas_call(attention_kernel, out_shape=(rows, rows) + (grads,) * 4, i...  55.4 us
    ppermute x7, waiting for transfers between devices, swap_z(): return lax.ppermute(value, ('zh', 'zl'), pairs)  19.3 us
    ppermute x7, starting transfers between devices, swap_z(): return lax.ppermute(value, ('zh', 'zl'), pairs)  16.3 us
    ppermute x6, waiting for transfers between devices, shift_row(): lax.ppermute(value, ('x', 'y'), [(r, (r + by) % 16) for r in range(16)])  15.3 us
    ppermute x6, starting transfers between devices, shift_row(): lax.ppermute(value, ('x', 'y'), [(r, (r + by) % 16) for r in range(16)])  4.03 us
    ppermute x2, waiting for transfers between devices, swap_head(): return lax.ppermute(value, 'zl', [(0, 1), (1, 0)])  3.89 us
    ppermute x8, waiting for transfers between devices, swap_core(): return lax.ppermute(value, 'core', [(0, 1), (1, 0)])  3.46 us
    convert_element_type x10, other arithmetic, added(): return total.astype(BF16)  3.07 us
  transfers between devices with their start and end apart: 23, of which 15 were waited for; matrix products, arithmetic and copies ran while one was open for 2% of the time, Pallas kernels for 0%

profile of v6, /device:TPU:30, one launch (start us, length us, event | category | flops | bytes accessed | tf_op | source)
XLA Modules:
  0.0 125.3 jit_solution(6362093896694756775)
XLA Ops:
  0.6 1.0 pad_maximum_fusion.refs_3_
  1.6 0.1 collective-permute-start.3
  1.8 6.0 %collective-permute-start.1 = (bf16[2,512,128]{2,1,0:T(8,128)(2,1)S(1)}, bf16[2,512,128]{2,1,0:T(8,128)(2,1)S(1)}, u32[]{:S(2)}, u32[]{:S(2)}) collective-permute-start(bf16[2,512,128]{2,1,0:T(8,128)(2,1)S(1)} %pad_maximum_fusion.refs_3_), channel_id=1, source_target_pairs={{0,5},{1,4},{2,7},{3,6},{8,13},{9,12},{10,15},{11,14},{16,21},{17,... | collective-permute-start | bytes 786440 | tf_op jit(solution)/shard_map/ppermute | solution.py:305
  7.8 2.0 %collective-permute-done.3.refs_7_ = bf16[2,512,128]{2,1,0:T(8,128)(2,1)S(1)} collective-permute-done((bf16[2,512,128]{2,1,0:T(8,128)(2,1)S(1)}, bf16[2,512,128]{2,1,0:T(8,128)(2,1)S(1)}, u32[]{:S(2)}, u32[]{:S(2)}) %collective-permute-start.3) | collective-permute-done | bytes 262176 | tf_op jit(solution)/shard_map/ppermute | solution.py:313
  9.8 3.6 %collective-permute-start.7 = (bf16[2,512,128]{2,1,0:T(8,128)(2,1)S(1)}, bf16[2,512,128]{2,1,0:T(8,128)(2,1)S(1)}, u32[]{:S(2)}, u32[]{:S(2)}) collective-permute-start(bf16[2,512,128]{2,1,0:T(8,128)(2,1)S(1)} %collective-permute-done.3.refs_7_), channel_id=1, source_target_pairs={{0,8},{8,16},{16,24},{24,32},{32,40},{40,48},{48,56},{56,64},{64,7... | collective-permute-start | bytes 786440 | tf_op jit(solution)/shard_map/ppermute | solution.py:313
  13.4 0.0 collective-permute-start
  13.4 4.1 %collective-permute-start.5 = (bf16[2,512,128]{2,1,0:T(8,128)(2,1)S(1)}, bf16[2,512,128]{2,1,0:T(8,128)(2,1)S(1)}, u32[]{:S(2)}, u32[]{:S(2)}) collective-permute-start(bf16[2,512,128]{2,1,0:T(8,128)(2,1)S(1)} %collective-permute-done.3.refs_7_), channel_id=1, source_target_pairs={{0,5},{1,4},{4,1},{5,0},{2,7},{3,6},{6,3},{7,2},{8,13},{9,12},{12,... | collective-permute-start | bytes 786440 | tf_op jit(solution)/shard_map/ppermute | solution.py:305
  17.5 0.8 collective-permute-done.7.refs_11_
  18.3 1.3 %collective-permute-start.9 = (bf16[2,512,128]{2,1,0:T(8,128)(2,1)S(1)}, bf16[2,512,128]{2,1,0:T(8,128)(2,1)S(1)}, u32[]{:S(2)}, u32[]{:S(2)}) collective-permute-start(bf16[2,512,128]{2,1,0:T(8,128)(2,1)S(1)} %collective-permute-done.7.refs_11_), channel_id=1, source_target_pairs={{4,1},{5,0},{6,3},{7,2},{12,9},{13,8},{14,11},{15,10},{20,17},{21,... | collective-permute-start | bytes 786440 | tf_op jit(solution)/shard_map/ppermute | solution.py:305
  19.6 0.1 collective-permute-start.4
  19.7 0.5 collective-permute-start.2
  20.2 0.1 collective-permute-start.8
  20.3 4.3 %collective-permute-done.5.refs_9_ = bf16[2,512,128]{2,1,0:T(8,128)(2,1)S(1)} collective-permute-done((bf16[2,512,128]{2,1,0:T(8,128)(2,1)S(1)}, bf16[2,512,128]{2,1,0:T(8,128)(2,1)S(1)}, u32[]{:S(2)}, u32[]{:S(2)}) %collective-permute-start.5) | collective-permute-done | bytes 262176 | tf_op jit(solution)/shard_map/ppermute | solution.py:305
  24.7 5.3 %collective-permute-done.9.refs_13_ = bf16[2,512,128]{2,1,0:T(8,128)(2,1)S(1)} collective-permute-done((bf16[2,512,128]{2,1,0:T(8,128)(2,1)S(1)}, bf16[2,512,128]{2,1,0:T(8,128)(2,1)S(1)}, u32[]{:S(2)}, u32[]{:S(2)}) %collective-permute-start.9) | collective-permute-done | bytes 262176 | tf_op jit(solution)/shard_map/ppermute | solution.py:305
  30.1 1.5 %collective-permute-done.10.refs_14_ = bf16[2,512,128]{2,1,0:T(8,128)(2,1)S(1)} collective-permute-done((bf16[2,512,128]{2,1,0:T(8,128)(2,1)S(1)}, bf16[2,512,128]{2,1,0:T(8,128)(2,1)S(1)}, u32[]{:S(2)}, u32[]{:S(2)}) %collective-permute-start.10) | collective-permute-done | bytes 262176 | tf_op jit(solution)/shard_map/ppermute | solution.py:300
  31.6 0.7 copy-done.13
  32.3 55.4 %attention.1 = (bf16[4,512,128]{2,1,0:T(8,128)(2,1)}, bf16[4,512,128]{2,1,0:T(8,128)(2,1)}, bf16[3,2,512,128]{3,2,1,0:T(8,128)(2,1)}, bf16[3,2,512,128]{3,2,1,0:...) custom-call(s32[16]{0:T(128)} %refs_0_.1, bf16[4,512,128]{2,1,0:T(8,128)(2,1)} %refs_1_.1, ...), custom_call_target="tpu_custom_call" | custom-call | flops 8589934592 | bytes 16777216 | tf_op jit(solution)/shard_map/attention/pallas_call | solution.py:266
  87.8 0.2 collective-permute-start.17
  88.0 0.4 collective-permute-start.11
  88.4 2.0 %collective-permute-done.17 = bf16[3,2,512,128]{3,2,1,0:T(8,128)(2,1)S(1)} collective-permute-done((bf16[3,2,512,128]{3,2,1,0:T(8,128)(2,1)}, bf16[3,2,512,128]{3,2,1,0:T(8,128)(2,1)S(1)}, u32[]{:S(2)}, u32[]{:S(2)}) %collective-permute-start.17) | collective-permute-done | bytes 786464 | tf_op jit(solution)/shard_map/ppermute | solution.py:300
  90.4 1.1 fusion.13
  91.5 0.1 collective-permute-start.18
  91.6 0.1 fusion.11
  91.8 3.3 %collective-permute-start.12 = (bf16[512,128]{1,0:T(8,128)(2,1)S(1)}, bf16[512,128]{1,0:T(8,128)(2,1)S(1)}, u32[]{:S(2)}, u32[]{:S(2)}) collective-permute-start(bf16[512,128]{1,0:T(8,128)(2,1)S(1)} %get-tuple-element.25), channel_id=1, source_target_pairs={{0,5},{1,4},{4,1},{5,0},{2,7},{3,6},{6,3},{7,2},{8,13},{9,12},{12,... | collective-permute-start | bytes 393224 | tf_op jit(solution)/shard_map/ppermute | solution.py:305
  95.0 4.1 %collective-permute-done.18 = bf16[512,128]{1,0:T(8,128)(2,1)S(1)} collective-permute-done((bf16[512,128]{1,0:T(8,128)(2,1)S(1)}, bf16[512,128]{1,0:T(8,128)(2,1)S(1)}, u32[]{:S(2)}, u32[]{:S(2)}) %collective-permute-start.18) | collective-permute-done | bytes 131104 | tf_op jit(solution)/shard_map/ppermute | solution.py:305
  99.2 0.1 fusion
  99.2 0.1 collective-permute-start.20
  99.3 1.8 %collective-permute-done.12 = bf16[512,128]{1,0:T(8,128)(2,1)S(1)} collective-permute-done((bf16[512,128]{1,0:T(8,128)(2,1)S(1)}, bf16[512,128]{1,0:T(8,128)(2,1)S(1)}, u32[]{:S(2)}, u32[]{:S(2)}) %collective-permute-start.12) | collective-permute-done | bytes 131104 | tf_op jit(solution)/shard_map/ppermute | solution.py:305
  101.2 1.5 %collective-permute-start.13 = (bf16[512,128]{1,0:T(8,128)(2,1)S(1)}, bf16[512,128]{1,0:T(8,128)(2,1)S(1)}, u32[]{:S(2)}, u32[]{:S(2)}) collective-permute-start(bf16[512,128]{1,0:T(8,128)(2,1)S(1)} %get-tuple-element.18), channel_id=1, source_target_pairs={{0,5},{1,4},{4,1},{5,0},{2,7},{3,6},{6,3},{7,2},{8,13},{9,12},{12,... | collective-permute-start | bytes 393224 | tf_op jit(solution)/shard_map/ppermute | solution.py:305
  102.7 0.1 fusion.5
  102.7 0.1 collective-permute-start.14
  102.8 3.6 %collective-permute-done.19 = bf16[512,128]{1,0:T(8,128)(2,1)S(1)} collective-permute-done((bf16[512,128]{1,0:T(8,128)(2,1)S(1)}, bf16[512,128]{1,0:T(8,128)(2,1)S(1)}, u32[]{:S(2)}, u32[]{:S(2)}) %collective-permute-start.19) | collective-permute-done | bytes 131104 | tf_op jit(solution)/shard_map/ppermute | solution.py:305
  106.5 2.2 %collective-permute-done.20 = bf16[512,128]{1,0:T(8,128)(2,1)S(1)} collective-permute-done((bf16[512,128]{1,0:T(8,128)(2,1)S(1)}, bf16[512,128]{1,0:T(8,128)(2,1)S(1)}, u32[]{:S(2)}, u32[]{:S(2)}) %collective-permute-start.20) | collective-permute-done | bytes 131104 | tf_op jit(solution)/shard_map/ppermute | solution.py:313
  108.7 0.1 fusion.2
  108.8 0.1 collective-permute-start.21
  108.9 2.2 %collective-permute-done.14 = bf16[512,128]{1,0:T(8,128)(2,1)S(1)} collective-permute-done((bf16[512,128]{1,0:T(8,128)(2,1)S(1)}, bf16[512,128]{1,0:T(8,128)(2,1)S(1)}, u32[]{:S(2)}, u32[]{:S(2)}) %collective-permute-start.14) | collective-permute-done | bytes 131104 | tf_op jit(solution)/shard_map/ppermute | solution.py:313
  111.1 0.1 fusion.7
  111.2 0.1 collective-permute-start.15
  111.2 6.5 %collective-permute-done.21 = bf16[512,128]{1,0:T(8,128)(2,1)S(1)} collective-permute-done((bf16[512,128]{1,0:T(8,128)(2,1)S(1)}, bf16[512,128]{1,0:T(8,128)(2,1)S(1)}, u32[]{:S(2)}, u32[]{:S(2)}) %collective-permute-start.21) | collective-permute-done | bytes 131104 | tf_op jit(solution)/shard_map/ppermute | solution.py:313
  117.7 0.1 fusion.4
  117.8 0.1 collective-permute-start.22
  117.9 1.6 %collective-permute-done.15 = bf16[512,128]{1,0:T(8,128)(2,1)S(1)} collective-permute-done((bf16[512,128]{1,0:T(8,128)(2,1)S(1)}, bf16[512,128]{1,0:T(8,128)(2,1)S(1)}, u32[]{:S(2)}, u32[]{:S(2)}) %collective-permute-start.15) | collective-permute-done | bytes 131104 | tf_op jit(solution)/shard_map/ppermute | solution.py:313
  119.5 0.1 fusion.9
  119.6 0.5 collective-permute-start.16
  120.1 2.8 %collective-permute-done.22 = bf16[512,128]{1,0:T(8,128)(2,1)S(1)} collective-permute-done((bf16[512,128]{1,0:T(8,128)(2,1)S(1)}, bf16[512,128]{1,0:T(8,128)(2,1)S(1)}, u32[]{:S(2)}, u32[]{:S(2)}) %collective-permute-start.22) | collective-permute-done | bytes 131104 | tf_op jit(solution)/shard_map/ppermute | solution.py:309
  122.8 0.7 add_convert_fusion
  123.5 1.1 collective-permute-done.16
  124.6 0.7 add_convert_fusion.3
  (38 shorter events, 0.1 us)
Async XLA Ops:
  1.6 29.9 %copy-start.2 = (bf16[2,512,128]{2,1,0:T(8,128)(2,1)}, bf16[2,512,128]{2,1,0:T(8,128)(2,1)S(1)}, u32[]{:S(2)}) copy-start(bf16[2,512,128]{2,1,0:T(8,128)(2,1)S(1)} %pad_maximum_fusion.refs_3_) | copy-start | bytes 786436
  1.6 8.1 %collective-permute-start.3 = (bf16[2,512,128]{2,1,0:T(8,128)(2,1)S(1)}, bf16[2,512,128]{2,1,0:T(8,128)(2,1)S(1)}, u32[]{:S(2)}, u32[]{:S(2)}) collective-permute-start(bf16[2,512,128]{2,1,0:T(8,128)(2,1)S(1)} %pad_maximum_fusion.refs_3_), channel_id=1, source_target_pairs={{0,8},{8,16},{16,24},{24,32},{32,40},{40,48},{48,56},{56,64},{64,7... | collective-permute-start | bytes 786440 | tf_op jit(solution)/shard_map/ppermute | solution.py:313
  1.8 11.6 %collective-permute-start.1 = (bf16[2,512,128]{2,1,0:T(8,128)(2,1)S(1)}, bf16[2,512,128]{2,1,0:T(8,128)(2,1)S(1)}, u32[]{:S(2)}, u32[]{:S(2)}) collective-permute-start(bf16[2,512,128]{2,1,0:T(8,128)(2,1)S(1)} %pad_maximum_fusion.refs_3_), channel_id=1, source_target_pairs={{0,5},{1,4},{2,7},{3,6},{8,13},{9,12},{10,15},{11,14},{16,21},{17,... | collective-permute-start | bytes 786440 | tf_op jit(solution)/shard_map/ppermute | solution.py:305
  9.8 21.8 %copy-start.3 = (bf16[2,512,128]{2,1,0:T(8,128)(2,1)}, bf16[2,512,128]{2,1,0:T(8,128)(2,1)S(1)}, u32[]{:S(2)}) copy-start(bf16[2,512,128]{2,1,0:T(8,128)(2,1)S(1)} %collective-permute-done.3.refs_7_) | copy-start | bytes 786436
  9.8 8.6 %collective-permute-start.7 = (bf16[2,512,128]{2,1,0:T(8,128)(2,1)S(1)}, bf16[2,512,128]{2,1,0:T(8,128)(2,1)S(1)}, u32[]{:S(2)}, u32[]{:S(2)}) collective-permute-start(bf16[2,512,128]{2,1,0:T(8,128)(2,1)S(1)} %collective-permute-done.3.refs_7_), channel_id=1, source_target_pairs={{0,8},{8,16},{16,24},{24,32},{32,40},{40,48},{48,56},{56,64},{64,7... | collective-permute-start | bytes 786440 | tf_op jit(solution)/shard_map/ppermute | solution.py:313
  13.4 6.8 %collective-permute-start = (bf16[2,512,128]{2,1,0:T(8,128)(2,1)S(1)}, bf16[2,512,128]{2,1,0:T(8,128)(2,1)S(1)}, u32[]{:S(2)}, u32[]{:S(2)}) collective-permute-start(bf16[2,512,128]{2,1,0:T(8,128)(2,1)S(1)} %pad_maximum_fusion.refs_3_), channel_id=1, source_target_pairs={{0,2},{2,0},{1,3},{3,1},{4,6},{6,4},{5,7},{7,5},{8,10},{10,8},{9,1... | collective-permute-start | bytes 786440 | tf_op jit(solution)/shard_map/ppermute | solution.py:300
  13.4 18.2 %copy-start.4 = (bf16[2,512,128]{2,1,0:T(8,128)(2,1)}, bf16[2,512,128]{2,1,0:T(8,128)(2,1)S(1)}, u32[]{:S(2)}) copy-start(bf16[2,512,128]{2,1,0:T(8,128)(2,1)S(1)} %collective-permute-done.1.refs_5_) | copy-start | bytes 786436
  13.4 11.3 %collective-permute-start.5 = (bf16[2,512,128]{2,1,0:T(8,128)(2,1)S(1)}, bf16[2,512,128]{2,1,0:T(8,128)(2,1)S(1)}, u32[]{:S(2)}, u32[]{:S(2)}) collective-permute-start(bf16[2,512,128]{2,1,0:T(8,128)(2,1)S(1)} %collective-permute-done.3.refs_7_), channel_id=1, source_target_pairs={{0,5},{1,4},{4,1},{5,0},{2,7},{3,6},{6,3},{7,2},{8,13},{9,12},{12,... | collective-permute-start | bytes 786440 | tf_op jit(solution)/shard_map/ppermute | solution.py:305
  18.3 13.2 %copy-start.5 = (bf16[2,512,128]{2,1,0:T(8,128)(2,1)}, bf16[2,512,128]{2,1,0:T(8,128)(2,1)S(1)}, u32[]{:S(2)}) copy-start(bf16[2,512,128]{2,1,0:T(8,128)(2,1)S(1)} %collective-permute-done.7.refs_11_) | copy-start | bytes 786436
  18.3 11.7 %collective-permute-start.9 = (bf16[2,512,128]{2,1,0:T(8,128)(2,1)S(1)}, bf16[2,512,128]{2,1,0:T(8,128)(2,1)S(1)}, u32[]{:S(2)}, u32[]{:S(2)}) collective-permute-start(bf16[2,512,128]{2,1,0:T(8,128)(2,1)S(1)} %collective-permute-done.7.refs_11_), channel_id=1, source_target_pairs={{4,1},{5,0},{6,3},{7,2},{12,9},{13,8},{14,11},{15,10},{20,17},{21,... | collective-permute-start | bytes 786440 | tf_op jit(solution)/shard_map/ppermute | solution.py:305
  19.6 10.4 %collective-permute-start.4 = (bf16[2,512,128]{2,1,0:T(8,128)(2,1)S(1)}, bf16[2,512,128]{2,1,0:T(8,128)(2,1)S(1)}, u32[]{:S(2)}, u32[]{:S(2)}) collective-permute-start(bf16[2,512,128]{2,1,0:T(8,128)(2,1)S(1)} %collective-permute-done.3.refs_7_), channel_id=1, source_target_pairs={{0,2},{2,0},{1,3},{3,1},{4,6},{6,4},{5,7},{7,5},{8,10},{10,8},{9,1... | collective-permute-start | bytes 786440 | tf_op jit(solution)/shard_map/ppermute | solution.py:300
  19.7 10.3 %collective-permute-start.2 = (bf16[2,512,128]{2,1,0:T(8,128)(2,1)S(1)}, bf16[2,512,128]{2,1,0:T(8,128)(2,1)S(1)}, u32[]{:S(2)}, u32[]{:S(2)}) collective-permute-start(bf16[2,512,128]{2,1,0:T(8,128)(2,1)S(1)} %collective-permute-done.1.refs_5_), channel_id=1, source_target_pairs={{0,2},{2,0},{1,3},{3,1},{4,6},{6,4},{5,7},{7,5},{8,10},{10,8},{9,1... | collective-permute-start | bytes 786440 | tf_op jit(solution)/shard_map/ppermute | solution.py:300
  20.2 11.4 %copy-start.6 = (bf16[2,512,128]{2,1,0:T(8,128)(2,1)}, bf16[2,512,128]{2,1,0:T(8,128)(2,1)S(1)}, u32[]{:S(2)}) copy-start(bf16[2,512,128]{2,1,0:T(8,128)(2,1)S(1)} %collective-permute-done.refs_4_) | copy-start | bytes 786436
  20.2 9.9 %collective-permute-start.8 = (bf16[2,512,128]{2,1,0:T(8,128)(2,1)S(1)}, bf16[2,512,128]{2,1,0:T(8,128)(2,1)S(1)}, u32[]{:S(2)}, u32[]{:S(2)}) collective-permute-start(bf16[2,512,128]{2,1,0:T(8,128)(2,1)S(1)} %collective-permute-done.7.refs_11_), channel_id=1, source_target_pairs={{0,2},{2,0},{1,3},{3,1},{4,6},{6,4},{5,7},{7,5},{8,10},{10,8},{9,1... | collective-permute-start | bytes 786440 | tf_op jit(solution)/shard_map/ppermute | solution.py:300
  24.6 6.9 %copy-start.7 = (bf16[2,512,128]{2,1,0:T(8,128)(2,1)}, bf16[2,512,128]{2,1,0:T(8,128)(2,1)S(1)}, u32[]{:S(2)}) copy-start(bf16[2,512,128]{2,1,0:T(8,128)(2,1)S(1)} %collective-permute-done.5.refs_9_) | copy-start | bytes 786436
  24.6 5.4 %collective-permute-start.6 = (bf16[2,512,128]{2,1,0:T(8,128)(2,1)S(1)}, bf16[2,512,128]{2,1,0:T(8,128)(2,1)S(1)}, u32[]{:S(2)}, u32[]{:S(2)}) collective-permute-start(bf16[2,512,128]{2,1,0:T(8,128)(2,1)S(1)} %collective-permute-done.5.refs_9_), channel_id=1, source_target_pairs={{0,2},{2,0},{1,3},{3,1},{4,6},{6,4},{5,7},{7,5},{8,10},{10,8},{9,1... | collective-permute-start | bytes 786440 | tf_op jit(solution)/shard_map/ppermute | solution.py:300
  30.0 1.6 %copy-start.8 = (bf16[2,512,128]{2,1,0:T(8,128)(2,1)}, bf16[2,512,128]{2,1,0:T(8,128)(2,1)S(1)}, u32[]{:S(2)}) copy-start(bf16[2,512,128]{2,1,0:T(8,128)(2,1)S(1)} %collective-permute-done.9.refs_13_) | copy-start | bytes 786436
  30.0 1.5 %collective-permute-start.10 = (bf16[2,512,128]{2,1,0:T(8,128)(2,1)S(1)}, bf16[2,512,128]{2,1,0:T(8,128)(2,1)S(1)}, u32[]{:S(2)}, u32[]{:S(2)}) collective-permute-start(bf16[2,512,128]{2,1,0:T(8,128)(2,1)S(1)} %collective-permute-done.9.refs_13_), channel_id=1, source_target_pairs={{0,2},{2,0},{1,3},{3,1},{4,6},{6,4},{5,7},{7,5},{8,10},{10,8},{9,1... | collective-permute-start | bytes 786440 | tf_op jit(solution)/shard_map/ppermute | solution.py:300
  30.0 1.6 %copy-start.9 = (bf16[2,512,128]{2,1,0:T(8,128)(2,1)}, bf16[2,512,128]{2,1,0:T(8,128)(2,1)S(1)}, u32[]{:S(2)}) copy-start(bf16[2,512,128]{2,1,0:T(8,128)(2,1)S(1)} %collective-permute-done.4.refs_8_) | copy-start | bytes 786436
  30.0 1.6 %copy-start.10 = (bf16[2,512,128]{2,1,0:T(8,128)(2,1)}, bf16[2,512,128]{2,1,0:T(8,128)(2,1)S(1)}, u32[]{:S(2)}) copy-start(bf16[2,512,128]{2,1,0:T(8,128)(2,1)S(1)} %collective-permute-done.2.refs_6_) | copy-start | bytes 786436
  30.1 1.6 %copy-start.12 = (bf16[2,512,128]{2,1,0:T(8,128)(2,1)}, bf16[2,512,128]{2,1,0:T(8,128)(2,1)S(1)}, u32[]{:S(2)}) copy-start(bf16[2,512,128]{2,1,0:T(8,128)(2,1)S(1)} %collective-permute-done.6.refs_10_) | copy-start | bytes 786436
  30.1 1.5 %copy-start.11 = (bf16[2,512,128]{2,1,0:T(8,128)(2,1)}, bf16[2,512,128]{2,1,0:T(8,128)(2,1)S(1)}, u32[]{:S(2)}) copy-start(bf16[2,512,128]{2,1,0:T(8,128)(2,1)S(1)} %collective-permute-done.8.refs_12_) | copy-start | bytes 786436
  31.6 0.7 copy-start.13
  87.8 3.8 %copy-start = (bf16[3,2,512,128]{3,2,1,0:T(8,128)(2,1)S(1)}, bf16[3,2,512,128]{3,2,1,0:T(8,128)(2,1)}, u32[]{:S(2)}) copy-start(bf16[3,2,512,128]{3,2,1,0:T(8,128)(2,1)} %get-tuple-element.16) | copy-start | bytes 2359300
  87.8 2.6 %collective-permute-start.17 = (bf16[3,2,512,128]{3,2,1,0:T(8,128)(2,1)}, bf16[3,2,512,128]{3,2,1,0:T(8,128)(2,1)S(1)}, u32[]{:S(2)}, u32[]{:S(2)}) collective-permute-start(bf16[3,2,512,128]{3,2,1,0:T(8,128)(2,1)} %get-tuple-element.20), channel_id=1, source_target_pairs={{0,2},{2,0},{1,3},{3,1},{4,6},{6,4},{5,7},{7,5},{8,10},{10,8},{9,1... | collective-permute-start | bytes 2359304 | tf_op jit(solution)/shard_map/ppermute | solution.py:300
  88.0 3.6 %collective-permute-start.11 = (bf16[3,2,512,128]{3,2,1,0:T(8,128)(2,1)}, bf16[3,2,512,128]{3,2,1,0:T(8,128)(2,1)S(1)}, u32[]{:S(2)}, u32[]{:S(2)}) collective-permute-start(bf16[3,2,512,128]{3,2,1,0:T(8,128)(2,1)} %get-tuple-element.17), channel_id=1, source_target_pairs={{0,2},{2,0},{1,3},{3,1},{4,6},{6,4},{5,7},{7,5},{8,10},{10,8},{9,1... | collective-permute-start | bytes 2359304 | tf_op jit(solution)/shard_map/ppermute | solution.py:300
  91.5 7.7 %copy-start.1 = (bf16[3,2,512,128]{3,2,1,0:T(8,128)(2,1)S(1)}, bf16[3,2,512,128]{3,2,1,0:T(8,128)(2,1)}, u32[]{:S(2)}) copy-start(bf16[3,2,512,128]{3,2,1,0:T(8,128)(2,1)} %get-tuple-element.19) | copy-start | bytes 2359300
  91.5 7.7 %collective-permute-start.18 = (bf16[512,128]{1,0:T(8,128)(2,1)S(1)}, bf16[512,128]{1,0:T(8,128)(2,1)S(1)}, u32[]{:S(2)}, u32[]{:S(2)}) collective-permute-start(bf16[512,128]{1,0:T(8,128)(2,1)S(1)} %get-tuple-element.23), channel_id=1, source_target_pairs={{0,5},{1,4},{4,1},{5,0},{2,7},{3,6},{6,3},{7,2},{8,13},{9,12},{12,... | collective-permute-start | bytes 393224 | tf_op jit(solution)/shard_map/ppermute | solution.py:305
  91.8 9.4 %collective-permute-start.12 = (bf16[512,128]{1,0:T(8,128)(2,1)S(1)}, bf16[512,128]{1,0:T(8,128)(2,1)S(1)}, u32[]{:S(2)}, u32[]{:S(2)}) collective-permute-start(bf16[512,128]{1,0:T(8,128)(2,1)S(1)} %get-tuple-element.25), channel_id=1, source_target_pairs={{0,5},{1,4},{4,1},{5,0},{2,7},{3,6},{6,3},{7,2},{8,13},{9,12},{12,... | collective-permute-start | bytes 393224 | tf_op jit(solution)/shard_map/ppermute | solution.py:305
  99.2 7.3 %collective-permute-start.19 = (bf16[512,128]{1,0:T(8,128)(2,1)S(1)}, bf16[512,128]{1,0:T(8,128)(2,1)S(1)}, u32[]{:S(2)}, u32[]{:S(2)}) collective-permute-start(bf16[512,128]{1,0:T(8,128)(2,1)S(1)} %get-tuple-element.21), channel_id=1, source_target_pairs={{0,5},{1,4},{4,1},{5,0},{2,7},{3,6},{6,3},{7,2},{8,13},{9,12},{12,... | collective-permute-start | bytes 393224 | tf_op jit(solution)/shard_map/ppermute | solution.py:305
  99.2 9.4 %collective-permute-start.20 = (bf16[512,128]{1,0:T(8,128)(2,1)S(1)}, bf16[512,128]{1,0:T(8,128)(2,1)S(1)}, u32[]{:S(2)}, u32[]{:S(2)}) collective-permute-start(bf16[512,128]{1,0:T(8,128)(2,1)S(1)} %fusion), channel_id=1, source_target_pairs={{0,120},{8,0},{16,8},{24,16},{32,24},{40,32},{48,40},{56,48},{64,5... | collective-permute-start | bytes 393224 | tf_op jit(solution)/shard_map/ppermute | solution.py:313
  101.2 7.7 %collective-permute-start.13 = (bf16[512,128]{1,0:T(8,128)(2,1)S(1)}, bf16[512,128]{1,0:T(8,128)(2,1)S(1)}, u32[]{:S(2)}, u32[]{:S(2)}) collective-permute-start(bf16[512,128]{1,0:T(8,128)(2,1)S(1)} %get-tuple-element.18), channel_id=1, source_target_pairs={{0,5},{1,4},{4,1},{5,0},{2,7},{3,6},{6,3},{7,2},{8,13},{9,12},{12,... | collective-permute-start | bytes 393224 | tf_op jit(solution)/shard_map/ppermute | solution.py:305
  102.7 8.4 %collective-permute-start.14 = (bf16[512,128]{1,0:T(8,128)(2,1)S(1)}, bf16[512,128]{1,0:T(8,128)(2,1)S(1)}, u32[]{:S(2)}, u32[]{:S(2)}) collective-permute-start(bf16[512,128]{1,0:T(8,128)(2,1)S(1)} %fusion.5), channel_id=1, source_target_pairs={{0,120},{8,0},{16,8},{24,16},{32,24},{40,32},{48,40},{56,48},{64,5... | collective-permute-start | bytes 393224 | tf_op jit(solution)/shard_map/ppermute | solution.py:313
  108.8 8.9 %collective-permute-start.21 = (bf16[512,128]{1,0:T(8,128)(2,1)S(1)}, bf16[512,128]{1,0:T(8,128)(2,1)S(1)}, u32[]{:S(2)}, u32[]{:S(2)}) collective-permute-start(bf16[512,128]{1,0:T(8,128)(2,1)S(1)} %fusion.2), channel_id=1, source_target_pairs={{0,120},{8,0},{16,8},{24,16},{32,24},{40,32},{48,40},{56,48},{64,5... | collective-permute-start | bytes 393224 | tf_op jit(solution)/shard_map/ppermute | solution.py:313
  111.2 8.4 %collective-permute-start.15 = (bf16[512,128]{1,0:T(8,128)(2,1)S(1)}, bf16[512,128]{1,0:T(8,128)(2,1)S(1)}, u32[]{:S(2)}, u32[]{:S(2)}) collective-permute-start(bf16[512,128]{1,0:T(8,128)(2,1)S(1)} %fusion.7), channel_id=1, source_target_pairs={{0,120},{8,0},{16,8},{24,16},{32,24},{40,32},{48,40},{56,48},{64,5... | collective-permute-start | bytes 393224 | tf_op jit(solution)/shard_map/ppermute | solution.py:313
  117.8 5.0 %collective-permute-start.22 = (bf16[512,128]{1,0:T(8,128)(2,1)S(1)}, bf16[512,128]{1,0:T(8,128)(2,1)S(1)}, u32[]{:S(2)}, u32[]{:S(2)}) collective-permute-start(bf16[512,128]{1,0:T(8,128)(2,1)S(1)} %fusion.4), channel_id=1, source_target_pairs={{0,1},{1,0},{2,3},{3,2},{4,5},{5,4},{6,7},{7,6},{8,9},{9,8},{10,11... | collective-permute-start | bytes 393224 | tf_op jit(solution)/shard_map/ppermute | solution.py:309
  119.6 5.0 %collective-permute-start.16 = (bf16[512,128]{1,0:T(8,128)(2,1)S(1)}, bf16[512,128]{1,0:T(8,128)(2,1)S(1)}, u32[]{:S(2)}, u32[]{:S(2)}) collective-permute-start(bf16[512,128]{1,0:T(8,128)(2,1)S(1)} %fusion.9), channel_id=1, source_target_pairs={{0,1},{1,0},{2,3},{3,2},{4,5},{5,4},{6,7},{7,6},{8,9},{9,8},{10,11... | collective-permute-start | bytes 393224 | tf_op jit(solution)/shard_map/ppermute | solution.py:309

commit v7 on v6

--- a/solution.py
+++ b/solution.py
@@ -320,22 +320,34 @@
     return total.astype(BF16)
 
 
+def shift_both(value):
+    same = shift_row(value, -1)
+    pairs = [(2 * r + zl, 2 * ((r - 1) % 16) + 1 - zl) for r in range(16) for zl in range(2)]
+    return same, lax.ppermute(value, ("x", "y", "zl"), pairs)
+
+
 def returned(keep, send):
     first = lax.axis_index("zh") == 0
     zero = jnp.zeros((), BF16)
     given = [swap_core(part) for part in send]
     outer, middle = [], []
-    for a, b in zip(keep, given):
+    for n, (a, b) in enumerate(zip(keep, given)):
         outer.append(added(jnp.where(first, a[2, 1], a[0, 1]), jnp.where(first, b[2, 1], b[0, 1])))
+        a, b, outer[n] = lax.optimization_barrier((a, b, outer[n]))
+        keep, given = [*keep[:n], a, *keep[n + 1:]], [*given[:n], b, *given[n + 1:]]
         middle.append(added(a[1, 1], b[1, 1]))
     outer = [swap_z(value) for value in outer]
     middle = [swap_z(lax.optimization_barrier(both)[0]) for both in zip(middle, outer)]
+    back = [
+        shift_row(added(a[2, 0], b[2, 0], jnp.where(first, zero, far)), -1) for a, b, far in zip(keep, given, outer)
+    ]
+    halves = [added(a[0, 0], b[0, 0], jnp.where(first, far, zero)) for a, b, far in zip(keep, given, outer)]
+    others = [swap_head(half) for half in halves]
     done = []
-    for a, b, far, near in zip(keep, given, outer, middle):
-        back = shift_row(added(a[2, 0], b[2, 0], jnp.where(first, zero, far)), -1)
-        back = shift_row(added(a[1, 0], b[1, 0], near, back), -1)
-        done.append(added(a[0, 0], b[0, 0], jnp.where(first, far, zero), back))
-    return [added(half, swap_head(half)) for half in done]
+    for a, b, near, far, half, other in zip(keep, given, middle, back, halves, others):
+        same, cross = (value.astype(F32) for value in shift_both(added(a[1, 0], b[1, 0], near, far)))
+        done.append(((half.astype(F32) + other.astype(F32)) + (same + cross)).astype(BF16))
+    return done
 
 
 def on_device(queries, key_rows, value_rows, d_out, seq_lengths):

time: 126 us -> 124 us (0.984)
  Pallas kernels: 55.4 us -> 39.1 us
  starting transfers between devices: 22.1 us -> 37.7 us
    pallas_call x1, Pallas kernels: 55.4 us -> 39.1 us  [attention(): pl.pallas_call(attention_kernel, out_shape=(rows, rows) + (grads,) * 4, i...]
    ppermute x8, starting transfers between devices: 1.27 us -> 17.3 us  [swap_core(): return lax.ppermute(value, 'core', [(0, 1), (1, 0)])]
    ppermute x0 -> x2, waiting for transfers between devices: none -> 5.13 us  [shift_both(): return (same, lax.ppermute(value, ('x', 'y', 'zl'), pairs))]
    ppermute x2, waiting for transfers between devices: 3.89 us -> 0.01 us  [swap_head(): return lax.ppermute(value, 'zl', [(0, 1), (1, 0)])]
    convert_element_type x0 -> x2, other arithmetic: none -> 1.45 us  [returned(): (half.astype(F32) + other.astype(F32) + (same + cross)).astype(BF16)]
    ppermute x7, waiting for transfers between devices: 19.3 us -> 18 us  [swap_z(): return lax.ppermute(value, ('zh', 'zl'), pairs)]
    convert_element_type x10 -> x8, other arithmetic: 3.07 us -> 2.61 us  [added(): return total.astype(BF16)]
  transfers between devices with their start and end apart: 23 -> 25, of which waited for: 15 -> 16; matrix products, arithmetic and copies ran while one was open for 2% -> 3% of each run, Pallas kernels for 0% -> 0%
where the time goes in v7:
time: 124 us
  waiting for transfers between devices  40.8 us (33%)
  Pallas kernels  39.1 us (32%)
  starting transfers between devices  37.7 us (30%)
  other arithmetic  5.06 us (4%)
    pallas_call x1, Pallas kernels, attention(): pl.pallas_call(attention_kernel, out_shape=(rows, rows) + (grads,) * 4, i...  39.1 us
    ppermute x7, waiting for transfers between devices, swap_z(): return lax.ppermute(value, ('zh', 'zl'), pairs)  18 us
    ppermute x8, starting transfers between devices, swap_core(): return lax.ppermute(value, 'core', [(0, 1), (1, 0)])  17.3 us
    ppermute x7, starting transfers between devices, swap_z(): return lax.ppermute(value, ('zh', 'zl'), pairs)  16.2 us
    ppermute x6, waiting for transfers between devices, shift_row(): lax.ppermute(value, ('x', 'y'), [(r, (r + by) % 16) for r in range(16)])  14.2 us
    ppermute x2, waiting for transfers between devices, shift_both(): return (same, lax.ppermute(value, ('x', 'y', 'zl'), pairs))  5.13 us
    ppermute x6, starting transfers between devices, shift_row(): lax.ppermute(value, ('x', 'y'), [(r, (r + by) % 16) for r in range(16)])  4.03 us
    ppermute x8, waiting for transfers between devices, swap_core(): return lax.ppermute(value, 'core', [(0, 1), (1, 0)])  3.5 us
  transfers between devices with their start and end apart: 25, of which 16 were waited for; matrix products, arithmetic and copies ran while one was open for 3% of the time, Pallas kernels for 0%

profile of v7, /device:TPU:30, one launch (start us, length us, event | category | flops | bytes accessed | tf_op | source)
XLA Modules:
  0.0 124.4 jit_solution(18011947822883552494)
XLA Ops:
  0.6 1.0 pad_maximum_fusion.refs_3_
  1.6 0.1 collective-permute-start.3
  1.8 6.0 %collective-permute-start.1 = (bf16[2,512,128]{2,1,0:T(8,128)(2,1)S(1)}, bf16[2,512,128]{2,1,0:T(8,128)(2,1)S(1)}, u32[]{:S(2)}, u32[]{:S(2)}) collective-permute-start(bf16[2,512,128]{2,1,0:T(8,128)(2,1)S(1)} %pad_maximum_fusion.refs_3_), channel_id=1, source_target_pairs={{0,5},{1,4},{2,7},{3,6},{8,13},{9,12},{10,15},{11,14},{16,21},{17,... | collective-permute-start | bytes 786440 | tf_op jit(solution)/shard_map/ppermute | solution.py:305
  7.8 2.0 %collective-permute-done.3.refs_7_ = bf16[2,512,128]{2,1,0:T(8,128)(2,1)S(1)} collective-permute-done((bf16[2,512,128]{2,1,0:T(8,128)(2,1)S(1)}, bf16[2,512,128]{2,1,0:T(8,128)(2,1)S(1)}, u32[]{:S(2)}, u32[]{:S(2)}) %collective-permute-start.3) | collective-permute-done | bytes 262176 | tf_op jit(solution)/shard_map/ppermute | solution.py:313
  9.8 3.6 %collective-permute-start.7 = (bf16[2,512,128]{2,1,0:T(8,128)(2,1)S(1)}, bf16[2,512,128]{2,1,0:T(8,128)(2,1)S(1)}, u32[]{:S(2)}, u32[]{:S(2)}) collective-permute-start(bf16[2,512,128]{2,1,0:T(8,128)(2,1)S(1)} %collective-permute-done.3.refs_7_), channel_id=1, source_target_pairs={{0,8},{8,16},{16,24},{24,32},{32,40},{40,48},{48,56},{56,64},{64,7... | collective-permute-start | bytes 786440 | tf_op jit(solution)/shard_map/ppermute | solution.py:313
  13.4 0.0 collective-permute-start
  13.4 0.0 collective-permute-done.1.refs_5_
  13.4 4.1 %collective-permute-start.5 = (bf16[2,512,128]{2,1,0:T(8,128)(2,1)S(1)}, bf16[2,512,128]{2,1,0:T(8,128)(2,1)S(1)}, u32[]{:S(2)}, u32[]{:S(2)}) collective-permute-start(bf16[2,512,128]{2,1,0:T(8,128)(2,1)S(1)} %collective-permute-done.3.refs_7_), channel_id=1, source_target_pairs={{0,5},{1,4},{4,1},{5,0},{2,7},{3,6},{6,3},{7,2},{8,13},{9,12},{12,... | collective-permute-start | bytes 786440 | tf_op jit(solution)/shard_map/ppermute | solution.py:305
  17.5 0.8 collective-permute-done.7.refs_11_
  18.3 1.3 %collective-permute-start.9 = (bf16[2,512,128]{2,1,0:T(8,128)(2,1)S(1)}, bf16[2,512,128]{2,1,0:T(8,128)(2,1)S(1)}, u32[]{:S(2)}, u32[]{:S(2)}) collective-permute-start(bf16[2,512,128]{2,1,0:T(8,128)(2,1)S(1)} %collective-permute-done.7.refs_11_), channel_id=1, source_target_pairs={{4,1},{5,0},{6,3},{7,2},{12,9},{13,8},{14,11},{15,10},{20,17},{21,... | collective-permute-start | bytes 786440 | tf_op jit(solution)/shard_map/ppermute | solution.py:305
  19.6 0.1 collective-permute-start.4
  19.7 0.5 collective-permute-start.2
  20.2 0.1 collective-permute-start.8
  20.3 4.3 %collective-permute-done.5.refs_9_ = bf16[2,512,128]{2,1,0:T(8,128)(2,1)S(1)} collective-permute-done((bf16[2,512,128]{2,1,0:T(8,128)(2,1)S(1)}, bf16[2,512,128]{2,1,0:T(8,128)(2,1)S(1)}, u32[]{:S(2)}, u32[]{:S(2)}) %collective-permute-start.5) | collective-permute-done | bytes 262176 | tf_op jit(solution)/shard_map/ppermute | solution.py:305
  24.7 5.3 %collective-permute-done.9.refs_13_ = bf16[2,512,128]{2,1,0:T(8,128)(2,1)S(1)} collective-permute-done((bf16[2,512,128]{2,1,0:T(8,128)(2,1)S(1)}, bf16[2,512,128]{2,1,0:T(8,128)(2,1)S(1)}, u32[]{:S(2)}, u32[]{:S(2)}) %collective-permute-start.9) | collective-permute-done | bytes 262176 | tf_op jit(solution)/shard_map/ppermute | solution.py:305
  30.1 1.5 %collective-permute-done.10.refs_14_ = bf16[2,512,128]{2,1,0:T(8,128)(2,1)S(1)} collective-permute-done((bf16[2,512,128]{2,1,0:T(8,128)(2,1)S(1)}, bf16[2,512,128]{2,1,0:T(8,128)(2,1)S(1)}, u32[]{:S(2)}, u32[]{:S(2)}) %collective-permute-start.10) | collective-permute-done | bytes 262176 | tf_op jit(solution)/shard_map/ppermute | solution.py:300
  31.6 0.7 copy-done.13
  32.3 39.1 %attention.1 = (bf16[4,512,128]{2,1,0:T(8,128)(2,1)}, bf16[4,512,128]{2,1,0:T(8,128)(2,1)}, bf16[3,2,512,128]{3,2,1,0:T(8,128)(2,1)}, bf16[3,2,512,128]{3,2,1,0:...) custom-call(s32[16]{0:T(128)} %refs_0_.1, bf16[4,512,128]{2,1,0:T(8,128)(2,1)} %refs_1_.1, ...), custom_call_target="tpu_custom_call" | custom-call | flops 8589934592 | bytes 16777216 | tf_op jit(solution)/shard_map/attention/pallas_call | solution.py:266
  71.5 16.5 %collective-permute-start.18 = (bf16[3,2,512,128]{3,2,1,0:T(8,128)(2,1)}, bf16[3,2,512,128]{3,2,1,0:T(8,128)(2,1)S(1)}, u32[]{:S(2)}, u32[]{:S(2)}) collective-permute-start(bf16[3,2,512,128]{3,2,1,0:T(8,128)(2,1)} %get-tuple-element.29), channel_id=1, source_target_pairs={{0,2},{2,0},{1,3},{3,1},{4,6},{6,4},{5,7},{7,5},{8,10},{10,8},{9,1... | collective-permute-start | bytes 2359304 | tf_op jit(solution)/shard_map/ppermute | solution.py:300
  88.0 0.1 collective-permute-start.11
  88.1 2.0 %collective-permute-done.18 = bf16[3,2,512,128]{3,2,1,0:T(8,128)(2,1)S(1)} collective-permute-done((bf16[3,2,512,128]{3,2,1,0:T(8,128)(2,1)}, bf16[3,2,512,128]{3,2,1,0:T(8,128)(2,1)S(1)}, u32[]{:S(2)}, u32[]{:S(2)}) %collective-permute-start.18) | collective-permute-done | bytes 786464 | tf_op jit(solution)/shard_map/ppermute | solution.py:300
  90.1 1.1 fusion.10
  91.3 0.1 collective-permute-start.19
  91.4 1.0 fusion.8
  92.4 3.3 %collective-permute-start.12 = (bf16[512,128]{1,0:T(8,128)(2,1)S(1)}, bf16[512,128]{1,0:T(8,128)(2,1)S(1)}, u32[]{:S(2)}, u32[]{:S(2)}) collective-permute-start(bf16[512,128]{1,0:T(8,128)(2,1)S(1)} %fusion.8), channel_id=1, source_target_pairs={{0,5},{1,4},{4,1},{5,0},{2,7},{3,6},{6,3},{7,2},{8,13},{9,12},{12,... | collective-permute-start | bytes 393224 | tf_op jit(solution)/shard_map/ppermute | solution.py:305
  95.8 3.1 %collective-permute-done.19 = bf16[512,128]{1,0:T(8,128)(2,1)S(1)} collective-permute-done((bf16[512,128]{1,0:T(8,128)(2,1)S(1)}, bf16[512,128]{1,0:T(8,128)(2,1)S(1)}, u32[]{:S(2)}, u32[]{:S(2)}) %collective-permute-start.19) | collective-permute-done | bytes 131104 | tf_op jit(solution)/shard_map/ppermute | solution.py:305
  98.9 0.1 fusion.3
  99.0 0.1 collective-permute-start.22
  99.1 0.1 collective-permute-start.20
  99.2 2.0 %collective-permute-done.12 = bf16[512,128]{1,0:T(8,128)(2,1)S(1)} collective-permute-done((bf16[512,128]{1,0:T(8,128)(2,1)S(1)}, bf16[512,128]{1,0:T(8,128)(2,1)S(1)}, u32[]{:S(2)}, u32[]{:S(2)}) %collective-permute-start.12) | collective-permute-done | bytes 131104 | tf_op jit(solution)/shard_map/ppermute | solution.py:305
  101.1 1.4 %collective-permute-start.14 = (bf16[512,128]{1,0:T(8,128)(2,1)S(1)}, bf16[512,128]{1,0:T(8,128)(2,1)S(1)}, u32[]{:S(2)}, u32[]{:S(2)}) collective-permute-start(bf16[512,128]{1,0:T(8,128)(2,1)S(1)} %fusion.9), channel_id=1, source_target_pairs={{0,5},{1,4},{4,1},{5,0},{2,7},{3,6},{6,3},{7,2},{8,13},{9,12},{12,... | collective-permute-start | bytes 393224 | tf_op jit(solution)/shard_map/ppermute | solution.py:305
  102.5 0.1 fusion.7
  102.7 0.1 collective-permute-start.15
  102.7 2.9 %collective-permute-done.21 = bf16[512,128]{1,0:T(8,128)(2,1)S(1)} collective-permute-done((bf16[512,128]{1,0:T(8,128)(2,1)S(1)}, bf16[512,128]{1,0:T(8,128)(2,1)S(1)}, u32[]{:S(2)}, u32[]{:S(2)}) %collective-permute-start.21) | collective-permute-done | bytes 131104 | tf_op jit(solution)/shard_map/ppermute | solution.py:305
  105.6 1.7 %collective-permute-done.22 = bf16[512,128]{1,0:T(8,128)(2,1)S(1)} collective-permute-done((bf16[512,128]{1,0:T(8,128)(2,1)S(1)}, bf16[512,128]{1,0:T(8,128)(2,1)S(1)}, u32[]{:S(2)}, u32[]{:S(2)}) %collective-permute-start.22) | collective-permute-done | bytes 131104 | tf_op jit(solution)/shard_map/ppermute | solution.py:313
  107.4 0.1 fusion.2
  107.4 0.1 collective-permute-start.23
  107.5 0.3 collective-permute-done.14
  107.9 3.1 %collective-permute-done.15 = bf16[512,128]{1,0:T(8,128)(2,1)S(1)} collective-permute-done((bf16[512,128]{1,0:T(8,128)(2,1)S(1)}, bf16[512,128]{1,0:T(8,128)(2,1)S(1)}, u32[]{:S(2)}, u32[]{:S(2)}) %collective-permute-start.15) | collective-permute-done | bytes 131104 | tf_op jit(solution)/shard_map/ppermute | solution.py:313
  111.0 0.1 fusion.6
  111.1 0.1 collective-permute-start.16
  111.2 0.1 collective-permute-start.17
  111.3 5.7 %collective-permute-done.23 = bf16[512,128]{1,0:T(8,128)(2,1)S(1)} collective-permute-done((bf16[512,128]{1,0:T(8,128)(2,1)S(1)}, bf16[512,128]{1,0:T(8,128)(2,1)S(1)}, u32[]{:S(2)}, u32[]{:S(2)}) %collective-permute-start.23) | collective-permute-done | bytes 131104 | tf_op jit(solution)/shard_map/ppermute | solution.py:313
  116.9 2.8 %collective-permute-done.24 = bf16[512,128]{1,0:T(8,128)(2,1)S(1)} collective-permute-done((bf16[512,128]{1,0:T(8,128)(2,1)S(1)}, bf16[512,128]{1,0:T(8,128)(2,1)S(1)}, u32[]{:S(2)}, u32[]{:S(2)}) %collective-permute-start.24) | collective-permute-done | bytes 131104 | tf_op jit(solution)/shard_map/ppermute | solution.py:326
  119.8 0.7 add_convert_fusion
  120.5 0.9 collective-permute-done.16
  121.4 2.3 %collective-permute-done.17 = bf16[512,128]{1,0:T(8,128)(2,1)S(1)} collective-permute-done((bf16[512,128]{1,0:T(8,128)(2,1)S(1)}, bf16[512,128]{1,0:T(8,128)(2,1)S(1)}, u32[]{:S(2)}, u32[]{:S(2)}) %collective-permute-start.17) | collective-permute-done | bytes 131104 | tf_op jit(solution)/shard_map/ppermute | solution.py:326
  123.7 0.7 add_convert_fusion.3
  (42 shorter events, 0.2 us)
Async XLA Ops:
  1.6 29.9 %copy-start.2 = (bf16[2,512,128]{2,1,0:T(8,128)(2,1)}, bf16[2,512,128]{2,1,0:T(8,128)(2,1)S(1)}, u32[]{:S(2)}) copy-start(bf16[2,512,128]{2,1,0:T(8,128)(2,1)S(1)} %pad_maximum_fusion.refs_3_) | copy-start | bytes 786436
  1.6 8.1 %collective-permute-start.3 = (bf16[2,512,128]{2,1,0:T(8,128)(2,1)S(1)}, bf16[2,512,128]{2,1,0:T(8,128)(2,1)S(1)}, u32[]{:S(2)}, u32[]{:S(2)}) collective-permute-start(bf16[2,512,128]{2,1,0:T(8,128)(2,1)S(1)} %pad_maximum_fusion.refs_3_), channel_id=1, source_target_pairs={{0,8},{8,16},{16,24},{24,32},{32,40},{40,48},{48,56},{56,64},{64,7... | collective-permute-start | bytes 786440 | tf_op jit(solution)/shard_map/ppermute | solution.py:313
  1.8 11.6 %collective-permute-start.1 = (bf16[2,512,128]{2,1,0:T(8,128)(2,1)S(1)}, bf16[2,512,128]{2,1,0:T(8,128)(2,1)S(1)}, u32[]{:S(2)}, u32[]{:S(2)}) collective-permute-start(bf16[2,512,128]{2,1,0:T(8,128)(2,1)S(1)} %pad_maximum_fusion.refs_3_), channel_id=1, source_target_pairs={{0,5},{1,4},{2,7},{3,6},{8,13},{9,12},{10,15},{11,14},{16,21},{17,... | collective-permute-start | bytes 786440 | tf_op jit(solution)/shard_map/ppermute | solution.py:305
  9.8 21.8 %copy-start.3 = (bf16[2,512,128]{2,1,0:T(8,128)(2,1)}, bf16[2,512,128]{2,1,0:T(8,128)(2,1)S(1)}, u32[]{:S(2)}) copy-start(bf16[2,512,128]{2,1,0:T(8,128)(2,1)S(1)} %collective-permute-done.3.refs_7_) | copy-start | bytes 786436
  9.8 8.6 %collective-permute-start.7 = (bf16[2,512,128]{2,1,0:T(8,128)(2,1)S(1)}, bf16[2,512,128]{2,1,0:T(8,128)(2,1)S(1)}, u32[]{:S(2)}, u32[]{:S(2)}) collective-permute-start(bf16[2,512,128]{2,1,0:T(8,128)(2,1)S(1)} %collective-permute-done.3.refs_7_), channel_id=1, source_target_pairs={{0,8},{8,16},{16,24},{24,32},{32,40},{40,48},{48,56},{56,64},{64,7... | collective-permute-start | bytes 786440 | tf_op jit(solution)/shard_map/ppermute | solution.py:313
  13.4 6.8 %collective-permute-start = (bf16[2,512,128]{2,1,0:T(8,128)(2,1)S(1)}, bf16[2,512,128]{2,1,0:T(8,128)(2,1)S(1)}, u32[]{:S(2)}, u32[]{:S(2)}) collective-permute-start(bf16[2,512,128]{2,1,0:T(8,128)(2,1)S(1)} %pad_maximum_fusion.refs_3_), channel_id=1, source_target_pairs={{0,2},{2,0},{1,3},{3,1},{4,6},{6,4},{5,7},{7,5},{8,10},{10,8},{9,1... | collective-permute-start | bytes 786440 | tf_op jit(solution)/shard_map/ppermute | solution.py:300
  13.4 18.2 %copy-start.4 = (bf16[2,512,128]{2,1,0:T(8,128)(2,1)}, bf16[2,512,128]{2,1,0:T(8,128)(2,1)S(1)}, u32[]{:S(2)}) copy-start(bf16[2,512,128]{2,1,0:T(8,128)(2,1)S(1)} %collective-permute-done.1.refs_5_) | copy-start | bytes 786436
  13.4 11.3 %collective-permute-start.5 = (bf16[2,512,128]{2,1,0:T(8,128)(2,1)S(1)}, bf16[2,512,128]{2,1,0:T(8,128)(2,1)S(1)}, u32[]{:S(2)}, u32[]{:S(2)}) collective-permute-start(bf16[2,512,128]{2,1,0:T(8,128)(2,1)S(1)} %collective-permute-done.3.refs_7_), channel_id=1, source_target_pairs={{0,5},{1,4},{4,1},{5,0},{2,7},{3,6},{6,3},{7,2},{8,13},{9,12},{12,... | collective-permute-start | bytes 786440 | tf_op jit(solution)/shard_map/ppermute | solution.py:305
  18.3 13.2 %copy-start.5 = (bf16[2,512,128]{2,1,0:T(8,128)(2,1)}, bf16[2,512,128]{2,1,0:T(8,128)(2,1)S(1)}, u32[]{:S(2)}) copy-start(bf16[2,512,128]{2,1,0:T(8,128)(2,1)S(1)} %collective-permute-done.7.refs_11_) | copy-start | bytes 786436
  18.3 11.7 %collective-permute-start.9 = (bf16[2,512,128]{2,1,0:T(8,128)(2,1)S(1)}, bf16[2,512,128]{2,1,0:T(8,128)(2,1)S(1)}, u32[]{:S(2)}, u32[]{:S(2)}) collective-permute-start(bf16[2,512,128]{2,1,0:T(8,128)(2,1)S(1)} %collective-permute-done.7.refs_11_), channel_id=1, source_target_pairs={{4,1},{5,0},{6,3},{7,2},{12,9},{13,8},{14,11},{15,10},{20,17},{21,... | collective-permute-start | bytes 786440 | tf_op jit(solution)/shard_map/ppermute | solution.py:305
  19.6 10.4 %collective-permute-start.4 = (bf16[2,512,128]{2,1,0:T(8,128)(2,1)S(1)}, bf16[2,512,128]{2,1,0:T(8,128)(2,1)S(1)}, u32[]{:S(2)}, u32[]{:S(2)}) collective-permute-start(bf16[2,512,128]{2,1,0:T(8,128)(2,1)S(1)} %collective-permute-done.3.refs_7_), channel_id=1, source_target_pairs={{0,2},{2,0},{1,3},{3,1},{4,6},{6,4},{5,7},{7,5},{8,10},{10,8},{9,1... | collective-permute-start | bytes 786440 | tf_op jit(solution)/shard_map/ppermute | solution.py:300
  19.7 10.3 %collective-permute-start.2 = (bf16[2,512,128]{2,1,0:T(8,128)(2,1)S(1)}, bf16[2,512,128]{2,1,0:T(8,128)(2,1)S(1)}, u32[]{:S(2)}, u32[]{:S(2)}) collective-permute-start(bf16[2,512,128]{2,1,0:T(8,128)(2,1)S(1)} %collective-permute-done.1.refs_5_), channel_id=1, source_target_pairs={{0,2},{2,0},{1,3},{3,1},{4,6},{6,4},{5,7},{7,5},{8,10},{10,8},{9,1... | collective-permute-start | bytes 786440 | tf_op jit(solution)/shard_map/ppermute | solution.py:300
  20.2 11.4 %copy-start.6 = (bf16[2,512,128]{2,1,0:T(8,128)(2,1)}, bf16[2,512,128]{2,1,0:T(8,128)(2,1)S(1)}, u32[]{:S(2)}) copy-start(bf16[2,512,128]{2,1,0:T(8,128)(2,1)S(1)} %collective-permute-done.refs_4_) | copy-start | bytes 786436
  20.2 9.9 %collective-permute-start.8 = (bf16[2,512,128]{2,1,0:T(8,128)(2,1)S(1)}, bf16[2,512,128]{2,1,0:T(8,128)(2,1)S(1)}, u32[]{:S(2)}, u32[]{:S(2)}) collective-permute-start(bf16[2,512,128]{2,1,0:T(8,128)(2,1)S(1)} %collective-permute-done.7.refs_11_), channel_id=1, source_target_pairs={{0,2},{2,0},{1,3},{3,1},{4,6},{6,4},{5,7},{7,5},{8,10},{10,8},{9,1... | collective-permute-start | bytes 786440 | tf_op jit(solution)/shard_map/ppermute | solution.py:300
  24.6 6.9 %copy-start.7 = (bf16[2,512,128]{2,1,0:T(8,128)(2,1)}, bf16[2,512,128]{2,1,0:T(8,128)(2,1)S(1)}, u32[]{:S(2)}) copy-start(bf16[2,512,128]{2,1,0:T(8,128)(2,1)S(1)} %collective-permute-done.5.refs_9_) | copy-start | bytes 786436
  24.6 5.4 %collective-permute-start.6 = (bf16[2,512,128]{2,1,0:T(8,128)(2,1)S(1)}, bf16[2,512,128]{2,1,0:T(8,128)(2,1)S(1)}, u32[]{:S(2)}, u32[]{:S(2)}) collective-permute-start(bf16[2,512,128]{2,1,0:T(8,128)(2,1)S(1)} %collective-permute-done.5.refs_9_), channel_id=1, source_target_pairs={{0,2},{2,0},{1,3},{3,1},{4,6},{6,4},{5,7},{7,5},{8,10},{10,8},{9,1... | collective-permute-start | bytes 786440 | tf_op jit(solution)/shard_map/ppermute | solution.py:300
  30.0 1.6 %copy-start.8 = (bf16[2,512,128]{2,1,0:T(8,128)(2,1)}, bf16[2,512,128]{2,1,0:T(8,128)(2,1)S(1)}, u32[]{:S(2)}) copy-start(bf16[2,512,128]{2,1,0:T(8,128)(2,1)S(1)} %collective-permute-done.9.refs_13_) | copy-start | bytes 786436
  30.0 1.5 %collective-permute-start.10 = (bf16[2,512,128]{2,1,0:T(8,128)(2,1)S(1)}, bf16[2,512,128]{2,1,0:T(8,128)(2,1)S(1)}, u32[]{:S(2)}, u32[]{:S(2)}) collective-permute-start(bf16[2,512,128]{2,1,0:T(8,128)(2,1)S(1)} %collective-permute-done.9.refs_13_), channel_id=1, source_target_pairs={{0,2},{2,0},{1,3},{3,1},{4,6},{6,4},{5,7},{7,5},{8,10},{10,8},{9,1... | collective-permute-start | bytes 786440 | tf_op jit(solution)/shard_map/ppermute | solution.py:300
  30.0 1.6 %copy-start.9 = (bf16[2,512,128]{2,1,0:T(8,128)(2,1)}, bf16[2,512,128]{2,1,0:T(8,128)(2,1)S(1)}, u32[]{:S(2)}) copy-start(bf16[2,512,128]{2,1,0:T(8,128)(2,1)S(1)} %collective-permute-done.4.refs_8_) | copy-start | bytes 786436
  30.0 1.6 %copy-start.10 = (bf16[2,512,128]{2,1,0:T(8,128)(2,1)}, bf16[2,512,128]{2,1,0:T(8,128)(2,1)S(1)}, u32[]{:S(2)}) copy-start(bf16[2,512,128]{2,1,0:T(8,128)(2,1)S(1)} %collective-permute-done.2.refs_6_) | copy-start | bytes 786436
  30.1 1.6 %copy-start.12 = (bf16[2,512,128]{2,1,0:T(8,128)(2,1)}, bf16[2,512,128]{2,1,0:T(8,128)(2,1)S(1)}, u32[]{:S(2)}) copy-start(bf16[2,512,128]{2,1,0:T(8,128)(2,1)S(1)} %collective-permute-done.6.refs_10_) | copy-start | bytes 786436
  30.1 1.5 %copy-start.11 = (bf16[2,512,128]{2,1,0:T(8,128)(2,1)}, bf16[2,512,128]{2,1,0:T(8,128)(2,1)S(1)}, u32[]{:S(2)}) copy-start(bf16[2,512,128]{2,1,0:T(8,128)(2,1)S(1)} %collective-permute-done.8.refs_12_) | copy-start | bytes 786436
  31.6 0.7 copy-start.13
  71.5 24.2 %copy-start.1 = (bf16[3,2,512,128]{3,2,1,0:T(8,128)(2,1)S(1)}, bf16[3,2,512,128]{3,2,1,0:T(8,128)(2,1)}, u32[]{:S(2)}) copy-start(bf16[3,2,512,128]{3,2,1,0:T(8,128)(2,1)} %get-tuple-element.30) | copy-start | bytes 2359300
  71.5 18.6 %collective-permute-start.18 = (bf16[3,2,512,128]{3,2,1,0:T(8,128)(2,1)}, bf16[3,2,512,128]{3,2,1,0:T(8,128)(2,1)S(1)}, u32[]{:S(2)}, u32[]{:S(2)}) collective-permute-start(bf16[3,2,512,128]{3,2,1,0:T(8,128)(2,1)} %get-tuple-element.29), channel_id=1, source_target_pairs={{0,2},{2,0},{1,3},{3,1},{4,6},{6,4},{5,7},{7,5},{8,10},{10,8},{9,1... | collective-permute-start | bytes 2359304 | tf_op jit(solution)/shard_map/ppermute | solution.py:300
  88.0 3.3 %collective-permute-start.11 = (bf16[3,2,512,128]{3,2,1,0:T(8,128)(2,1)}, bf16[3,2,512,128]{3,2,1,0:T(8,128)(2,1)S(1)}, u32[]{:S(2)}, u32[]{:S(2)}) collective-permute-start(bf16[3,2,512,128]{3,2,1,0:T(8,128)(2,1)} %get-tuple-element.23), channel_id=1, source_target_pairs={{0,2},{2,0},{1,3},{3,1},{4,6},{6,4},{5,7},{7,5},{8,10},{10,8},{9,1... | collective-permute-start | bytes 2359304 | tf_op jit(solution)/shard_map/ppermute | solution.py:300
  90.1 5.6 %copy-start = (bf16[3,2,512,128]{3,2,1,0:T(8,128)(2,1)S(1)}, bf16[3,2,512,128]{3,2,1,0:T(8,128)(2,1)}, u32[]{:S(2)}) copy-start(bf16[3,2,512,128]{3,2,1,0:T(8,128)(2,1)} %get-tuple-element.24) | copy-start | bytes 2359300
  91.3 7.6 %collective-permute-start.19 = (bf16[512,128]{1,0:T(8,128)(2,1)S(1)}, bf16[512,128]{1,0:T(8,128)(2,1)S(1)}, u32[]{:S(2)}, u32[]{:S(2)}) collective-permute-start(bf16[512,128]{1,0:T(8,128)(2,1)S(1)} %fusion.10), channel_id=1, source_target_pairs={{0,5},{1,4},{4,1},{5,0},{2,7},{3,6},{6,3},{7,2},{8,13},{9,12},{12,... | collective-permute-start | bytes 393224 | tf_op jit(solution)/shard_map/ppermute | solution.py:305
  92.4 8.7 %collective-permute-start.12 = (bf16[512,128]{1,0:T(8,128)(2,1)S(1)}, bf16[512,128]{1,0:T(8,128)(2,1)S(1)}, u32[]{:S(2)}, u32[]{:S(2)}) collective-permute-start(bf16[512,128]{1,0:T(8,128)(2,1)S(1)} %fusion.8), channel_id=1, source_target_pairs={{0,5},{1,4},{4,1},{5,0},{2,7},{3,6},{6,3},{7,2},{8,13},{9,12},{12,... | collective-permute-start | bytes 393224 | tf_op jit(solution)/shard_map/ppermute | solution.py:305
  98.9 6.8 %collective-permute-start.21 = (bf16[512,128]{1,0:T(8,128)(2,1)S(1)}, bf16[512,128]{1,0:T(8,128)(2,1)S(1)}, u32[]{:S(2)}, u32[]{:S(2)}) collective-permute-start(bf16[512,128]{1,0:T(8,128)(2,1)S(1)} %fusion.11), channel_id=1, source_target_pairs={{0,5},{1,4},{4,1},{5,0},{2,7},{3,6},{6,3},{7,2},{8,13},{9,12},{12,... | collective-permute-start | bytes 393224 | tf_op jit(solution)/shard_map/ppermute | solution.py:305
  99.0 8.4 %collective-permute-start.22 = (bf16[512,128]{1,0:T(8,128)(2,1)S(1)}, bf16[512,128]{1,0:T(8,128)(2,1)S(1)}, u32[]{:S(2)}, u32[]{:S(2)}) collective-permute-start(bf16[512,128]{1,0:T(8,128)(2,1)S(1)} %get-tuple-element.35), channel_id=1, source_target_pairs={{0,120},{8,0},{16,8},{24,16},{32,24},{40,32},{48,40},{56,48},{64,5... | collective-permute-start | bytes 393224 | tf_op jit(solution)/shard_map/ppermute | solution.py:313
  99.1 12.1 %collective-permute-start.20 = (bf16[512,128]{1,0:T(8,128)(2,1)S(1)}, bf16[512,128]{1,0:T(8,128)(2,1)S(1)}, u32[]{:S(2)}, u32[]{:S(2)}) collective-permute-start(bf16[512,128]{1,0:T(8,128)(2,1)S(1)} %get-tuple-element.34), channel_id=1, source_target_pairs={{0,1},{1,0},{2,3},{3,2},{4,5},{5,4},{6,7},{7,6},{8,9},{9,8},{10,11... | collective-permute-start | bytes 393224 | tf_op jit(solution)/shard_map/ppermute | solution.py:309
  101.1 6.7 %collective-permute-start.14 = (bf16[512,128]{1,0:T(8,128)(2,1)S(1)}, bf16[512,128]{1,0:T(8,128)(2,1)S(1)}, u32[]{:S(2)}, u32[]{:S(2)}) collective-permute-start(bf16[512,128]{1,0:T(8,128)(2,1)S(1)} %fusion.9), channel_id=1, source_target_pairs={{0,5},{1,4},{4,1},{5,0},{2,7},{3,6},{6,3},{7,2},{8,13},{9,12},{12,... | collective-permute-start | bytes 393224 | tf_op jit(solution)/shard_map/ppermute | solution.py:305
  102.7 8.4 %collective-permute-start.15 = (bf16[512,128]{1,0:T(8,128)(2,1)S(1)}, bf16[512,128]{1,0:T(8,128)(2,1)S(1)}, u32[]{:S(2)}, u32[]{:S(2)}) collective-permute-start(bf16[512,128]{1,0:T(8,128)(2,1)S(1)} %get-tuple-element.37), channel_id=1, source_target_pairs={{0,120},{8,0},{16,8},{24,16},{32,24},{40,32},{48,40},{56,48},{64,5... | collective-permute-start | bytes 393224 | tf_op jit(solution)/shard_map/ppermute | solution.py:313
  105.6 14.8 %collective-permute-start.13 = (bf16[512,128]{1,0:T(8,128)(2,1)S(1)}, bf16[512,128]{1,0:T(8,128)(2,1)S(1)}, u32[]{:S(2)}, u32[]{:S(2)}) collective-permute-start(bf16[512,128]{1,0:T(8,128)(2,1)S(1)} %get-tuple-element.36), channel_id=1, source_target_pairs={{0,1},{1,0},{2,3},{3,2},{4,5},{5,4},{6,7},{7,6},{8,9},{9,8},{10,11... | collective-permute-start | bytes 393224 | tf_op jit(solution)/shard_map/ppermute | solution.py:309
  107.4 9.5 %collective-permute-start.23 = (bf16[512,128]{1,0:T(8,128)(2,1)S(1)}, bf16[512,128]{1,0:T(8,128)(2,1)S(1)}, u32[]{:S(2)}, u32[]{:S(2)}) collective-permute-start(bf16[512,128]{1,0:T(8,128)(2,1)S(1)} %fusion.2), channel_id=1, source_target_pairs={{0,120},{8,0},{16,8},{24,16},{32,24},{40,32},{48,40},{56,48},{64,5... | collective-permute-start | bytes 393224 | tf_op jit(solution)/shard_map/ppermute | solution.py:313
  107.9 11.9 %collective-permute-start.24 = (bf16[512,128]{1,0:T(8,128)(2,1)S(1)}, bf16[512,128]{1,0:T(8,128)(2,1)S(1)}, u32[]{:S(2)}, u32[]{:S(2)}) collective-permute-start(bf16[512,128]{1,0:T(8,128)(2,1)S(1)} %fusion.2), channel_id=1, source_target_pairs={{0,121},{1,120},{8,1},{9,0},{16,9},{17,8},{24,17},{25,16},{32,25},... | collective-permute-start | bytes 393224 | tf_op jit(solution)/shard_map/ppermute | solution.py:326
  111.1 10.3 %collective-permute-start.16 = (bf16[512,128]{1,0:T(8,128)(2,1)S(1)}, bf16[512,128]{1,0:T(8,128)(2,1)S(1)}, u32[]{:S(2)}, u32[]{:S(2)}) collective-permute-start(bf16[512,128]{1,0:T(8,128)(2,1)S(1)} %fusion.6), channel_id=1, source_target_pairs={{0,120},{8,0},{16,8},{24,16},{32,24},{40,32},{48,40},{56,48},{64,5... | collective-permute-start | bytes 393224 | tf_op jit(solution)/shard_map/ppermute | solution.py:313
  111.2 12.5 %collective-permute-start.17 = (bf16[512,128]{1,0:T(8,128)(2,1)S(1)}, bf16[512,128]{1,0:T(8,128)(2,1)S(1)}, u32[]{:S(2)}, u32[]{:S(2)}) collective-permute-start(bf16[512,128]{1,0:T(8,128)(2,1)S(1)} %fusion.6), channel_id=1, source_target_pairs={{0,121},{1,120},{8,1},{9,0},{16,9},{17,8},{24,17},{25,16},{32,25},... | collective-permute-start | bytes 393224 | tf_op jit(solution)/shard_map/ppermute | solution.py:326

commit v8 on v6

--- a/solution.py
+++ b/solution.py
@@ -74,8 +74,8 @@
     len_ref, q_hbm, do_hbm = refs[:3]
     kv_refs = refs[3:15]
     o_hbm, dq_hbm = refs[15:17]
-    out_refs = refs[17:21]
-    kvs, dkvs, qt, dot_t, do_s, probs, row_max, total, acc, dq_acc, stage, delta, norms, q_ref, do_ref, o_ref, dq_ref, row_sem, in_sem, out_sem = refs[21:]
+    out_refs = refs[17:19]
+    kvs, dkvs, qt, dot_t, do_s, probs, row_max, total, acc, dq_acc, stage, delta, norms, q_ref, do_ref, o_ref, dq_ref, row_sem, in_sem, out_sem = refs[19:]
     loads = [[pltpu.make_async_copy(a.at[h], b.at[h], row_sem.at[n, h]) for n, (a, b) in enumerate(((q_hbm, q_ref), (do_hbm, do_ref)))] for h in range(HEADS)]
     for pair in loads:
         for copy in pair:
@@ -89,9 +89,9 @@
     def arrived(t):
         pltpu.make_async_copy(kv_refs[0], kvs.at[t], in_sem.at[t]).wait()
 
-    def out_copy(n, part, t):
+    def out_copy(n, t):
         j, dz, dc = order[n]
-        return pltpu.make_async_copy(dkvs.at[t, part], out_refs[part * 2 + dc].at[j, dz], out_sem.at[n, part])
+        return pltpu.make_async_copy(dkvs.at[t], out_refs[dc].at[j, dz], out_sem.at[n])
 
     begin = at.lo
     end = begin + (at.hi - begin + GROUP) // GROUP * GROUP
@@ -103,8 +103,7 @@
 
         @pl.when((slot < begin) | (slot >= end))
         def _():
-            for part in range(2):
-                out_copy(n, part, SLOTS + GROUP - 1).start()
+            out_copy(n, SLOTS + GROUP - 1).start()
 
     for h in range(HEADS):
         cols = slice(h * BLK, (h + 1) * BLK)
@@ -236,8 +235,7 @@
 
             @pl.when((slot >= first) & (slot < first + GROUP))
             def _():
-                for part in range(2):
-                    out_copy(n, part, slot).start()
+                out_copy(n, slot).start()
 
         return carry
 
@@ -253,8 +251,7 @@
     lax.fori_loop(0, begin, rest, 0)
     lax.fori_loop(jnp.minimum(end, SLOTS), SLOTS, rest, 0)
     for n in range(len(order)):
-        for part in range(2):
-            out_copy(n, part, 0).wait()
+        out_copy(n, 0).wait()
     for h in range(HEADS):
         pltpu.make_async_copy(o_ref.at[h], o_hbm.at[h], row_sem.at[2, h]).wait()
         pltpu.make_async_copy(dq_ref.at[h], dq_hbm.at[h], row_sem.at[3, h]).wait()
@@ -262,12 +259,12 @@
 
 def attention(seq_lengths, queries, d_out, blocks):
     rows = shape((HEADS, BLK, HD), BF16)
-    grads = shape((ROWS, 2, BLK, HD), BF16)
+    grads = shape((ROWS, 2, 2, BLK, HD), BF16)
     return pl.pallas_call(
         attention_kernel,
-        out_shape=(rows, rows) + (grads,) * 4,
+        out_shape=(rows, rows) + (grads,) * 2,
         in_specs=[SMEM] + [ANY] * (2 + SLOTS),
-        out_specs=[ANY] * 6,
+        out_specs=[ANY] * 4,
         scratch_shapes=[
             pltpu.VMEM((SLOTS + GROUP - 1, 2, BLK, HD), BF16),
             pltpu.VMEM((SLOTS + GROUP, 2, BLK, HD), BF16),
@@ -288,7 +285,7 @@
             pltpu.VMEM((HEADS, BLK, HD), BF16),
             DMA((4, HEADS)),
             DMA((SLOTS,)),
-            DMA((SLOTS, 2)),
+            DMA((SLOTS,)),
         ],
         compiler_params=pltpu.CompilerParams(vmem_limit_bytes=56 << 20),
         cost_estimate=pl.CostEstimate(flops=8 << 30, bytes_accessed=16 << 20, transcendentals=9 << 20),
@@ -323,19 +320,16 @@
 def returned(keep, send):
     first = lax.axis_index("zh") == 0
     zero = jnp.zeros((), BF16)
-    given = [swap_core(part) for part in send]
-    outer, middle = [], []
-    for a, b in zip(keep, given):
-        outer.append(added(jnp.where(first, a[2, 1], a[0, 1]), jnp.where(first, b[2, 1], b[0, 1])))
-        middle.append(added(a[1, 1], b[1, 1]))
-    outer = [swap_z(value) for value in outer]
-    middle = [swap_z(lax.optimization_barrier(both)[0]) for both in zip(middle, outer)]
-    done = []
-    for a, b, far, near in zip(keep, given, outer, middle):
-        back = shift_row(added(a[2, 0], b[2, 0], jnp.where(first, zero, far)), -1)
-        back = shift_row(added(a[1, 0], b[1, 0], near, back), -1)
-        done.append(added(a[0, 0], b[0, 0], jnp.where(first, far, zero), back))
-    return [added(half, swap_head(half)) for half in done]
+    given = swap_core(send)
+    outer = swap_z(added(jnp.where(first, keep[2, 1], keep[0, 1]), jnp.where(first, given[2, 1], given[0, 1])))
+    middle = added(keep[1, 1], given[1, 1])
+    middle, outer = lax.optimization_barrier((middle, outer))
+    middle = swap_z(middle)
+    back = shift_row(added(keep[2, 0], given[2, 0], jnp.where(first, zero, outer)), -1)
+    back = shift_row(added(keep[1, 0], given[1, 0], middle, back), -1)
+    half = added(keep[0, 0], given[0, 0], jnp.where(first, outer, zero), back)
+    other = swap_head(half)
+    return [added(half[part], other[part]) for part in range(2)]
 
 
 def on_device(queries, key_rows, value_rows, d_out, seq_lengths):
@@ -349,7 +343,7 @@
     for block in (own, side0, row1, side1, row2, side2):
         blocks += [block, swap_core(block)]
     attended, grad_queries, *parts = attention(seq_lengths, queries, d_out, blocks)
-    grad_keys, grad_values = returned(parts[::2], parts[1::2])
+    grad_keys, grad_values = returned(*parts)
     return attended, grad_queries, grad_keys, grad_values
 
 

time: 126 us -> 129 us (1.024)
  the two profiles are of different devices: /device:TPU:30 before, /device:TPU:28 now
where the time goes in v8:
time: 129 us; the launch traced here: 126 us
  waiting for transfers between devices  49.3 us (38%)
  Pallas kernels  39 us (30%)
  starting transfers between devices  33 us (26%)
  other arithmetic  3.5 us (3%)
    pallas_call x1, Pallas kernels, attention(): pl.pallas_call(attention_kernel, out_shape=(rows, rows) + (grads,) * 2, i...  39 us
    ppermute x5, waiting for transfers between devices, swap_z(): return lax.ppermute(value, ('zh', 'zl'), pairs)  23.4 us
    ppermute x4, starting transfers between devices, shift_row(): lax.ppermute(value, ('x', 'y'), [(r, (r + by) % 16) for r in range(16)])  20.7 us
    ppermute x4, waiting for transfers between devices, shift_row(): lax.ppermute(value, ('x', 'y'), [(r, (r + by) % 16) for r in range(16)])  14.6 us
    ppermute x5, starting transfers between devices, swap_z(): return lax.ppermute(value, ('zh', 'zl'), pairs)  11.3 us
    ppermute x1, waiting for transfers between devices, swap_head(): return lax.ppermute(value, 'zl', [(0, 1), (1, 0)])  6.36 us
    ppermute x7, waiting for transfers between devices, swap_core(): return lax.ppermute(value, 'core', [(0, 1), (1, 0)])  4.96 us
  transfers between devices with their start and end apart: 17, of which 11 were waited for; matrix products, arithmetic and copies ran while one was open for 0% of the time, Pallas kernels for 0%

profile of v8, /device:TPU:28, one launch (start us, length us, event | category | flops | bytes accessed | tf_op | source)
XLA Modules:
  0.0 126.4 jit_solution(8330970231088937725)
XLA Ops:
  0.6 1.0 pad_maximum_fusion.refs_3_
  1.6 0.0 copy-start.1
  1.6 0.9 collective-permute-start.3
  2.6 5.9 %collective-permute-start.1 = (bf16[2,512,128]{2,1,0:T(8,128)(2,1)S(1)}, bf16[2,512,128]{2,1,0:T(8,128)(2,1)S(1)}, u32[]{:S(2)}, u32[]{:S(2)}) collective-permute-start(bf16[2,512,128]{2,1,0:T(8,128)(2,1)S(1)} %pad_maximum_fusion.refs_3_), channel_id=1, source_target_pairs={{0,5},{1,4},{2,7},{3,6},{8,13},{9,12},{10,15},{11,14},{16,21},{17,... | collective-permute-start | bytes 786440 | tf_op jit(solution)/shard_map/ppermute | solution.py:302
  8.5 1.2 collective-permute-done.3.refs_7_
  9.8 3.0 %collective-permute-start.7 = (bf16[2,512,128]{2,1,0:T(8,128)(2,1)S(1)}, bf16[2,512,128]{2,1,0:T(8,128)(2,1)S(1)}, u32[]{:S(2)}, u32[]{:S(2)}) collective-permute-start(bf16[2,512,128]{2,1,0:T(8,128)(2,1)S(1)} %collective-permute-done.3.refs_7_), channel_id=1, source_target_pairs={{0,8},{8,16},{16,24},{24,32},{32,40},{40,48},{48,56},{56,64},{64,7... | collective-permute-start | bytes 786440 | tf_op jit(solution)/shard_map/ppermute | solution.py:310
  12.7 0.0 collective-permute-start
  12.7 1.0 collective-permute-done.1.refs_5_
  13.8 3.7 %collective-permute-start.5 = (bf16[2,512,128]{2,1,0:T(8,128)(2,1)S(1)}, bf16[2,512,128]{2,1,0:T(8,128)(2,1)S(1)}, u32[]{:S(2)}, u32[]{:S(2)}) collective-permute-start(bf16[2,512,128]{2,1,0:T(8,128)(2,1)S(1)} %collective-permute-done.3.refs_7_), channel_id=1, source_target_pairs={{0,5},{1,4},{4,1},{5,0},{2,7},{3,6},{6,3},{7,2},{8,13},{9,12},{12,... | collective-permute-start | bytes 786440 | tf_op jit(solution)/shard_map/ppermute | solution.py:302
  17.5 0.0 collective-permute-done.7.refs_11_
  17.5 1.3 %collective-permute-start.9 = (bf16[2,512,128]{2,1,0:T(8,128)(2,1)S(1)}, bf16[2,512,128]{2,1,0:T(8,128)(2,1)S(1)}, u32[]{:S(2)}, u32[]{:S(2)}) collective-permute-start(bf16[2,512,128]{2,1,0:T(8,128)(2,1)S(1)} %collective-permute-done.7.refs_11_), channel_id=1, source_target_pairs={{4,1},{5,0},{6,3},{7,2},{12,9},{13,8},{14,11},{15,10},{20,17},{21,... | collective-permute-start | bytes 786440 | tf_op jit(solution)/shard_map/ppermute | solution.py:302
  18.8 0.1 collective-permute-start.4
  18.8 0.5 collective-permute-start.2
  19.3 0.0 collective-permute-done.refs_4_
  19.4 0.1 collective-permute-start.8
  19.4 5.1 %collective-permute-done.5.refs_9_ = bf16[2,512,128]{2,1,0:T(8,128)(2,1)S(1)} collective-permute-done((bf16[2,512,128]{2,1,0:T(8,128)(2,1)S(1)}, bf16[2,512,128]{2,1,0:T(8,128)(2,1)S(1)}, u32[]{:S(2)}, u32[]{:S(2)}) %collective-permute-start.5) | collective-permute-done | bytes 262176 | tf_op jit(solution)/shard_map/ppermute | solution.py:302
  24.6 0.0 collective-permute-start.6
  24.6 4.8 %collective-permute-done.9.refs_13_ = bf16[2,512,128]{2,1,0:T(8,128)(2,1)S(1)} collective-permute-done((bf16[2,512,128]{2,1,0:T(8,128)(2,1)S(1)}, bf16[2,512,128]{2,1,0:T(8,128)(2,1)S(1)}, u32[]{:S(2)}, u32[]{:S(2)}) %collective-permute-start.9) | collective-permute-done | bytes 262176 | tf_op jit(solution)/shard_map/ppermute | solution.py:302
  29.4 0.0 collective-permute-start.10
  29.4 0.0 collective-permute-done.4.refs_8_
  29.4 0.0 copy-start.8
  29.4 0.0 collective-permute-done.2.refs_6_
  29.4 0.0 copy-start.9
  29.4 0.0 collective-permute-done.6.refs_10_
  29.4 0.0 copy-start.11
  29.4 0.0 collective-permute-done.8.refs_12_
  29.4 0.0 copy-start.10
  29.4 1.5 %collective-permute-done.10.refs_14_ = bf16[2,512,128]{2,1,0:T(8,128)(2,1)S(1)} collective-permute-done((bf16[2,512,128]{2,1,0:T(8,128)(2,1)S(1)}, bf16[2,512,128]{2,1,0:T(8,128)(2,1)S(1)}, u32[]{:S(2)}, u32[]{:S(2)}) %collective-permute-start.10) | collective-permute-done | bytes 262176 | tf_op jit(solution)/shard_map/ppermute | solution.py:297
  30.9 0.0 copy-done.2
  31.0 0.7 copy-done.12
  31.7 39.0 %attention.1 = (bf16[4,512,128]{2,1,0:T(8,128)(2,1)}, bf16[4,512,128]{2,1,0:T(8,128)(2,1)}, bf16[3,2,2,512,128]{4,3,2,1,0:T(8,128)(2,1)}, bf16[3,2,2,512,128]{4,3,2,1,0:T(8,128)(2,1)}) custom-call(s32[16]{0:T(128)} %refs_0_.1, bf16[4,512,128]{2,1,0:T(8,128)(2,1)} %refs_1_.1, bf16[4,512,128]{2,1,0:T(8,128)(2,1)} %refs_2_.1, bf16[2,512,128]{2,1,0:T(8,128)(2,1)} %copy-done.1, ...), custom_call_target="tpu_custom_call" | custom-call | flops 8589934592 | bytes 16777216 | tf_op jit(solution)/shard_map/attention/pallas_call | solution.py:263
  70.7 0.2 collective-permute-start.11
  70.9 3.5 %collective-permute-done.11 = bf16[3,2,2,512,128]{4,3,2,1,0:T(8,128)(2,1)S(1)} collective-permute-done((bf16[3,2,2,512,128]{4,3,2,1,0:T(8,128)(2,1)}, bf16[3,2,2,512,128]{4,3,2,1,0:T(8,128)(2,1)S(1)}, u32[]{:S(2)}, u32[]{:S(2)}) %collective-permute-start.11) | collective-permute-done | bytes 1572896 | tf_op jit(solution)/shard_map/ppermute | solution.py:297
  74.4 1.3 %fusion.6 = (bf16[2,512,128]{2,1,0:T(8,128)(2,1)S(1)}, bf16[2,512,128]{2,1,0:T(8,128)(2,1)S(1)}) fusion(bf16[3,2,2,512,128]{4,3,2,1,0:T(8,128)(2,1)S(1)} %collective-permute-done.11, bf16[3,2,2,512,128]{4,3,2,1,0:T(8,128)(2,1)} %get-tuple-element.14, pred[]{:T(512)S(6)} %eq.3), kind=kLoop, calls=%fused_computation.11 | loop fusion | flops 1310720 | bytes 2097153 | tf_op jit(solution)/shard_map/convert_element_type | solution.py:317
  75.7 0.1 collective-permute-start.12
  75.8 9.5 %collective-permute-done.12 = bf16[2,512,128]{2,1,0:T(8,128)(2,1)S(1)} collective-permute-done((bf16[2,512,128]{2,1,0:T(8,128)(2,1)S(1)}, bf16[2,512,128]{2,1,0:T(8,128)(2,1)S(1)}, u32[]{:S(2)}, u32[]{:S(2)}) %collective-permute-start.12) | collective-permute-done | bytes 262176 | tf_op jit(solution)/shard_map/ppermute | solution.py:302
  85.4 0.1 fusion
  85.5 16.4 %collective-permute-start.14 = (bf16[2,512,128]{2,1,0:T(8,128)(2,1)S(1)}, bf16[2,512,128]{2,1,0:T(8,128)(2,1)S(1)}, u32[]{:S(2)}, u32[]{:S(2)}) collective-permute-start(bf16[2,512,128]{2,1,0:T(8,128)(2,1)S(1)} %fusion), channel_id=1, source_target_pairs={{0,120},{8,0},{16,8},{24,16},{32,24},{40,32},{48,40},{56,48},{64,5... | collective-permute-start | bytes 786440 | tf_op jit(solution)/shard_map/ppermute | solution.py:310
  101.9 0.3 collective-permute-start.13
  102.2 5.2 %collective-permute-done.14 = bf16[2,512,128]{2,1,0:T(8,128)(2,1)S(1)} collective-permute-done((bf16[2,512,128]{2,1,0:T(8,128)(2,1)S(1)}, bf16[2,512,128]{2,1,0:T(8,128)(2,1)S(1)}, u32[]{:S(2)}, u32[]{:S(2)}) %collective-permute-start.14) | collective-permute-done | bytes 262176 | tf_op jit(solution)/shard_map/ppermute | solution.py:310
  107.4 2.9 %collective-permute-done.13 = bf16[2,512,128]{2,1,0:T(8,128)(2,1)S(1)} collective-permute-done((bf16[2,512,128]{2,1,0:T(8,128)(2,1)S(1)}, bf16[2,512,128]{2,1,0:T(8,128)(2,1)S(1)}, u32[]{:S(2)}, u32[]{:S(2)}) %collective-permute-start.13) | collective-permute-done | bytes 262176 | tf_op jit(solution)/shard_map/ppermute | solution.py:302
  110.3 0.1 fusion.2
  110.5 0.4 collective-permute-start.15
  110.9 8.1 %collective-permute-done.15 = bf16[2,512,128]{2,1,0:T(8,128)(2,1)S(1)} collective-permute-done((bf16[2,512,128]{2,1,0:T(8,128)(2,1)S(1)}, bf16[2,512,128]{2,1,0:T(8,128)(2,1)S(1)}, u32[]{:S(2)}, u32[]{:S(2)}) %collective-permute-start.15) | collective-permute-done | bytes 262176 | tf_op jit(solution)/shard_map/ppermute | solution.py:310
  119.0 0.2 fusion.4
  119.2 0.1 collective-permute-start.16
  119.3 6.4 %collective-permute-done.16 = bf16[2,512,128]{2,1,0:T(8,128)(2,1)S(1)} collective-permute-done((bf16[2,512,128]{2,1,0:T(8,128)(2,1)S(1)}, bf16[2,512,128]{2,1,0:T(8,128)(2,1)S(1)}, u32[]{:S(2)}, u32[]{:S(2)}) %collective-permute-start.16) | collective-permute-done | bytes 262176 | tf_op jit(solution)/shard_map/ppermute | solution.py:306
  125.6 0.8 fusion.8
  (19 shorter events, 0.0 us)
Async XLA Ops:
  1.6 29.3 %copy-start.1 = (bf16[2,512,128]{2,1,0:T(8,128)(2,1)}, bf16[2,512,128]{2,1,0:T(8,128)(2,1)S(1)}, u32[]{:S(2)}) copy-start(bf16[2,512,128]{2,1,0:T(8,128)(2,1)S(1)} %pad_maximum_fusion.refs_3_) | copy-start | bytes 786436
  1.6 8.1 %collective-permute-start.3 = (bf16[2,512,128]{2,1,0:T(8,128)(2,1)S(1)}, bf16[2,512,128]{2,1,0:T(8,128)(2,1)S(1)}, u32[]{:S(2)}, u32[]{:S(2)}) collective-permute-start(bf16[2,512,128]{2,1,0:T(8,128)(2,1)S(1)} %pad_maximum_fusion.refs_3_), channel_id=1, source_target_pairs={{0,8},{8,16},{16,24},{24,32},{32,40},{40,48},{48,56},{56,64},{64,7... | collective-permute-start | bytes 786440 | tf_op jit(solution)/shard_map/ppermute | solution.py:310
  2.6 11.2 %collective-permute-start.1 = (bf16[2,512,128]{2,1,0:T(8,128)(2,1)S(1)}, bf16[2,512,128]{2,1,0:T(8,128)(2,1)S(1)}, u32[]{:S(2)}, u32[]{:S(2)}) collective-permute-start(bf16[2,512,128]{2,1,0:T(8,128)(2,1)S(1)} %pad_maximum_fusion.refs_3_), channel_id=1, source_target_pairs={{0,5},{1,4},{2,7},{3,6},{8,13},{9,12},{10,15},{11,14},{16,21},{17,... | collective-permute-start | bytes 786440 | tf_op jit(solution)/shard_map/ppermute | solution.py:302
  9.8 21.2 %copy-start.2 = (bf16[2,512,128]{2,1,0:T(8,128)(2,1)}, bf16[2,512,128]{2,1,0:T(8,128)(2,1)S(1)}, u32[]{:S(2)}) copy-start(bf16[2,512,128]{2,1,0:T(8,128)(2,1)S(1)} %collective-permute-done.3.refs_7_) | copy-start | bytes 786436
  9.8 7.7 %collective-permute-start.7 = (bf16[2,512,128]{2,1,0:T(8,128)(2,1)S(1)}, bf16[2,512,128]{2,1,0:T(8,128)(2,1)S(1)}, u32[]{:S(2)}, u32[]{:S(2)}) collective-permute-start(bf16[2,512,128]{2,1,0:T(8,128)(2,1)S(1)} %collective-permute-done.3.refs_7_), channel_id=1, source_target_pairs={{0,8},{8,16},{16,24},{24,32},{32,40},{40,48},{48,56},{56,64},{64,7... | collective-permute-start | bytes 786440 | tf_op jit(solution)/shard_map/ppermute | solution.py:310
  12.7 6.6 %collective-permute-start = (bf16[2,512,128]{2,1,0:T(8,128)(2,1)S(1)}, bf16[2,512,128]{2,1,0:T(8,128)(2,1)S(1)}, u32[]{:S(2)}, u32[]{:S(2)}) collective-permute-start(bf16[2,512,128]{2,1,0:T(8,128)(2,1)S(1)} %pad_maximum_fusion.refs_3_), channel_id=1, source_target_pairs={{0,2},{2,0},{1,3},{3,1},{4,6},{6,4},{5,7},{7,5},{8,10},{10,8},{9,1... | collective-permute-start | bytes 786440 | tf_op jit(solution)/shard_map/ppermute | solution.py:297
  13.8 17.1 %copy-start.3 = (bf16[2,512,128]{2,1,0:T(8,128)(2,1)}, bf16[2,512,128]{2,1,0:T(8,128)(2,1)S(1)}, u32[]{:S(2)}) copy-start(bf16[2,512,128]{2,1,0:T(8,128)(2,1)S(1)} %collective-permute-done.1.refs_5_) | copy-start | bytes 786436
  13.8 10.8 %collective-permute-start.5 = (bf16[2,512,128]{2,1,0:T(8,128)(2,1)S(1)}, bf16[2,512,128]{2,1,0:T(8,128)(2,1)S(1)}, u32[]{:S(2)}, u32[]{:S(2)}) collective-permute-start(bf16[2,512,128]{2,1,0:T(8,128)(2,1)S(1)} %collective-permute-done.3.refs_7_), channel_id=1, source_target_pairs={{0,5},{1,4},{4,1},{5,0},{2,7},{3,6},{6,3},{7,2},{8,13},{9,12},{12,... | collective-permute-start | bytes 786440 | tf_op jit(solution)/shard_map/ppermute | solution.py:302
  17.5 13.4 %copy-start.4 = (bf16[2,512,128]{2,1,0:T(8,128)(2,1)}, bf16[2,512,128]{2,1,0:T(8,128)(2,1)S(1)}, u32[]{:S(2)}) copy-start(bf16[2,512,128]{2,1,0:T(8,128)(2,1)S(1)} %collective-permute-done.7.refs_11_) | copy-start | bytes 786436
  17.5 11.9 %collective-permute-start.9 = (bf16[2,512,128]{2,1,0:T(8,128)(2,1)S(1)}, bf16[2,512,128]{2,1,0:T(8,128)(2,1)S(1)}, u32[]{:S(2)}, u32[]{:S(2)}) collective-permute-start(bf16[2,512,128]{2,1,0:T(8,128)(2,1)S(1)} %collective-permute-done.7.refs_11_), channel_id=1, source_target_pairs={{4,1},{5,0},{6,3},{7,2},{12,9},{13,8},{14,11},{15,10},{20,17},{21,... | collective-permute-start | bytes 786440 | tf_op jit(solution)/shard_map/ppermute | solution.py:302
  18.8 10.6 %collective-permute-start.4 = (bf16[2,512,128]{2,1,0:T(8,128)(2,1)S(1)}, bf16[2,512,128]{2,1,0:T(8,128)(2,1)S(1)}, u32[]{:S(2)}, u32[]{:S(2)}) collective-permute-start(bf16[2,512,128]{2,1,0:T(8,128)(2,1)S(1)} %collective-permute-done.3.refs_7_), channel_id=1, source_target_pairs={{0,2},{2,0},{1,3},{3,1},{4,6},{6,4},{5,7},{7,5},{8,10},{10,8},{9,1... | collective-permute-start | bytes 786440 | tf_op jit(solution)/shard_map/ppermute | solution.py:297
  18.8 10.5 %collective-permute-start.2 = (bf16[2,512,128]{2,1,0:T(8,128)(2,1)S(1)}, bf16[2,512,128]{2,1,0:T(8,128)(2,1)S(1)}, u32[]{:S(2)}, u32[]{:S(2)}) collective-permute-start(bf16[2,512,128]{2,1,0:T(8,128)(2,1)S(1)} %collective-permute-done.1.refs_5_), channel_id=1, source_target_pairs={{0,2},{2,0},{1,3},{3,1},{4,6},{6,4},{5,7},{7,5},{8,10},{10,8},{9,1... | collective-permute-start | bytes 786440 | tf_op jit(solution)/shard_map/ppermute | solution.py:297
  19.3 11.6 %copy-start.5 = (bf16[2,512,128]{2,1,0:T(8,128)(2,1)}, bf16[2,512,128]{2,1,0:T(8,128)(2,1)S(1)}, u32[]{:S(2)}) copy-start(bf16[2,512,128]{2,1,0:T(8,128)(2,1)S(1)} %collective-permute-done.refs_4_) | copy-start | bytes 786436
  19.4 10.1 %collective-permute-start.8 = (bf16[2,512,128]{2,1,0:T(8,128)(2,1)S(1)}, bf16[2,512,128]{2,1,0:T(8,128)(2,1)S(1)}, u32[]{:S(2)}, u32[]{:S(2)}) collective-permute-start(bf16[2,512,128]{2,1,0:T(8,128)(2,1)S(1)} %collective-permute-done.7.refs_11_), channel_id=1, source_target_pairs={{0,2},{2,0},{1,3},{3,1},{4,6},{6,4},{5,7},{7,5},{8,10},{10,8},{9,1... | collective-permute-start | bytes 786440 | tf_op jit(solution)/shard_map/ppermute | solution.py:297
  24.6 6.3 %copy-start.6 = (bf16[2,512,128]{2,1,0:T(8,128)(2,1)}, bf16[2,512,128]{2,1,0:T(8,128)(2,1)S(1)}, u32[]{:S(2)}) copy-start(bf16[2,512,128]{2,1,0:T(8,128)(2,1)S(1)} %collective-permute-done.5.refs_9_) | copy-start | bytes 786436
  24.6 4.8 %collective-permute-start.6 = (bf16[2,512,128]{2,1,0:T(8,128)(2,1)S(1)}, bf16[2,512,128]{2,1,0:T(8,128)(2,1)S(1)}, u32[]{:S(2)}, u32[]{:S(2)}) collective-permute-start(bf16[2,512,128]{2,1,0:T(8,128)(2,1)S(1)} %collective-permute-done.5.refs_9_), channel_id=1, source_target_pairs={{0,2},{2,0},{1,3},{3,1},{4,6},{6,4},{5,7},{7,5},{8,10},{10,8},{9,1... | collective-permute-start | bytes 786440 | tf_op jit(solution)/shard_map/ppermute | solution.py:297
  29.4 1.6 %copy-start.7 = (bf16[2,512,128]{2,1,0:T(8,128)(2,1)}, bf16[2,512,128]{2,1,0:T(8,128)(2,1)S(1)}, u32[]{:S(2)}) copy-start(bf16[2,512,128]{2,1,0:T(8,128)(2,1)S(1)} %collective-permute-done.9.refs_13_) | copy-start | bytes 786436
  29.4 1.5 %collective-permute-start.10 = (bf16[2,512,128]{2,1,0:T(8,128)(2,1)S(1)}, bf16[2,512,128]{2,1,0:T(8,128)(2,1)S(1)}, u32[]{:S(2)}, u32[]{:S(2)}) collective-permute-start(bf16[2,512,128]{2,1,0:T(8,128)(2,1)S(1)} %collective-permute-done.9.refs_13_), channel_id=1, source_target_pairs={{0,2},{2,0},{1,3},{3,1},{4,6},{6,4},{5,7},{7,5},{8,10},{10,8},{9,1... | collective-permute-start | bytes 786440 | tf_op jit(solution)/shard_map/ppermute | solution.py:297
  29.4 1.6 %copy-start.8 = (bf16[2,512,128]{2,1,0:T(8,128)(2,1)}, bf16[2,512,128]{2,1,0:T(8,128)(2,1)S(1)}, u32[]{:S(2)}) copy-start(bf16[2,512,128]{2,1,0:T(8,128)(2,1)S(1)} %collective-permute-done.4.refs_8_) | copy-start | bytes 786436
  29.4 1.6 %copy-start.9 = (bf16[2,512,128]{2,1,0:T(8,128)(2,1)}, bf16[2,512,128]{2,1,0:T(8,128)(2,1)S(1)}, u32[]{:S(2)}) copy-start(bf16[2,512,128]{2,1,0:T(8,128)(2,1)S(1)} %collective-permute-done.2.refs_6_) | copy-start | bytes 786436
  29.4 1.6 %copy-start.11 = (bf16[2,512,128]{2,1,0:T(8,128)(2,1)}, bf16[2,512,128]{2,1,0:T(8,128)(2,1)S(1)}, u32[]{:S(2)}) copy-start(bf16[2,512,128]{2,1,0:T(8,128)(2,1)S(1)} %collective-permute-done.6.refs_10_) | copy-start | bytes 786436
  29.4 1.5 %copy-start.10 = (bf16[2,512,128]{2,1,0:T(8,128)(2,1)}, bf16[2,512,128]{2,1,0:T(8,128)(2,1)S(1)}, u32[]{:S(2)}) copy-start(bf16[2,512,128]{2,1,0:T(8,128)(2,1)S(1)} %collective-permute-done.8.refs_12_) | copy-start | bytes 786436
  31.0 0.7 copy-start.12
  70.7 14.7 %copy-start = (bf16[3,2,2,512,128]{4,3,2,1,0:T(8,128)(2,1)S(1)}, bf16[3,2,2,512,128]{4,3,2,1,0:T(8,128)(2,1)}, u32[]{:S(2)}) copy-start(bf16[3,2,2,512,128]{4,3,2,1,0:T(8,128)(2,1)} %get-tuple-element.14) | copy-start | bytes 4718596
  70.7 3.7 %collective-permute-start.11 = (bf16[3,2,2,512,128]{4,3,2,1,0:T(8,128)(2,1)}, bf16[3,2,2,512,128]{4,3,2,1,0:T(8,128)(2,1)S(1)}, u32[]{:S(2)}, u32[]{:S(2)}) collective-permute-start(bf16[3,2,2,512,128]{4,3,2,1,0:T(8,128)(2,1)} %get-tuple-element.15), channel_id=1, source_target_pairs={{0,2},{2,0},{1,3},{3,1},{4,6},{6,4},{5,7},{7,5},{8,10},{10,8},{9,1... | collective-permute-start | bytes 4718600 | tf_op jit(solution)/shard_map/ppermute | solution.py:297
  75.7 9.6 %collective-permute-start.12 = (bf16[2,512,128]{2,1,0:T(8,128)(2,1)S(1)}, bf16[2,512,128]{2,1,0:T(8,128)(2,1)S(1)}, u32[]{:S(2)}, u32[]{:S(2)}) collective-permute-start(bf16[2,512,128]{2,1,0:T(8,128)(2,1)S(1)} %get-tuple-element.18), channel_id=1, source_target_pairs={{0,5},{1,4},{4,1},{5,0},{2,7},{3,6},{6,3},{7,2},{8,13},{9,12},{12,... | collective-permute-start | bytes 786440 | tf_op jit(solution)/shard_map/ppermute | solution.py:302
  85.5 21.9 %collective-permute-start.14 = (bf16[2,512,128]{2,1,0:T(8,128)(2,1)S(1)}, bf16[2,512,128]{2,1,0:T(8,128)(2,1)S(1)}, u32[]{:S(2)}, u32[]{:S(2)}) collective-permute-start(bf16[2,512,128]{2,1,0:T(8,128)(2,1)S(1)} %fusion), channel_id=1, source_target_pairs={{0,120},{8,0},{16,8},{24,16},{32,24},{40,32},{48,40},{56,48},{64,5... | collective-permute-start | bytes 786440 | tf_op jit(solution)/shard_map/ppermute | solution.py:310
  101.9 8.5 %collective-permute-start.13 = (bf16[2,512,128]{2,1,0:T(8,128)(2,1)S(1)}, bf16[2,512,128]{2,1,0:T(8,128)(2,1)S(1)}, u32[]{:S(2)}, u32[]{:S(2)}) collective-permute-start(bf16[2,512,128]{2,1,0:T(8,128)(2,1)S(1)} %get-tuple-element.17), channel_id=1, source_target_pairs={{0,5},{1,4},{4,1},{5,0},{2,7},{3,6},{6,3},{7,2},{8,13},{9,12},{12,... | collective-permute-start | bytes 786440 | tf_op jit(solution)/shard_map/ppermute | solution.py:302
  110.5 8.6 %collective-permute-start.15 = (bf16[2,512,128]{2,1,0:T(8,128)(2,1)S(1)}, bf16[2,512,128]{2,1,0:T(8,128)(2,1)S(1)}, u32[]{:S(2)}, u32[]{:S(2)}) collective-permute-start(bf16[2,512,128]{2,1,0:T(8,128)(2,1)S(1)} %fusion.2), channel_id=1, source_target_pairs={{0,120},{8,0},{16,8},{24,16},{32,24},{40,32},{48,40},{56,48},{64,5... | collective-permute-start | bytes 786440 | tf_op jit(solution)/shard_map/ppermute | solution.py:310
  119.2 6.5 %collective-permute-start.16 = (bf16[2,512,128]{2,1,0:T(8,128)(2,1)S(1)}, bf16[2,512,128]{2,1,0:T(8,128)(2,1)S(1)}, u32[]{:S(2)}, u32[]{:S(2)}) collective-permute-start(bf16[2,512,128]{2,1,0:T(8,128)(2,1)S(1)} %fusion.4), channel_id=1, source_target_pairs={{0,1},{1,0},{2,3},{3,2},{4,5},{5,4},{6,7},{7,6},{8,9},{9,8},{10,11... | collective-permute-start | bytes 786440 | tf_op jit(solution)/shard_map/ppermute | solution.py:306

commit v9 on v6

--- a/solution.py
+++ b/solution.py
@@ -72,10 +72,10 @@
 
 def attention_kernel(*refs):
     len_ref, q_hbm, do_hbm = refs[:3]
-    kv_refs = refs[3:15]
-    o_hbm, dq_hbm = refs[15:17]
-    out_refs = refs[17:21]
-    kvs, dkvs, qt, dot_t, do_s, probs, row_max, total, acc, dq_acc, stage, delta, norms, q_ref, do_ref, o_ref, dq_ref, row_sem, in_sem, out_sem = refs[21:]
+    kv_refs = refs[3:17]
+    o_hbm, dq_hbm = refs[17:19]
+    out_refs = refs[19:23]
+    kvs, dkvs, qt, dot_t, do_s, probs, row_max, total, acc, dq_acc, stage, delta, norms, q_ref, do_ref, o_ref, dq_ref, row_sem, in_sem, out_sem = refs[23:]
     loads = [[pltpu.make_async_copy(a.at[h], b.at[h], row_sem.at[n, h]) for n, (a, b) in enumerate(((q_hbm, q_ref), (do_hbm, do_ref)))] for h in range(HEADS)]
     for pair in loads:
         for copy in pair:
@@ -84,7 +84,11 @@
     order = [(j, dz, dc) for j in range(ROWS) for dz, dc in NEAR]
     for n, where in enumerate(order):
         slot = at.slot(*where)
-        pltpu.make_async_copy(kv_refs[n], kvs.at[slot], in_sem.at[slot]).start()
+        if n < SLOTS - 2:
+            pltpu.make_async_copy(kv_refs[n], kvs.at[slot], in_sem.at[slot]).start()
+        else:
+            for part in range(2):
+                pltpu.make_async_copy(kv_refs[n + 2 * part], kvs.at[slot, part], in_sem.at[slot]).start()
 
     def arrived(t):
         pltpu.make_async_copy(kv_refs[0], kvs.at[t], in_sem.at[t]).wait()
@@ -266,7 +270,7 @@
     return pl.pallas_call(
         attention_kernel,
         out_shape=(rows, rows) + (grads,) * 4,
-        in_specs=[SMEM] + [ANY] * (2 + SLOTS),
+        in_specs=[SMEM] + [ANY] * (4 + SLOTS),
         out_specs=[ANY] * 6,
         scratch_shapes=[
             pltpu.VMEM((SLOTS + GROUP - 1, 2, BLK, HD), BF16),
@@ -344,9 +348,9 @@
     side0 = swap_z(own, (0,))
     row2 = shift_row(row1, 1)
     side1 = swap_z(lax.optimization_barrier((row1, side0))[0])
-    side2 = swap_z(row2, (1,))
+    side2 = [swap_z(row2[part], (1,)) for part in range(2)]
     blocks = []
-    for block in (own, side0, row1, side1, row2, side2):
+    for block in (own, side0, row1, side1, row2, *side2):
         blocks += [block, swap_core(block)]
     attended, grad_queries, *parts = attention(seq_lengths, queries, d_out, blocks)
     grad_keys, grad_values = returned(parts[::2], parts[1::2])

time: 126 us -> 129 us (1.024)
  waiting for transfers between devices: 42 us -> 44.2 us
  starting transfers between devices: 22.1 us -> 23.4 us
    ppermute x7 -> x8, waiting for transfers between devices: 19.3 us -> 22.2 us  [swap_z(): return lax.ppermute(value, ('zh', 'zl'), pairs)]
    ppermute x7 -> x8, starting transfers between devices: 16.3 us -> 17.6 us  [swap_z(): return lax.ppermute(value, ('zh', 'zl'), pairs)]
    ppermute x8 -> x9, waiting for transfers between devices: 3.46 us -> 3.27 us  [swap_core(): return lax.ppermute(value, 'core', [(0, 1), (1, 0)])]
  transfers between devices with their start and end apart: 23 -> 25, of which waited for: 15 -> 16; matrix products, arithmetic and copies ran while one was open for 2% -> 2% of each run, Pallas kernels for 0% -> 0%
where the time goes in v9:
time: 129 us
  Pallas kernels  55.4 us (43%)
  waiting for transfers between devices  44.2 us (34%)
  starting transfers between devices  23.4 us (18%)
  other arithmetic  4.07 us (3%)
    pallas_call x1, Pallas kernels, attention(): pl.pallas_call(attention_kernel, out_shape=(rows, rows) + (grads,) * 4, i...  55.4 us
    ppermute x8, waiting for transfers between devices, swap_z(): return lax.ppermute(value, ('zh', 'zl'), pairs)  22.2 us
    ppermute x8, starting transfers between devices, swap_z(): return lax.ppermute(value, ('zh', 'zl'), pairs)  17.6 us
    ppermute x6, waiting for transfers between devices, shift_row(): lax.ppermute(value, ('x', 'y'), [(r, (r + by) % 16) for r in range(16)])  14.8 us
    ppermute x6, starting transfers between devices, shift_row(): lax.ppermute(value, ('x', 'y'), [(r, (r + by) % 16) for r in range(16)])  4.03 us
    ppermute x2, waiting for transfers between devices, swap_head(): return lax.ppermute(value, 'zl', [(0, 1), (1, 0)])  3.89 us
    ppermute x9, waiting for transfers between devices, swap_core(): return lax.ppermute(value, 'core', [(0, 1), (1, 0)])  3.27 us
    convert_element_type x10, other arithmetic, added(): return total.astype(BF16)  3.07 us
  transfers between devices with their start and end apart: 25, of which 16 were waited for; matrix products, arithmetic and copies ran while one was open for 2% of the time, Pallas kernels for 0%

profile of v9, /device:TPU:30, one launch (start us, length us, event | category | flops | bytes accessed | tf_op | source)
XLA Modules:
  0.0 128.7 jit_solution(17085070060153265218)
XLA Ops:
  0.6 1.0 pad_maximum_fusion.refs_3_
  1.6 0.1 collective-permute-start.3
  1.8 6.0 %collective-permute-start.1 = (bf16[2,512,128]{2,1,0:T(8,128)(2,1)S(1)}, bf16[2,512,128]{2,1,0:T(8,128)(2,1)S(1)}, u32[]{:S(2)}, u32[]{:S(2)}) collective-permute-start(bf16[2,512,128]{2,1,0:T(8,128)(2,1)S(1)} %pad_maximum_fusion.refs_3_), channel_id=1, source_target_pairs={{0,5},{1,4},{2,7},{3,6},{8,13},{9,12},{10,15},{11,14},{16,21},{17,... | collective-permute-start | bytes 786440 | tf_op jit(solution)/shard_map/ppermute | solution.py:309
  7.8 2.0 %collective-permute-done.3.refs_7_ = bf16[2,512,128]{2,1,0:T(8,128)(2,1)S(1)} collective-permute-done((bf16[2,512,128]{2,1,0:T(8,128)(2,1)S(1)}, bf16[2,512,128]{2,1,0:T(8,128)(2,1)S(1)}, u32[]{:S(2)}, u32[]{:S(2)}) %collective-permute-start.3) | collective-permute-done | bytes 262176 | tf_op jit(solution)/shard_map/ppermute | solution.py:317
  9.8 3.6 %collective-permute-start.7 = (bf16[2,512,128]{2,1,0:T(8,128)(2,1)S(1)}, bf16[2,512,128]{2,1,0:T(8,128)(2,1)S(1)}, u32[]{:S(2)}, u32[]{:S(2)}) collective-permute-start(bf16[2,512,128]{2,1,0:T(8,128)(2,1)S(1)} %collective-permute-done.3.refs_7_), channel_id=1, source_target_pairs={{0,8},{8,16},{16,24},{24,32},{32,40},{40,48},{48,56},{56,64},{64,7... | collective-permute-start | bytes 786440 | tf_op jit(solution)/shard_map/ppermute | solution.py:317
  13.4 4.1 %collective-permute-start.5 = (bf16[2,512,128]{2,1,0:T(8,128)(2,1)S(1)}, bf16[2,512,128]{2,1,0:T(8,128)(2,1)S(1)}, u32[]{:S(2)}, u32[]{:S(2)}) collective-permute-start(bf16[2,512,128]{2,1,0:T(8,128)(2,1)S(1)} %collective-permute-done.3.refs_7_), channel_id=1, source_target_pairs={{0,5},{1,4},{4,1},{5,0},{2,7},{3,6},{6,3},{7,2},{8,13},{9,12},{12,... | collective-permute-start | bytes 786440 | tf_op jit(solution)/shard_map/ppermute | solution.py:309
  17.5 0.2 collective-permute-start.4
  17.6 0.3 collective-permute-start.2
  18.0 0.3 collective-permute-done.7.refs_11_
  18.4 1.3 %collective-permute-start.9 = (bf16[512,128]{1,0:T(8,128)(2,1)S(1)}, bf16[512,128]{1,0:T(8,128)(2,1)S(1)}, u32[]{:S(2)}, u32[]{:S(2)}) collective-permute-start(bf16[512,128]{1,0:T(8,128)(2,1)S(1)} %get-tuple-element.27), channel_id=1, source_target_pairs={{4,1},{5,0},{6,3},{7,2},{12,9},{13,8},{14,11},{15,10},{20,17},{21,... | collective-permute-start | bytes 393224 | tf_op jit(solution)/shard_map/ppermute | solution.py:309
  19.7 0.1 collective-permute-start.8
  19.8 4.9 %collective-permute-done.5.refs_9_ = bf16[2,512,128]{2,1,0:T(8,128)(2,1)S(1)} collective-permute-done((bf16[2,512,128]{2,1,0:T(8,128)(2,1)S(1)}, bf16[2,512,128]{2,1,0:T(8,128)(2,1)S(1)}, u32[]{:S(2)}, u32[]{:S(2)}) %collective-permute-start.5) | collective-permute-done | bytes 262176 | tf_op jit(solution)/shard_map/ppermute | solution.py:309
  24.7 1.3 %collective-permute-start.11 = (bf16[512,128]{1,0:T(8,128)(2,1)S(1)}, bf16[512,128]{1,0:T(8,128)(2,1)S(1)}, u32[]{:S(2)}, u32[]{:S(2)}) collective-permute-start(bf16[512,128]{1,0:T(8,128)(2,1)S(1)} %get-tuple-element.26), channel_id=1, source_target_pairs={{4,1},{5,0},{6,3},{7,2},{12,9},{13,8},{14,11},{15,10},{20,17},{21,... | collective-permute-start | bytes 393224 | tf_op jit(solution)/shard_map/ppermute | solution.py:309
  26.0 1.2 collective-permute-done.9.refs_13_
  27.2 6.5 %collective-permute-done.11.refs_15_ = bf16[512,128]{1,0:T(8,128)(2,1)S(1)} collective-permute-done((bf16[512,128]{1,0:T(8,128)(2,1)S(1)}, bf16[512,128]{1,0:T(8,128)(2,1)S(1)}, u32[]{:S(2)}, u32[]{:S(2)}) %collective-permute-start.11) | collective-permute-done | bytes 131104 | tf_op jit(solution)/shard_map/ppermute | solution.py:309
  33.7 1.3 collective-permute-done.12.refs_16_
  35.1 0.7 copy-done.15
  35.8 55.4 %attention.1 = (bf16[4,512,128]{2,1,0:T(8,128)(2,1)}, bf16[4,512,128]{2,1,0:T(8,128)(2,1)}, bf16[3,2,512,128]{3,2,1,0:T(8,128)(2,1)}, bf16[3,2,512,128]{3,2,1,0:...) custom-call(s32[16]{0:T(128)} %refs_0_.1, bf16[4,512,128]{2,1,0:T(8,128)(2,1)} %refs_1_.1, ...), custom_call_target="tpu_custom_call" | custom-call | flops 8589934592 | bytes 16777216 | tf_op jit(solution)/shard_map/attention/pallas_call | solution.py:270
  91.2 0.1 collective-permute-start.19
  91.3 0.5 collective-permute-start.13
  91.8 2.0 %collective-permute-done.19 = bf16[3,2,512,128]{3,2,1,0:T(8,128)(2,1)S(1)} collective-permute-done((bf16[3,2,512,128]{3,2,1,0:T(8,128)(2,1)}, bf16[3,2,512,128]{3,2,1,0:T(8,128)(2,1)S(1)}, u32[]{:S(2)}, u32[]{:S(2)}) %collective-permute-start.19) | collective-permute-done | bytes 786464 | tf_op jit(solution)/shard_map/ppermute | solution.py:304
  93.8 1.1 fusion.13
  94.9 0.1 collective-permute-start.20
  95.0 0.1 fusion.11
  95.1 3.3 %collective-permute-start.14 = (bf16[512,128]{1,0:T(8,128)(2,1)S(1)}, bf16[512,128]{1,0:T(8,128)(2,1)S(1)}, u32[]{:S(2)}, u32[]{:S(2)}) collective-permute-start(bf16[512,128]{1,0:T(8,128)(2,1)S(1)} %get-tuple-element.25), channel_id=1, source_target_pairs={{0,5},{1,4},{4,1},{5,0},{2,7},{3,6},{6,3},{7,2},{8,13},{9,12},{12,... | collective-permute-start | bytes 393224 | tf_op jit(solution)/shard_map/ppermute | solution.py:309
  98.4 4.1 %collective-permute-done.20 = bf16[512,128]{1,0:T(8,128)(2,1)S(1)} collective-permute-done((bf16[512,128]{1,0:T(8,128)(2,1)S(1)}, bf16[512,128]{1,0:T(8,128)(2,1)S(1)}, u32[]{:S(2)}, u32[]{:S(2)}) %collective-permute-start.20) | collective-permute-done | bytes 131104 | tf_op jit(solution)/shard_map/ppermute | solution.py:309
  102.6 0.1 collective-permute-start.22
  102.7 1.8 %collective-permute-done.14 = bf16[512,128]{1,0:T(8,128)(2,1)S(1)} collective-permute-done((bf16[512,128]{1,0:T(8,128)(2,1)S(1)}, bf16[512,128]{1,0:T(8,128)(2,1)S(1)}, u32[]{:S(2)}, u32[]{:S(2)}) %collective-permute-start.14) | collective-permute-done | bytes 131104 | tf_op jit(solution)/shard_map/ppermute | solution.py:309
  104.5 1.5 %collective-permute-start.15 = (bf16[512,128]{1,0:T(8,128)(2,1)S(1)}, bf16[512,128]{1,0:T(8,128)(2,1)S(1)}, u32[]{:S(2)}, u32[]{:S(2)}) collective-permute-start(bf16[512,128]{1,0:T(8,128)(2,1)S(1)} %get-tuple-element.18), channel_id=1, source_target_pairs={{0,5},{1,4},{4,1},{5,0},{2,7},{3,6},{6,3},{7,2},{8,13},{9,12},{12,... | collective-permute-start | bytes 393224 | tf_op jit(solution)/shard_map/ppermute | solution.py:309
  106.0 0.1 fusion.5
  106.1 0.1 collective-permute-start.16
  106.2 3.6 %collective-permute-done.21 = bf16[512,128]{1,0:T(8,128)(2,1)S(1)} collective-permute-done((bf16[512,128]{1,0:T(8,128)(2,1)S(1)}, bf16[512,128]{1,0:T(8,128)(2,1)S(1)}, u32[]{:S(2)}, u32[]{:S(2)}) %collective-permute-start.21) | collective-permute-done | bytes 131104 | tf_op jit(solution)/shard_map/ppermute | solution.py:309
  109.8 2.2 %collective-permute-done.22 = bf16[512,128]{1,0:T(8,128)(2,1)S(1)} collective-permute-done((bf16[512,128]{1,0:T(8,128)(2,1)S(1)}, bf16[512,128]{1,0:T(8,128)(2,1)S(1)}, u32[]{:S(2)}, u32[]{:S(2)}) %collective-permute-start.22) | collective-permute-done | bytes 131104 | tf_op jit(solution)/shard_map/ppermute | solution.py:317
  112.1 0.1 fusion.2
  112.2 0.1 collective-permute-start.23
  112.2 2.2 %collective-permute-done.16 = bf16[512,128]{1,0:T(8,128)(2,1)S(1)} collective-permute-done((bf16[512,128]{1,0:T(8,128)(2,1)S(1)}, bf16[512,128]{1,0:T(8,128)(2,1)S(1)}, u32[]{:S(2)}, u32[]{:S(2)}) %collective-permute-start.16) | collective-permute-done | bytes 131104 | tf_op jit(solution)/shard_map/ppermute | solution.py:317
  114.5 0.1 fusion.7
  114.5 0.1 collective-permute-start.17
  114.6 6.5 %collective-permute-done.23 = bf16[512,128]{1,0:T(8,128)(2,1)S(1)} collective-permute-done((bf16[512,128]{1,0:T(8,128)(2,1)S(1)}, bf16[512,128]{1,0:T(8,128)(2,1)S(1)}, u32[]{:S(2)}, u32[]{:S(2)}) %collective-permute-start.23) | collective-permute-done | bytes 131104 | tf_op jit(solution)/shard_map/ppermute | solution.py:317
  121.1 0.1 fusion.4
  121.2 0.1 collective-permute-start.24
  121.3 1.6 %collective-permute-done.17 = bf16[512,128]{1,0:T(8,128)(2,1)S(1)} collective-permute-done((bf16[512,128]{1,0:T(8,128)(2,1)S(1)}, bf16[512,128]{1,0:T(8,128)(2,1)S(1)}, u32[]{:S(2)}, u32[]{:S(2)}) %collective-permute-start.17) | collective-permute-done | bytes 131104 | tf_op jit(solution)/shard_map/ppermute | solution.py:317
  122.9 0.1 fusion.9
  123.0 0.5 collective-permute-start.18
  123.4 2.8 %collective-permute-done.24 = bf16[512,128]{1,0:T(8,128)(2,1)S(1)} collective-permute-done((bf16[512,128]{1,0:T(8,128)(2,1)S(1)}, bf16[512,128]{1,0:T(8,128)(2,1)S(1)}, u32[]{:S(2)}, u32[]{:S(2)}) %collective-permute-start.24) | collective-permute-done | bytes 131104 | tf_op jit(solution)/shard_map/ppermute | solution.py:313
  126.2 0.7 add_convert_fusion
  126.9 1.1 collective-permute-done.18
  128.0 0.7 add_convert_fusion.3
  (47 shorter events, 0.2 us)
Async XLA Ops:
  1.6 16.7 %copy-start.2 = (bf16[2,512,128]{2,1,0:T(8,128)(2,1)}, bf16[2,512,128]{2,1,0:T(8,128)(2,1)S(1)}, u32[]{:S(2)}) copy-start(bf16[2,512,128]{2,1,0:T(8,128)(2,1)S(1)} %pad_maximum_fusion.refs_3_) | copy-start | bytes 786436
  1.6 8.1 %collective-permute-start.3 = (bf16[2,512,128]{2,1,0:T(8,128)(2,1)S(1)}, bf16[2,512,128]{2,1,0:T(8,128)(2,1)S(1)}, u32[]{:S(2)}, u32[]{:S(2)}) collective-permute-start(bf16[2,512,128]{2,1,0:T(8,128)(2,1)S(1)} %pad_maximum_fusion.refs_3_), channel_id=1, source_target_pairs={{0,8},{8,16},{16,24},{24,32},{32,40},{40,48},{48,56},{56,64},{64,7... | collective-permute-start | bytes 786440 | tf_op jit(solution)/shard_map/ppermute | solution.py:317
  1.8 11.6 %collective-permute-start.1 = (bf16[2,512,128]{2,1,0:T(8,128)(2,1)S(1)}, bf16[2,512,128]{2,1,0:T(8,128)(2,1)S(1)}, u32[]{:S(2)}, u32[]{:S(2)}) collective-permute-start(bf16[2,512,128]{2,1,0:T(8,128)(2,1)S(1)} %pad_maximum_fusion.refs_3_), channel_id=1, source_target_pairs={{0,5},{1,4},{2,7},{3,6},{8,13},{9,12},{10,15},{11,14},{16,21},{17,... | collective-permute-start | bytes 786440 | tf_op jit(solution)/shard_map/ppermute | solution.py:309
  9.8 25.3 %copy-start.4 = (bf16[2,512,128]{2,1,0:T(8,128)(2,1)}, bf16[2,512,128]{2,1,0:T(8,128)(2,1)S(1)}, u32[]{:S(2)}) copy-start(bf16[2,512,128]{2,1,0:T(8,128)(2,1)S(1)} %collective-permute-done.3.refs_7_) | copy-start | bytes 786436
  9.8 8.6 %collective-permute-start.7 = (bf16[2,512,128]{2,1,0:T(8,128)(2,1)S(1)}, bf16[2,512,128]{2,1,0:T(8,128)(2,1)S(1)}, u32[]{:S(2)}, u32[]{:S(2)}) collective-permute-start(bf16[2,512,128]{2,1,0:T(8,128)(2,1)S(1)} %collective-permute-done.3.refs_7_), channel_id=1, source_target_pairs={{0,8},{8,16},{16,24},{24,32},{32,40},{40,48},{48,56},{56,64},{64,7... | collective-permute-start | bytes 786440 | tf_op jit(solution)/shard_map/ppermute | solution.py:317
  13.4 6.3 %collective-permute-start = (bf16[2,512,128]{2,1,0:T(8,128)(2,1)S(1)}, bf16[2,512,128]{2,1,0:T(8,128)(2,1)S(1)}, u32[]{:S(2)}, u32[]{:S(2)}) collective-permute-start(bf16[2,512,128]{2,1,0:T(8,128)(2,1)S(1)} %pad_maximum_fusion.refs_3_), channel_id=1, source_target_pairs={{0,2},{2,0},{1,3},{3,1},{4,6},{6,4},{5,7},{7,5},{8,10},{10,8},{9,1... | collective-permute-start | bytes 786440 | tf_op jit(solution)/shard_map/ppermute | solution.py:304
  13.4 21.6 %copy-start.5 = (bf16[2,512,128]{2,1,0:T(8,128)(2,1)}, bf16[2,512,128]{2,1,0:T(8,128)(2,1)S(1)}, u32[]{:S(2)}) copy-start(bf16[2,512,128]{2,1,0:T(8,128)(2,1)S(1)} %collective-permute-done.1.refs_5_) | copy-start | bytes 786436
  13.4 11.3 %collective-permute-start.5 = (bf16[2,512,128]{2,1,0:T(8,128)(2,1)S(1)}, bf16[2,512,128]{2,1,0:T(8,128)(2,1)S(1)}, u32[]{:S(2)}, u32[]{:S(2)}) collective-permute-start(bf16[2,512,128]{2,1,0:T(8,128)(2,1)S(1)} %collective-permute-done.3.refs_7_), channel_id=1, source_target_pairs={{0,5},{1,4},{4,1},{5,0},{2,7},{3,6},{6,3},{7,2},{8,13},{9,12},{12,... | collective-permute-start | bytes 786440 | tf_op jit(solution)/shard_map/ppermute | solution.py:309
  17.5 7.2 %collective-permute-start.4 = (bf16[2,512,128]{2,1,0:T(8,128)(2,1)S(1)}, bf16[2,512,128]{2,1,0:T(8,128)(2,1)S(1)}, u32[]{:S(2)}, u32[]{:S(2)}) collective-permute-start(bf16[2,512,128]{2,1,0:T(8,128)(2,1)S(1)} %collective-permute-done.3.refs_7_), channel_id=1, source_target_pairs={{0,2},{2,0},{1,3},{3,1},{4,6},{6,4},{5,7},{7,5},{8,10},{10,8},{9,1... | collective-permute-start | bytes 786440 | tf_op jit(solution)/shard_map/ppermute | solution.py:304
  17.6 16.0 %collective-permute-start.2 = (bf16[2,512,128]{2,1,0:T(8,128)(2,1)S(1)}, bf16[2,512,128]{2,1,0:T(8,128)(2,1)S(1)}, u32[]{:S(2)}, u32[]{:S(2)}) collective-permute-start(bf16[2,512,128]{2,1,0:T(8,128)(2,1)S(1)} %collective-permute-done.1.refs_5_), channel_id=1, source_target_pairs={{0,2},{2,0},{1,3},{3,1},{4,6},{6,4},{5,7},{7,5},{8,10},{10,8},{9,1... | collective-permute-start | bytes 786440 | tf_op jit(solution)/shard_map/ppermute | solution.py:304
  18.3 1.3 %copy-start.3 = (bf16[2,512,128]{2,1,0:T(8,128)(2,1)}, bf16[2,512,128]{2,1,0:T(8,128)(2,1)S(1)}, u32[]{:S(2)}) copy-start(bf16[2,512,128]{2,1,0:T(8,128)(2,1)S(1)} %collective-permute-done.7.refs_11_) | copy-start | bytes 786436
  18.4 8.8 %collective-permute-start.9 = (bf16[512,128]{1,0:T(8,128)(2,1)S(1)}, bf16[512,128]{1,0:T(8,128)(2,1)S(1)}, u32[]{:S(2)}, u32[]{:S(2)}) collective-permute-start(bf16[512,128]{1,0:T(8,128)(2,1)S(1)} %get-tuple-element.27), channel_id=1, source_target_pairs={{4,1},{5,0},{6,3},{7,2},{12,9},{13,8},{14,11},{15,10},{20,17},{21,... | collective-permute-start | bytes 393224 | tf_op jit(solution)/shard_map/ppermute | solution.py:309
  19.7 15.3 %copy-start.6 = (bf16[2,512,128]{2,1,0:T(8,128)(2,1)}, bf16[2,512,128]{2,1,0:T(8,128)(2,1)S(1)}, u32[]{:S(2)}) copy-start(bf16[2,512,128]{2,1,0:T(8,128)(2,1)S(1)} %collective-permute-done.refs_4_) | copy-start | bytes 786436
  19.7 14.0 %collective-permute-start.8 = (bf16[2,512,128]{2,1,0:T(8,128)(2,1)S(1)}, bf16[2,512,128]{2,1,0:T(8,128)(2,1)S(1)}, u32[]{:S(2)}, u32[]{:S(2)}) collective-permute-start(bf16[2,512,128]{2,1,0:T(8,128)(2,1)S(1)} %collective-permute-done.7.refs_11_), channel_id=1, source_target_pairs={{0,2},{2,0},{1,3},{3,1},{4,6},{6,4},{5,7},{7,5},{8,10},{10,8},{9,1... | collective-permute-start | bytes 786440 | tf_op jit(solution)/shard_map/ppermute | solution.py:304
  24.6 10.4 %copy-start.7 = (bf16[2,512,128]{2,1,0:T(8,128)(2,1)}, bf16[2,512,128]{2,1,0:T(8,128)(2,1)S(1)}, u32[]{:S(2)}) copy-start(bf16[2,512,128]{2,1,0:T(8,128)(2,1)S(1)} %collective-permute-done.5.refs_9_) | copy-start | bytes 786436
  24.6 9.0 %collective-permute-start.6 = (bf16[2,512,128]{2,1,0:T(8,128)(2,1)S(1)}, bf16[2,512,128]{2,1,0:T(8,128)(2,1)S(1)}, u32[]{:S(2)}, u32[]{:S(2)}) collective-permute-start(bf16[2,512,128]{2,1,0:T(8,128)(2,1)S(1)} %collective-permute-done.5.refs_9_), channel_id=1, source_target_pairs={{0,2},{2,0},{1,3},{3,1},{4,6},{6,4},{5,7},{7,5},{8,10},{10,8},{9,1... | collective-permute-start | bytes 786440 | tf_op jit(solution)/shard_map/ppermute | solution.py:304
  24.7 10.4 %copy-start.8 = (bf16[2,512,128]{2,1,0:T(8,128)(2,1)}, bf16[2,512,128]{2,1,0:T(8,128)(2,1)S(1)}, u32[]{:S(2)}) copy-start(bf16[2,512,128]{2,1,0:T(8,128)(2,1)S(1)} %collective-permute-done.4.refs_8_) | copy-start | bytes 786436
  24.7 9.0 %collective-permute-start.11 = (bf16[512,128]{1,0:T(8,128)(2,1)S(1)}, bf16[512,128]{1,0:T(8,128)(2,1)S(1)}, u32[]{:S(2)}, u32[]{:S(2)}) collective-permute-start(bf16[512,128]{1,0:T(8,128)(2,1)S(1)} %get-tuple-element.26), channel_id=1, source_target_pairs={{4,1},{5,0},{6,3},{7,2},{12,9},{13,8},{14,11},{15,10},{20,17},{21,... | collective-permute-start | bytes 393224 | tf_op jit(solution)/shard_map/ppermute | solution.py:309
  27.2 7.9 %copy-start.12 = (bf16[512,128]{1,0:T(8,128)(2,1)}, bf16[512,128]{1,0:T(8,128)(2,1)S(1)}, u32[]{:S(2)}) copy-start(bf16[512,128]{1,0:T(8,128)(2,1)S(1)} %collective-permute-done.9.refs_13_) | copy-start | bytes 393220
  27.2 6.5 %collective-permute-start.10 = (bf16[512,128]{1,0:T(8,128)(2,1)S(1)}, bf16[512,128]{1,0:T(8,128)(2,1)S(1)}, u32[]{:S(2)}, u32[]{:S(2)}) collective-permute-start(bf16[512,128]{1,0:T(8,128)(2,1)S(1)} %collective-permute-done.9.refs_13_), channel_id=1, source_target_pairs={{0,2},{2,0},{1,3},{3,1},{4,6},{6,4},{5,7},{7,5},{8,10},{10,8},{9,1... | collective-permute-start | bytes 393224 | tf_op jit(solution)/shard_map/ppermute | solution.py:304
  33.7 1.4 %copy-start.13 = (bf16[512,128]{1,0:T(8,128)(2,1)}, bf16[512,128]{1,0:T(8,128)(2,1)S(1)}, u32[]{:S(2)}) copy-start(bf16[512,128]{1,0:T(8,128)(2,1)S(1)} %collective-permute-done.11.refs_15_) | copy-start | bytes 393220
  33.7 1.3 %collective-permute-start.12 = (bf16[512,128]{1,0:T(8,128)(2,1)S(1)}, bf16[512,128]{1,0:T(8,128)(2,1)S(1)}, u32[]{:S(2)}, u32[]{:S(2)}) collective-permute-start(bf16[512,128]{1,0:T(8,128)(2,1)S(1)} %collective-permute-done.11.refs_15_), channel_id=1, source_target_pairs={{0,2},{2,0},{1,3},{3,1},{4,6},{6,4},{5,7},{7,5},{8,10},{10,8},{9,1... | collective-permute-start | bytes 393224 | tf_op jit(solution)/shard_map/ppermute | solution.py:304
  33.7 1.4 %copy-start.9 = (bf16[2,512,128]{2,1,0:T(8,128)(2,1)}, bf16[2,512,128]{2,1,0:T(8,128)(2,1)S(1)}, u32[]{:S(2)}) copy-start(bf16[2,512,128]{2,1,0:T(8,128)(2,1)S(1)} %collective-permute-done.2.refs_6_) | copy-start | bytes 786436
  33.7 1.4 %copy-start.11 = (bf16[2,512,128]{2,1,0:T(8,128)(2,1)}, bf16[2,512,128]{2,1,0:T(8,128)(2,1)S(1)}, u32[]{:S(2)}) copy-start(bf16[2,512,128]{2,1,0:T(8,128)(2,1)S(1)} %collective-permute-done.6.refs_10_) | copy-start | bytes 786436
  33.7 1.4 %copy-start.10 = (bf16[2,512,128]{2,1,0:T(8,128)(2,1)}, bf16[2,512,128]{2,1,0:T(8,128)(2,1)S(1)}, u32[]{:S(2)}) copy-start(bf16[2,512,128]{2,1,0:T(8,128)(2,1)S(1)} %collective-permute-done.8.refs_12_) | copy-start | bytes 786436
  33.7 1.4 %copy-start.14 = (bf16[512,128]{1,0:T(8,128)(2,1)}, bf16[512,128]{1,0:T(8,128)(2,1)S(1)}, u32[]{:S(2)}) copy-start(bf16[512,128]{1,0:T(8,128)(2,1)S(1)} %collective-permute-done.10.refs_14_) | copy-start | bytes 393220
  35.1 0.7 copy-start.15
  91.2 3.8 %copy-start = (bf16[3,2,512,128]{3,2,1,0:T(8,128)(2,1)S(1)}, bf16[3,2,512,128]{3,2,1,0:T(8,128)(2,1)}, u32[]{:S(2)}) copy-start(bf16[3,2,512,128]{3,2,1,0:T(8,128)(2,1)} %get-tuple-element.16) | copy-start | bytes 2359300
  91.2 2.6 %collective-permute-start.19 = (bf16[3,2,512,128]{3,2,1,0:T(8,128)(2,1)}, bf16[3,2,512,128]{3,2,1,0:T(8,128)(2,1)S(1)}, u32[]{:S(2)}, u32[]{:S(2)}) collective-permute-start(bf16[3,2,512,128]{3,2,1,0:T(8,128)(2,1)} %get-tuple-element.20), channel_id=1, source_target_pairs={{0,2},{2,0},{1,3},{3,1},{4,6},{6,4},{5,7},{7,5},{8,10},{10,8},{9,1... | collective-permute-start | bytes 2359304 | tf_op jit(solution)/shard_map/ppermute | solution.py:304
  91.3 3.7 %collective-permute-start.13 = (bf16[3,2,512,128]{3,2,1,0:T(8,128)(2,1)}, bf16[3,2,512,128]{3,2,1,0:T(8,128)(2,1)S(1)}, u32[]{:S(2)}, u32[]{:S(2)}) collective-permute-start(bf16[3,2,512,128]{3,2,1,0:T(8,128)(2,1)} %get-tuple-element.17), channel_id=1, source_target_pairs={{0,2},{2,0},{1,3},{3,1},{4,6},{6,4},{5,7},{7,5},{8,10},{10,8},{9,1... | collective-permute-start | bytes 2359304 | tf_op jit(solution)/shard_map/ppermute | solution.py:304
  94.9 7.7 %copy-start.1 = (bf16[3,2,512,128]{3,2,1,0:T(8,128)(2,1)S(1)}, bf16[3,2,512,128]{3,2,1,0:T(8,128)(2,1)}, u32[]{:S(2)}) copy-start(bf16[3,2,512,128]{3,2,1,0:T(8,128)(2,1)} %get-tuple-element.19) | copy-start | bytes 2359300
  94.9 7.7 %collective-permute-start.20 = (bf16[512,128]{1,0:T(8,128)(2,1)S(1)}, bf16[512,128]{1,0:T(8,128)(2,1)S(1)}, u32[]{:S(2)}, u32[]{:S(2)}) collective-permute-start(bf16[512,128]{1,0:T(8,128)(2,1)S(1)} %get-tuple-element.23), channel_id=1, source_target_pairs={{0,5},{1,4},{4,1},{5,0},{2,7},{3,6},{6,3},{7,2},{8,13},{9,12},{12,... | collective-permute-start | bytes 393224 | tf_op jit(solution)/shard_map/ppermute | solution.py:309
  95.1 9.4 %collective-permute-start.14 = (bf16[512,128]{1,0:T(8,128)(2,1)S(1)}, bf16[512,128]{1,0:T(8,128)(2,1)S(1)}, u32[]{:S(2)}, u32[]{:S(2)}) collective-permute-start(bf16[512,128]{1,0:T(8,128)(2,1)S(1)} %get-tuple-element.25), channel_id=1, source_target_pairs={{0,5},{1,4},{4,1},{5,0},{2,7},{3,6},{6,3},{7,2},{8,13},{9,12},{12,... | collective-permute-start | bytes 393224 | tf_op jit(solution)/shard_map/ppermute | solution.py:309
  102.6 7.3 %collective-permute-start.21 = (bf16[512,128]{1,0:T(8,128)(2,1)S(1)}, bf16[512,128]{1,0:T(8,128)(2,1)S(1)}, u32[]{:S(2)}, u32[]{:S(2)}) collective-permute-start(bf16[512,128]{1,0:T(8,128)(2,1)S(1)} %get-tuple-element.21), channel_id=1, source_target_pairs={{0,5},{1,4},{4,1},{5,0},{2,7},{3,6},{6,3},{7,2},{8,13},{9,12},{12,... | collective-permute-start | bytes 393224 | tf_op jit(solution)/shard_map/ppermute | solution.py:309
  102.6 9.4 %collective-permute-start.22 = (bf16[512,128]{1,0:T(8,128)(2,1)S(1)}, bf16[512,128]{1,0:T(8,128)(2,1)S(1)}, u32[]{:S(2)}, u32[]{:S(2)}) collective-permute-start(bf16[512,128]{1,0:T(8,128)(2,1)S(1)} %fusion), channel_id=1, source_target_pairs={{0,120},{8,0},{16,8},{24,16},{32,24},{40,32},{48,40},{56,48},{64,5... | collective-permute-start | bytes 393224 | tf_op jit(solution)/shard_map/ppermute | solution.py:317
  104.5 7.7 %collective-permute-start.15 = (bf16[512,128]{1,0:T(8,128)(2,1)S(1)}, bf16[512,128]{1,0:T(8,128)(2,1)S(1)}, u32[]{:S(2)}, u32[]{:S(2)}) collective-permute-start(bf16[512,128]{1,0:T(8,128)(2,1)S(1)} %get-tuple-element.18), channel_id=1, source_target_pairs={{0,5},{1,4},{4,1},{5,0},{2,7},{3,6},{6,3},{7,2},{8,13},{9,12},{12,... | collective-permute-start | bytes 393224 | tf_op jit(solution)/shard_map/ppermute | solution.py:309
  106.1 8.4 %collective-permute-start.16 = (bf16[512,128]{1,0:T(8,128)(2,1)S(1)}, bf16[512,128]{1,0:T(8,128)(2,1)S(1)}, u32[]{:S(2)}, u32[]{:S(2)}) collective-permute-start(bf16[512,128]{1,0:T(8,128)(2,1)S(1)} %fusion.5), channel_id=1, source_target_pairs={{0,120},{8,0},{16,8},{24,16},{32,24},{40,32},{48,40},{56,48},{64,5... | collective-permute-start | bytes 393224 | tf_op jit(solution)/shard_map/ppermute | solution.py:317
  112.2 8.9 %collective-permute-start.23 = (bf16[512,128]{1,0:T(8,128)(2,1)S(1)}, bf16[512,128]{1,0:T(8,128)(2,1)S(1)}, u32[]{:S(2)}, u32[]{:S(2)}) collective-permute-start(bf16[512,128]{1,0:T(8,128)(2,1)S(1)} %fusion.2), channel_id=1, source_target_pairs={{0,120},{8,0},{16,8},{24,16},{32,24},{40,32},{48,40},{56,48},{64,5... | collective-permute-start | bytes 393224 | tf_op jit(solution)/shard_map/ppermute | solution.py:317
  114.5 8.4 %collective-permute-start.17 = (bf16[512,128]{1,0:T(8,128)(2,1)S(1)}, bf16[512,128]{1,0:T(8,128)(2,1)S(1)}, u32[]{:S(2)}, u32[]{:S(2)}) collective-permute-start(bf16[512,128]{1,0:T(8,128)(2,1)S(1)} %fusion.7), channel_id=1, source_target_pairs={{0,120},{8,0},{16,8},{24,16},{32,24},{40,32},{48,40},{56,48},{64,5... | collective-permute-start | bytes 393224 | tf_op jit(solution)/shard_map/ppermute | solution.py:317
  121.2 5.0 %collective-permute-start.24 = (bf16[512,128]{1,0:T(8,128)(2,1)S(1)}, bf16[512,128]{1,0:T(8,128)(2,1)S(1)}, u32[]{:S(2)}, u32[]{:S(2)}) collective-permute-start(bf16[512,128]{1,0:T(8,128)(2,1)S(1)} %fusion.4), channel_id=1, source_target_pairs={{0,1},{1,0},{2,3},{3,2},{4,5},{5,4},{6,7},{7,6},{8,9},{9,8},{10,11... | collective-permute-start | bytes 393224 | tf_op jit(solution)/shard_map/ppermute | solution.py:313
  123.0 5.0 %collective-permute-start.18 = (bf16[512,128]{1,0:T(8,128)(2,1)S(1)}, bf16[512,128]{1,0:T(8,128)(2,1)S(1)}, u32[]{:S(2)}, u32[]{:S(2)}) collective-permute-start(bf16[512,128]{1,0:T(8,128)(2,1)S(1)} %fusion.9), channel_id=1, source_target_pairs={{0,1},{1,0},{2,3},{3,2},{4,5},{5,4},{6,7},{7,6},{8,9},{9,8},{10,11... | collective-permute-start | bytes 393224 | tf_op jit(solution)/shard_map/ppermute | solution.py:313
